TPU v7x, 32 devices: a whole 2x2x4 slice. The times are simulated.
32 devices in a mesh: frames: 2 (over y), gz: 16 (over z, x, core).
Axes of the slice: x: 2, y: 2, z: 4, core: 2. Of those that a mesh axis runs over, the one named last changes fastest.
Arguments:
- volume: float32 [64, 512, 1024], P('gz', 'frames'), parts along dimension 1, may hold values from -6 to 6
- tf_index: int32 [64, 512, 1024], P('gz', 'frames'), parts along dimension 1, may hold values from 0 to 7
- tf_color: float32 [3, 8], replicated, may hold values from 0.2 to 1
- tf_opacity: float32 [8], replicated, may hold values from 0.003 to 0.03
- order: int32 [32], P('frames'), parts along dimension 0, may hold values from 0 to 15, each once
Outputs:
- image: float32 [8, 256, 1024], P('frames', 'gz'), parts along dimension 0
There are 2 independent parts, one for each index of `frames`. A program takes and returns all parts, laid end to end along the dimension named above; an argument that names none is the same for every part. Nothing has to cross between parts.
Inputs may be any that keep to these rules, and one draw needn't show every extreme that they name: `order`: each brick has a distinct rank; every rank of 0 to 15 appears once.
All inputs are finite; a program needn't handle non-finite values.
Results may differ from a plain program's by a relative error of at most 0.00076.
Values may be sent and summed in bfloat16 or wider, within the bound.
No kernel may reach another device: no remote copies, remote signals or barrier semaphores. Data moves between devices by JAX's collectives and lax.ppermute only.
A program may use at most 128 MiB of HBM per device.

v0:
```python
import jax
import jax.numpy as jnp
from jax import lax
from jax.sharding import PartitionSpec as P


def extended(x, sides, width):
    for axis, dim in sides:
        size, length = (lax.axis_size(axis), x.shape[dim])
        up = [(i, (i + 1) % size) for i in range(size - 1)]
        down = [(j, i) for i, j in up]
        last = lax.slice_in_dim(x, length - width, length, axis=dim)
        initial = lax.slice_in_dim(x, 0, width, axis=dim)
        before = lax.ppermute(last, axis, up)
        after = lax.ppermute(initial, axis, down)
        x = jnp.concatenate([before, x, after], axis=dim)
    return x


def sample_brick(padded, materials_here, tf_color, tf_opacity):
    centre = padded[1:-1]
    grad_depth = 0.5 * (padded[2:] - padded[:-2])
    rows_padded = jnp.pad(centre, ((0, 0), (1, 1), (0, 0)))
    grad_row = 0.5 * (rows_padded[:, 2:] - rows_padded[:, :-2])
    cols_padded = jnp.pad(centre, ((0, 0), (0, 0), (1, 1)))
    grad_col = 0.5 * (cols_padded[:, :, 2:] - cols_padded[:, :, :-2])
    facing = jnp.abs(0.48 * grad_depth + 0.6 * grad_row + 0.64 * grad_col)
    shading = 0.35 + 0.65 * facing / jnp.sqrt(
        grad_depth * grad_depth + grad_row * grad_row + grad_col * grad_col + 1.0
    )
    opacity_cell = jnp.zeros_like(centre)
    tint_cell = jnp.zeros((3,) + centre.shape, centre.dtype)
    for material in range(tf_opacity.shape[0]):
        matches = materials_here == material
        opacity_cell = jnp.where(matches, tf_opacity[material], opacity_cell)
        tint_cell = jnp.where(matches[None], tf_color[:, material][:, None, None, None], tint_cell)
    alphas_cell = opacity_cell * (1.0 - jnp.exp(-centre * centre))
    colour = tint_cell * (shading * alphas_cell)[None]

    def advance(carry, sample_pair):
        colour_sum, transmit = carry
        alpha_slice, colour_slice = sample_pair
        return ((colour_sum + transmit[None] * colour_slice, transmit * (1.0 - alpha_slice)), None)

    initial = (
        jnp.zeros((3,) + centre.shape[1:], centre.dtype),
        jnp.ones(centre.shape[1:], centre.dtype),
    )
    (colour_sum, transmit), _ = lax.scan(
        advance, initial, (alphas_cell, jnp.moveaxis(colour, 1, 0))
    )
    return jnp.concatenate([colour_sum, (1.0 - transmit)[None]], 0).astype(jnp.bfloat16)


def over_stack(front_layers, back_layers):
    return front_layers + (1.0 - front_layers[:, 3:4]) * back_layers


def composite(layers_stack):
    layers = layers_stack.astype(jnp.float32)
    while layers.shape[0] > 1:
        layers = over_stack(layers[0::2], layers[1::2])
    return layers[0]


def shards(volume, tf_index, tf_color, tf_opacity, order):
    padded = extended(volume, (("gz", 0),), 1)
    partial_value = sample_brick(padded, tf_index, tf_color, tf_opacity)
    devices = lax.axis_size("gz")
    places = jnp.arange(devices, dtype=jnp.int32)
    inverse = jnp.zeros((devices,), jnp.int32).at[order].set(places)
    return composite(
        jnp.take(
            lax.all_to_all(partial_value[None], "gz", split_axis=2, concat_axis=0, tiled=True),
            inverse,
            axis=0,
        )
    )


def solution(mesh):
    placed = (P("gz", "frames", None), P("gz", "frames", None), P(), P(), P("frames"))
    return jax.shard_map(
        shards, mesh=mesh, in_specs=placed, out_specs=P("frames", "gz", None), check_vma=False
    )
```

profile of v0, /device:TPU:13, one launch (start us, length us, event | category | flops | bytes accessed | tf_op | source)
XLA Modules:
  0.0 151.8 jit_solution(1842459133493196575)
XLA Ops:
  0.0 3.3 %fusion.15 = (f32[1,256,1024]{2,1,0:T(8,128)}, f32[1,256,1024]{2,1,0:T(8,128)}) fusion(f32[4,256,1024]{2,1,0:T(8,128)} %param.7), kind=kLoop, calls=%fused_computation.60 | loop fusion | bytes 4194304 | tf_op jit(solution)/shard_map/slice | solution.py:13
  3.3 2.6 %collective-permute-start = (f32[1,256,1024]{2,1,0:T(8,128)}, f32[1,256,1024]{2,1,0:T(8,128)}, u32[]{:S(2)}, u32[]{:S(2)}) collective-permute-start(f32[1,256,1024]{2,1,0:T(8,128)} %get-tuple-element.82), channel_id=1, source_target_pairs={{1,0},{2,1},{3,2},{4,3},{5,4},{6,5},{7,6},{8,7},{9,8},{10,9},{11,1... | collective-permute-start | bytes 3145736 | tf_op jit(solution)/shard_map/ppermute | solution.py:15
  5.9 3.0 %collective-permute-start.1 = (f32[1,256,1024]{2,1,0:T(8,128)}, f32[1,256,1024]{2,1,0:T(8,128)}, u32[]{:S(2)}, u32[]{:S(2)}) collective-permute-start(f32[1,256,1024]{2,1,0:T(8,128)} %get-tuple-element.83), channel_id=1, source_target_pairs={{0,1},{1,2},{2,3},{3,4},{4,5},{5,6},{6,7},{7,8},{8,9},{9,10},{10,1... | collective-permute-start | bytes 3145736 | tf_op jit(solution)/shard_map/ppermute | solution.py:14
  8.9 0.7 fusion.16
  9.6 15.1 %fusion.4 = (f32[4,256,1024]{2,1,0:T(8,128)}, pred[4,256,1024]{2,1,0:T(8,128)(4,1)}, pred[4,256,1024]{2,1,0:T(8,128)(4,1)}, pred[4,256,1024]{2,1,0:T(8,128)(4,1)...) fusion(f32[4,256,1024]{2,1,0:T(8,128)S(1)} %copy-done.1, ...), kind=kLoop, calls=%fused_computation.13 | loop fusion | flops 20971520 | bytes 20971552 | tf_op jit(solution)/shard_map/mul | solution.py:37
  24.7 0.3 slice_reduce_fusion.7
  25.0 6.0 %collective-permute-done = f32[1,256,1024]{2,1,0:T(8,128)} collective-permute-done((f32[1,256,1024]{2,1,0:T(8,128)}, f32[1,256,1024]{2,1,0:T(8,128)}, u32[]{:S(2)}, u32[]{:S(2)}) %collective-permute-start) | collective-permute-done | bytes 1048608 | tf_op jit(solution)/shard_map/ppermute | solution.py:15
  31.0 0.2 collective-permute-done.1
  31.2 22.5 %add_multiply_fusion = f32[4,256,1024]{2,1,0:T(8,128)S(1)} fusion(f32[4,256,1024]{2,1,0:T(8,128)} %param.7, f32[1,256,1024]{2,1,0:T(8,128)} %collective-permute-done.1, f32[1,256,1024]{2,1,0:T(8,128)} %collective-permute-done, pred[4,256,1024]{2,1,0:T(8,128)(4,1)} %get-tuple-element.81, pred[4,256,1024]{2,1,0:T(8,128)(4,1)} %get-tuple-element.80, ...), kind=kLoop, calls=%fused_computation.17 | loop fusion | flops 37748736 | bytes 18874400 | tf_op jit(solution)/shard_map/mul | solution.py:38
  53.7 9.9 %select_multiply_fusion = f32[4,3,256,1024]{3,2,1,0:T(8,128)} fusion(f32[4,256,1024]{2,1,0:T(8,128)S(1)} %add_multiply_fusion, f32[3]{0:T(128)S(1)} %get-tuple-element.59, f32[3]{0:T(128)S(1)} %get-tuple-element.60, f32[3]{0:T(128)S(1)} %get-tuple-element.54, f32[3]{0:T(128)S(1)} %get-tuple-element.55, f32[3]{0:T(128)S(1)} %get-tuple-element.56, ...), kind=kLoop, calls=%fused_computation.6 | loop fusion | flops 28311552 | bytes 25165920 | tf_op jit(solution)/shard_map/mul | solution.py:38
  63.6 23.2 %while.13 = (s32[]{:T(128)}, f32[3,256,1024]{2,1,0:T(8,128)S(1)}, f32[256,1024]{1,0:T(8,128)}, f32[4,3,256,1024]{3,2,1,0:T(8,128)}, f32[4,256,1024]{2,1,0:T(8,128)}, /*index=5*/s32[]{:T(128)}, s32[]{:T(128)}) while((s32[]{:T(128)}, f32[3,256,1024]{2,1,0:T(8,128)S(1)}, f32[256,1024]{1,0:T(8,128)}, f32[4,3,256,1024]{3,2,1,0:T(8,128)}, ...), condition=%wide.region_2.3_spmd.clone, body=%wide.region_1.2_spmd.clone.sunk | while | flops 3145731 | bytes 14680160 | solution.py:49
  63.6 2.5 %bitcast_multiply_fusion.3 = (f32[256,1024]{1,0:T(8,128)}, f32[256,1024]{1,0:T(8,128)S(1)}) fusion(f32[4,256,1024]{2,1,0:T(8,128)} %get-tuple-element.145, s32[]{:T(128)} %get-tuple-element.134, f32[256,1024]{1,0:T(8,128)} %get-tuple-element.136, pred[]{:T(512)S(6)} %compare.5), kind=kLoop, calls=%fused_computation.4.clone.1 | loop fusion | flops 786432 | bytes 4194309 | tf_op jit(solution)/shard_map/while/body/eval_jaxpr/mul | solution.py:43
  66.1 3.0 %fusion.18 = f32[3,256,1024]{2,1,0:T(8,128)S(1)} fusion(f32[3,256,1024]{2,1,0:T(8,128)S(1)} %get-tuple-element.135, f32[4,3,256,1024]{3,2,1,0:T(8,128)} %get-tuple-element.144, s32[]{:T(128)} %get-tuple-element.134, f32[256,1024]{1,0:T(8,128)S(1)} %get-tuple-element.125, pred[]{:T(512)S(6)} %compare.5), kind=kLoop, calls=%fused_computation.3.clone.1 | loop fusion | flops 2359296 | bytes 10485765 | tf_op jit(solution)/shard_map/while/body/eval_jaxpr/add | solution.py:43
  69.1 2.8 %bitcast_multiply_fusion.3 = (f32[256,1024]{1,0:T(8,128)}, f32[256,1024]{1,0:T(8,128)S(1)}) fusion(f32[4,256,1024]{2,1,0:T(8,128)} %get-tuple-element.145, s32[]{:T(128)} %get-tuple-element.134, f32[256,1024]{1,0:T(8,128)} %get-tuple-element.136, pred[]{:T(512)S(6)} %compare.5), kind=kLoop, calls=%fused_computation.4.clone.1 | loop fusion | flops 786432 | bytes 4194309 | tf_op jit(solution)/shard_map/while/body/eval_jaxpr/mul | solution.py:43
  71.9 3.0 %fusion.18 = f32[3,256,1024]{2,1,0:T(8,128)S(1)} fusion(f32[3,256,1024]{2,1,0:T(8,128)S(1)} %get-tuple-element.135, f32[4,3,256,1024]{3,2,1,0:T(8,128)} %get-tuple-element.144, s32[]{:T(128)} %get-tuple-element.134, f32[256,1024]{1,0:T(8,128)S(1)} %get-tuple-element.125, pred[]{:T(512)S(6)} %compare.5), kind=kLoop, calls=%fused_computation.3.clone.1 | loop fusion | flops 2359296 | bytes 10485765 | tf_op jit(solution)/shard_map/while/body/eval_jaxpr/add | solution.py:43
  75.0 2.8 %bitcast_multiply_fusion.3 = (f32[256,1024]{1,0:T(8,128)}, f32[256,1024]{1,0:T(8,128)S(1)}) fusion(f32[4,256,1024]{2,1,0:T(8,128)} %get-tuple-element.145, s32[]{:T(128)} %get-tuple-element.134, f32[256,1024]{1,0:T(8,128)} %get-tuple-element.136, pred[]{:T(512)S(6)} %compare.5), kind=kLoop, calls=%fused_computation.4.clone.1 | loop fusion | flops 786432 | bytes 4194309 | tf_op jit(solution)/shard_map/while/body/eval_jaxpr/mul | solution.py:43
  77.8 3.0 %fusion.18 = f32[3,256,1024]{2,1,0:T(8,128)S(1)} fusion(f32[3,256,1024]{2,1,0:T(8,128)S(1)} %get-tuple-element.135, f32[4,3,256,1024]{3,2,1,0:T(8,128)} %get-tuple-element.144, s32[]{:T(128)} %get-tuple-element.134, f32[256,1024]{1,0:T(8,128)S(1)} %get-tuple-element.125, pred[]{:T(512)S(6)} %compare.5), kind=kLoop, calls=%fused_computation.3.clone.1 | loop fusion | flops 2359296 | bytes 10485765 | tf_op jit(solution)/shard_map/while/body/eval_jaxpr/add | solution.py:43
  80.8 2.8 %bitcast_multiply_fusion.3 = (f32[256,1024]{1,0:T(8,128)}, f32[256,1024]{1,0:T(8,128)S(1)}) fusion(f32[4,256,1024]{2,1,0:T(8,128)} %get-tuple-element.145, s32[]{:T(128)} %get-tuple-element.134, f32[256,1024]{1,0:T(8,128)} %get-tuple-element.136, pred[]{:T(512)S(6)} %compare.5), kind=kLoop, calls=%fused_computation.4.clone.1 | loop fusion | flops 786432 | bytes 4194309 | tf_op jit(solution)/shard_map/while/body/eval_jaxpr/mul | solution.py:43
  83.6 3.0 %fusion.18 = f32[3,256,1024]{2,1,0:T(8,128)S(1)} fusion(f32[3,256,1024]{2,1,0:T(8,128)S(1)} %get-tuple-element.135, f32[4,3,256,1024]{3,2,1,0:T(8,128)} %get-tuple-element.144, s32[]{:T(128)} %get-tuple-element.134, f32[256,1024]{1,0:T(8,128)S(1)} %get-tuple-element.125, pred[]{:T(512)S(6)} %compare.5), kind=kLoop, calls=%fused_computation.3.clone.1 | loop fusion | flops 2359296 | bytes 10485765 | tf_op jit(solution)/shard_map/while/body/eval_jaxpr/add | solution.py:43
  86.9 0.2 convert.11
  87.1 1.4 copy.18
  88.6 0.8 copy.10
  89.4 3.3 %pad_maximum_fusion.2 = bf16[1,4,256,1024]{3,1,0,2:T(4,128)(2,1)} fusion(bf16[1,1,256,1024]{3,1,0,2:T(2,128)(2,1)S(1)} %copy.10, bf16[1,3,256,1024]{3,1,0,2:T(4,128)(2,1)S(1)} %bitcast.39), kind=kLoop, calls=%fused_computation.19 | loop fusion | flops 4194304 | bytes 4194304 | tf_op jit(solution)/shard_map/concatenate | solution.py:52
  92.7 6.3 %all-to-all-start = ((bf16[1,4,256,1024]{3,1,0,2:T(4,128)(2,1)}), bf16[1,4,256,1024]{3,1,0,2:T(4,128)(2,1)S(1)}, u32[]{:S(2)}, u32[]{:S(2)}) async-start(bf16[1,4,256,1024]{3,1,0,2:T(4,128)(2,1)} %pad_maximum_fusion.2), calls=%async_computation | async-start | bytes 4194304 | tf_op jit(solution)/shard_map/all_to_all | solution.py:74
  99.0 0.6 scatter_custom_fusion
  99.6 45.3 %all-to-all-done = bf16[1,4,256,1024]{3,1,0,2:T(4,128)(2,1)S(1)} async-done(((bf16[1,4,256,1024]{3,1,0,2:T(4,128)(2,1)}), bf16[1,4,256,1024]{3,1,0,2:T(4,128)(2,1)S(1)}, u32[]{:S(2)}, u32[]{:S(2)}) %all-to-all-start) | async-done | bytes 2097184 | tf_op jit(solution)/shard_map/all_to_all | solution.py:74
  144.9 2.1 %copy.19 = bf16[1,4,16,16,1024]{4,3,1,2,0:T(8,128)(2,1)} copy(bf16[1,4,16,16,1024]{4,1,3,2,0:T(4,128)(2,1)S(1)} %bitcast.40) | data formatting | bytes 4194304 | tf_op jit(solution)/shard_map/all_to_all | solution.py:74
  147.0 2.3 %gather_fusion = bf16[16,4,16,1024]{3,2,1,0:T(8,128)(2,1)S(1)} fusion(bf16[16,4,16,1024]{3,2,1,0:T(8,128)(2,1)} %bitcast.41, s32[1024]{0:T(1024)S(1)} %pad_clamp_fusion), kind=kCustom, calls=%fused_computation | custom fusion | bytes 4194368 | tf_op jit(solution)/shard_map/jit(_take)/gather | solution.py:73
  149.3 0.3 select_convert_fusion
  149.9 0.7 multiply_add_fusion
  150.7 0.2 multiply_add_fusion.1
  151.0 0.7 fusion.9
  (32 shorter events, 0.5 us)
Async XLA Ops:
  0.0 9.6 %copy-start.1 = (f32[4,256,1024]{2,1,0:T(8,128)S(1)}, f32[4,256,1024]{2,1,0:T(8,128)}, u32[]{:S(2)}) copy-start(f32[4,256,1024]{2,1,0:T(8,128)} %param.7) | copy-start | bytes 12582916
  0.0 8.9 %copy-start.6 = (f32[8]{0:T(128)S(1)}, f32[8]{0:T(128)}, u32[]{:S(2)}) copy-start(f32[8]{0:T(128)} %param.10) | copy-start | bytes 100
  3.3 27.7 %collective-permute-start = (f32[1,256,1024]{2,1,0:T(8,128)}, f32[1,256,1024]{2,1,0:T(8,128)}, u32[]{:S(2)}, u32[]{:S(2)}) collective-permute-start(f32[1,256,1024]{2,1,0:T(8,128)} %get-tuple-element.82), channel_id=1, source_target_pairs={{1,0},{2,1},{3,2},{4,3},{5,4},{6,5},{7,6},{8,7},{9,8},{10,9},{11,1... | collective-permute-start | bytes 3145736 | tf_op jit(solution)/shard_map/ppermute | solution.py:15
  5.9 25.3 %collective-permute-start.1 = (f32[1,256,1024]{2,1,0:T(8,128)}, f32[1,256,1024]{2,1,0:T(8,128)}, u32[]{:S(2)}, u32[]{:S(2)}) collective-permute-start(f32[1,256,1024]{2,1,0:T(8,128)} %get-tuple-element.83), channel_id=1, source_target_pairs={{0,1},{1,2},{2,3},{3,4},{4,5},{5,6},{6,7},{7,8},{8,9},{9,10},{10,1... | collective-permute-start | bytes 3145736 | tf_op jit(solution)/shard_map/ppermute | solution.py:14
  9.6 15.1 %copy-start.5 = (f32[3,8]{1,0:T(4,128)S(1)}, f32[3,8]{1,0:T(4,128)}, u32[]{:S(2)}) copy-start(f32[3,8]{1,0:T(4,128)} %param.9) | copy-start | bytes 292
  31.2 22.5 %copy-start.2 = (pred[4,256,1024]{2,1,0:T(8,128)(4,1)S(1)}, pred[4,256,1024]{2,1,0:T(8,128)(4,1)}, u32[]{:S(2)}) copy-start(pred[4,256,1024]{2,1,0:T(8,128)(4,1)} %get-tuple-element.74) | copy-start | bytes 3145732
  31.2 22.5 %copy-start.3 = (pred[4,256,1024]{2,1,0:T(8,128)(4,1)S(1)}, pred[4,256,1024]{2,1,0:T(8,128)(4,1)}, u32[]{:S(2)}) copy-start(pred[4,256,1024]{2,1,0:T(8,128)(4,1)} %get-tuple-element.75) | copy-start | bytes 3145732
  31.2 22.5 %copy-start.4 = (pred[4,256,1024]{2,1,0:T(8,128)(4,1)S(1)}, pred[4,256,1024]{2,1,0:T(8,128)(4,1)}, u32[]{:S(2)}) copy-start(pred[4,256,1024]{2,1,0:T(8,128)(4,1)} %get-tuple-element.76) | copy-start | bytes 3145732
  86.9 1.6 %copy-start = (f32[256,1024]{1,0:T(8,128)S(1)}, f32[256,1024]{1,0:T(8,128)}, u32[]{:S(2)}) copy-start(f32[256,1024]{1,0:T(8,128)} %get-tuple-element.34) | copy-start | bytes 3145732
  89.4 9.6 %copy-start.7 = (s32[16]{0:T(128)S(1)}, s32[16]{0:T(128)}, u32[]{:S(2)}) copy-start(s32[16]{0:T(128)} %param.11) | copy-start | bytes 196
  92.7 52.3 %all-to-all-start = ((bf16[1,4,256,1024]{3,1,0,2:T(4,128)(2,1)}), bf16[1,4,256,1024]{3,1,0,2:T(4,128)(2,1)S(1)}, u32[]{:S(2)}, u32[]{:S(2)}) async-start(bf16[1,4,256,1024]{3,1,0,2:T(4,128)(2,1)} %pad_maximum_fusion.2), calls=%async_computation | async-start | bytes 4194304 | tf_op jit(solution)/shard_map/all_to_all | solution.py:74
where the time goes:
time: 154 us; the launch traced here: 152 us
  other arithmetic  76.2 us (49%)
  waiting for transfers between devices  51.5 us (33%)
  starting transfers between devices  11.9 us (8%)
  local copies, waits for them, and re-layouts  11.7 us (8%)
    all_to_all x1, waiting for transfers between devices, shards(): lax.all_to_all(partial_value[None], 'gz', split_axis=2, concat_axis=0, ti...  45.3 us
    mul x2, other arithmetic, sample_brick(): colour = tint_cell * (shading * alphas_cell)[None]  32.4 us
    mul x1, other arithmetic, sample_brick(): alphas_cell = opacity_cell * (1.0 - jnp.exp(-centre * centre))  15.1 us
    add x4, other arithmetic, advance(): colour_sum + transmit[None] * colour_slice  12.1 us
    mul x4, other arithmetic, advance(): transmit * (1.0 - alpha_slice)  10.9 us
    all_to_all x1, starting transfers between devices, shards(): lax.all_to_all(partial_value[None], 'gz', split_axis=2, concat_axis=0, ti...  6.28 us
    ppermute x1, waiting for transfers between devices, extended(): after = lax.ppermute(initial, axis, down)  6.01 us
    concatenate x2, other arithmetic, sample_brick(): jnp.concatenate([colour_sum, (1.0 - transmit)[None]], 0)  3.34 us
  transfers between devices with their start and end apart: 3, of which 3 were waited for; matrix products, arithmetic and copies ran while one was open for 11% of the time, Pallas kernels for 0%

commit v1 on v0

v1 whole, which is shorter than its diff:
```python
import functools

import jax
import jax.numpy as jnp
from jax import lax
from jax.experimental import pallas as pl
from jax.experimental.pallas import tpu as pltpu
from jax.sharding import PartitionSpec as P

REACH = 6.0
STEPS = 32767.0
BLOCK = 16
LANES = 128
PAD = 8
LIMIT = 40 * 1024 * 1024


def lookup(table, bits, row=None):
    b0, b1, b2 = bits
    at = (lambda m: table[m]) if row is None else (lambda m: table[row, m])
    pairs = [jnp.where(b0, at(2 * i + 1), at(2 * i)) for i in range(4)]
    low, high = jnp.where(b1, pairs[1], pairs[0]), jnp.where(b1, pairs[3], pairs[2])
    return jnp.where(b2, high, low)


def bits_of(index):
    return [(index & (1 << i)) != 0 for i in range(3)]


def alpha_of(centre, bits, opacity_ref):
    return lookup(opacity_ref, bits) * (1.0 - jnp.exp(-centre * centre))


def opacity_kernel(slices, blocks, volume_hbm, index_hbm, opacity_ref, out_ref, vol, idx, sems):
    def copies(i):
        rows = pl.ds(pl.multiple_of(i * BLOCK, BLOCK), BLOCK)
        return (
            pltpu.make_async_copy(volume_hbm.at[:, rows], vol.at[:, rows], sems.at[0, i]),
            pltpu.make_async_copy(index_hbm.at[:, rows], idx.at[:, rows], sems.at[1, i]),
        )

    @pl.loop(0, blocks)
    def _(i):
        for copy in copies(i):
            copy.start()

    @pl.loop(0, blocks)
    def _(i):
        for copy in copies(i):
            copy.wait()
        rows = pl.ds(pl.multiple_of(i * BLOCK, BLOCK), BLOCK)
        for j in range(vol.shape[2] // LANES):
            cols = pl.ds(j * LANES, LANES)
            transmit = None
            for k in range(slices):
                clear = 1.0 - alpha_of(vol[k, rows, cols], bits_of(idx[k, rows, cols]), opacity_ref)
                transmit = clear if transmit is None else transmit * clear
            out_ref[rows, cols] = (1.0 - transmit).astype(jnp.bfloat16)


def opacities(volume, tf_index, tf_opacity):
    slices, height, width = volume.shape
    blocks = height // BLOCK
    return pl.pallas_call(
        functools.partial(opacity_kernel, slices, blocks),
        out_shape=jax.ShapeDtypeStruct((height, width), jnp.bfloat16),
        in_specs=[
            pl.BlockSpec(memory_space=pl.ANY),
            pl.BlockSpec(memory_space=pl.ANY),
            pl.BlockSpec(memory_space=pltpu.SMEM),
        ],
        out_specs=pl.BlockSpec(memory_space=pltpu.VMEM),
        scratch_shapes=[
            pltpu.VMEM(volume.shape, jnp.float32),
            pltpu.VMEM(volume.shape, jnp.int32),
            pltpu.SemaphoreType.DMA((2, blocks)),
        ],
        compiler_params=pltpu.CompilerParams(vmem_limit_bytes=LIMIT),
        cost_estimate=pl.CostEstimate(
            flops=30 * volume.size, bytes_accessed=9 * volume.size, transcendentals=volume.size
        ),
        name="opacities",
    )(volume, tf_index, tf_opacity)


def colour_kernel(
    slices, blocks, first, count, volume_hbm, index_hbm, before_ref, after_ref, colour_ref, opacity_ref, out_ref, vol, idx, sems
):
    height, width = blocks * BLOCK, vol.shape[2]
    tiles = width // LANES

    def copies(i):
        start = pl.multiple_of(i * BLOCK, BLOCK)
        rows, padded = pl.ds(start, BLOCK), pl.ds(pl.multiple_of(start + PAD, PAD), BLOCK)
        return (
            pltpu.make_async_copy(volume_hbm.at[:, rows], vol.at[:, padded], sems.at[0, i]),
            pltpu.make_async_copy(index_hbm.at[:, rows], idx.at[:, rows], sems.at[1, i]),
        )

    @pl.loop(0, blocks)
    def _(i):
        for copy in copies(i):
            copy.start()

    edge = jnp.zeros((slices, PAD, width), jnp.float32)
    vol[:, pl.ds(0, PAD), :] = edge
    vol[:, pl.ds(PAD + height, PAD), :] = edge
    lane = lax.broadcasted_iota(jnp.int32, (BLOCK, LANES), 1)
    row = lax.broadcasted_iota(jnp.int32, (BLOCK, LANES), 0)
    at_left, at_right = lane == 0, lane == LANES - 1
    at_top, at_bottom = row == 0, row == BLOCK - 1
    copies(0)[0].wait()

    @pl.loop(0, blocks)
    def _(i):
        @pl.when(i + 1 < blocks)
        def _():
            copies(i + 1)[0].wait()

        copies(i)[1].wait()
        start = pl.multiple_of(i * BLOCK, BLOCK)
        rows = pl.ds(start, BLOCK)
        centre_rows = pl.ds(pl.multiple_of(start + PAD, PAD), BLOCK)
        upper_rows = pl.ds(start, PAD)
        lower_rows = pl.ds(pl.multiple_of(start + PAD + BLOCK, PAD), PAD)
        for j in range(count):
            tile = first + j
            cols = pl.ds(tile * LANES, LANES)
            halo = [
                ref[rows, cols].astype(jnp.float32) * (REACH / STEPS) for ref in (before_ref, after_ref)
            ]
            centres = [halo[0]] + [vol[k, centre_rows, cols] for k in range(slices)] + [halo[1]]
            transmit, sums = None, None
            for k in range(slices):
                centre = centres[k + 1]
                depth = centres[k + 2] - centres[k]
                upper, lower = vol[k, upper_rows, cols], vol[k, lower_rows, cols]
                up = jnp.where(
                    at_top, jnp.concatenate([pltpu.roll(upper, 1, 0)] * 2, 0), pltpu.roll(centre, 1, 0)
                )
                down = jnp.where(
                    at_bottom,
                    jnp.concatenate([pltpu.roll(lower, PAD - 1, 0)] * 2, 0),
                    pltpu.roll(centre, BLOCK - 1, 0),
                )
                across = down - up
                left_tile = vol[k, centre_rows, pl.ds((tile - 1) * LANES, LANES)] if tile > 0 else None
                right_tile = vol[k, centre_rows, pl.ds((tile + 1) * LANES, LANES)] if tile + 1 < tiles else None
                left_edge = 0.0 if left_tile is None else pltpu.roll(left_tile, 1, 1)
                right_edge = 0.0 if right_tile is None else pltpu.roll(right_tile, LANES - 1, 1)
                left = jnp.where(at_left, left_edge, pltpu.roll(centre, 1, 1))
                right = jnp.where(at_right, right_edge, pltpu.roll(centre, LANES - 1, 1))
                along = right - left
                facing = jnp.abs(0.48 * depth + 0.6 * across + 0.64 * along)
                squares = depth * depth + across * across + along * along + 4.0
                shading = 0.35 + 0.65 * facing * lax.rsqrt(squares)
                bits = bits_of(idx[k, rows, cols])
                alpha = alpha_of(centre, bits, opacity_ref)
                shown = shading * alpha
                if transmit is not None:
                    shown = transmit * shown
                terms = [lookup(colour_ref, bits, c) * shown for c in range(3)]
                sums = terms if sums is None else [s + t for s, t in zip(sums, terms)]
                if k + 1 < slices:
                    transmit = 1.0 - alpha if transmit is None else transmit * (1.0 - alpha)
            for c in range(3):
                out_ref[i, c, :, pl.ds(j * LANES, LANES)] = sums[c].astype(jnp.bfloat16)


def colours(volume, tf_index, before, after, tf_color, tf_opacity, first, count):
    slices, height, width = volume.shape
    blocks = height // BLOCK
    return pl.pallas_call(
        functools.partial(colour_kernel, slices, blocks, first, count),
        out_shape=jax.ShapeDtypeStruct((blocks, 3, BLOCK, count * LANES), jnp.bfloat16),
        in_specs=[
            pl.BlockSpec(memory_space=pl.ANY),
            pl.BlockSpec(memory_space=pl.ANY),
            pl.BlockSpec(memory_space=pltpu.VMEM),
            pl.BlockSpec(memory_space=pltpu.VMEM),
            pl.BlockSpec(memory_space=pltpu.SMEM),
            pl.BlockSpec(memory_space=pltpu.SMEM),
        ],
        out_specs=pl.BlockSpec(memory_space=pltpu.VMEM),
        scratch_shapes=[
            pltpu.VMEM((slices, height + 2 * PAD, width), jnp.float32),
            pltpu.VMEM(volume.shape, jnp.int32),
            pltpu.SemaphoreType.DMA((2, blocks)),
        ],
        compiler_params=pltpu.CompilerParams(vmem_limit_bytes=LIMIT),
        cost_estimate=pl.CostEstimate(
            flops=90 * slices * height * count * LANES,
            bytes_accessed=10 * volume.size,
            transcendentals=2 * slices * height * count * LANES,
        ),
        name="colours",
    )(volume, tf_index, before, after, tf_color, tf_opacity)


def blend_kernel(ranks, halves, order_ref, opacity_ref, *rest):
    colour_refs, out_ref, place = rest[:halves], rest[halves], rest[halves + 1]
    for b in range(ranks):
        place[order_ref[b]] = b
    for half, ref in enumerate(colour_refs):
        for j in range(ref.shape[3] // LANES):
            here = pl.ds(j * LANES, LANES)
            cols = pl.ds(half * ref.shape[3] + j * LANES, LANES)

            def step(rank, canvas):
                b = place[rank]
                opacity = opacity_ref[b, :, cols].astype(jnp.float32)
                clear = 1.0 - canvas[3]
                layers = [ref[b, c, :, here].astype(jnp.float32) for c in range(3)] + [opacity]
                return tuple(front + clear * back for front, back in zip(canvas, layers))

            canvas = lax.fori_loop(
                0, ranks, step, (jnp.zeros((opacity_ref.shape[1], LANES), jnp.float32),) * 4, unroll=True
            )
            for c in range(4):
                out_ref[c, :, cols] = canvas[c]


def blend(order, opacity, colour_parts):
    ranks, height, width = opacity.shape
    return pl.pallas_call(
        functools.partial(blend_kernel, ranks, len(colour_parts)),
        out_shape=jax.ShapeDtypeStruct((4, height, width), jnp.float32),
        in_specs=[pl.BlockSpec(memory_space=pltpu.SMEM)]
        + [pl.BlockSpec(memory_space=pltpu.VMEM)] * (1 + len(colour_parts)),
        out_specs=pl.BlockSpec(memory_space=pltpu.VMEM),
        scratch_shapes=[pltpu.SMEM((ranks,), jnp.int32)],
        compiler_params=pltpu.CompilerParams(vmem_limit_bytes=LIMIT),
        name="blend",
    )(order, opacity, *colour_parts)


def blend_plain(order, opacity, colour_parts):
    ranks = opacity.shape[0]
    place = jnp.zeros((ranks,), jnp.int32).at[order].set(jnp.arange(ranks, dtype=jnp.int32))
    layers = jnp.concatenate([jnp.concatenate(colour_parts, -1), opacity[:, None]], 1)

    def step(canvas, b):
        layer = lax.dynamic_index_in_dim(layers, b, 0, keepdims=False).astype(jnp.float32)
        return canvas + (1.0 - canvas[3:4]) * layer, None

    return lax.scan(step, jnp.zeros(layers.shape[1:], jnp.float32), place)[0]


def by_owner(blocks_first, devices):
    blocks, width = blocks_first.shape[0], blocks_first.shape[-1]
    middle = blocks_first.shape[1:-2]
    if blocks == devices:
        return blocks_first
    each = devices // blocks
    split = blocks_first.reshape((blocks,) + middle + (each, BLOCK // each, width))
    moved = jnp.moveaxis(split, len(middle) + 1, 1)
    return moved.reshape((devices,) + middle + (BLOCK // each, width))


def exchange(x):
    return lax.all_to_all(x, "gz", split_axis=0, concat_axis=0, tiled=True)


def coded(a_slice):
    return jnp.round(a_slice * (STEPS / REACH)).astype(jnp.int16)


def shards(volume, tf_index, tf_color, tf_opacity, order):
    devices = lax.axis_size("gz")
    slices, height, width = volume.shape
    up = [(i, i + 1) for i in range(devices - 1)]
    down = [(j, i) for i, j in up]
    before = lax.ppermute(coded(volume[slices - 1]), "gz", up)
    after = lax.ppermute(coded(volume[0]), "gz", down)
    opacity = opacities(volume, tf_index, tf_opacity).reshape(height // BLOCK, BLOCK, width)
    opacity = exchange(by_owner(opacity, devices))
    tiles = width // LANES
    half = tiles // 2
    parts = []
    for first in range(0, tiles, half):
        part = colours(volume, tf_index, before, after, tf_color, tf_opacity, first, half)
        parts.append(exchange(by_owner(part, devices)))
    whole_blocks = (height // devices) % BLOCK == 0
    return (blend if whole_blocks else blend_plain)(order, opacity, parts)


def solution(mesh):
    placed = (P("gz", "frames", None), P("gz", "frames", None), P(), P(), P("frames"))
    return jax.shard_map(
        shards, mesh=mesh, in_specs=placed, out_specs=P("frames", "gz", None), check_vma=False
    )
```

time: 154 us -> 105 us (0.68)
  other arithmetic: 76.2 us -> 1.9 us
  waiting for transfers between devices: 51.5 us -> 23.1 us
  blocking collectives: 0 us -> 24.4 us
  Pallas kernels: 0 us -> 23.4 us
  starting transfers between devices: 11.9 us -> 15.9 us
  local copies, waits for them, and re-layouts: 11.7 us -> 13.8 us
    mul x11 -> x0, other arithmetic: 58.5 us -> none  [the longest x2 32.4 us: sample_brick(): colour = tint_cell * (shading * alphas_cell)[None]]
    all_to_all x1 -> x2, waiting for transfers between devices: 45.3 us -> 7.59 us  [exchange(): return lax.all_to_all(x, 'gz', split_axis=0, concat_axis=0, tiled=True)]
    all_to_all x0 -> x1, blocking collectives: none -> 24.4 us  [exchange(): return lax.all_to_all(x, 'gz', split_axis=0, concat_axis=0, tiled=True)]
    pallas_call x0 -> x4, Pallas kernels: none -> 23.4 us  [the longest x2 16.2 us: colours(): pl.pallas_call(functools.partial(colour_kernel, slices, blocks, first, co...]
    add x7 -> x0, other arithmetic: 13 us -> none  [the longest x4 12.1 us: advance(): colour_sum + transmit[None] * colour_slice]
    unnamed x17 -> x20, local copies, waits for them, and re-layouts: 1.39 us -> 13.8 us
    ppermute x2, waiting for transfers between devices: 6.18 us -> 15.5 us  [the longest x1 12.4 us: shards(): before = lax.ppermute(coded(volume[slices - 1]), 'gz', up)]
    slice x6 -> x0, local copies, waits for them, and re-layouts: 4.52 us -> none  [the longest x1 3.3 us: extended(): initial = lax.slice_in_dim(x, 0, width, axis=dim)]
  transfers between devices with their start and end apart: 3 -> 4, of which waited for: 3 -> 3; matrix products, arithmetic and copies ran while one was open for 11% -> 2% of each run, Pallas kernels for 0% -> 16%
where the time goes in v1:
time: 105 us; the launch traced here: 103 us
  blocking collectives  24.4 us (23%)
  Pallas kernels  23.4 us (22%)
  waiting for transfers between devices  23.1 us (22%)
  starting transfers between devices  15.9 us (15%)
  local copies, waits for them, and re-layouts  13.8 us (13%)
  other arithmetic  1.9 us (2%)
    all_to_all x1, blocking collectives, exchange(): return lax.all_to_all(x, 'gz', split_axis=0, concat_axis=0, tiled=True)  24.4 us
    pallas_call x2, Pallas kernels, colours(): pl.pallas_call(functools.partial(colour_kernel, slices, blocks, first, co...  16.2 us
    unnamed x20, local copies, waits for them, and re-layouts  13.8 us
    ppermute x1, waiting for transfers between devices, shards(): before = lax.ppermute(coded(volume[slices - 1]), 'gz', up)  12.4 us
    all_to_all x2, starting transfers between devices, exchange(): return lax.all_to_all(x, 'gz', split_axis=0, concat_axis=0, tiled=True)  10.6 us
    all_to_all x2, waiting for transfers between devices, exchange(): return lax.all_to_all(x, 'gz', split_axis=0, concat_axis=0, tiled=True)  7.59 us
    pallas_call x1, Pallas kernels, opacities(): pl.pallas_call(functools.partial(opacity_kernel, slices, blocks), out_sha...  5.49 us
    ppermute x1, starting transfers between devices, shards(): before = lax.ppermute(coded(volume[slices - 1]), 'gz', up)  3.34 us
  transfers between devices with their start and end apart: 4, of which 3 were waited for; matrix products, arithmetic and copies ran while one was open for 2% of the time, Pallas kernels for 16%

profile of v1, /device:TPU:13, one launch (start us, length us, event | category | flops | bytes accessed | tf_op | source)
XLA Modules:
  0.0 102.6 jit_solution(2238932183557125265)
XLA Ops:
  0.0 0.0 copy-start
  0.0 2.2 %copy-done = f32[4,256,1024]{2,1,0:T(8,128)S(1)} copy-done((f32[4,256,1024]{2,1,0:T(8,128)S(1)}, f32[4,256,1024]{2,1,0:T(8,128)}, u32[]{:S(2)}) %copy-start) | copy-done | bytes 4194328
  2.2 0.0 copy-start.3
  2.2 2.2 %copy-done.3 = s32[4,256,1024]{2,1,0:T(8,128)S(1)} copy-done((s32[4,256,1024]{2,1,0:T(8,128)S(1)}, s32[4,256,1024]{2,1,0:T(8,128)}, u32[]{:S(2)}) %copy-start.3) | copy-done | bytes 4194328
  4.4 0.7 copy-done.7
  5.0 5.5 %opacities.1 = bf16[256,1024]{1,0:T(8,128)(2,1)} custom-call(f32[4,256,1024]{2,1,0:T(8,128)S(1)} %copy-done, s32[4,256,1024]{2,1,0:T(8,128)S(1)} %copy-done.3, f32[8]{0:T(128)S(1)} %copy-done.7), custom_call_target="tpu_custom_call" | custom-call | flops 31457280 | bytes 9437184 | tf_op jit(solution)/shard_map/opacities/pallas_call | solution.py:64
  10.5 0.0 copy-start.6
  10.5 0.0 copy-start.8
  10.6 6.6 %all-to-all-start = ((bf16[16,16,1024]{2,1,0:T(8,128)(2,1)}), bf16[16,16,1024]{2,1,0:T(8,128)(2,1)S(1)}, u32[]{:S(2)}, u32[]{:S(2)}) async-start(bf16[16,16,1024]{2,1,0:T(8,128)(2,1)} %bitcast), calls=%async_computation | async-start | bytes 1048576 | tf_op jit(solution)/shard_map/all_to_all | solution.py:261
  17.1 1.9 %fusion.1 = (s16[256,1024]{1,0:T(8,128)(2,1)S(1)}, s16[256,1024]{1,0:T(8,128)(2,1)S(1)}) fusion(f32[4,256,1024]{2,1,0:T(8,128)} %volume_hbm.5), kind=kLoop, calls=%fused_computation.3 | loop fusion | flops 1572864 | bytes 3145728 | tf_op jit(solution)/shard_map/convert_element_type | solution.py:265
  19.1 3.3 %collective-permute-start = (s16[256,1024]{1,0:T(8,128)(2,1)S(1)}, s16[256,1024]{1,0:T(8,128)(2,1)S(1)}, u32[]{:S(2)}, u32[]{:S(2)}) collective-permute-start(s16[256,1024]{1,0:T(8,128)(2,1)S(1)} %get-tuple-element.6), channel_id=1, source_target_pairs={{0,1},{1,2},{2,3},{3,4},{4,5},{5,6},{6,7},{7,8},{8,9},{9,10},{10,1... | collective-permute-start | bytes 1572872 | tf_op jit(solution)/shard_map/ppermute | solution.py:273
  22.4 1.9 %collective-permute-start.1 = (s16[256,1024]{1,0:T(8,128)(2,1)S(1)}, s16[256,1024]{1,0:T(8,128)(2,1)S(1)}, u32[]{:S(2)}, u32[]{:S(2)}) collective-permute-start(s16[256,1024]{1,0:T(8,128)(2,1)S(1)} %get-tuple-element.5), channel_id=1, source_target_pairs={{1,0},{2,1},{3,2},{4,3},{5,4},{6,5},{7,6},{8,7},{9,8},{10,9},{11,1... | collective-permute-start | bytes 1572872 | tf_op jit(solution)/shard_map/ppermute | solution.py:274
  24.3 12.4 %collective-permute-done.before_ref = s16[256,1024]{1,0:T(8,128)(2,1)S(1)} collective-permute-done((s16[256,1024]{1,0:T(8,128)(2,1)S(1)}, s16[256,1024]{1,0:T(8,128)(2,1)S(1)}, u32[]{:S(2)}, u32[]{:S(2)}) %collective-permute-start) | collective-permute-done | bytes 524320 | tf_op jit(solution)/shard_map/ppermute | solution.py:273
  36.8 3.1 %collective-permute-done.1.after_ref = s16[256,1024]{1,0:T(8,128)(2,1)S(1)} collective-permute-done((s16[256,1024]{1,0:T(8,128)(2,1)S(1)}, s16[256,1024]{1,0:T(8,128)(2,1)S(1)}, u32[]{:S(2)}, u32[]{:S(2)}) %collective-permute-start.1) | collective-permute-done | bytes 524320 | tf_op jit(solution)/shard_map/ppermute | solution.py:274
  39.9 0.0 copy-done.6
  39.9 0.0 copy-done.8
  39.9 0.0 copy-start.1
  39.9 2.2 %copy-done.1 = f32[4,256,1024]{2,1,0:T(8,128)S(1)} copy-done((f32[4,256,1024]{2,1,0:T(8,128)S(1)}, f32[4,256,1024]{2,1,0:T(8,128)}, u32[]{:S(2)}) %copy-start.1) | copy-done | bytes 4194328
  42.1 0.0 copy-start.4
  42.1 2.2 %copy-done.4 = s32[4,256,1024]{2,1,0:T(8,128)S(1)} copy-done((s32[4,256,1024]{2,1,0:T(8,128)S(1)}, s32[4,256,1024]{2,1,0:T(8,128)}, u32[]{:S(2)}) %copy-start.4) | copy-done | bytes 4194328
  44.3 8.6 %colours.3 = bf16[16,3,16,512]{3,2,1,0:T(8,128)(2,1)} custom-call(f32[4,256,1024]{2,1,0:T(8,128)S(1)} %copy-done.1, s32[4,256,1024]{2,1,0:T(8,128)S(1)} %copy-done.4, s16[256,1024]{1,0:T(8,128)(2,1)S(1)} %collective-permute-done.before_ref, s16[256,1024]{1,0:T(8,128)(2,1)S(1)} %collective-permute-done.1.after_ref, f32[3,8]{1,0:T(4,128)S(1)} %copy-done.6, ...), custom_call_target="tpu_custom_call" | custom-call | flops 47185920 | bytes 10485760 | tf_op jit(solution)/shard_map/colours/pallas_call | solution.py:173
  52.8 0.0 all-to-all-done.opacity_ref
  52.8 4.0 %all-to-all-start.2 = ((bf16[16,3,16,512]{3,2,1,0:T(8,128)(2,1)}), bf16[16,3,16,512]{3,2,1,0:T(8,128)(2,1)S(1)}, u32[]{:S(2)}, u32[]{:S(2)}) async-start(bf16[16,3,16,512]{3,2,1,0:T(8,128)(2,1)} %colours.3), calls=%async_computation.2 | async-start | bytes 1572864 | tf_op jit(solution)/shard_map/all_to_all | solution.py:261
  56.9 0.0 copy-start.2
  56.9 2.2 %copy-done.2 = f32[4,256,1024]{2,1,0:T(8,128)S(1)} copy-done((f32[4,256,1024]{2,1,0:T(8,128)S(1)}, f32[4,256,1024]{2,1,0:T(8,128)}, u32[]{:S(2)}) %copy-start.2) | copy-done | bytes 4194328
  59.1 0.0 copy-start.5
  59.1 2.2 %copy-done.5 = s32[4,256,1024]{2,1,0:T(8,128)S(1)} copy-done((s32[4,256,1024]{2,1,0:T(8,128)S(1)}, s32[4,256,1024]{2,1,0:T(8,128)}, u32[]{:S(2)}) %copy-start.5) | copy-done | bytes 4194328
  61.3 7.6 %colours.2 = bf16[16,3,16,512]{3,2,1,0:T(8,128)(2,1)S(1)} custom-call(f32[4,256,1024]{2,1,0:T(8,128)S(1)} %copy-done.2, s32[4,256,1024]{2,1,0:T(8,128)S(1)} %copy-done.5, s16[256,1024]{1,0:T(8,128)(2,1)S(1)} %collective-permute-done.before_ref, s16[256,1024]{1,0:T(8,128)(2,1)S(1)} %collective-permute-done.1.after_ref, f32[3,8]{1,0:T(4,128)S(1)} %copy-done.6, ...), custom_call_target="tpu_custom_call" | custom-call | flops 47185920 | bytes 10485760 | tf_op jit(solution)/shard_map/colours/pallas_call | solution.py:173
  68.9 7.6 %all-to-all-done.2.rest_1_ = bf16[16,3,16,512]{3,2,1,0:T(8,128)(2,1)S(1)} async-done(((bf16[16,3,16,512]{3,2,1,0:T(8,128)(2,1)}), bf16[16,3,16,512]{3,2,1,0:T(8,128)(2,1)S(1)}, u32[]{:S(2)}, u32[]{:S(2)}) %all-to-all-start.2) | async-done | bytes 786464 | tf_op jit(solution)/shard_map/all_to_all | solution.py:261
  76.4 24.4 %all_to_all.15.rest_0_ = bf16[16,3,16,512]{3,2,1,0:T(8,128)(2,1)S(1)} all-to-all(bf16[16,3,16,512]{3,2,1,0:T(8,128)(2,1)S(1)} %colours.2), channel_id=1, replica_groups=mesh['frames'=2,'gz'=16] {'gz'}, dimensions={0} | all-to-all | bytes 1572864 | tf_op jit(solution)/shard_map/all_to_all | solution.py:261
  100.8 0.0 copy-done.9
  100.8 1.8 %blend.1 = f32[4,16,1024]{2,1,0:T(8,128)} custom-call(s32[16]{0:T(128)S(1)} %copy-done.9, bf16[16,16,1024]{2,1,0:T(8,128)(2,1)S(1)} %all-to-all-done.opacity_ref, bf16[16,3,16,512]{3,2,1,0:T(8,128)(2,1)S(1)} %all_to_all.15.rest_0_, bf16[16,3,16,512]{3,2,1,0:T(8,128)(2,1)S(1)} %all-to-all-done.2.rest_1_), custom_call_target="tpu_custom_call" | custom-call | tf_op jit(solution)/shard_map/blend/pallas_call | solution.py:225
  (2 shorter events, 0.0 us)
Async XLA Ops:
  0.0 2.2 %copy-start = (f32[4,256,1024]{2,1,0:T(8,128)S(1)}, f32[4,256,1024]{2,1,0:T(8,128)}, u32[]{:S(2)}) copy-start(f32[4,256,1024]{2,1,0:T(8,128)} %volume_hbm.5) | copy-start | bytes 12582916
  2.2 2.2 %copy-start.3 = (s32[4,256,1024]{2,1,0:T(8,128)S(1)}, s32[4,256,1024]{2,1,0:T(8,128)}, u32[]{:S(2)}) copy-start(s32[4,256,1024]{2,1,0:T(8,128)} %index_hbm.5) | copy-start | bytes 12582916
  4.4 0.7 copy-start.7
  10.5 29.3 %copy-start.6 = (f32[3,8]{1,0:T(4,128)S(1)}, f32[3,8]{1,0:T(4,128)}, u32[]{:S(2)}) copy-start(f32[3,8]{1,0:T(4,128)} %colour_ref.3) | copy-start | bytes 292
  10.5 29.3 %copy-start.8 = (f32[8]{0:T(128)S(1)}, f32[8]{0:T(128)}, u32[]{:S(2)}) copy-start(f32[8]{0:T(128)} %opacity_ref.5) | copy-start | bytes 100
  10.6 42.3 %all-to-all-start = ((bf16[16,16,1024]{2,1,0:T(8,128)(2,1)}), bf16[16,16,1024]{2,1,0:T(8,128)(2,1)S(1)}, u32[]{:S(2)}, u32[]{:S(2)}) async-start(bf16[16,16,1024]{2,1,0:T(8,128)(2,1)} %bitcast), calls=%async_computation | async-start | bytes 1048576 | tf_op jit(solution)/shard_map/all_to_all | solution.py:261
  19.1 17.7 %collective-permute-start = (s16[256,1024]{1,0:T(8,128)(2,1)S(1)}, s16[256,1024]{1,0:T(8,128)(2,1)S(1)}, u32[]{:S(2)}, u32[]{:S(2)}) collective-permute-start(s16[256,1024]{1,0:T(8,128)(2,1)S(1)} %get-tuple-element.6), channel_id=1, source_target_pairs={{0,1},{1,2},{2,3},{3,4},{4,5},{5,6},{6,7},{7,8},{8,9},{9,10},{10,1... | collective-permute-start | bytes 1572872 | tf_op jit(solution)/shard_map/ppermute | solution.py:273
  22.4 17.5 %collective-permute-start.1 = (s16[256,1024]{1,0:T(8,128)(2,1)S(1)}, s16[256,1024]{1,0:T(8,128)(2,1)S(1)}, u32[]{:S(2)}, u32[]{:S(2)}) collective-permute-start(s16[256,1024]{1,0:T(8,128)(2,1)S(1)} %get-tuple-element.5), channel_id=1, source_target_pairs={{1,0},{2,1},{3,2},{4,3},{5,4},{6,5},{7,6},{8,7},{9,8},{10,9},{11,1... | collective-permute-start | bytes 1572872 | tf_op jit(solution)/shard_map/ppermute | solution.py:274
  39.9 2.2 %copy-start.1 = (f32[4,256,1024]{2,1,0:T(8,128)S(1)}, f32[4,256,1024]{2,1,0:T(8,128)}, u32[]{:S(2)}) copy-start(f32[4,256,1024]{2,1,0:T(8,128)} %volume_hbm.5) | copy-start | bytes 12582916
  42.1 2.2 %copy-start.4 = (s32[4,256,1024]{2,1,0:T(8,128)S(1)}, s32[4,256,1024]{2,1,0:T(8,128)}, u32[]{:S(2)}) copy-start(s32[4,256,1024]{2,1,0:T(8,128)} %index_hbm.5) | copy-start | bytes 12582916
  52.8 23.6 %all-to-all-start.2 = ((bf16[16,3,16,512]{3,2,1,0:T(8,128)(2,1)}), bf16[16,3,16,512]{3,2,1,0:T(8,128)(2,1)S(1)}, u32[]{:S(2)}, u32[]{:S(2)}) async-start(bf16[16,3,16,512]{3,2,1,0:T(8,128)(2,1)} %colours.3), calls=%async_computation.2 | async-start | bytes 1572864 | tf_op jit(solution)/shard_map/all_to_all | solution.py:261
  56.9 2.2 %copy-start.2 = (f32[4,256,1024]{2,1,0:T(8,128)S(1)}, f32[4,256,1024]{2,1,0:T(8,128)}, u32[]{:S(2)}) copy-start(f32[4,256,1024]{2,1,0:T(8,128)} %volume_hbm.5) | copy-start | bytes 12582916
  59.1 2.2 %copy-start.5 = (s32[4,256,1024]{2,1,0:T(8,128)S(1)}, s32[4,256,1024]{2,1,0:T(8,128)}, u32[]{:S(2)}) copy-start(s32[4,256,1024]{2,1,0:T(8,128)} %index_hbm.5) | copy-start | bytes 12582916
  61.3 39.5 %copy-start.9 = (s32[16]{0:T(128)S(1)}, s32[16]{0:T(128)}, u32[]{:S(2)}) copy-start(s32[16]{0:T(128)} %order_ref.1) | copy-start | bytes 196

commit v2 on v1

v2 whole, which is shorter than its diff:
```python
import functools

import jax
import jax.numpy as jnp
from jax import lax
from jax.experimental import pallas as pl
from jax.experimental.pallas import tpu as pltpu
from jax.sharding import PartitionSpec as P

REACH = 6.0
STEPS = 32767.0
BLOCK = 16
LANES = 128
PAD = 8
NT = 8
LIMIT = 40 * 1024 * 1024


def spread(table_ref, *row):
    sublane = lax.broadcasted_iota(jnp.int32, (NT, LANES), 0)
    table = jnp.zeros((NT, LANES), jnp.float32)
    for m in range(NT):
        table = jnp.where(sublane == m, table_ref[(*row, m)], table)
    return table


def lookup(table, index):
    parts = [
        jnp.take_along_axis(table, index[r : r + NT], axis=0, mode="promise_in_bounds")
        for r in range(0, index.shape[0], NT)
    ]
    return jnp.concatenate(parts, 0)


def alpha_of(centre, index, table):
    return lookup(table, index) * (1.0 - jnp.exp(-centre * centre))


def fetched(source, target, sems, kind, tile, row):
    height = source.shape[1]
    return pltpu.make_async_copy(
        source.at[:, :, pl.ds(tile * LANES, LANES)], target.at[:, tile, pl.ds(row, height), :], sems.at[kind, tile]
    )


def opacity_kernel(slices, tiles, volume_hbm, index_hbm, opacity_ref, out_ref, vol, idx, sems):
    copies = [(fetched(volume_hbm, vol, sems, 0, t, 0), fetched(index_hbm, idx, sems, 1, t, 0)) for t in range(tiles)]
    for pair in copies:
        for copy in pair:
            copy.start()
    table = spread(opacity_ref)
    for t in range(tiles):
        for copy in copies[t]:
            copy.wait()

        @pl.loop(0, vol.shape[2] // BLOCK)
        def _(i):
            rows = pl.ds(pl.multiple_of(i * BLOCK, BLOCK), BLOCK)
            transmit = None
            for k in range(slices):
                clear = 1.0 - alpha_of(vol[k, t, rows, :], idx[k, t, rows, :], table)
                transmit = clear if transmit is None else transmit * clear
            out_ref[rows, pl.ds(t * LANES, LANES)] = (1.0 - transmit).astype(jnp.bfloat16)


def opacities(volume, tf_index, tf_opacity):
    slices, height, width = volume.shape
    tiles = width // LANES
    tiled = (slices, tiles, height, LANES)
    return pl.pallas_call(
        functools.partial(opacity_kernel, slices, tiles),
        out_shape=jax.ShapeDtypeStruct((height, width), jnp.bfloat16),
        in_specs=[
            pl.BlockSpec(memory_space=pltpu.HBM),
            pl.BlockSpec(memory_space=pltpu.HBM),
            pl.BlockSpec(memory_space=pltpu.SMEM),
        ],
        out_specs=pl.BlockSpec(memory_space=pltpu.VMEM),
        scratch_shapes=[
            pltpu.VMEM(tiled, jnp.float32),
            pltpu.VMEM(tiled, jnp.int32),
            pltpu.SemaphoreType.DMA((2, tiles)),
        ],
        compiler_params=pltpu.CompilerParams(vmem_limit_bytes=LIMIT),
        cost_estimate=pl.CostEstimate(
            flops=15 * volume.size, bytes_accessed=9 * volume.size, transcendentals=volume.size
        ),
        name="opacities",
    )(volume, tf_index, tf_opacity)


def colour_kernel(
    slices, tiles, first, count, volume_hbm, index_hbm, before_ref, after_ref, colour_ref, opacity_ref, out_ref, vol, idx, sems
):
    height = before_ref.shape[0]
    here = range(first, first + count)
    around = range(max(first - 1, 0), min(first + count + 1, tiles))
    volumes = {t: fetched(volume_hbm, vol, sems, 0, t, PAD) for t in around}
    indices = {t: fetched(index_hbm, idx, sems, 1, t, 0) for t in here}
    for t in around:
        volumes[t].start()
        if t in indices:
            indices[t].start()
    edge = jnp.zeros((slices, tiles, PAD, LANES), jnp.float32)
    vol[:, :, pl.ds(0, PAD), :] = edge
    vol[:, :, pl.ds(PAD + height, PAD), :] = edge
    lane = lax.broadcasted_iota(jnp.int32, (BLOCK, LANES), 1)
    at_left, at_right = lane == 0, lane == LANES - 1
    opacity_table = spread(opacity_ref)
    colour_tables = [spread(colour_ref, c) for c in range(3)]
    arrived = set()
    for t in here:
        for near in (t - 1, t, t + 1):
            if near in volumes and near not in arrived:
                volumes[near].wait()
                arrived.add(near)
        indices[t].wait()

        @pl.loop(0, height // BLOCK)
        def _(i):
            start = pl.multiple_of(i * BLOCK, BLOCK)
            rows = pl.ds(start, BLOCK)
            cols = pl.ds(t * LANES, LANES)
            halo = [ref[rows, cols].astype(jnp.float32) * (REACH / STEPS) for ref in (before_ref, after_ref)]
            inside = pl.ds(pl.multiple_of(start + PAD, PAD), BLOCK)
            centres = [halo[0]] + [vol[k, t, inside, :] for k in range(slices)] + [halo[1]]
            transmit, sums = None, None
            for k in range(slices):
                centre = centres[k + 1]
                depth = centres[k + 2] - centres[k]
                across = vol[k, t, pl.ds(start + (PAD + 1), BLOCK), :] - vol[k, t, pl.ds(start + (PAD - 1), BLOCK), :]
                left_edge = pltpu.roll(vol[k, t - 1, inside, :], 1, 1) if t > 0 else 0.0
                right_edge = pltpu.roll(vol[k, t + 1, inside, :], LANES - 1, 1) if t + 1 < tiles else 0.0
                left = jnp.where(at_left, left_edge, pltpu.roll(centre, 1, 1))
                right = jnp.where(at_right, right_edge, pltpu.roll(centre, LANES - 1, 1))
                along = right - left
                facing = jnp.abs(0.48 * depth + 0.6 * across + 0.64 * along)
                squares = depth * depth + across * across + along * along + 4.0
                shading = 0.35 + 0.65 * facing * lax.rsqrt(squares)
                index = idx[k, t, rows, :]
                alpha = alpha_of(centre, index, opacity_table)
                shown = shading * alpha
                if transmit is not None:
                    shown = transmit * shown
                terms = [lookup(table, index) * shown for table in colour_tables]
                sums = terms if sums is None else [s + add for s, add in zip(sums, terms)]
                if k + 1 < slices:
                    transmit = 1.0 - alpha if transmit is None else transmit * (1.0 - alpha)
            for c in range(3):
                out_ref[i, c, :, pl.ds((t - first) * LANES, LANES)] = sums[c].astype(jnp.bfloat16)


def colours(volume, tf_index, before, after, tf_color, tf_opacity, first, count):
    slices, height, width = volume.shape
    blocks, tiles = height // BLOCK, width // LANES
    return pl.pallas_call(
        functools.partial(colour_kernel, slices, tiles, first, count),
        out_shape=jax.ShapeDtypeStruct((blocks, 3, BLOCK, count * LANES), jnp.bfloat16),
        in_specs=[
            pl.BlockSpec(memory_space=pltpu.HBM),
            pl.BlockSpec(memory_space=pltpu.HBM),
            pl.BlockSpec(memory_space=pltpu.VMEM),
            pl.BlockSpec(memory_space=pltpu.VMEM),
            pl.BlockSpec(memory_space=pltpu.SMEM),
            pl.BlockSpec(memory_space=pltpu.SMEM),
        ],
        out_specs=pl.BlockSpec(memory_space=pltpu.VMEM),
        scratch_shapes=[
            pltpu.VMEM((slices, tiles, height + 2 * PAD, LANES), jnp.float32),
            pltpu.VMEM((slices, tiles, height, LANES), jnp.int32),
            pltpu.SemaphoreType.DMA((2, tiles)),
        ],
        compiler_params=pltpu.CompilerParams(vmem_limit_bytes=LIMIT),
        cost_estimate=pl.CostEstimate(
            flops=50 * slices * height * count * LANES,
            bytes_accessed=10 * volume.size,
            transcendentals=2 * slices * height * count * LANES,
        ),
        name="colours",
    )(volume, tf_index, before, after, tf_color, tf_opacity)


def blend_kernel(ranks, halves, order_ref, opacity_ref, *rest):
    colour_refs, out_ref, place = rest[:halves], rest[halves], rest[halves + 1]
    for b in range(ranks):
        place[order_ref[b]] = b
    for half, ref in enumerate(colour_refs):
        for j in range(ref.shape[3] // LANES):
            here = pl.ds(j * LANES, LANES)
            cols = pl.ds(half * ref.shape[3] + j * LANES, LANES)

            def step(rank, canvas):
                b = place[rank]
                opacity = opacity_ref[b, :, cols].astype(jnp.float32)
                clear = 1.0 - canvas[3]
                layers = [ref[b, c, :, here].astype(jnp.float32) for c in range(3)] + [opacity]
                return tuple(front + clear * back for front, back in zip(canvas, layers))

            canvas = lax.fori_loop(
                0, ranks, step, (jnp.zeros((opacity_ref.shape[1], LANES), jnp.float32),) * 4, unroll=True
            )
            for c in range(4):
                out_ref[c, :, cols] = canvas[c]


def blend(order, opacity, colour_parts):
    ranks, height, width = opacity.shape
    return pl.pallas_call(
        functools.partial(blend_kernel, ranks, len(colour_parts)),
        out_shape=jax.ShapeDtypeStruct((4, height, width), jnp.float32),
        in_specs=[pl.BlockSpec(memory_space=pltpu.SMEM)]
        + [pl.BlockSpec(memory_space=pltpu.VMEM)] * (1 + len(colour_parts)),
        out_specs=pl.BlockSpec(memory_space=pltpu.VMEM),
        scratch_shapes=[pltpu.SMEM((ranks,), jnp.int32)],
        compiler_params=pltpu.CompilerParams(vmem_limit_bytes=LIMIT),
        name="blend",
    )(order, opacity, *colour_parts)


def blend_plain(order, opacity, colour_parts):
    ranks = opacity.shape[0]
    place = jnp.zeros((ranks,), jnp.int32).at[order].set(jnp.arange(ranks, dtype=jnp.int32))
    layers = jnp.concatenate([jnp.concatenate(colour_parts, -1), opacity[:, None]], 1)

    def step(canvas, b):
        layer = lax.dynamic_index_in_dim(layers, b, 0, keepdims=False).astype(jnp.float32)
        return canvas + (1.0 - canvas[3:4]) * layer, None

    return lax.scan(step, jnp.zeros(layers.shape[1:], jnp.float32), place)[0]


def by_owner(blocks_first, devices):
    blocks, width = blocks_first.shape[0], blocks_first.shape[-1]
    middle = blocks_first.shape[1:-2]
    if blocks == devices:
        return blocks_first
    each = devices // blocks
    split = blocks_first.reshape((blocks,) + middle + (each, BLOCK // each, width))
    moved = jnp.moveaxis(split, len(middle) + 1, 1)
    return moved.reshape((devices,) + middle + (BLOCK // each, width))


def exchange(x):
    return lax.all_to_all(x, "gz", split_axis=0, concat_axis=0, tiled=True)


def coded(a_slice):
    return jnp.round(a_slice * (STEPS / REACH)).astype(jnp.int16)


def shards(volume, tf_index, tf_color, tf_opacity, order):
    devices = lax.axis_size("gz")
    slices, height, width = volume.shape
    up = [(i, i + 1) for i in range(devices - 1)]
    down = [(j, i) for i, j in up]
    last, initial = coded(volume[slices - 1]), coded(volume[0])
    before = lax.ppermute(last, "gz", up)
    after = lax.ppermute(initial, "gz", down)
    later, _ = lax.optimization_barrier((volume, (last, initial)))
    opacity = opacities(later, tf_index, tf_opacity).reshape(height // BLOCK, BLOCK, width)
    opacity = exchange(by_owner(opacity, devices))
    tiles = width // LANES
    half = tiles // 2
    parts = []
    for first in range(0, tiles, half):
        part = colours(volume, tf_index, before, after, tf_color, tf_opacity, first, half)
        parts.append(exchange(by_owner(part, devices)))
    whole_blocks = (height // devices) % BLOCK == 0
    return (blend if whole_blocks else blend_plain)(order, opacity, parts)


def solution(mesh):
    placed = (P("gz", "frames", None), P("gz", "frames", None), P(), P(), P("frames"))
    return jax.shard_map(
        shards, mesh=mesh, in_specs=placed, out_specs=P("frames", "gz", None), check_vma=False
    )
```

time: 105 us -> 107 us (1.019)
  Pallas kernels: 23.4 us -> 26.2 us
  waiting for transfers between devices: 23.1 us -> 20.8 us
  starting transfers between devices: 15.9 us -> 17.8 us
    pallas_call x3, Pallas kernels: 21.6 us -> 24.5 us  [the longest x2 18.8 us: colours(): pl.pallas_call(functools.partial(colour_kernel, slices, tiles, first, cou...]
    all_to_all x2, starting transfers between devices: 10.6 us -> 12.2 us  [exchange(): return lax.all_to_all(x, 'gz', split_axis=0, concat_axis=0, tiled=True)]
    all_to_all x2, waiting for transfers between devices: 7.59 us -> 6.24 us  [exchange(): return lax.all_to_all(x, 'gz', split_axis=0, concat_axis=0, tiled=True)]
  transfers between devices with their start and end apart: 4 -> 4, of which waited for: 3 -> 2; matrix products, arithmetic and copies ran while one was open for 2% -> 0% of each run, Pallas kernels for 16% -> 18%
where the time goes in v2:
time: 107 us; the launch traced here: 105 us
  Pallas kernels  26.2 us (24%)
  blocking collectives  24.4 us (23%)
  waiting for transfers between devices  20.8 us (19%)
  starting transfers between devices  17.8 us (17%)
  local copies, waits for them, and re-layouts  13.8 us (13%)
  other arithmetic  1.9 us (2%)
    all_to_all x1, blocking collectives, exchange(): return lax.all_to_all(x, 'gz', split_axis=0, concat_axis=0, tiled=True)  24.4 us
    pallas_call x2, Pallas kernels, colours(): pl.pallas_call(functools.partial(colour_kernel, slices, tiles, first, cou...  18.8 us
    ppermute x1, waiting for transfers between devices, shards(): after = lax.ppermute(initial, 'gz', down)  14.5 us
    unnamed x20, local copies, waits for them, and re-layouts  13.8 us
    all_to_all x2, starting transfers between devices, exchange(): return lax.all_to_all(x, 'gz', split_axis=0, concat_axis=0, tiled=True)  12.2 us
    all_to_all x2, waiting for transfers between devices, exchange(): return lax.all_to_all(x, 'gz', split_axis=0, concat_axis=0, tiled=True)  6.24 us
    pallas_call x1, Pallas kernels, opacities(): pl.pallas_call(functools.partial(opacity_kernel, slices, tiles), out_shap...  5.7 us
    ppermute x1, starting transfers between devices, shards(): before = lax.ppermute(last, 'gz', up)  3.29 us
  transfers between devices with their start and end apart: 4, of which 2 were waited for; matrix products, arithmetic and copies ran while one was open for 0% of the time, Pallas kernels for 18%

profile of v2, /device:TPU:13, one launch (start us, length us, event | category | flops | bytes accessed | tf_op | source)
XLA Modules:
  0.0 104.9 jit_solution(11777080305843938573)
XLA Ops:
  0.0 1.9 %fusion.1 = (s16[256,1024]{1,0:T(8,128)(2,1)S(1)}, s16[256,1024]{1,0:T(8,128)(2,1)S(1)}) fusion(f32[4,256,1024]{2,1,0:T(8,128)} %volume_hbm.4), kind=kLoop, calls=%fused_computation.3 | loop fusion | flops 1572864 | bytes 3145728 | tf_op jit(solution)/shard_map/convert_element_type | solution.py:248
  1.9 0.0 copy-start
  1.9 2.2 %copy-done = f32[4,256,1024]{2,1,0:T(8,128)S(1)} copy-done((f32[4,256,1024]{2,1,0:T(8,128)S(1)}, f32[4,256,1024]{2,1,0:T(8,128)}, u32[]{:S(2)}) %copy-start) | copy-done | bytes 4194328
  4.1 0.0 copy-start.3
  4.1 2.2 %copy-done.3 = s32[4,256,1024]{2,1,0:T(8,128)S(1)} copy-done((s32[4,256,1024]{2,1,0:T(8,128)S(1)}, s32[4,256,1024]{2,1,0:T(8,128)}, u32[]{:S(2)}) %copy-start.3) | copy-done | bytes 4194328
  6.3 0.0 copy-start.7
  6.3 0.7 copy-done.7
  6.9 0.0 copy-start.6
  6.9 0.0 copy-start.8
  6.9 5.7 %opacities.1 = bf16[256,1024]{1,0:T(8,128)(2,1)} custom-call(f32[4,256,1024]{2,1,0:T(8,128)S(1)} %copy-done, s32[4,256,1024]{2,1,0:T(8,128)S(1)} %copy-done.3, f32[8]{0:T(128)S(1)} %copy-done.7), custom_call_target="tpu_custom_call" | custom-call | flops 15728640 | bytes 9437184 | tf_op jit(solution)/shard_map/opacities/pallas_call | solution.py:70
  12.7 6.6 %all-to-all-start = ((bf16[16,16,1024]{2,1,0:T(8,128)(2,1)}), bf16[16,16,1024]{2,1,0:T(8,128)(2,1)S(1)}, u32[]{:S(2)}, u32[]{:S(2)}) async-start(bf16[16,16,1024]{2,1,0:T(8,128)(2,1)} %bitcast.2), calls=%async_computation | async-start | bytes 1048576 | tf_op jit(solution)/shard_map/all_to_all | solution.py:244
  19.2 2.3 %collective-permute-start.1 = (s16[256,1024]{1,0:T(8,128)(2,1)S(1)}, s16[256,1024]{1,0:T(8,128)(2,1)S(1)}, u32[]{:S(2)}, u32[]{:S(2)}) collective-permute-start(s16[256,1024]{1,0:T(8,128)(2,1)S(1)} %get-tuple-element.7), channel_id=1, source_target_pairs={{1,0},{2,1},{3,2},{4,3},{5,4},{6,5},{7,6},{8,7},{9,8},{10,9},{11,1... | collective-permute-start | bytes 1572872 | tf_op jit(solution)/shard_map/ppermute | solution.py:258
  21.5 3.3 %collective-permute-start = (s16[256,1024]{1,0:T(8,128)(2,1)S(1)}, s16[256,1024]{1,0:T(8,128)(2,1)S(1)}, u32[]{:S(2)}, u32[]{:S(2)}) collective-permute-start(s16[256,1024]{1,0:T(8,128)(2,1)S(1)} %get-tuple-element.8), channel_id=1, source_target_pairs={{0,1},{1,2},{2,3},{3,4},{4,5},{5,6},{6,7},{7,8},{8,9},{9,10},{10,1... | collective-permute-start | bytes 1572872 | tf_op jit(solution)/shard_map/ppermute | solution.py:257
  24.8 14.5 %collective-permute-done.1.after_ref = s16[256,1024]{1,0:T(8,128)(2,1)S(1)} collective-permute-done((s16[256,1024]{1,0:T(8,128)(2,1)S(1)}, s16[256,1024]{1,0:T(8,128)(2,1)S(1)}, u32[]{:S(2)}, u32[]{:S(2)}) %collective-permute-start.1) | collective-permute-done | bytes 524320 | tf_op jit(solution)/shard_map/ppermute | solution.py:258
  39.3 0.0 collective-permute-done.before_ref
  39.3 0.0 copy-done.6
  39.3 0.0 copy-done.8
  39.3 0.0 copy-start.1
  39.4 2.2 %copy-done.1 = f32[4,256,1024]{2,1,0:T(8,128)S(1)} copy-done((f32[4,256,1024]{2,1,0:T(8,128)S(1)}, f32[4,256,1024]{2,1,0:T(8,128)}, u32[]{:S(2)}) %copy-start.1) | copy-done | bytes 4194328
  41.5 0.0 copy-start.4
  41.5 2.2 %copy-done.4 = s32[4,256,1024]{2,1,0:T(8,128)S(1)} copy-done((s32[4,256,1024]{2,1,0:T(8,128)S(1)}, s32[4,256,1024]{2,1,0:T(8,128)}, u32[]{:S(2)}) %copy-start.4) | copy-done | bytes 4194328
  43.7 9.8 %colours.2 = bf16[16,3,16,512]{3,2,1,0:T(8,128)(2,1)} custom-call(f32[4,256,1024]{2,1,0:T(8,128)S(1)} %copy-done.1, s32[4,256,1024]{2,1,0:T(8,128)S(1)} %copy-done.4, s16[256,1024]{1,0:T(8,128)(2,1)S(1)} %collective-permute-done.before_ref, s16[256,1024]{1,0:T(8,128)(2,1)S(1)} %collective-permute-done.1.after_ref, f32[3,8]{1,0:T(4,128)S(1)} %copy-done.6, ...), custom_call_target="tpu_custom_call" | custom-call | flops 26214400 | bytes 10485760 | tf_op jit(solution)/shard_map/colours/pallas_call | solution.py:156
  53.6 0.0 all-to-all-done.opacity_ref
  53.6 5.6 %all-to-all-start.1 = ((bf16[16,3,16,512]{3,2,1,0:T(8,128)(2,1)}), bf16[16,3,16,512]{3,2,1,0:T(8,128)(2,1)S(1)}, u32[]{:S(2)}, u32[]{:S(2)}) async-start(bf16[16,3,16,512]{3,2,1,0:T(8,128)(2,1)} %colours.2), calls=%async_computation.1 | async-start | bytes 1572864 | tf_op jit(solution)/shard_map/all_to_all | solution.py:244
  59.2 0.0 copy-start.2
  59.2 2.2 %copy-done.2 = f32[4,256,1024]{2,1,0:T(8,128)S(1)} copy-done((f32[4,256,1024]{2,1,0:T(8,128)S(1)}, f32[4,256,1024]{2,1,0:T(8,128)}, u32[]{:S(2)}) %copy-start.2) | copy-done | bytes 4194328
  61.4 2.2 %copy-done.5 = s32[4,256,1024]{2,1,0:T(8,128)S(1)} copy-done((s32[4,256,1024]{2,1,0:T(8,128)S(1)}, s32[4,256,1024]{2,1,0:T(8,128)}, u32[]{:S(2)}) %copy-start.5) | copy-done | bytes 4194328
  63.6 8.9 %colours.3 = bf16[16,3,16,512]{3,2,1,0:T(8,128)(2,1)S(1)} custom-call(f32[4,256,1024]{2,1,0:T(8,128)S(1)} %copy-done.2, s32[4,256,1024]{2,1,0:T(8,128)S(1)} %copy-done.5, s16[256,1024]{1,0:T(8,128)(2,1)S(1)} %collective-permute-done.before_ref, s16[256,1024]{1,0:T(8,128)(2,1)S(1)} %collective-permute-done.1.after_ref, f32[3,8]{1,0:T(4,128)S(1)} %copy-done.6, ...), custom_call_target="tpu_custom_call" | custom-call | flops 26214400 | bytes 10485760 | tf_op jit(solution)/shard_map/colours/pallas_call | solution.py:156
  72.5 6.2 %all-to-all-done.1.rest_0_ = bf16[16,3,16,512]{3,2,1,0:T(8,128)(2,1)S(1)} async-done(((bf16[16,3,16,512]{3,2,1,0:T(8,128)(2,1)}), bf16[16,3,16,512]{3,2,1,0:T(8,128)(2,1)S(1)}, u32[]{:S(2)}, u32[]{:S(2)}) %all-to-all-start.1) | async-done | bytes 786464 | tf_op jit(solution)/shard_map/all_to_all | solution.py:244
  78.8 24.4 %all_to_all.15.rest_1_ = bf16[16,3,16,512]{3,2,1,0:T(8,128)(2,1)S(1)} all-to-all(bf16[16,3,16,512]{3,2,1,0:T(8,128)(2,1)S(1)} %colours.3), channel_id=1, replica_groups=mesh['frames'=2,'gz'=16] {'gz'}, dimensions={0} | all-to-all | bytes 1572864 | tf_op jit(solution)/shard_map/all_to_all | solution.py:244
  103.1 0.0 copy-done.9
  103.1 1.8 %blend.1 = f32[4,16,1024]{2,1,0:T(8,128)} custom-call(s32[16]{0:T(128)S(1)} %copy-done.9, bf16[16,16,1024]{2,1,0:T(8,128)(2,1)S(1)} %all-to-all-done.opacity_ref, bf16[16,3,16,512]{3,2,1,0:T(8,128)(2,1)S(1)} %all-to-all-done.1.rest_0_, bf16[16,3,16,512]{3,2,1,0:T(8,128)(2,1)S(1)} %all_to_all.15.rest_1_), custom_call_target="tpu_custom_call" | custom-call | tf_op jit(solution)/shard_map/blend/pallas_call | solution.py:208
  (2 shorter events, 0.0 us)
Async XLA Ops:
  1.9 2.2 %copy-start = (f32[4,256,1024]{2,1,0:T(8,128)S(1)}, f32[4,256,1024]{2,1,0:T(8,128)}, u32[]{:S(2)}) copy-start(f32[4,256,1024]{2,1,0:T(8,128)} %volume_hbm.4) | copy-start | bytes 12582916
  4.1 2.2 %copy-start.3 = (s32[4,256,1024]{2,1,0:T(8,128)S(1)}, s32[4,256,1024]{2,1,0:T(8,128)}, u32[]{:S(2)}) copy-start(s32[4,256,1024]{2,1,0:T(8,128)} %index_hbm.5) | copy-start | bytes 12582916
  6.3 0.7 copy-start.7
  6.9 32.4 %copy-start.6 = (f32[3,8]{1,0:T(4,128)S(1)}, f32[3,8]{1,0:T(4,128)}, u32[]{:S(2)}) copy-start(f32[3,8]{1,0:T(4,128)} %colour_ref.3) | copy-start | bytes 292
  6.9 32.4 %copy-start.8 = (f32[8]{0:T(128)S(1)}, f32[8]{0:T(128)}, u32[]{:S(2)}) copy-start(f32[8]{0:T(128)} %opacity_ref.5) | copy-start | bytes 100
  12.7 40.9 %all-to-all-start = ((bf16[16,16,1024]{2,1,0:T(8,128)(2,1)}), bf16[16,16,1024]{2,1,0:T(8,128)(2,1)S(1)}, u32[]{:S(2)}, u32[]{:S(2)}) async-start(bf16[16,16,1024]{2,1,0:T(8,128)(2,1)} %bitcast.2), calls=%async_computation | async-start | bytes 1048576 | tf_op jit(solution)/shard_map/all_to_all | solution.py:244
  19.2 20.1 %collective-permute-start.1 = (s16[256,1024]{1,0:T(8,128)(2,1)S(1)}, s16[256,1024]{1,0:T(8,128)(2,1)S(1)}, u32[]{:S(2)}, u32[]{:S(2)}) collective-permute-start(s16[256,1024]{1,0:T(8,128)(2,1)S(1)} %get-tuple-element.7), channel_id=1, source_target_pairs={{1,0},{2,1},{3,2},{4,3},{5,4},{6,5},{7,6},{8,7},{9,8},{10,9},{11,1... | collective-permute-start | bytes 1572872 | tf_op jit(solution)/shard_map/ppermute | solution.py:258
  21.5 17.8 %collective-permute-start = (s16[256,1024]{1,0:T(8,128)(2,1)S(1)}, s16[256,1024]{1,0:T(8,128)(2,1)S(1)}, u32[]{:S(2)}, u32[]{:S(2)}) collective-permute-start(s16[256,1024]{1,0:T(8,128)(2,1)S(1)} %get-tuple-element.8), channel_id=1, source_target_pairs={{0,1},{1,2},{2,3},{3,4},{4,5},{5,6},{6,7},{7,8},{8,9},{9,10},{10,1... | collective-permute-start | bytes 1572872 | tf_op jit(solution)/shard_map/ppermute | solution.py:257
  39.3 2.2 %copy-start.1 = (f32[4,256,1024]{2,1,0:T(8,128)S(1)}, f32[4,256,1024]{2,1,0:T(8,128)}, u32[]{:S(2)}) copy-start(f32[4,256,1024]{2,1,0:T(8,128)} %volume_hbm.4) | copy-start | bytes 12582916
  41.5 2.2 %copy-start.4 = (s32[4,256,1024]{2,1,0:T(8,128)S(1)}, s32[4,256,1024]{2,1,0:T(8,128)}, u32[]{:S(2)}) copy-start(s32[4,256,1024]{2,1,0:T(8,128)} %index_hbm.5) | copy-start | bytes 12582916
  53.6 25.2 %all-to-all-start.1 = ((bf16[16,3,16,512]{3,2,1,0:T(8,128)(2,1)}), bf16[16,3,16,512]{3,2,1,0:T(8,128)(2,1)S(1)}, u32[]{:S(2)}, u32[]{:S(2)}) async-start(bf16[16,3,16,512]{3,2,1,0:T(8,128)(2,1)} %colours.2), calls=%async_computation.1 | async-start | bytes 1572864 | tf_op jit(solution)/shard_map/all_to_all | solution.py:244
  59.2 2.2 %copy-start.2 = (f32[4,256,1024]{2,1,0:T(8,128)S(1)}, f32[4,256,1024]{2,1,0:T(8,128)}, u32[]{:S(2)}) copy-start(f32[4,256,1024]{2,1,0:T(8,128)} %volume_hbm.4) | copy-start | bytes 12582916
  61.4 2.2 %copy-start.5 = (s32[4,256,1024]{2,1,0:T(8,128)S(1)}, s32[4,256,1024]{2,1,0:T(8,128)}, u32[]{:S(2)}) copy-start(s32[4,256,1024]{2,1,0:T(8,128)} %index_hbm.5) | copy-start | bytes 12582916
  63.6 39.5 %copy-start.9 = (s32[16]{0:T(128)S(1)}, s32[16]{0:T(128)}, u32[]{:S(2)}) copy-start(s32[16]{0:T(128)} %order_ref.1) | copy-start | bytes 196

commit v3 on v2

--- a/solution.py
+++ b/solution.py
@@ -13,7 +13,8 @@
 LANES = 128
 PAD = 8
 NT = 8
-LIMIT = 40 * 1024 * 1024
+LIMIT = 58 * 1024 * 1024
+UNROLL = 4
 
 
 def spread(table_ref, *row):
@@ -53,7 +54,7 @@
         for copy in copies[t]:
             copy.wait()
 
-        @pl.loop(0, vol.shape[2] // BLOCK)
+        @pl.loop(0, vol.shape[2] // BLOCK, unroll=UNROLL)
         def _(i):
             rows = pl.ds(pl.multiple_of(i * BLOCK, BLOCK), BLOCK)
             transmit = None
@@ -116,7 +117,7 @@
                 arrived.add(near)
         indices[t].wait()
 
-        @pl.loop(0, height // BLOCK)
+        @pl.loop(0, height // BLOCK, unroll=UNROLL)
         def _(i):
             start = pl.multiple_of(i * BLOCK, BLOCK)
             rows = pl.ds(start, BLOCK)
@@ -173,7 +174,7 @@
         compiler_params=pltpu.CompilerParams(vmem_limit_bytes=LIMIT),
         cost_estimate=pl.CostEstimate(
             flops=50 * slices * height * count * LANES,
-            bytes_accessed=10 * volume.size,
+            bytes_accessed=400 * volume.size,
             transcendentals=2 * slices * height * count * LANES,
         ),
         name="colours",
@@ -259,12 +260,8 @@
     later, _ = lax.optimization_barrier((volume, (last, initial)))
     opacity = opacities(later, tf_index, tf_opacity).reshape(height // BLOCK, BLOCK, width)
     opacity = exchange(by_owner(opacity, devices))
-    tiles = width // LANES
-    half = tiles // 2
-    parts = []
-    for first in range(0, tiles, half):
-        part = colours(volume, tf_index, before, after, tf_color, tf_opacity, first, half)
-        parts.append(exchange(by_owner(part, devices)))
+    colour = colours(volume, tf_index, before, after, tf_color, tf_opacity, 0, width // LANES)
+    parts = [exchange(by_owner(colour, devices))]
     whole_blocks = (height // devices) % BLOCK == 0
     return (blend if whole_blocks else blend_plain)(order, opacity, parts)
 

time: 107 us -> 92.3 us (0.86); the launches traced: 105 us -> 91.3 us
  blocking collectives: 24.4 us -> 41.6 us
  local copies, waits for them, and re-layouts: 13.8 us -> 1.6 us
  Pallas kernels: 26.2 us -> 19.5 us
  waiting for transfers between devices: 20.8 us -> 14.5 us
  starting transfers between devices: 17.8 us -> 12.1 us
    all_to_all x1, blocking collectives: 24.4 us -> 41.6 us  [exchange(): return lax.all_to_all(x, 'gz', split_axis=0, concat_axis=0, tiled=True)]
    unnamed x20 -> x6, local copies, waits for them, and re-layouts: 13.8 us -> 1.6 us
    pallas_call x2 -> x1, Pallas kernels: 18.8 us -> 11.2 us  [colours(): pl.pallas_call(functools.partial(colour_kernel, slices, tiles, first, cou...]
    all_to_all x2 -> x1, waiting for transfers between devices: 6.24 us -> 0.01 us  [exchange(): return lax.all_to_all(x, 'gz', split_axis=0, concat_axis=0, tiled=True)]
    all_to_all x2 -> x1, starting transfers between devices: 12.2 us -> 6.59 us  [exchange(): return lax.all_to_all(x, 'gz', split_axis=0, concat_axis=0, tiled=True)]
    pallas_call x1, Pallas kernels: 1.77 us -> 2.91 us  [blend(): pl.pallas_call(functools.partial(blend_kernel, ranks, len(colour_parts)),...]
  transfers between devices with their start and end apart: 4 -> 3, of which waited for: 2 -> 1; matrix products, arithmetic and copies ran while one was open for 0% -> 0% of each run, Pallas kernels for 18% -> 12%
where the time goes in v3:
time: 92.3 us; the launch traced here: 91.3 us
  blocking collectives  41.6 us (45%)
  Pallas kernels  19.5 us (21%)
  waiting for transfers between devices  14.5 us (16%)
  starting transfers between devices  12.1 us (13%)
  other arithmetic  1.9 us (2%)
  local copies, waits for them, and re-layouts  1.6 us (2%)
    all_to_all x1, blocking collectives, exchange(): return lax.all_to_all(x, 'gz', split_axis=0, concat_axis=0, tiled=True)  41.6 us
    ppermute x1, waiting for transfers between devices, shards(): after = lax.ppermute(initial, 'gz', down)  14.5 us
    pallas_call x1, Pallas kernels, colours(): pl.pallas_call(functools.partial(colour_kernel, slices, tiles, first, cou...  11.2 us
    all_to_all x1, starting transfers between devices, exchange(): return lax.all_to_all(x, 'gz', split_axis=0, concat_axis=0, tiled=True)  6.59 us
    pallas_call x1, Pallas kernels, opacities(): pl.pallas_call(functools.partial(opacity_kernel, slices, tiles), out_shap...  5.39 us
    ppermute x1, starting transfers between devices, shards(): before = lax.ppermute(last, 'gz', up)  3.29 us
    pallas_call x1, Pallas kernels, blend(): pl.pallas_call(functools.partial(blend_kernel, ranks, len(colour_parts)),...  2.91 us
    ppermute x1, starting transfers between devices, shards(): after = lax.ppermute(initial, 'gz', down)  2.26 us
  transfers between devices with their start and end apart: 3, of which 1 were waited for; matrix products, arithmetic and copies ran while one was open for 0% of the time, Pallas kernels for 12%

profile of v3, /device:TPU:13, one launch (start us, length us, event | category | flops | bytes accessed | tf_op | source)
XLA Modules:
  0.0 91.3 jit_solution(3707928906303462415)
XLA Ops:
  0.0 1.9 %fusion.1 = (s16[256,1024]{1,0:T(8,128)(2,1)S(1)}, s16[256,1024]{1,0:T(8,128)(2,1)S(1)}) fusion(f32[4,256,1024]{2,1,0:T(8,128)} %volume_hbm.2), kind=kLoop, calls=%fused_computation.3 | loop fusion | flops 1572864 | bytes 3145728 | tf_op jit(solution)/shard_map/convert_element_type | solution.py:249
  1.9 5.4 %opacities.1 = bf16[256,1024]{1,0:T(8,128)(2,1)} custom-call(f32[4,256,1024]{2,1,0:T(8,128)} %volume_hbm.2, s32[4,256,1024]{2,1,0:T(8,128)} %index_hbm.3, f32[8]{0:T(128)} %opacity_ref.3), custom_call_target="tpu_custom_call" | custom-call | flops 15728640 | bytes 9437184 | tf_op jit(solution)/shard_map/opacities/pallas_call | solution.py:71
  7.3 6.6 %all-to-all-start = ((bf16[16,16,1024]{2,1,0:T(8,128)(2,1)}), bf16[16,16,1024]{2,1,0:T(8,128)(2,1)S(1)}, u32[]{:S(2)}, u32[]{:S(2)}) async-start(bf16[16,16,1024]{2,1,0:T(8,128)(2,1)} %bitcast.5), calls=%async_computation | async-start | bytes 1048576 | tf_op jit(solution)/shard_map/all_to_all | solution.py:245
  13.9 2.3 %collective-permute-start.1 = (s16[256,1024]{1,0:T(8,128)(2,1)S(1)}, s16[256,1024]{1,0:T(8,128)(2,1)S(1)}, u32[]{:S(2)}, u32[]{:S(2)}) collective-permute-start(s16[256,1024]{1,0:T(8,128)(2,1)S(1)} %get-tuple-element.7), channel_id=1, source_target_pairs={{1,0},{2,1},{3,2},{4,3},{5,4},{6,5},{7,6},{8,7},{9,8},{10,9},{11,1... | collective-permute-start | bytes 1572872 | tf_op jit(solution)/shard_map/ppermute | solution.py:259
  16.2 3.3 %collective-permute-start = (s16[256,1024]{1,0:T(8,128)(2,1)S(1)}, s16[256,1024]{1,0:T(8,128)(2,1)S(1)}, u32[]{:S(2)}, u32[]{:S(2)}) collective-permute-start(s16[256,1024]{1,0:T(8,128)(2,1)S(1)} %get-tuple-element.8), channel_id=1, source_target_pairs={{0,1},{1,2},{2,3},{3,4},{4,5},{5,6},{6,7},{7,8},{8,9},{9,10},{10,1... | collective-permute-start | bytes 1572872 | tf_op jit(solution)/shard_map/ppermute | solution.py:258
  19.5 14.5 %collective-permute-done.1.after_ref = s16[256,1024]{1,0:T(8,128)(2,1)S(1)} collective-permute-done((s16[256,1024]{1,0:T(8,128)(2,1)S(1)}, s16[256,1024]{1,0:T(8,128)(2,1)S(1)}, u32[]{:S(2)}, u32[]{:S(2)}) %collective-permute-start.1) | collective-permute-done | bytes 524320 | tf_op jit(solution)/shard_map/ppermute | solution.py:259
  34.0 0.0 copy-start.1
  34.0 0.0 collective-permute-done.before_ref
  34.0 0.8 copy-done.1
  34.8 0.0 copy-start.2
  34.8 0.8 copy-done.2
  35.6 11.2 %colours.1 = bf16[16,3,16,1024]{3,2,1,0:T(8,128)(2,1)} custom-call(f32[4,256,1024]{2,1,0:T(8,128)} %volume_hbm.2, s32[4,256,1024]{2,1,0:T(8,128)} %index_hbm.3, s16[256,1024]{1,0:T(8,128)(2,1)} %copy-done.2, s16[256,1024]{1,0:T(8,128)(2,1)} %copy-done.1, f32[3,8]{1,0:T(4,128)} %colour_ref.1, f32[8]{0:T(128)} %opacity_ref.3), custom_call_target="tpu_custom_call" | custom-call | flops 52428800 | bytes 419430400 | tf_op jit(solution)/shard_map/colours/pallas_call | solution.py:157
  46.8 0.0 all-to-all-done.opacity_ref
  46.8 0.0 copy-start
  46.8 41.6 %all_to_all.10.rest_0_ = bf16[16,3,16,1024]{3,2,1,0:T(8,128)(2,1)} all-to-all(bf16[16,3,16,1024]{3,2,1,0:T(8,128)(2,1)} %colours.1), channel_id=1, replica_groups=mesh['frames'=2,'gz'=16] {'gz'}, dimensions={0} | all-to-all | bytes 3145728 | tf_op jit(solution)/shard_map/all_to_all | solution.py:245
  88.4 0.0 copy-done
  88.4 2.9 %blend.1 = f32[4,16,1024]{2,1,0:T(8,128)} custom-call(s32[16]{0:T(128)} %order_ref.1, bf16[16,16,1024]{2,1,0:T(8,128)(2,1)} %copy-done, bf16[16,3,16,1024]{3,2,1,0:T(8,128)(2,1)} %all_to_all.10.rest_0_), custom_call_target="tpu_custom_call" | custom-call | tf_op jit(solution)/shard_map/blend/pallas_call | solution.py:209
Async XLA Ops:
  7.3 39.5 %all-to-all-start = ((bf16[16,16,1024]{2,1,0:T(8,128)(2,1)}), bf16[16,16,1024]{2,1,0:T(8,128)(2,1)S(1)}, u32[]{:S(2)}, u32[]{:S(2)}) async-start(bf16[16,16,1024]{2,1,0:T(8,128)(2,1)} %bitcast.5), calls=%async_computation | async-start | bytes 1048576 | tf_op jit(solution)/shard_map/all_to_all | solution.py:245
  13.9 20.1 %collective-permute-start.1 = (s16[256,1024]{1,0:T(8,128)(2,1)S(1)}, s16[256,1024]{1,0:T(8,128)(2,1)S(1)}, u32[]{:S(2)}, u32[]{:S(2)}) collective-permute-start(s16[256,1024]{1,0:T(8,128)(2,1)S(1)} %get-tuple-element.7), channel_id=1, source_target_pairs={{1,0},{2,1},{3,2},{4,3},{5,4},{6,5},{7,6},{8,7},{9,8},{10,9},{11,1... | collective-permute-start | bytes 1572872 | tf_op jit(solution)/shard_map/ppermute | solution.py:259
  16.2 17.8 %collective-permute-start = (s16[256,1024]{1,0:T(8,128)(2,1)S(1)}, s16[256,1024]{1,0:T(8,128)(2,1)S(1)}, u32[]{:S(2)}, u32[]{:S(2)}) collective-permute-start(s16[256,1024]{1,0:T(8,128)(2,1)S(1)} %get-tuple-element.8), channel_id=1, source_target_pairs={{0,1},{1,2},{2,3},{3,4},{4,5},{5,6},{6,7},{7,8},{8,9},{9,10},{10,1... | collective-permute-start | bytes 1572872 | tf_op jit(solution)/shard_map/ppermute | solution.py:258
  34.0 0.8 copy-start.1
  34.8 0.8 copy-start.2
  46.8 41.6 %copy-start = (bf16[16,16,1024]{2,1,0:T(8,128)(2,1)}, bf16[16,16,1024]{2,1,0:T(8,128)(2,1)S(1)}, u32[]{:S(2)}) copy-start(bf16[16,16,1024]{2,1,0:T(8,128)(2,1)S(1)} %all-to-all-done.opacity_ref) | copy-start | bytes 1572868

commit v4 on v3

--- a/solution.py
+++ b/solution.py
@@ -14,6 +14,7 @@
 PAD = 8
 NT = 8
 LIMIT = 58 * 1024 * 1024
+BLEND_LIMIT = 16 * 1024 * 1024
 UNROLL = 4
 
 
@@ -84,7 +85,7 @@
         ],
         compiler_params=pltpu.CompilerParams(vmem_limit_bytes=LIMIT),
         cost_estimate=pl.CostEstimate(
-            flops=15 * volume.size, bytes_accessed=9 * volume.size, transcendentals=volume.size
+            flops=15 * volume.size, bytes_accessed=40 * volume.size, transcendentals=volume.size
         ),
         name="opacities",
     )(volume, tf_index, tf_opacity)
@@ -174,7 +175,7 @@
         compiler_params=pltpu.CompilerParams(vmem_limit_bytes=LIMIT),
         cost_estimate=pl.CostEstimate(
             flops=50 * slices * height * count * LANES,
-            bytes_accessed=400 * volume.size,
+            bytes_accessed=1000000 * volume.size,
             transcendentals=2 * slices * height * count * LANES,
         ),
         name="colours",
@@ -213,7 +214,7 @@
         + [pl.BlockSpec(memory_space=pltpu.VMEM)] * (1 + len(colour_parts)),
         out_specs=pl.BlockSpec(memory_space=pltpu.VMEM),
         scratch_shapes=[pltpu.SMEM((ranks,), jnp.int32)],
-        compiler_params=pltpu.CompilerParams(vmem_limit_bytes=LIMIT),
+        compiler_params=pltpu.CompilerParams(vmem_limit_bytes=BLEND_LIMIT),
         name="blend",
     )(order, opacity, *colour_parts)
 

time: 92.3 us -> 91.1 us (0.987)
  Pallas kernels: 19.5 us -> 18.4 us
    pallas_call x1, Pallas kernels: 2.91 us -> 1.86 us  [blend(): pl.pallas_call(functools.partial(blend_kernel, ranks, len(colour_parts)),...]
where the time goes in v4:
time: 91.1 us; the launch traced here: 90.1 us
  blocking collectives  41.5 us (46%)
  Pallas kernels  18.4 us (20%)
  waiting for transfers between devices  14.5 us (16%)
  starting transfers between devices  12.2 us (13%)
  other arithmetic  1.9 us (2%)
  local copies, waits for them, and re-layouts  1.6 us (2%)
    all_to_all x1, blocking collectives, exchange(): return lax.all_to_all(x, 'gz', split_axis=0, concat_axis=0, tiled=True)  41.5 us
    ppermute x1, waiting for transfers between devices, shards(): after = lax.ppermute(initial, 'gz', down)  14.5 us
    pallas_call x1, Pallas kernels, colours(): pl.pallas_call(functools.partial(colour_kernel, slices, tiles, first, cou...  11.2 us
    all_to_all x1, starting transfers between devices, exchange(): return lax.all_to_all(x, 'gz', split_axis=0, concat_axis=0, tiled=True)  6.59 us
    pallas_call x1, Pallas kernels, opacities(): pl.pallas_call(functools.partial(opacity_kernel, slices, tiles), out_shap...  5.39 us
    ppermute x1, starting transfers between devices, shards(): before = lax.ppermute(last, 'gz', up)  3.29 us
    ppermute x1, starting transfers between devices, shards(): after = lax.ppermute(initial, 'gz', down)  2.27 us
    convert_element_type x1, other arithmetic, coded(): return jnp.round(a_slice * (STEPS / REACH)).astype(jnp.int16)  1.9 us
  transfers between devices with their start and end apart: 3, of which 1 were waited for; matrix products, arithmetic and copies ran while one was open for 0% of the time, Pallas kernels for 12%

profile of v4, /device:TPU:13, one launch (start us, length us, event | category | flops | bytes accessed | tf_op | source)
XLA Modules:
  0.0 90.1 jit_solution(6733617978223899866)
XLA Ops:
  0.0 1.9 %fusion.1 = (s16[256,1024]{1,0:T(8,128)(2,1)S(1)}, s16[256,1024]{1,0:T(8,128)(2,1)S(1)}) fusion(f32[4,256,1024]{2,1,0:T(8,128)} %volume_hbm.2), kind=kLoop, calls=%fused_computation.3 | loop fusion | flops 1572864 | bytes 3145728 | tf_op jit(solution)/shard_map/convert_element_type | solution.py:250
  1.9 5.4 %opacities.1 = bf16[256,1024]{1,0:T(8,128)(2,1)} custom-call(f32[4,256,1024]{2,1,0:T(8,128)} %volume_hbm.2, s32[4,256,1024]{2,1,0:T(8,128)} %index_hbm.3, f32[8]{0:T(128)} %opacity_ref.3), custom_call_target="tpu_custom_call" | custom-call | flops 15728640 | bytes 41943040 | tf_op jit(solution)/shard_map/opacities/pallas_call | solution.py:72
  7.3 6.6 %all-to-all-start = ((bf16[16,16,1024]{2,1,0:T(8,128)(2,1)}), bf16[16,16,1024]{2,1,0:T(8,128)(2,1)S(1)}, u32[]{:S(2)}, u32[]{:S(2)}) async-start(bf16[16,16,1024]{2,1,0:T(8,128)(2,1)} %bitcast.5), calls=%async_computation | async-start | bytes 1048576 | tf_op jit(solution)/shard_map/all_to_all | solution.py:246
  13.9 0.0 copy-start
  13.9 2.3 %collective-permute-start.1 = (s16[256,1024]{1,0:T(8,128)(2,1)S(1)}, s16[256,1024]{1,0:T(8,128)(2,1)S(1)}, u32[]{:S(2)}, u32[]{:S(2)}) collective-permute-start(s16[256,1024]{1,0:T(8,128)(2,1)S(1)} %get-tuple-element.7), channel_id=1, source_target_pairs={{1,0},{2,1},{3,2},{4,3},{5,4},{6,5},{7,6},{8,7},{9,8},{10,9},{11,1... | collective-permute-start | bytes 1572872 | tf_op jit(solution)/shard_map/ppermute | solution.py:260
  16.2 3.3 %collective-permute-start = (s16[256,1024]{1,0:T(8,128)(2,1)S(1)}, s16[256,1024]{1,0:T(8,128)(2,1)S(1)}, u32[]{:S(2)}, u32[]{:S(2)}) collective-permute-start(s16[256,1024]{1,0:T(8,128)(2,1)S(1)} %get-tuple-element.8), channel_id=1, source_target_pairs={{0,1},{1,2},{2,3},{3,4},{4,5},{5,6},{6,7},{7,8},{8,9},{9,10},{10,1... | collective-permute-start | bytes 1572872 | tf_op jit(solution)/shard_map/ppermute | solution.py:259
  19.5 14.5 %collective-permute-done.1.after_ref = s16[256,1024]{1,0:T(8,128)(2,1)S(1)} collective-permute-done((s16[256,1024]{1,0:T(8,128)(2,1)S(1)}, s16[256,1024]{1,0:T(8,128)(2,1)S(1)}, u32[]{:S(2)}, u32[]{:S(2)}) %collective-permute-start.1) | collective-permute-done | bytes 524320 | tf_op jit(solution)/shard_map/ppermute | solution.py:260
  34.0 0.0 copy-start.1
  34.0 0.0 collective-permute-done.before_ref
  34.0 0.8 copy-done.1
  34.8 0.0 copy-start.2
  34.8 0.8 copy-done.2
  35.6 11.2 %colours.1 = bf16[16,3,16,1024]{3,2,1,0:T(8,128)(2,1)} custom-call(f32[4,256,1024]{2,1,0:T(8,128)} %volume_hbm.2, s32[4,256,1024]{2,1,0:T(8,128)} %index_hbm.3, s16[256,1024]{1,0:T(8,128)(2,1)} %copy-done.2, s16[256,1024]{1,0:T(8,128)(2,1)} %copy-done.1, f32[3,8]{1,0:T(4,128)} %colour_ref.1, f32[8]{0:T(128)} %opacity_ref.3), custom_call_target="tpu_custom_call" | custom-call | flops 52428800 | bytes 1048576000000 | tf_op jit(solution)/shard_map/colours/pallas_call | solution.py:158
  46.8 0.0 all-to-all-done.opacity_ref
  46.8 41.5 %all_to_all.10.rest_0_ = bf16[16,3,16,1024]{3,2,1,0:T(8,128)(2,1)S(1)} all-to-all(bf16[16,3,16,1024]{3,2,1,0:T(8,128)(2,1)} %colours.1), channel_id=1, replica_groups=mesh['frames'=2,'gz'=16] {'gz'}, dimensions={0} | all-to-all | bytes 3145728 | tf_op jit(solution)/shard_map/all_to_all | solution.py:246
  88.3 0.0 copy-done
  88.3 1.9 %blend.1 = f32[4,16,1024]{2,1,0:T(8,128)} custom-call(s32[16]{0:T(128)S(1)} %copy-done, bf16[16,16,1024]{2,1,0:T(8,128)(2,1)S(1)} %all-to-all-done.opacity_ref, bf16[16,3,16,1024]{3,2,1,0:T(8,128)(2,1)S(1)} %all_to_all.10.rest_0_), custom_call_target="tpu_custom_call" | custom-call | tf_op jit(solution)/shard_map/blend/pallas_call | solution.py:210
Async XLA Ops:
  7.3 39.5 %all-to-all-start = ((bf16[16,16,1024]{2,1,0:T(8,128)(2,1)}), bf16[16,16,1024]{2,1,0:T(8,128)(2,1)S(1)}, u32[]{:S(2)}, u32[]{:S(2)}) async-start(bf16[16,16,1024]{2,1,0:T(8,128)(2,1)} %bitcast.5), calls=%async_computation | async-start | bytes 1048576 | tf_op jit(solution)/shard_map/all_to_all | solution.py:246
  13.9 74.4 %copy-start = (s32[16]{0:T(128)S(1)}, s32[16]{0:T(128)}, u32[]{:S(2)}) copy-start(s32[16]{0:T(128)} %order_ref.1) | copy-start | bytes 196
  13.9 20.1 %collective-permute-start.1 = (s16[256,1024]{1,0:T(8,128)(2,1)S(1)}, s16[256,1024]{1,0:T(8,128)(2,1)S(1)}, u32[]{:S(2)}, u32[]{:S(2)}) collective-permute-start(s16[256,1024]{1,0:T(8,128)(2,1)S(1)} %get-tuple-element.7), channel_id=1, source_target_pairs={{1,0},{2,1},{3,2},{4,3},{5,4},{6,5},{7,6},{8,7},{9,8},{10,9},{11,1... | collective-permute-start | bytes 1572872 | tf_op jit(solution)/shard_map/ppermute | solution.py:260
  16.2 17.8 %collective-permute-start = (s16[256,1024]{1,0:T(8,128)(2,1)S(1)}, s16[256,1024]{1,0:T(8,128)(2,1)S(1)}, u32[]{:S(2)}, u32[]{:S(2)}) collective-permute-start(s16[256,1024]{1,0:T(8,128)(2,1)S(1)} %get-tuple-element.8), channel_id=1, source_target_pairs={{0,1},{1,2},{2,3},{3,4},{4,5},{5,6},{6,7},{7,8},{8,9},{9,10},{10,1... | collective-permute-start | bytes 1572872 | tf_op jit(solution)/shard_map/ppermute | solution.py:259
  34.0 0.8 copy-start.1
  34.8 0.8 copy-start.2

commit v5 on v4

v5 whole, which is shorter than its diff:
```python
import functools

import jax
import jax.numpy as jnp
from jax import lax
from jax.experimental import pallas as pl
from jax.experimental.pallas import tpu as pltpu
from jax.sharding import PartitionSpec as P

REACH = 6.0
STEPS = 32767.0
BLOCK = 16
LANES = 128
PAD = 8
NT = 8
LIMIT = 58 * 1024 * 1024
BLEND_LIMIT = 16 * 1024 * 1024
UNROLL = 4
PLANES = 4


def spread(table_ref, *row):
    sublane = lax.broadcasted_iota(jnp.int32, (NT, LANES), 0)
    table = jnp.zeros((NT, LANES), jnp.float32)
    for m in range(NT):
        table = jnp.where(sublane == m, table_ref[(*row, m)], table)
    return table


def lookup(table, index):
    parts = [
        jnp.take_along_axis(table, index[r : r + NT], axis=0, mode="promise_in_bounds")
        for r in range(0, index.shape[0], NT)
    ]
    return jnp.concatenate(parts, 0)


def alpha_of(centre, index, table):
    return lookup(table, index) * (1.0 - jnp.exp(-centre * centre))


def fetched(source, target, sems, kind, tile, row):
    height = source.shape[1]
    return pltpu.make_async_copy(
        source.at[:, :, pl.ds(tile * LANES, LANES)], target.at[:, tile, pl.ds(row, height), :], sems.at[kind, tile]
    )


def opacity_kernel(slices, tiles, turns, volume_hbm, index_hbm, opacity_ref, *rest):
    out_refs, (vol, idx, sems) = rest[:turns], rest[turns:]
    copies = [(fetched(volume_hbm, vol, sems, 0, t, 0), fetched(index_hbm, idx, sems, 1, t, 0)) for t in range(tiles)]
    for pair in copies:
        for copy in pair:
            copy.start()
    table = spread(opacity_ref)
    height = vol.shape[2] // turns
    plane = lax.axis_index("gz") // (lax.axis_size("gz") // turns)
    for t in range(tiles):
        for copy in copies[t]:
            copy.wait()
        for turn, out_ref in enumerate(out_refs):
            base = lax.rem(plane + turn, turns) * height

            @pl.loop(0, height // BLOCK, unroll=UNROLL)
            def _(i):
                rows = pl.ds(pl.multiple_of(base + i * BLOCK, BLOCK), BLOCK)
                transmit = None
                for k in range(slices):
                    clear = 1.0 - alpha_of(vol[k, t, rows, :], idx[k, t, rows, :], table)
                    transmit = clear if transmit is None else transmit * clear
                out_ref[i, :, pl.ds(t * LANES, LANES)] = (1.0 - transmit).astype(jnp.bfloat16)


def opacities(volume, tf_index, tf_opacity, turns):
    slices, height, width = volume.shape
    tiles = width // LANES
    tiled = (slices, tiles, height, LANES)
    return pl.pallas_call(
        functools.partial(opacity_kernel, slices, tiles, turns),
        out_shape=[jax.ShapeDtypeStruct((height // BLOCK // turns, BLOCK, width), jnp.bfloat16)] * turns,
        in_specs=[
            pl.BlockSpec(memory_space=pltpu.HBM),
            pl.BlockSpec(memory_space=pltpu.HBM),
            pl.BlockSpec(memory_space=pltpu.SMEM),
        ],
        out_specs=[pl.BlockSpec(memory_space=pltpu.VMEM)] * turns,
        scratch_shapes=[
            pltpu.VMEM(tiled, jnp.float32),
            pltpu.VMEM(tiled, jnp.int32),
            pltpu.SemaphoreType.DMA((2, tiles)),
        ],
        compiler_params=pltpu.CompilerParams(vmem_limit_bytes=LIMIT),
        cost_estimate=pl.CostEstimate(
            flops=15 * volume.size, bytes_accessed=9 * volume.size, transcendentals=volume.size
        ),
        name="opacities",
    )(volume, tf_index, tf_opacity)


def colour_kernel(
    slices, tiles, volume_hbm, index_hbm, before_hbm, after_hbm, colour_ref, opacity_ref, out_hbm,
    vol, idx, before_ref, after_ref, out_ref, sems, halo_sems, out_sems,
):
    height = before_ref.shape[0]
    halos = [
        pltpu.make_async_copy(source, target, halo_sems.at[n])
        for n, (source, target) in enumerate([(before_hbm, before_ref), (after_hbm, after_ref)])
    ]
    volumes = [fetched(volume_hbm, vol, sems, 0, t, PAD) for t in range(tiles)]
    indices = [fetched(index_hbm, idx, sems, 1, t, 0) for t in range(tiles)]
    volumes[0].start()
    indices[0].start()
    for copy in halos:
        copy.start()
    for t in range(1, tiles):
        volumes[t].start()
        indices[t].start()
    edge = jnp.zeros((slices, tiles, PAD, LANES), jnp.float32)
    vol[:, :, pl.ds(0, PAD), :] = edge
    vol[:, :, pl.ds(PAD + height, PAD), :] = edge
    lane = lax.broadcasted_iota(jnp.int32, (BLOCK, LANES), 1)
    first_lane, last_lane = lane == 0, lane == LANES - 1
    opacity_table = spread(opacity_ref)
    colour_tables = [spread(colour_ref, c) for c in range(3)]
    volumes[0].wait()
    for copy in halos:
        copy.wait()
    for t in range(tiles):
        if t + 1 < tiles:
            volumes[t + 1].wait()
        indices[t].wait()
        cols = pl.ds(t * LANES, LANES)

        @pl.loop(0, height // BLOCK, unroll=UNROLL)
        def _(i):
            start = pl.multiple_of(i * BLOCK, BLOCK)
            rows = pl.ds(start, BLOCK)
            halo = [ref[rows, cols].astype(jnp.float32) * (REACH / STEPS) for ref in (before_ref, after_ref)]
            inside = pl.ds(pl.multiple_of(start + PAD, PAD), BLOCK)
            centres = [halo[0]] + [vol[k, t, inside, :] for k in range(slices)] + [halo[1]]
            transmit, sums = None, None
            for k in range(slices):
                centre = centres[k + 1]
                depth = centres[k + 2] - centres[k]
                across = vol[k, t, pl.ds(start + (PAD + 1), BLOCK), :] - vol[k, t, pl.ds(start + (PAD - 1), BLOCK), :]
                beside_left = vol[k, t - 1, inside, :] if t > 0 else 0.0
                beside_right = vol[k, t + 1, inside, :] if t + 1 < tiles else 0.0
                left = pltpu.roll(jnp.where(last_lane, beside_left, centre), 1, 1)
                right = pltpu.roll(jnp.where(first_lane, beside_right, centre), LANES - 1, 1)
                along = right - left
                facing = jnp.abs((0.65 * 0.48) * depth + (0.65 * 0.6) * across + (0.65 * 0.64) * along)
                squares = depth * depth + across * across + along * along + 4.0
                shading = 0.35 + facing * lax.rsqrt(squares)
                index = idx[k, t, rows, :]
                alpha = alpha_of(centre, index, opacity_table)
                shown = shading * alpha
                if transmit is not None:
                    shown = transmit * shown
                terms = [lookup(table, index) * shown for table in colour_tables]
                sums = terms if sums is None else [s + add for s, add in zip(sums, terms)]
                if k + 1 < slices:
                    transmit = 1.0 - alpha if transmit is None else transmit * (1.0 - alpha)
            for c in range(3):
                out_ref[i, c, :, cols] = sums[c].astype(jnp.bfloat16)

        pltpu.make_async_copy(out_ref.at[:, :, :, cols], out_hbm.at[:, :, :, cols], out_sems.at[t]).start()
    for t in range(tiles):
        cols = pl.ds(t * LANES, LANES)
        pltpu.make_async_copy(out_ref.at[:, :, :, cols], out_hbm.at[:, :, :, cols], out_sems.at[t]).wait()


def colours(volume, tf_index, before, after, tf_color, tf_opacity):
    slices, height, width = volume.shape
    tiles = width // LANES
    shape = (height // BLOCK, 3, BLOCK, width)
    return pl.pallas_call(
        functools.partial(colour_kernel, slices, tiles),
        out_shape=jax.ShapeDtypeStruct(shape, jnp.bfloat16),
        in_specs=[pl.BlockSpec(memory_space=pltpu.HBM)] * 4 + [pl.BlockSpec(memory_space=pltpu.SMEM)] * 2,
        out_specs=pl.BlockSpec(memory_space=pltpu.HBM),
        scratch_shapes=[
            pltpu.VMEM((slices, tiles, height + 2 * PAD, LANES), jnp.float32),
            pltpu.VMEM((slices, tiles, height, LANES), jnp.int32),
            pltpu.VMEM((height, width), jnp.int16),
            pltpu.VMEM((height, width), jnp.int16),
            pltpu.VMEM(shape, jnp.bfloat16),
            pltpu.SemaphoreType.DMA((2, tiles)),
            pltpu.SemaphoreType.DMA((2,)),
            pltpu.SemaphoreType.DMA((tiles,)),
        ],
        compiler_params=pltpu.CompilerParams(vmem_limit_bytes=LIMIT),
        cost_estimate=pl.CostEstimate(
            flops=50 * volume.size, bytes_accessed=40 * volume.size, transcendentals=2 * volume.size
        ),
        name="colours",
    )(volume, tf_index, before, after, tf_color, tf_opacity)


def regroup_kernel(turns, *refs):
    here = lax.rem(lax.axis_index("gz"), turns)
    for s, ref in enumerate(refs[:turns]):
        for m, out_ref in enumerate(refs[turns:]):
            out_ref[s] = ref[here ^ m]


def regroup(parts):
    turns = len(parts)
    return pl.pallas_call(
        functools.partial(regroup_kernel, turns),
        out_shape=[jax.ShapeDtypeStruct(parts[0].shape, parts[0].dtype)] * turns,
        in_specs=[pl.BlockSpec(memory_space=pltpu.VMEM)] * turns,
        out_specs=[pl.BlockSpec(memory_space=pltpu.VMEM)] * turns,
        compiler_params=pltpu.CompilerParams(vmem_limit_bytes=BLEND_LIMIT),
        name="regroup",
    )(*parts)


def blend_kernel(ranks, turns, order_ref, colour_ref, *rest):
    opacity_refs, (out_ref, place, opacity_ref) = rest[:turns], rest[turns:]
    device = lax.axis_index("gz")
    plane, member = device // turns, lax.rem(device, turns)
    for b in range(ranks):
        place[order_ref[b]] = b
    for m, ref in enumerate(opacity_refs):
        for s in range(turns):
            brick = lax.rem(plane + turns - s, turns) * turns + (member ^ m)
            opacity_ref[brick] = ref[s]
    for j in range(colour_ref.shape[3] // LANES):
        cols = pl.ds(j * LANES, LANES)
        canvas = (jnp.zeros((colour_ref.shape[2], LANES), jnp.float32),) * 4
        for rank in range(ranks):
            b = place[rank]
            clear = 1.0 - canvas[3]
            layers = [colour_ref[b, c, :, cols] for c in range(3)] + [opacity_ref[b, :, cols]]
            canvas = tuple(front + clear * back.astype(jnp.float32) for front, back in zip(canvas, layers))
        for c in range(4):
            out_ref[c, :, cols] = canvas[c]


def blend(order, colour, opacity_parts):
    ranks, channels, height, width = colour.shape
    turns = len(opacity_parts)
    return pl.pallas_call(
        functools.partial(blend_kernel, ranks, turns),
        out_shape=jax.ShapeDtypeStruct((4, height, width), jnp.float32),
        in_specs=[pl.BlockSpec(memory_space=pltpu.SMEM)] + [pl.BlockSpec(memory_space=pltpu.VMEM)] * (1 + turns),
        out_specs=pl.BlockSpec(memory_space=pltpu.VMEM),
        scratch_shapes=[pltpu.SMEM((ranks,), jnp.int32), pltpu.VMEM((ranks, height, width), colour.dtype)],
        compiler_params=pltpu.CompilerParams(vmem_limit_bytes=BLEND_LIMIT),
        name="blend",
    )(order, colour, *opacity_parts)


def blend_plain(order, colour, opacity):
    ranks = opacity.shape[0]
    place = jnp.zeros((ranks,), jnp.int32).at[order].set(jnp.arange(ranks, dtype=jnp.int32))
    layers = jnp.concatenate([colour, opacity[:, None]], 1)

    def step(canvas, b):
        layer = lax.dynamic_index_in_dim(layers, b, 0, keepdims=False).astype(jnp.float32)
        return canvas + (1.0 - canvas[3:4]) * layer, None

    return lax.scan(step, jnp.zeros(layers.shape[1:], jnp.float32), place)[0]


def by_owner(blocks_first, devices):
    blocks, width = blocks_first.shape[0], blocks_first.shape[-1]
    middle = blocks_first.shape[1:-2]
    if blocks == devices:
        return blocks_first
    each = devices // blocks
    split = blocks_first.reshape((blocks,) + middle + (each, BLOCK // each, width))
    moved = jnp.moveaxis(split, len(middle) + 1, 1)
    return moved.reshape((devices,) + middle + (BLOCK // each, width))


def exchange(x):
    return lax.all_to_all(x, "gz", split_axis=0, concat_axis=0, tiled=True)


def coded(a_slice):
    return jnp.round(a_slice * (STEPS / REACH)).astype(jnp.int16)


def shards(volume, tf_index, tf_color, tf_opacity, order):
    devices = lax.axis_size("gz")
    slices, height, width = volume.shape
    up = [(i, i + 1) for i in range(devices - 1)]
    down = [(j, i) for i, j in up]
    last, initial = coded(volume[slices - 1]), coded(volume[0])
    before = lax.ppermute(last, "gz", up)
    after = lax.ppermute(initial, "gz", down)
    later, _ = lax.optimization_barrier((volume, (last, initial)))
    turns = PLANES if devices == PLANES * PLANES and height // devices == BLOCK else 1
    own, *others = opacities(later, tf_index, tf_opacity, turns)
    colour = by_owner(colours(volume, tf_index, before, after, tf_color, tf_opacity), devices)
    if turns == 1:
        return blend_plain(order, exchange(colour), exchange(by_owner(own, devices)))
    shifted = [
        lax.ppermute(part, "gz", [(i, (i + s * turns) % devices) for i in range(devices)])
        for s, part in enumerate(others, 1)
    ]
    shifted, colour = lax.optimization_barrier((shifted, colour))
    mine, *swapped = regroup([own] + shifted)
    swapped = [lax.ppermute(part, "gz", [(i, i ^ m) for i in range(devices)]) for m, part in enumerate(swapped, 1)]
    return blend(order, exchange(colour), [mine] + swapped)


def solution(mesh):
    placed = (P("gz", "frames", None), P("gz", "frames", None), P(), P(), P("frames"))
    return jax.shard_map(
        shards, mesh=mesh, in_specs=placed, out_specs=P("frames", "gz", None), check_vma=False
    )
```

time: 91.1 us -> 74 us (0.81)
  blocking collectives: 41.5 us -> 0 us
  waiting for transfers between devices: 14.5 us -> 35 us
  starting transfers between devices: 12.2 us -> 17 us
  Pallas kernels: 18.4 us -> 17.4 us
    all_to_all x1 -> x0, blocking collectives: 41.5 us -> none  [exchange(): return lax.all_to_all(x, 'gz', split_axis=0, concat_axis=0, tiled=True)]
    all_to_all x1, waiting for transfers between devices: 0.01 us -> 17.8 us  [exchange(): return lax.all_to_all(x, 'gz', split_axis=0, concat_axis=0, tiled=True)]
    ppermute x0 -> x6, waiting for transfers between devices: none -> 15.5 us  [the longest x3 15.5 us: shards(): lax.ppermute(part, 'gz', [(i, i ^ m) for i in range(devices)])]
    ppermute x1, waiting for transfers between devices: 14.5 us -> 1.78 us  [shards(): after = lax.ppermute(initial, 'gz', down)]
    ppermute x0 -> x6, starting transfers between devices: none -> 6.05 us  [the longest x3 3.83 us: shards(): lax.ppermute(part, 'gz', [(i, (i + s * turns) % devices) for i in range(d...]
    all_to_all x1, starting transfers between devices: 6.59 us -> 5.35 us  [exchange(): return lax.all_to_all(x, 'gz', split_axis=0, concat_axis=0, tiled=True)]
    pallas_call x3 -> x4, Pallas kernels: 18.4 us -> 17.4 us  [the longest x1 10.3 us: colours(): pl.pallas_call(functools.partial(colour_kernel, slices, tiles), out_shape...]
  transfers between devices with their start and end apart: 3 -> 9, of which waited for: 1 -> 4; matrix products, arithmetic and copies ran while one was open for 0% -> 0% of each run, Pallas kernels for 12% -> 21%
where the time goes in v5:
time: 74 us; the launch traced here: 73 us
  waiting for transfers between devices  35 us (47%)
  Pallas kernels  17.4 us (24%)
  starting transfers between devices  17 us (23%)
  other arithmetic  1.9 us (3%)
  local copies, waits for them, and re-layouts  1.65 us (2%)
    all_to_all x1, waiting for transfers between devices, exchange(): return lax.all_to_all(x, 'gz', split_axis=0, concat_axis=0, tiled=True)  17.8 us
    ppermute x3, waiting for transfers between devices, shards(): lax.ppermute(part, 'gz', [(i, i ^ m) for i in range(devices)])  15.5 us
    pallas_call x1, Pallas kernels, colours(): pl.pallas_call(functools.partial(colour_kernel, slices, tiles), out_shape...  10.3 us
    all_to_all x1, starting transfers between devices, exchange(): return lax.all_to_all(x, 'gz', split_axis=0, concat_axis=0, tiled=True)  5.35 us
    pallas_call x1, Pallas kernels, opacities(): pl.pallas_call(functools.partial(opacity_kernel, slices, tiles, turns), o...  5.22 us
    ppermute x3, starting transfers between devices, shards(): lax.ppermute(part, 'gz', [(i, (i + s * turns) % devices) for i in range(d...  3.83 us
    ppermute x1, starting transfers between devices, shards(): before = lax.ppermute(last, 'gz', up)  3.02 us
    ppermute x1, starting transfers between devices, shards(): after = lax.ppermute(initial, 'gz', down)  2.58 us
  transfers between devices with their start and end apart: 9, of which 4 were waited for; matrix products, arithmetic and copies ran while one was open for 0% of the time, Pallas kernels for 21%

profile of v5, /device:TPU:13, one launch (start us, length us, event | category | flops | bytes accessed | tf_op | source)
XLA Modules:
  0.0 73.0 jit_solution(18100752394021129980)
XLA Ops:
  0.0 1.9 %fusion.1 = (s16[256,1024]{1,0:T(8,128)(2,1)S(1)}, s16[256,1024]{1,0:T(8,128)(2,1)S(1)}) fusion(f32[4,256,1024]{2,1,0:T(8,128)} %volume_hbm.2), kind=kLoop, calls=%fused_computation.3 | loop fusion | flops 1572864 | bytes 3145728 | tf_op jit(solution)/shard_map/convert_element_type | solution.py:282
  1.9 2.6 %collective-permute-start.4 = (s16[256,1024]{1,0:T(8,128)(2,1)S(1)}, s16[256,1024]{1,0:T(8,128)(2,1)S(1)}, u32[]{:S(2)}, u32[]{:S(2)}) collective-permute-start(s16[256,1024]{1,0:T(8,128)(2,1)S(1)} %get-tuple-element.31), channel_id=1, source_target_pairs={{1,0},{2,1},{3,2},{4,3},{5,4},{6,5},{7,6},{8,7},{9,8},{10,9},{11,1... | collective-permute-start | bytes 1572872 | tf_op jit(solution)/shard_map/ppermute | solution.py:292
  4.5 3.0 %collective-permute-start.3 = (s16[256,1024]{1,0:T(8,128)(2,1)S(1)}, s16[256,1024]{1,0:T(8,128)(2,1)S(1)}, u32[]{:S(2)}, u32[]{:S(2)}) collective-permute-start(s16[256,1024]{1,0:T(8,128)(2,1)S(1)} %get-tuple-element.32), channel_id=1, source_target_pairs={{0,1},{1,2},{2,3},{3,4},{4,5},{5,6},{6,7},{7,8},{8,9},{9,10},{10,1... | collective-permute-start | bytes 1572872 | tf_op jit(solution)/shard_map/ppermute | solution.py:291
  7.5 5.2 %opacities.1 = (bf16[4,16,1024]{2,1,0:T(8,128)(2,1)}, bf16[4,16,1024]{2,1,0:T(8,128)(2,1)}, bf16[4,16,1024]{2,1,0:T(8,128)(2,1)}, bf16[4,16,1024]{2,1,0:T(8,128)(2,1)}) custom-call(f32[4,256,1024]{2,1,0:T(8,128)} %volume_hbm.2, s32[4,256,1024]{2,1,0:T(8,128)} %index_hbm.3, f32[8]{0:T(128)} %opacity_ref.3), custom_call_target="tpu_custom_call" | custom-call | flops 15728640 | bytes 9437184 | tf_op jit(solution)/shard_map/opacities/pallas_call | solution.py:78
  12.7 1.3 %collective-permute-start = (bf16[4,16,1024]{2,1,0:T(8,128)(2,1)}, bf16[4,16,1024]{2,1,0:T(8,128)(2,1)S(1)}, u32[]{:S(2)}, u32[]{:S(2)}) collective-permute-start(bf16[4,16,1024]{2,1,0:T(8,128)(2,1)} %get-tuple-element.19), channel_id=1, source_target_pairs={{0,4},{1,5},{2,6},{3,7},{4,8},{5,9},{6,10},{7,11},{8,12},{9,13},{1... | collective-permute-start | bytes 393224 | tf_op jit(solution)/shard_map/ppermute | solution.py:300
  14.1 1.1 %collective-permute-start.1 = (bf16[4,16,1024]{2,1,0:T(8,128)(2,1)}, bf16[4,16,1024]{2,1,0:T(8,128)(2,1)S(1)}, u32[]{:S(2)}, u32[]{:S(2)}) collective-permute-start(bf16[4,16,1024]{2,1,0:T(8,128)(2,1)} %get-tuple-element.20), channel_id=1, source_target_pairs={{0,8},{1,9},{2,10},{3,11},{4,12},{5,13},{6,14},{7,15},{8,0},{9,1},... | collective-permute-start | bytes 393224 | tf_op jit(solution)/shard_map/ppermute | solution.py:300
  15.2 0.0 copy-start
  15.2 0.0 copy-start.1
  15.2 1.4 %collective-permute-start.2 = (bf16[4,16,1024]{2,1,0:T(8,128)(2,1)}, bf16[4,16,1024]{2,1,0:T(8,128)(2,1)S(1)}, u32[]{:S(2)}, u32[]{:S(2)}) collective-permute-start(bf16[4,16,1024]{2,1,0:T(8,128)(2,1)} %get-tuple-element.21), channel_id=1, source_target_pairs={{0,12},{1,13},{2,14},{3,15},{4,0},{5,1},{6,2},{7,3},{8,4},{9,5},{1... | collective-permute-start | bytes 393224 | tf_op jit(solution)/shard_map/ppermute | solution.py:300
  16.6 1.8 %collective-permute-done.4.after_hbm = s16[256,1024]{1,0:T(8,128)(2,1)S(1)} collective-permute-done((s16[256,1024]{1,0:T(8,128)(2,1)S(1)}, s16[256,1024]{1,0:T(8,128)(2,1)S(1)}, u32[]{:S(2)}, u32[]{:S(2)}) %collective-permute-start.4) | collective-permute-done | bytes 524320 | tf_op jit(solution)/shard_map/ppermute | solution.py:292
  18.4 0.0 copy-start.2
  18.4 0.0 collective-permute-done.3.before_hbm
  18.4 0.8 %copy-done.2 = s16[256,1024]{1,0:T(8,128)(2,1)} copy-done((s16[256,1024]{1,0:T(8,128)(2,1)}, s16[256,1024]{1,0:T(8,128)(2,1)S(1)}, u32[]{:S(2)}) %copy-start.2) | copy-done | bytes 524312
  19.2 0.0 copy-start.3
  19.2 0.8 %copy-done.3 = s16[256,1024]{1,0:T(8,128)(2,1)} copy-done((s16[256,1024]{1,0:T(8,128)(2,1)}, s16[256,1024]{1,0:T(8,128)(2,1)S(1)}, u32[]{:S(2)}) %copy-start.3) | copy-done | bytes 524312
  20.0 10.3 %colours.1 = bf16[16,3,16,1024]{3,2,1,0:T(8,128)(2,1)} custom-call(f32[4,256,1024]{2,1,0:T(8,128)} %volume_hbm.2, s32[4,256,1024]{2,1,0:T(8,128)} %index_hbm.3, s16[256,1024]{1,0:T(8,128)(2,1)} %copy-done.3, s16[256,1024]{1,0:T(8,128)(2,1)} %copy-done.2, f32[3,8]{1,0:T(4,128)} %colour_ref.1, f32[8]{0:T(128)} %opacity_ref.3), custom_call_target="tpu_custom_call" | custom-call | flops 52428800 | bytes 41943040 | tf_op jit(solution)/shard_map/colours/pallas_call | solution.py:176
  30.3 0.0 collective-permute-done.refs_1_
  30.3 0.0 collective-permute-done.1.refs_2_
  30.3 0.0 collective-permute-done.2.refs_3_
  30.4 5.3 %all-to-all-start = ((bf16[16,3,16,1024]{3,2,1,0:T(8,128)(2,1)}), bf16[16,3,16,1024]{3,2,1,0:T(8,128)(2,1)S(1)}, u32[]{:S(2)}, u32[]{:S(2)}) async-start(bf16[16,3,16,1024]{3,2,1,0:T(8,128)(2,1)} %colours.1), calls=%async_computation | async-start | bytes 3145728 | tf_op jit(solution)/shard_map/all_to_all | solution.py:278
  35.7 0.0 copy-done
  35.8 0.4 collective-permute-start.5
  36.2 1.2 %collective-permute-start.6 = (bf16[4,16,1024]{2,1,0:T(8,128)(2,1)S(1)}, bf16[4,16,1024]{2,1,0:T(8,128)(2,1)S(1)}, u32[]{:S(2)}, u32[]{:S(2)}) collective-permute-start(bf16[4,16,1024]{2,1,0:T(8,128)(2,1)S(1)} %get-tuple-element.29), channel_id=1, source_target_pairs={{0,2},{1,3},{2,0},{3,1},{4,6},{5,7},{6,4},{7,5},{8,10},{9,11},{10,... | collective-permute-start | bytes 393224 | tf_op jit(solution)/shard_map/ppermute | solution.py:305
  37.4 0.6 collective-permute-start.7
  38.0 0.0 collective-permute-done.5.rest_1_
  38.0 9.0 %collective-permute-done.6.rest_2_ = bf16[4,16,1024]{2,1,0:T(8,128)(2,1)S(1)} collective-permute-done((bf16[4,16,1024]{2,1,0:T(8,128)(2,1)S(1)}, bf16[4,16,1024]{2,1,0:T(8,128)(2,1)S(1)}, u32[]{:S(2)}, u32[]{:S(2)}) %collective-permute-start.6) | collective-permute-done | bytes 131104 | tf_op jit(solution)/shard_map/ppermute | solution.py:305
  47.0 6.5 %collective-permute-done.7.rest_3_ = bf16[4,16,1024]{2,1,0:T(8,128)(2,1)S(1)} collective-permute-done((bf16[4,16,1024]{2,1,0:T(8,128)(2,1)S(1)}, bf16[4,16,1024]{2,1,0:T(8,128)(2,1)S(1)}, u32[]{:S(2)}, u32[]{:S(2)}) %collective-permute-start.7) | collective-permute-done | bytes 131104 | tf_op jit(solution)/shard_map/ppermute | solution.py:305
  53.4 17.8 %all-to-all-done.colour_ref = bf16[16,3,16,1024]{3,2,1,0:T(8,128)(2,1)S(1)} async-done(((bf16[16,3,16,1024]{3,2,1,0:T(8,128)(2,1)}), bf16[16,3,16,1024]{3,2,1,0:T(8,128)(2,1)S(1)}, u32[]{:S(2)}, u32[]{:S(2)}) %all-to-all-start) | async-done | bytes 1572896 | tf_op jit(solution)/shard_map/all_to_all | solution.py:278
  71.2 0.0 copy-done.1
  71.2 1.8 %blend.1 = f32[4,16,1024]{2,1,0:T(8,128)} custom-call(s32[16]{0:T(128)S(1)} %copy-done.1, bf16[16,3,16,1024]{3,2,1,0:T(8,128)(2,1)S(1)} %all-to-all-done.colour_ref, bf16[4,16,1024]{2,1,0:T(8,128)(2,1)S(1)} %get-tuple-element.27.rest_0_, bf16[4,16,1024]{2,1,0:T(8,128)(2,1)S(1)} %collective-permute-done.5.rest_1_, ...), custom_call_target="tpu_custom_call" | custom-call | tf_op jit(solution)/shard_map/blend/pallas_call | solution.py:243
  (1 shorter events, 0.0 us)
Async XLA Ops:
  1.9 16.5 %collective-permute-start.4 = (s16[256,1024]{1,0:T(8,128)(2,1)S(1)}, s16[256,1024]{1,0:T(8,128)(2,1)S(1)}, u32[]{:S(2)}, u32[]{:S(2)}) collective-permute-start(s16[256,1024]{1,0:T(8,128)(2,1)S(1)} %get-tuple-element.31), channel_id=1, source_target_pairs={{1,0},{2,1},{3,2},{4,3},{5,4},{6,5},{7,6},{8,7},{9,8},{10,9},{11,1... | collective-permute-start | bytes 1572872 | tf_op jit(solution)/shard_map/ppermute | solution.py:292
  4.5 13.9 %collective-permute-start.3 = (s16[256,1024]{1,0:T(8,128)(2,1)S(1)}, s16[256,1024]{1,0:T(8,128)(2,1)S(1)}, u32[]{:S(2)}, u32[]{:S(2)}) collective-permute-start(s16[256,1024]{1,0:T(8,128)(2,1)S(1)} %get-tuple-element.32), channel_id=1, source_target_pairs={{0,1},{1,2},{2,3},{3,4},{4,5},{5,6},{6,7},{7,8},{8,9},{9,10},{10,1... | collective-permute-start | bytes 1572872 | tf_op jit(solution)/shard_map/ppermute | solution.py:291
  12.7 17.6 %collective-permute-start = (bf16[4,16,1024]{2,1,0:T(8,128)(2,1)}, bf16[4,16,1024]{2,1,0:T(8,128)(2,1)S(1)}, u32[]{:S(2)}, u32[]{:S(2)}) collective-permute-start(bf16[4,16,1024]{2,1,0:T(8,128)(2,1)} %get-tuple-element.19), channel_id=1, source_target_pairs={{0,4},{1,5},{2,6},{3,7},{4,8},{5,9},{6,10},{7,11},{8,12},{9,13},{1... | collective-permute-start | bytes 393224 | tf_op jit(solution)/shard_map/ppermute | solution.py:300
  14.1 16.2 %collective-permute-start.1 = (bf16[4,16,1024]{2,1,0:T(8,128)(2,1)}, bf16[4,16,1024]{2,1,0:T(8,128)(2,1)S(1)}, u32[]{:S(2)}, u32[]{:S(2)}) collective-permute-start(bf16[4,16,1024]{2,1,0:T(8,128)(2,1)} %get-tuple-element.20), channel_id=1, source_target_pairs={{0,8},{1,9},{2,10},{3,11},{4,12},{5,13},{6,14},{7,15},{8,0},{9,1},... | collective-permute-start | bytes 393224 | tf_op jit(solution)/shard_map/ppermute | solution.py:300
  15.2 20.5 %copy-start = (bf16[4,16,1024]{2,1,0:T(8,128)(2,1)S(1)}, bf16[4,16,1024]{2,1,0:T(8,128)(2,1)}, u32[]{:S(2)}) copy-start(bf16[4,16,1024]{2,1,0:T(8,128)(2,1)} %get-tuple-element.23.refs_0_) | copy-start | bytes 393220
  15.2 56.0 %copy-start.1 = (s32[16]{0:T(128)S(1)}, s32[16]{0:T(128)}, u32[]{:S(2)}) copy-start(s32[16]{0:T(128)} %order_ref.1) | copy-start | bytes 196
  15.2 15.2 %collective-permute-start.2 = (bf16[4,16,1024]{2,1,0:T(8,128)(2,1)}, bf16[4,16,1024]{2,1,0:T(8,128)(2,1)S(1)}, u32[]{:S(2)}, u32[]{:S(2)}) collective-permute-start(bf16[4,16,1024]{2,1,0:T(8,128)(2,1)} %get-tuple-element.21), channel_id=1, source_target_pairs={{0,12},{1,13},{2,14},{3,15},{4,0},{5,1},{6,2},{7,3},{8,4},{9,5},{1... | collective-permute-start | bytes 393224 | tf_op jit(solution)/shard_map/ppermute | solution.py:300
  18.4 0.8 %copy-start.2 = (s16[256,1024]{1,0:T(8,128)(2,1)}, s16[256,1024]{1,0:T(8,128)(2,1)S(1)}, u32[]{:S(2)}) copy-start(s16[256,1024]{1,0:T(8,128)(2,1)S(1)} %collective-permute-done.4.after_hbm) | copy-start | bytes 1572868
  19.2 0.8 %copy-start.3 = (s16[256,1024]{1,0:T(8,128)(2,1)}, s16[256,1024]{1,0:T(8,128)(2,1)S(1)}, u32[]{:S(2)}) copy-start(s16[256,1024]{1,0:T(8,128)(2,1)S(1)} %collective-permute-done.3.before_hbm) | copy-start | bytes 1572868
  30.4 40.8 %all-to-all-start = ((bf16[16,3,16,1024]{3,2,1,0:T(8,128)(2,1)}), bf16[16,3,16,1024]{3,2,1,0:T(8,128)(2,1)S(1)}, u32[]{:S(2)}, u32[]{:S(2)}) async-start(bf16[16,3,16,1024]{3,2,1,0:T(8,128)(2,1)} %colours.1), calls=%async_computation | async-start | bytes 3145728 | tf_op jit(solution)/shard_map/all_to_all | solution.py:278
  35.8 2.2 %collective-permute-start.5 = (bf16[4,16,1024]{2,1,0:T(8,128)(2,1)S(1)}, bf16[4,16,1024]{2,1,0:T(8,128)(2,1)S(1)}, u32[]{:S(2)}, u32[]{:S(2)}) collective-permute-start(bf16[4,16,1024]{2,1,0:T(8,128)(2,1)S(1)} %get-tuple-element.28), channel_id=1, source_target_pairs={{0,1},{1,0},{2,3},{3,2},{4,5},{5,4},{6,7},{7,6},{8,9},{9,8},{10,11... | collective-permute-start | bytes 393224 | tf_op jit(solution)/shard_map/ppermute | solution.py:305
  36.2 10.8 %collective-permute-start.6 = (bf16[4,16,1024]{2,1,0:T(8,128)(2,1)S(1)}, bf16[4,16,1024]{2,1,0:T(8,128)(2,1)S(1)}, u32[]{:S(2)}, u32[]{:S(2)}) collective-permute-start(bf16[4,16,1024]{2,1,0:T(8,128)(2,1)S(1)} %get-tuple-element.29), channel_id=1, source_target_pairs={{0,2},{1,3},{2,0},{3,1},{4,6},{5,7},{6,4},{7,5},{8,10},{9,11},{10,... | collective-permute-start | bytes 393224 | tf_op jit(solution)/shard_map/ppermute | solution.py:305
  37.4 16.1 %collective-permute-start.7 = (bf16[4,16,1024]{2,1,0:T(8,128)(2,1)S(1)}, bf16[4,16,1024]{2,1,0:T(8,128)(2,1)S(1)}, u32[]{:S(2)}, u32[]{:S(2)}) collective-permute-start(bf16[4,16,1024]{2,1,0:T(8,128)(2,1)S(1)} %get-tuple-element.30), channel_id=1, source_target_pairs={{0,3},{1,2},{2,1},{3,0},{4,7},{5,6},{6,5},{7,4},{8,11},{9,10},{10,... | collective-permute-start | bytes 393224 | tf_op jit(solution)/shard_map/ppermute | solution.py:305

commit v6 on v5

--- a/solution.py
+++ b/solution.py
@@ -13,7 +13,7 @@
 LANES = 128
 PAD = 8
 NT = 8
-LIMIT = 58 * 1024 * 1024
+LIMIT = 24 * 1024 * 1024
 BLEND_LIMIT = 16 * 1024 * 1024
 UNROLL = 4
 PLANES = 4
@@ -39,56 +39,32 @@
     return lookup(table, index) * (1.0 - jnp.exp(-centre * centre))
 
 
-def fetched(source, target, sems, kind, tile, row):
-    height = source.shape[1]
-    return pltpu.make_async_copy(
-        source.at[:, :, pl.ds(tile * LANES, LANES)], target.at[:, tile, pl.ds(row, height), :], sems.at[kind, tile]
-    )
-
-
-def opacity_kernel(slices, tiles, turns, volume_hbm, index_hbm, opacity_ref, *rest):
-    out_refs, (vol, idx, sems) = rest[:turns], rest[turns:]
-    copies = [(fetched(volume_hbm, vol, sems, 0, t, 0), fetched(index_hbm, idx, sems, 1, t, 0)) for t in range(tiles)]
-    for pair in copies:
-        for copy in pair:
-            copy.start()
+def opacity_kernel(slices, tiles, turns, vol, idx, opacity_ref, *out_refs):
     table = spread(opacity_ref)
-    height = vol.shape[2] // turns
+    height = vol.shape[1] // turns
     plane = lax.axis_index("gz") // (lax.axis_size("gz") // turns)
-    for t in range(tiles):
-        for copy in copies[t]:
-            copy.wait()
-        for turn, out_ref in enumerate(out_refs):
-            base = lax.rem(plane + turn, turns) * height
-
-            @pl.loop(0, height // BLOCK, unroll=UNROLL)
-            def _(i):
-                rows = pl.ds(pl.multiple_of(base + i * BLOCK, BLOCK), BLOCK)
+    for turn, out_ref in enumerate(out_refs):
+        base = lax.rem(plane + turn, turns) * height
+
+        @pl.loop(0, height // BLOCK)
+        def _(i):
+            rows = pl.ds(pl.multiple_of(base + i * BLOCK, BLOCK), BLOCK)
+            for t in range(tiles):
+                cols = pl.ds(t * LANES, LANES)
                 transmit = None
                 for k in range(slices):
-                    clear = 1.0 - alpha_of(vol[k, t, rows, :], idx[k, t, rows, :], table)
+                    clear = 1.0 - alpha_of(vol[k, rows, cols], idx[k, rows, cols], table)
                     transmit = clear if transmit is None else transmit * clear
-                out_ref[i, :, pl.ds(t * LANES, LANES)] = (1.0 - transmit).astype(jnp.bfloat16)
+                out_ref[i, :, cols] = (1.0 - transmit).astype(jnp.bfloat16)
 
 
 def opacities(volume, tf_index, tf_opacity, turns):
     slices, height, width = volume.shape
-    tiles = width // LANES
-    tiled = (slices, tiles, height, LANES)
-    return pl.pallas_call(
-        functools.partial(opacity_kernel, slices, tiles, turns),
+    return pl.pallas_call(
+        functools.partial(opacity_kernel, slices, width // LANES, turns),
         out_shape=[jax.ShapeDtypeStruct((height // BLOCK // turns, BLOCK, width), jnp.bfloat16)] * turns,
-        in_specs=[
-            pl.BlockSpec(memory_space=pltpu.HBM),
-            pl.BlockSpec(memory_space=pltpu.HBM),
-            pl.BlockSpec(memory_space=pltpu.SMEM),
-        ],
+        in_specs=[pl.BlockSpec(memory_space=pltpu.VMEM)] * 2 + [pl.BlockSpec(memory_space=pltpu.SMEM)],
         out_specs=[pl.BlockSpec(memory_space=pltpu.VMEM)] * turns,
-        scratch_shapes=[
-            pltpu.VMEM(tiled, jnp.float32),
-            pltpu.VMEM(tiled, jnp.int32),
-            pltpu.SemaphoreType.DMA((2, tiles)),
-        ],
         compiler_params=pltpu.CompilerParams(vmem_limit_bytes=LIMIT),
         cost_estimate=pl.CostEstimate(
             flops=15 * volume.size, bytes_accessed=9 * volume.size, transcendentals=volume.size
@@ -98,60 +74,51 @@
 
 
 def colour_kernel(
-    slices, tiles, volume_hbm, index_hbm, before_hbm, after_hbm, colour_ref, opacity_ref, out_hbm,
-    vol, idx, before_ref, after_ref, out_ref, sems, halo_sems, out_sems,
+    slices, tiles, vol, idx, before_ref, after_ref, colour_ref, opacity_ref, out_hbm, out_ref, out_sems
 ):
     height = before_ref.shape[0]
-    halos = [
-        pltpu.make_async_copy(source, target, halo_sems.at[n])
-        for n, (source, target) in enumerate([(before_hbm, before_ref), (after_hbm, after_ref)])
-    ]
-    volumes = [fetched(volume_hbm, vol, sems, 0, t, PAD) for t in range(tiles)]
-    indices = [fetched(index_hbm, idx, sems, 1, t, 0) for t in range(tiles)]
-    volumes[0].start()
-    indices[0].start()
-    for copy in halos:
-        copy.start()
-    for t in range(1, tiles):
-        volumes[t].start()
-        indices[t].start()
-    edge = jnp.zeros((slices, tiles, PAD, LANES), jnp.float32)
-    vol[:, :, pl.ds(0, PAD), :] = edge
-    vol[:, :, pl.ds(PAD + height, PAD), :] = edge
+    blocks = height // BLOCK
     lane = lax.broadcasted_iota(jnp.int32, (BLOCK, LANES), 1)
     first_lane, last_lane = lane == 0, lane == LANES - 1
+    sublane = lax.broadcasted_iota(jnp.int32, (PAD, LANES), 0)
+    first_row, last_row = sublane == 0, sublane == PAD - 1
     opacity_table = spread(opacity_ref)
     colour_tables = [spread(colour_ref, c) for c in range(3)]
-    volumes[0].wait()
-    for copy in halos:
-        copy.wait()
-    for t in range(tiles):
-        if t + 1 < tiles:
-            volumes[t + 1].wait()
-        indices[t].wait()
-        cols = pl.ds(t * LANES, LANES)
-
-        @pl.loop(0, height // BLOCK, unroll=UNROLL)
-        def _(i):
-            start = pl.multiple_of(i * BLOCK, BLOCK)
-            rows = pl.ds(start, BLOCK)
+    steps = blocks // UNROLL
+
+    def shade(i):
+        start = pl.multiple_of(i * BLOCK, BLOCK)
+        rows = pl.ds(start, BLOCK)
+        above = pl.ds(pl.multiple_of(jnp.maximum(start - PAD, 0), PAD), PAD)
+        below = pl.ds(pl.multiple_of(jnp.minimum(start + BLOCK, height - PAD), PAD), PAD)
+        for t in range(tiles):
+            cols = pl.ds(t * LANES, LANES)
             halo = [ref[rows, cols].astype(jnp.float32) * (REACH / STEPS) for ref in (before_ref, after_ref)]
-            inside = pl.ds(pl.multiple_of(start + PAD, PAD), BLOCK)
-            centres = [halo[0]] + [vol[k, t, inside, :] for k in range(slices)] + [halo[1]]
+            centres = [halo[0]] + [vol[k, rows, cols] for k in range(slices)] + [halo[1]]
             transmit, sums = None, None
             for k in range(slices):
                 centre = centres[k + 1]
                 depth = centres[k + 2] - centres[k]
-                across = vol[k, t, pl.ds(start + (PAD + 1), BLOCK), :] - vol[k, t, pl.ds(start + (PAD - 1), BLOCK), :]
-                beside_left = vol[k, t - 1, inside, :] if t > 0 else 0.0
-                beside_right = vol[k, t + 1, inside, :] if t + 1 < tiles else 0.0
+                upper = jnp.where(i > 0, vol[k, above, cols], 0.0)
+                lower = jnp.where(i + 1 < blocks, vol[k, below, cols], 0.0)
+                eights = [upper] + [centre[r : r + PAD] for r in range(0, BLOCK, PAD)] + [lower]
+                across = jnp.concatenate(
+                    [
+                        pltpu.roll(jnp.where(first_row, eights[e + 1], eights[e]), PAD - 1, 0)
+                        - pltpu.roll(jnp.where(last_row, eights[e - 1], eights[e]), 1, 0)
+                        for e in range(1, len(eights) - 1)
+                    ],
+                    0,
+                )
+                beside_left = vol[k, rows, pl.ds((t - 1) * LANES, LANES)] if t > 0 else 0.0
+                beside_right = vol[k, rows, pl.ds((t + 1) * LANES, LANES)] if t + 1 < tiles else 0.0
                 left = pltpu.roll(jnp.where(last_lane, beside_left, centre), 1, 1)
                 right = pltpu.roll(jnp.where(first_lane, beside_right, centre), LANES - 1, 1)
                 along = right - left
                 facing = jnp.abs((0.65 * 0.48) * depth + (0.65 * 0.6) * across + (0.65 * 0.64) * along)
                 squares = depth * depth + across * across + along * along + 4.0
                 shading = 0.35 + facing * lax.rsqrt(squares)
-                index = idx[k, t, rows, :]
+                index = idx[k, rows, cols]
                 alpha = alpha_of(centre, index, opacity_table)
                 shown = shading * alpha
                 if transmit is not None:
@@ -163,31 +130,30 @@
             for c in range(3):
                 out_ref[i, c, :, cols] = sums[c].astype(jnp.bfloat16)
 
-        pltpu.make_async_copy(out_ref.at[:, :, :, cols], out_hbm.at[:, :, :, cols], out_sems.at[t]).start()
-    for t in range(tiles):
-        cols = pl.ds(t * LANES, LANES)
-        pltpu.make_async_copy(out_ref.at[:, :, :, cols], out_hbm.at[:, :, :, cols], out_sems.at[t]).wait()
+    def sent(step):
+        some = pl.ds(step * UNROLL, UNROLL)
+        return pltpu.make_async_copy(out_ref.at[some], out_hbm.at[some], out_sems.at[step])
+
+    for step in range(steps):
+        @pl.loop(step * UNROLL, (step + 1) * UNROLL)
+        def _(i):
+            shade(i)
+
+        sent(step).start()
+    for step in range(steps):
+        sent(step).wait()
 
 
 def colours(volume, tf_index, before, after, tf_color, tf_opacity):
     slices, height, width = volume.shape
-    tiles = width // LANES
-    shape = (height // BLOCK, 3, BLOCK, width)
-    return pl.pallas_call(
-        functools.partial(colour_kernel, slices, tiles),
+    blocks = height // BLOCK
+    shape = (blocks, 3, BLOCK, width)
+    return pl.pallas_call(
+        functools.partial(colour_kernel, slices, width // LANES),
         out_shape=jax.ShapeDtypeStruct(shape, jnp.bfloat16),
-        in_specs=[pl.BlockSpec(memory_space=pltpu.HBM)] * 4 + [pl.BlockSpec(memory_space=pltpu.SMEM)] * 2,
+        in_specs=[pl.BlockSpec(memory_space=pltpu.VMEM)] * 4 + [pl.BlockSpec(memory_space=pltpu.SMEM)] * 2,
         out_specs=pl.BlockSpec(memory_space=pltpu.HBM),
-        scratch_shapes=[
-            pltpu.VMEM((slices, tiles, height + 2 * PAD, LANES), jnp.float32),
-            pltpu.VMEM((slices, tiles, height, LANES), jnp.int32),
-            pltpu.VMEM((height, width), jnp.int16),
-            pltpu.VMEM((height, width), jnp.int16),
-            pltpu.VMEM(shape, jnp.bfloat16),
-            pltpu.SemaphoreType.DMA((2, tiles)),
-            pltpu.SemaphoreType.DMA((2,)),
-            pltpu.SemaphoreType.DMA((tiles,)),
-        ],
+        scratch_shapes=[pltpu.VMEM(shape, jnp.bfloat16), pltpu.SemaphoreType.DMA((blocks // UNROLL,))],
         compiler_params=pltpu.CompilerParams(vmem_limit_bytes=LIMIT),
         cost_estimate=pl.CostEstimate(
             flops=50 * volume.size, bytes_accessed=40 * volume.size, transcendentals=2 * volume.size
@@ -290,9 +256,8 @@
     last, initial = coded(volume[slices - 1]), coded(volume[0])
     before = lax.ppermute(last, "gz", up)
     after = lax.ppermute(initial, "gz", down)
-    later, _ = lax.optimization_barrier((volume, (last, initial)))
     turns = PLANES if devices == PLANES * PLANES and height // devices == BLOCK else 1
-    own, *others = opacities(later, tf_index, tf_opacity, turns)
+    own, *others = opacities(volume, tf_index, tf_opacity, turns)
     colour = by_owner(colours(volume, tf_index, before, after, tf_color, tf_opacity), devices)
     if turns == 1:
         return blend_plain(order, exchange(colour), exchange(by_owner(own, devices)))

time: 74 us -> 72.9 us (0.985)
  Pallas kernels: 17.4 us -> 12.6 us
  local copies, waits for them, and re-layouts: 1.65 us -> 5.03 us
  waiting for transfers between devices: 35 us -> 35.8 us
    pallas_call x2, Pallas kernels: 15.5 us -> 10.8 us  [the longest x1 8.23 us: colours(): pl.pallas_call(functools.partial(colour_kernel, slices, width // LANES),...]
    unnamed x8 -> x10, local copies, waits for them, and re-layouts: 1.65 us -> 5.03 us
    ppermute x3, waiting for transfers between devices: 0.01 us -> 2.61 us  [shards(): lax.ppermute(part, 'gz', [(i, (i + s * turns) % devices) for i in range(d...]
    ppermute x1, waiting for transfers between devices: 1.78 us -> 0.01 us  [shards(): after = lax.ppermute(initial, 'gz', down)]
  transfers between devices with their start and end apart: 9 -> 9, of which waited for: 4 -> 5; matrix products, arithmetic and copies ran while one was open for 0% -> 0% of each run, Pallas kernels for 21% -> 15%
where the time goes in v6:
time: 72.9 us; the launch traced here: 71.8 us
  waiting for transfers between devices  35.8 us (49%)
  starting transfers between devices  16.4 us (22%)
  Pallas kernels  12.6 us (17%)
  local copies, waits for them, and re-layouts  5.03 us (7%)
  other arithmetic  1.9 us (3%)
    all_to_all x1, waiting for transfers between devices, exchange(): return lax.all_to_all(x, 'gz', split_axis=0, concat_axis=0, tiled=True)  17.8 us
    ppermute x3, waiting for transfers between devices, shards(): lax.ppermute(part, 'gz', [(i, i ^ m) for i in range(devices)])  15.5 us
    pallas_call x1, Pallas kernels, colours(): pl.pallas_call(functools.partial(colour_kernel, slices, width // LANES),...  8.23 us
    unnamed x10, local copies, waits for them, and re-layouts  5.03 us
    all_to_all x1, starting transfers between devices, exchange(): return lax.all_to_all(x, 'gz', split_axis=0, concat_axis=0, tiled=True)  4.77 us
    ppermute x3, starting transfers between devices, shards(): lax.ppermute(part, 'gz', [(i, (i + s * turns) % devices) for i in range(d...  3.83 us
    ppermute x1, starting transfers between devices, shards(): before = lax.ppermute(last, 'gz', up)  3.02 us
    ppermute x3, waiting for transfers between devices, shards(): lax.ppermute(part, 'gz', [(i, (i + s * turns) % devices) for i in range(d...  2.61 us
  transfers between devices with their start and end apart: 9, of which 5 were waited for; matrix products, arithmetic and copies ran while one was open for 0% of the time, Pallas kernels for 15%

profile of v6, /device:TPU:13, one launch (start us, length us, event | category | flops | bytes accessed | tf_op | source)
XLA Modules:
  0.0 71.8 jit_solution(16719178430085328682)
XLA Ops:
  0.0 1.9 %fusion.1 = (s16[256,1024]{1,0:T(8,128)(2,1)S(1)}, s16[256,1024]{1,0:T(8,128)(2,1)S(1)}) fusion(f32[4,256,1024]{2,1,0:T(8,128)} %vol.3), kind=kLoop, calls=%fused_computation.3 | loop fusion | flops 1572864 | bytes 3145728 | tf_op jit(solution)/shard_map/convert_element_type | solution.py:248
  1.9 2.6 %collective-permute-start.4 = (s16[256,1024]{1,0:T(8,128)(2,1)S(1)}, s16[256,1024]{1,0:T(8,128)(2,1)S(1)}, u32[]{:S(2)}, u32[]{:S(2)}) collective-permute-start(s16[256,1024]{1,0:T(8,128)(2,1)S(1)} %get-tuple-element.29), channel_id=1, source_target_pairs={{1,0},{2,1},{3,2},{4,3},{5,4},{6,5},{7,6},{8,7},{9,8},{10,9},{11,1... | collective-permute-start | bytes 1572872 | tf_op jit(solution)/shard_map/ppermute | solution.py:258
  4.5 3.0 %collective-permute-start.3 = (s16[256,1024]{1,0:T(8,128)(2,1)S(1)}, s16[256,1024]{1,0:T(8,128)(2,1)S(1)}, u32[]{:S(2)}, u32[]{:S(2)}) collective-permute-start(s16[256,1024]{1,0:T(8,128)(2,1)S(1)} %get-tuple-element.30), channel_id=1, source_target_pairs={{0,1},{1,2},{2,3},{3,4},{4,5},{5,6},{6,7},{7,8},{8,9},{9,10},{10,1... | collective-permute-start | bytes 1572872 | tf_op jit(solution)/shard_map/ppermute | solution.py:257
  7.5 0.0 copy-start
  7.5 2.2 %copy-done = f32[4,256,1024]{2,1,0:T(8,128)S(1)} copy-done((f32[4,256,1024]{2,1,0:T(8,128)S(1)}, f32[4,256,1024]{2,1,0:T(8,128)}, u32[]{:S(2)}) %copy-start) | copy-done | bytes 4194328
  9.7 0.0 copy-start.1
  9.7 2.2 %copy-done.1 = s32[4,256,1024]{2,1,0:T(8,128)S(1)} copy-done((s32[4,256,1024]{2,1,0:T(8,128)S(1)}, s32[4,256,1024]{2,1,0:T(8,128)}, u32[]{:S(2)}) %copy-start.1) | copy-done | bytes 4194328
  11.9 0.0 copy-start.3
  11.9 0.7 copy-done.3
  12.6 0.0 copy-start.2
  12.6 2.5 %opacities.1 = (bf16[4,16,1024]{2,1,0:T(8,128)(2,1)S(1)}, bf16[4,16,1024]{2,1,0:T(8,128)(2,1)S(1)}, bf16[4,16,1024]{2,1,0:T(8,128)(2,1)S(1)}, bf16[4,16,1024]{2,1,0:T(8,128)(2,1)S(1)}) custom-call(f32[4,256,1024]{2,1,0:T(8,128)S(1)} %copy-done, s32[4,256,1024]{2,1,0:T(8,128)S(1)} %copy-done.1, f32[8]{0:T(128)S(1)} %copy-done.3), custom_call_target="tpu_custom_call" | custom-call | flops 15728640 | bytes 9437184 | tf_op jit(solution)/shard_map/opacities/pallas_call | solution.py:63
  15.1 1.3 %collective-permute-start = (bf16[4,16,1024]{2,1,0:T(8,128)(2,1)S(1)}, bf16[4,16,1024]{2,1,0:T(8,128)(2,1)S(1)}, u32[]{:S(2)}, u32[]{:S(2)}) collective-permute-start(bf16[4,16,1024]{2,1,0:T(8,128)(2,1)S(1)} %get-tuple-element.17), channel_id=1, source_target_pairs={{0,4},{1,5},{2,6},{3,7},{4,8},{5,9},{6,10},{7,11},{8,12},{9,13},{1... | collective-permute-start | bytes 393224 | tf_op jit(solution)/shard_map/ppermute | solution.py:265
  16.4 1.1 %collective-permute-start.1 = (bf16[4,16,1024]{2,1,0:T(8,128)(2,1)S(1)}, bf16[4,16,1024]{2,1,0:T(8,128)(2,1)S(1)}, u32[]{:S(2)}, u32[]{:S(2)}) collective-permute-start(bf16[4,16,1024]{2,1,0:T(8,128)(2,1)S(1)} %get-tuple-element.18), channel_id=1, source_target_pairs={{0,8},{1,9},{2,10},{3,11},{4,12},{5,13},{6,14},{7,15},{8,0},{9,1},... | collective-permute-start | bytes 393224 | tf_op jit(solution)/shard_map/ppermute | solution.py:265
  17.5 0.0 copy-start.4
  17.5 1.4 %collective-permute-start.2 = (bf16[4,16,1024]{2,1,0:T(8,128)(2,1)S(1)}, bf16[4,16,1024]{2,1,0:T(8,128)(2,1)S(1)}, u32[]{:S(2)}, u32[]{:S(2)}) collective-permute-start(bf16[4,16,1024]{2,1,0:T(8,128)(2,1)S(1)} %get-tuple-element.19), channel_id=1, source_target_pairs={{0,12},{1,13},{2,14},{3,15},{4,0},{5,1},{6,2},{7,3},{8,4},{9,5},{1... | collective-permute-start | bytes 393224 | tf_op jit(solution)/shard_map/ppermute | solution.py:265
  18.9 0.0 collective-permute-done.4.after_ref
  18.9 0.0 collective-permute-done.3.before_ref
  18.9 0.0 copy-done.2
  18.9 8.2 %colours.1 = bf16[16,3,16,1024]{3,2,1,0:T(8,128)(2,1)} custom-call(f32[4,256,1024]{2,1,0:T(8,128)S(1)} %copy-done, s32[4,256,1024]{2,1,0:T(8,128)S(1)} %copy-done.1, s16[256,1024]{1,0:T(8,128)(2,1)S(1)} %collective-permute-done.3.before_ref, s16[256,1024]{1,0:T(8,128)(2,1)S(1)} %collective-permute-done.4.after_ref, f32[3,8]{1,0:T(4,128)S(1)} %copy-done.2, ...), custom_call_target="tpu_custom_call" | custom-call | flops 52428800 | bytes 41943040 | tf_op jit(solution)/shard_map/colours/pallas_call | solution.py:151
  27.2 0.0 collective-permute-done.refs_1_
  27.2 0.8 %collective-permute-done.1.refs_2_ = bf16[4,16,1024]{2,1,0:T(8,128)(2,1)S(1)} collective-permute-done((bf16[4,16,1024]{2,1,0:T(8,128)(2,1)S(1)}, bf16[4,16,1024]{2,1,0:T(8,128)(2,1)S(1)}, u32[]{:S(2)}, u32[]{:S(2)}) %collective-permute-start.1) | collective-permute-done | bytes 131104 | tf_op jit(solution)/shard_map/ppermute | solution.py:265
  28.0 1.8 %collective-permute-done.2.refs_3_ = bf16[4,16,1024]{2,1,0:T(8,128)(2,1)S(1)} collective-permute-done((bf16[4,16,1024]{2,1,0:T(8,128)(2,1)S(1)}, bf16[4,16,1024]{2,1,0:T(8,128)(2,1)S(1)}, u32[]{:S(2)}, u32[]{:S(2)}) %collective-permute-start.2) | collective-permute-done | bytes 131104 | tf_op jit(solution)/shard_map/ppermute | solution.py:265
  29.8 4.8 %all-to-all-start = ((bf16[16,3,16,1024]{3,2,1,0:T(8,128)(2,1)}), bf16[16,3,16,1024]{3,2,1,0:T(8,128)(2,1)S(1)}, u32[]{:S(2)}, u32[]{:S(2)}) async-start(bf16[16,3,16,1024]{3,2,1,0:T(8,128)(2,1)} %colours.1), calls=%async_computation | async-start | bytes 3145728 | tf_op jit(solution)/shard_map/all_to_all | solution.py:244
  34.6 0.4 collective-permute-start.5
  35.0 1.2 %collective-permute-start.6 = (bf16[4,16,1024]{2,1,0:T(8,128)(2,1)S(1)}, bf16[4,16,1024]{2,1,0:T(8,128)(2,1)S(1)}, u32[]{:S(2)}, u32[]{:S(2)}) collective-permute-start(bf16[4,16,1024]{2,1,0:T(8,128)(2,1)S(1)} %get-tuple-element.27), channel_id=1, source_target_pairs={{0,2},{1,3},{2,0},{3,1},{4,6},{5,7},{6,4},{7,5},{8,10},{9,11},{10,... | collective-permute-start | bytes 393224 | tf_op jit(solution)/shard_map/ppermute | solution.py:270
  36.2 0.6 collective-permute-start.7
  36.8 0.0 collective-permute-done.5.rest_1_
  36.8 9.0 %collective-permute-done.6.rest_2_ = bf16[4,16,1024]{2,1,0:T(8,128)(2,1)S(1)} collective-permute-done((bf16[4,16,1024]{2,1,0:T(8,128)(2,1)S(1)}, bf16[4,16,1024]{2,1,0:T(8,128)(2,1)S(1)}, u32[]{:S(2)}, u32[]{:S(2)}) %collective-permute-start.6) | collective-permute-done | bytes 131104 | tf_op jit(solution)/shard_map/ppermute | solution.py:270
  45.8 6.5 %collective-permute-done.7.rest_3_ = bf16[4,16,1024]{2,1,0:T(8,128)(2,1)S(1)} collective-permute-done((bf16[4,16,1024]{2,1,0:T(8,128)(2,1)S(1)}, bf16[4,16,1024]{2,1,0:T(8,128)(2,1)S(1)}, u32[]{:S(2)}, u32[]{:S(2)}) %collective-permute-start.7) | collective-permute-done | bytes 131104 | tf_op jit(solution)/shard_map/ppermute | solution.py:270
  52.3 17.8 %all-to-all-done.colour_ref = bf16[16,3,16,1024]{3,2,1,0:T(8,128)(2,1)S(1)} async-done(((bf16[16,3,16,1024]{3,2,1,0:T(8,128)(2,1)}), bf16[16,3,16,1024]{3,2,1,0:T(8,128)(2,1)S(1)}, u32[]{:S(2)}, u32[]{:S(2)}) %all-to-all-start) | async-done | bytes 1572896 | tf_op jit(solution)/shard_map/all_to_all | solution.py:244
  70.1 0.0 copy-done.4
  70.1 1.8 %blend.1 = f32[4,16,1024]{2,1,0:T(8,128)} custom-call(s32[16]{0:T(128)S(1)} %copy-done.4, bf16[16,3,16,1024]{3,2,1,0:T(8,128)(2,1)S(1)} %all-to-all-done.colour_ref, bf16[4,16,1024]{2,1,0:T(8,128)(2,1)S(1)} %get-tuple-element.25.rest_0_, bf16[4,16,1024]{2,1,0:T(8,128)(2,1)S(1)} %collective-permute-done.5.rest_1_, ...), custom_call_target="tpu_custom_call" | custom-call | tf_op jit(solution)/shard_map/blend/pallas_call | solution.py:209
  (1 shorter events, 0.0 us)
Async XLA Ops:
  1.9 17.0 %collective-permute-start.4 = (s16[256,1024]{1,0:T(8,128)(2,1)S(1)}, s16[256,1024]{1,0:T(8,128)(2,1)S(1)}, u32[]{:S(2)}, u32[]{:S(2)}) collective-permute-start(s16[256,1024]{1,0:T(8,128)(2,1)S(1)} %get-tuple-element.29), channel_id=1, source_target_pairs={{1,0},{2,1},{3,2},{4,3},{5,4},{6,5},{7,6},{8,7},{9,8},{10,9},{11,1... | collective-permute-start | bytes 1572872 | tf_op jit(solution)/shard_map/ppermute | solution.py:258
  4.5 14.4 %collective-permute-start.3 = (s16[256,1024]{1,0:T(8,128)(2,1)S(1)}, s16[256,1024]{1,0:T(8,128)(2,1)S(1)}, u32[]{:S(2)}, u32[]{:S(2)}) collective-permute-start(s16[256,1024]{1,0:T(8,128)(2,1)S(1)} %get-tuple-element.30), channel_id=1, source_target_pairs={{0,1},{1,2},{2,3},{3,4},{4,5},{5,6},{6,7},{7,8},{8,9},{9,10},{10,1... | collective-permute-start | bytes 1572872 | tf_op jit(solution)/shard_map/ppermute | solution.py:257
  7.5 2.2 %copy-start = (f32[4,256,1024]{2,1,0:T(8,128)S(1)}, f32[4,256,1024]{2,1,0:T(8,128)}, u32[]{:S(2)}) copy-start(f32[4,256,1024]{2,1,0:T(8,128)} %vol.3) | copy-start | bytes 12582916
  9.7 2.2 %copy-start.1 = (s32[4,256,1024]{2,1,0:T(8,128)S(1)}, s32[4,256,1024]{2,1,0:T(8,128)}, u32[]{:S(2)}) copy-start(s32[4,256,1024]{2,1,0:T(8,128)} %idx.3) | copy-start | bytes 12582916
  11.9 0.7 copy-start.3
  12.6 6.4 %copy-start.2 = (f32[3,8]{1,0:T(4,128)S(1)}, f32[3,8]{1,0:T(4,128)}, u32[]{:S(2)}) copy-start(f32[3,8]{1,0:T(4,128)} %colour_ref.1) | copy-start | bytes 292
  15.1 12.1 %collective-permute-start = (bf16[4,16,1024]{2,1,0:T(8,128)(2,1)S(1)}, bf16[4,16,1024]{2,1,0:T(8,128)(2,1)S(1)}, u32[]{:S(2)}, u32[]{:S(2)}) collective-permute-start(bf16[4,16,1024]{2,1,0:T(8,128)(2,1)S(1)} %get-tuple-element.17), channel_id=1, source_target_pairs={{0,4},{1,5},{2,6},{3,7},{4,8},{5,9},{6,10},{7,11},{8,12},{9,13},{1... | collective-permute-start | bytes 393224 | tf_op jit(solution)/shard_map/ppermute | solution.py:265
  16.4 11.6 %collective-permute-start.1 = (bf16[4,16,1024]{2,1,0:T(8,128)(2,1)S(1)}, bf16[4,16,1024]{2,1,0:T(8,128)(2,1)S(1)}, u32[]{:S(2)}, u32[]{:S(2)}) collective-permute-start(bf16[4,16,1024]{2,1,0:T(8,128)(2,1)S(1)} %get-tuple-element.18), channel_id=1, source_target_pairs={{0,8},{1,9},{2,10},{3,11},{4,12},{5,13},{6,14},{7,15},{8,0},{9,1},... | collective-permute-start | bytes 393224 | tf_op jit(solution)/shard_map/ppermute | solution.py:265
  17.5 52.5 %copy-start.4 = (s32[16]{0:T(128)S(1)}, s32[16]{0:T(128)}, u32[]{:S(2)}) copy-start(s32[16]{0:T(128)} %order_ref.1) | copy-start | bytes 196
  17.5 12.3 %collective-permute-start.2 = (bf16[4,16,1024]{2,1,0:T(8,128)(2,1)S(1)}, bf16[4,16,1024]{2,1,0:T(8,128)(2,1)S(1)}, u32[]{:S(2)}, u32[]{:S(2)}) collective-permute-start(bf16[4,16,1024]{2,1,0:T(8,128)(2,1)S(1)} %get-tuple-element.19), channel_id=1, source_target_pairs={{0,12},{1,13},{2,14},{3,15},{4,0},{5,1},{6,2},{7,3},{8,4},{9,5},{1... | collective-permute-start | bytes 393224 | tf_op jit(solution)/shard_map/ppermute | solution.py:265
  29.8 40.3 %all-to-all-start = ((bf16[16,3,16,1024]{3,2,1,0:T(8,128)(2,1)}), bf16[16,3,16,1024]{3,2,1,0:T(8,128)(2,1)S(1)}, u32[]{:S(2)}, u32[]{:S(2)}) async-start(bf16[16,3,16,1024]{3,2,1,0:T(8,128)(2,1)} %colours.1), calls=%async_computation | async-start | bytes 3145728 | tf_op jit(solution)/shard_map/all_to_all | solution.py:244
  34.6 2.2 %collective-permute-start.5 = (bf16[4,16,1024]{2,1,0:T(8,128)(2,1)S(1)}, bf16[4,16,1024]{2,1,0:T(8,128)(2,1)S(1)}, u32[]{:S(2)}, u32[]{:S(2)}) collective-permute-start(bf16[4,16,1024]{2,1,0:T(8,128)(2,1)S(1)} %get-tuple-element.26), channel_id=1, source_target_pairs={{0,1},{1,0},{2,3},{3,2},{4,5},{5,4},{6,7},{7,6},{8,9},{9,8},{10,11... | collective-permute-start | bytes 393224 | tf_op jit(solution)/shard_map/ppermute | solution.py:270
  35.0 10.8 %collective-permute-start.6 = (bf16[4,16,1024]{2,1,0:T(8,128)(2,1)S(1)}, bf16[4,16,1024]{2,1,0:T(8,128)(2,1)S(1)}, u32[]{:S(2)}, u32[]{:S(2)}) collective-permute-start(bf16[4,16,1024]{2,1,0:T(8,128)(2,1)S(1)} %get-tuple-element.27), channel_id=1, source_target_pairs={{0,2},{1,3},{2,0},{3,1},{4,6},{5,7},{6,4},{7,5},{8,10},{9,11},{10,... | collective-permute-start | bytes 393224 | tf_op jit(solution)/shard_map/ppermute | solution.py:270
  36.2 16.1 %collective-permute-start.7 = (bf16[4,16,1024]{2,1,0:T(8,128)(2,1)S(1)}, bf16[4,16,1024]{2,1,0:T(8,128)(2,1)S(1)}, u32[]{:S(2)}, u32[]{:S(2)}) collective-permute-start(bf16[4,16,1024]{2,1,0:T(8,128)(2,1)S(1)} %get-tuple-element.28), channel_id=1, source_target_pairs={{0,3},{1,2},{2,1},{3,0},{4,7},{5,6},{6,5},{7,4},{8,11},{9,10},{10,... | collective-permute-start | bytes 393224 | tf_op jit(solution)/shard_map/ppermute | solution.py:270

commit v7 on v6

--- a/solution.py
+++ b/solution.py
@@ -14,6 +14,7 @@
 PAD = 8
 NT = 8
 LIMIT = 24 * 1024 * 1024
+FETCH_LIMIT = 43 * 1024 * 1024
 BLEND_LIMIT = 16 * 1024 * 1024
 UNROLL = 4
 PLANES = 4
@@ -39,12 +40,25 @@
     return lookup(table, index) * (1.0 - jnp.exp(-centre * centre))
 
 
-def opacity_kernel(slices, tiles, turns, vol, idx, opacity_ref, *out_refs):
-    table = spread(opacity_ref)
+def opacity_kernel(slices, tiles, turns, volume_hbm, index_hbm, opacity_ref, *rest):
+    out_refs, (vol, idx, sems) = rest[:turns], rest[turns:]
     height = vol.shape[1] // turns
     plane = lax.axis_index("gz") // (lax.axis_size("gz") // turns)
-    for turn, out_ref in enumerate(out_refs):
-        base = lax.rem(plane + turn, turns) * height
+    bases = [pl.multiple_of(lax.rem(plane + turn, turns) * height, height) for turn in range(turns)]
+    copies = []
+    for turn, base in enumerate(bases):
+        some = pl.ds(base, height)
+        pair = [
+            pltpu.make_async_copy(source.at[:, some, :], target.at[:, some, :], sems.at[kind, turn])
+            for kind, (source, target) in enumerate([(volume_hbm, vol), (index_hbm, idx)])
+        ]
+        for copy in pair:
+            copy.start()
+        copies.append(pair)
+    table = spread(opacity_ref)
+    for base, pair, out_ref in zip(bases, copies, out_refs):
+        for copy in pair:
+            copy.wait()
 
         @pl.loop(0, height // BLOCK)
         def _(i):
@@ -60,12 +74,15 @@
 
 def opacities(volume, tf_index, tf_opacity, turns):
     slices, height, width = volume.shape
+    part = jax.ShapeDtypeStruct((height // BLOCK // turns, BLOCK, width), jnp.bfloat16)
+    held = [jax.ShapeDtypeStruct(x.shape, x.dtype) for x in (volume, tf_index)]
     return pl.pallas_call(
         functools.partial(opacity_kernel, slices, width // LANES, turns),
-        out_shape=[jax.ShapeDtypeStruct((height // BLOCK // turns, BLOCK, width), jnp.bfloat16)] * turns,
-        in_specs=[pl.BlockSpec(memory_space=pltpu.VMEM)] * 2 + [pl.BlockSpec(memory_space=pltpu.SMEM)],
-        out_specs=[pl.BlockSpec(memory_space=pltpu.VMEM)] * turns,
-        compiler_params=pltpu.CompilerParams(vmem_limit_bytes=LIMIT),
+        out_shape=[part] * turns + held,
+        in_specs=[pl.BlockSpec(memory_space=pltpu.HBM)] * 2 + [pl.BlockSpec(memory_space=pltpu.SMEM)],
+        out_specs=[pl.BlockSpec(memory_space=pltpu.VMEM)] * (turns + 2),
+        scratch_shapes=[pltpu.SemaphoreType.DMA((2, turns))],
+        compiler_params=pltpu.CompilerParams(vmem_limit_bytes=FETCH_LIMIT),
         cost_estimate=pl.CostEstimate(
             flops=15 * volume.size, bytes_accessed=9 * volume.size, transcendentals=volume.size
         ),
@@ -73,25 +90,25 @@
     )(volume, tf_index, tf_opacity)
 
 
-def colour_kernel(
-    slices, tiles, vol, idx, before_ref, after_ref, colour_ref, opacity_ref, out_hbm, out_ref, out_sems
-):
-    height = before_ref.shape[0]
-    blocks = height // BLOCK
+def colour_kernel(slices, span, vol, idx, before_ref, after_ref, colour_ref, opacity_ref, *out_refs):
+    height, width = before_ref.shape
+    blocks, tiles = height // BLOCK, width // LANES
+    turns = len(out_refs)
+    each = blocks // turns
+    plane = lax.axis_index("gz") // (lax.axis_size("gz") // turns)
     lane = lax.broadcasted_iota(jnp.int32, (BLOCK, LANES), 1)
     first_lane, last_lane = lane == 0, lane == LANES - 1
     sublane = lax.broadcasted_iota(jnp.int32, (PAD, LANES), 0)
     first_row, last_row = sublane == 0, sublane == PAD - 1
     opacity_table = spread(opacity_ref)
     colour_tables = [spread(colour_ref, c) for c in range(3)]
-    steps = blocks // UNROLL
-
-    def shade(i):
+
+    def shade(i, out_ref, j):
         start = pl.multiple_of(i * BLOCK, BLOCK)
         rows = pl.ds(start, BLOCK)
         above = pl.ds(pl.multiple_of(jnp.maximum(start - PAD, 0), PAD), PAD)
         below = pl.ds(pl.multiple_of(jnp.minimum(start + BLOCK, height - PAD), PAD), PAD)
-        for t in range(tiles):
+        for t in range(*span):
             cols = pl.ds(t * LANES, LANES)
             halo = [ref[rows, cols].astype(jnp.float32) * (REACH / STEPS) for ref in (before_ref, after_ref)]
             centres = [halo[0]] + [vol[k, rows, cols] for k in range(slices)] + [halo[1]]
@@ -128,36 +145,27 @@
                 if k + 1 < slices:
                     transmit = 1.0 - alpha if transmit is None else transmit * (1.0 - alpha)
             for c in range(3):
-                out_ref[i, c, :, cols] = sums[c].astype(jnp.bfloat16)
-
-    def sent(step):
-        some = pl.ds(step * UNROLL, UNROLL)
-        return pltpu.make_async_copy(out_ref.at[some], out_hbm.at[some], out_sems.at[step])
-
-    for step in range(steps):
-        @pl.loop(step * UNROLL, (step + 1) * UNROLL)
-        def _(i):
-            shade(i)
-
-        sent(step).start()
-    for step in range(steps):
-        sent(step).wait()
-
-
-def colours(volume, tf_index, before, after, tf_color, tf_opacity):
-    slices, height, width = volume.shape
-    blocks = height // BLOCK
-    shape = (blocks, 3, BLOCK, width)
+                out_ref[j, c, :, pl.ds((t - span[0]) * LANES, LANES)] = sums[c].astype(jnp.bfloat16)
+
+    for turn, out_ref in enumerate(out_refs):
+        base = lax.rem(plane + turn, turns) * each
+
+        @pl.loop(0, each)
+        def _(j):
+            shade(base + j, out_ref, j)
+
+
+def colours(volume, tf_index, before, after, tf_color, tf_opacity, span, turns):
+    slices, height, _ = volume.shape
+    part = jax.ShapeDtypeStruct((height // BLOCK // turns, 3, BLOCK, (span[1] - span[0]) * LANES), jnp.bfloat16)
+    cells = slices * height * (span[1] - span[0]) * LANES
     return pl.pallas_call(
-        functools.partial(colour_kernel, slices, width // LANES),
-        out_shape=jax.ShapeDtypeStruct(shape, jnp.bfloat16),
+        functools.partial(colour_kernel, slices, span),
+        out_shape=[part] * turns,
         in_specs=[pl.BlockSpec(memory_space=pltpu.VMEM)] * 4 + [pl.BlockSpec(memory_space=pltpu.SMEM)] * 2,
-        out_specs=pl.BlockSpec(memory_space=pltpu.HBM),
-        scratch_shapes=[pltpu.VMEM(shape, jnp.bfloat16), pltpu.SemaphoreType.DMA((blocks // UNROLL,))],
+        out_specs=[pl.BlockSpec(memory_space=pltpu.VMEM)] * turns,
         compiler_params=pltpu.CompilerParams(vmem_limit_bytes=LIMIT),
-        cost_estimate=pl.CostEstimate(
-            flops=50 * volume.size, bytes_accessed=40 * volume.size, transcendentals=2 * volume.size
-        ),
+        cost_estimate=pl.CostEstimate(flops=50 * cells, bytes_accessed=40 * cells, transcendentals=2 * cells),
         name="colours",
     )(volume, tf_index, before, after, tf_color, tf_opacity)
 
@@ -181,40 +189,58 @@
     )(*parts)
 
 
-def blend_kernel(ranks, turns, order_ref, colour_ref, *rest):
-    opacity_refs, (out_ref, place, opacity_ref) = rest[:turns], rest[turns:]
+def blend_kernel(ranks, turns, colour_count, start, order_ref, *rest):
+    opacity_refs, rest = rest[:turns], rest[turns:]
+    colour_refs, (out_hbm, place, opacity_ref, out_ref, sem) = rest[:colour_count], rest[-5:]
     device = lax.axis_index("gz")
     plane, member = device // turns, lax.rem(device, turns)
+    width = out_ref.shape[2]
     for b in range(ranks):
         place[order_ref[b]] = b
     for m, ref in enumerate(opacity_refs):
         for s in range(turns):
             brick = lax.rem(plane + turns - s, turns) * turns + (member ^ m)
-            opacity_ref[brick] = ref[s]
-    for j in range(colour_ref.shape[3] // LANES):
+            opacity_ref[brick, 3] = ref[s, :, pl.ds(start, width)]
+            if len(colour_refs) > 1:
+                for c in range(3):
+                    opacity_ref[brick, c] = colour_refs[m][s, c]
+    colour_ref = opacity_ref if len(colour_refs) > 1 else colour_refs[0]
+    for j in range(width // LANES):
         cols = pl.ds(j * LANES, LANES)
-        canvas = (jnp.zeros((colour_ref.shape[2], LANES), jnp.float32),) * 4
+        canvas = (jnp.zeros((out_ref.shape[1], LANES), jnp.float32),) * 4
         for rank in range(ranks):
             b = place[rank]
             clear = 1.0 - canvas[3]
-            layers = [colour_ref[b, c, :, cols] for c in range(3)] + [opacity_ref[b, :, cols]]
+            layers = [colour_ref[b, c, :, cols] for c in range(3)] + [opacity_ref[b, 3, :, cols]]
             canvas = tuple(front + clear * back.astype(jnp.float32) for front, back in zip(canvas, layers))
         for c in range(4):
             out_ref[c, :, cols] = canvas[c]
-
-
-def blend(order, colour, opacity_parts):
-    ranks, channels, height, width = colour.shape
-    turns = len(opacity_parts)
+    copy = pltpu.make_async_copy(out_ref, out_hbm.at[:, :, pl.ds(start, width)], sem)
+    copy.start()
+    copy.wait()
+
+
+def blend(order, opacity_parts, colours_here, start, total, image=()):
+    turns, ranks = len(opacity_parts), order.shape[0]
+    height, width = colours_here[0].shape[-2:]
+    operands = [order, *opacity_parts, *colours_here]
     return pl.pallas_call(
-        functools.partial(blend_kernel, ranks, turns),
-        out_shape=jax.ShapeDtypeStruct((4, height, width), jnp.float32),
-        in_specs=[pl.BlockSpec(memory_space=pltpu.SMEM)] + [pl.BlockSpec(memory_space=pltpu.VMEM)] * (1 + turns),
-        out_specs=pl.BlockSpec(memory_space=pltpu.VMEM),
-        scratch_shapes=[pltpu.SMEM((ranks,), jnp.int32), pltpu.VMEM((ranks, height, width), colour.dtype)],
+        functools.partial(blend_kernel, ranks, turns, len(colours_here), start),
+        out_shape=jax.ShapeDtypeStruct((4, height, total), jnp.float32),
+        in_specs=[pl.BlockSpec(memory_space=pltpu.SMEM)]
+        + [pl.BlockSpec(memory_space=pltpu.VMEM)] * (len(operands) - 1)
+        + [pl.BlockSpec(memory_space=pltpu.HBM)] * len(image),
+        out_specs=pl.BlockSpec(memory_space=pltpu.HBM),
+        scratch_shapes=[
+            pltpu.SMEM((ranks,), jnp.int32),
+            pltpu.VMEM((ranks, 4, height, width), jnp.bfloat16),
+            pltpu.VMEM((4, height, width), jnp.float32),
+            pltpu.SemaphoreType.DMA,
+        ],
+        input_output_aliases={len(operands): 0} if image else {},
         compiler_params=pltpu.CompilerParams(vmem_limit_bytes=BLEND_LIMIT),
         name="blend",
-    )(order, colour, *opacity_parts)
+    )(*operands, *image)
 
 
 def blend_plain(order, colour, opacity):
@@ -248,6 +274,19 @@
     return jnp.round(a_slice * (STEPS / REACH)).astype(jnp.int16)
 
 
+def across_planes(parts, turns, devices):
+    return [parts[0]] + [
+        lax.ppermute(part, "gz", [(i, (i + s * turns) % devices) for i in range(devices)])
+        for s, part in enumerate(parts[1:], 1)
+    ]
+
+
+def in_plane(parts, devices):
+    return [parts[0]] + [
+        lax.ppermute(part, "gz", [(i, i ^ m) for i in range(devices)]) for m, part in enumerate(parts[1:], 1)
+    ]
+
+
 def shards(volume, tf_index, tf_color, tf_opacity, order):
     devices = lax.axis_size("gz")
     slices, height, width = volume.shape
@@ -257,18 +296,23 @@
     before = lax.ppermute(last, "gz", up)
     after = lax.ppermute(initial, "gz", down)
     turns = PLANES if devices == PLANES * PLANES and height // devices == BLOCK else 1
-    own, *others = opacities(volume, tf_index, tf_opacity, turns)
-    colour = by_owner(colours(volume, tf_index, before, after, tf_color, tf_opacity), devices)
+    *opacity, volume, tf_index = opacities(volume, tf_index, tf_opacity, turns)
+    tiles = width // LANES
+    held = (volume, tf_index, before, after, tf_color, tf_opacity)
     if turns == 1:
-        return blend_plain(order, exchange(colour), exchange(by_owner(own, devices)))
-    shifted = [
-        lax.ppermute(part, "gz", [(i, (i + s * turns) % devices) for i in range(devices)])
-        for s, part in enumerate(others, 1)
-    ]
-    shifted, colour = lax.optimization_barrier((shifted, colour))
-    mine, *swapped = regroup([own] + shifted)
-    swapped = [lax.ppermute(part, "gz", [(i, i ^ m) for i in range(devices)]) for m, part in enumerate(swapped, 1)]
-    return blend(order, exchange(colour), [mine] + swapped)
+        colour = by_owner(colours(*held, (0, tiles), 1)[0], devices)
+        return blend_plain(order, exchange(colour), exchange(by_owner(opacity[0], devices)))
+    opacity = across_planes(opacity, turns, devices)
+    first = colours(*held, (0, tiles // 2), turns)
+    first, held = lax.optimization_barrier((first, held))
+    first = across_planes(first, turns, devices)
+    (second,) = colours(*held, (tiles // 2, tiles), 1)
+    opacity, second = lax.optimization_barrier((opacity, second))
+    second = exchange(second)
+    opacity = in_plane(regroup(opacity), devices)
+    first = in_plane(regroup(first), devices)
+    image = blend(order, opacity, first, 0, width)
+    return blend(order, opacity, [second], width // 2, width, (image,))
 
 
 def solution(mesh):

time: 72.9 us -> 90.8 us (1.25)
  waiting for transfers between devices: 35.8 us -> 45.9 us
  starting transfers between devices: 16.4 us -> 24.8 us
  Pallas kernels: 12.6 us -> 17.1 us
  local copies, waits for them, and re-layouts: 5.03 us -> 0.66 us
    ppermute x6 -> x12, waiting for transfers between devices: 18.1 us -> 44.1 us  [the longest x6 31.1 us: across_planes(): lax.ppermute(part, 'gz', [(i, (i + s * turns) % devices) for i in range(d...]
    all_to_all x1, waiting for transfers between devices: 17.8 us -> 0.01 us  [exchange(): return lax.all_to_all(x, 'gz', split_axis=0, concat_axis=0, tiled=True)]
    ppermute x6 -> x12, starting transfers between devices: 6.05 us -> 13.1 us  [the longest x6 7.38 us: across_planes(): lax.ppermute(part, 'gz', [(i, (i + s * turns) % devices) for i in range(d...]
    unnamed x10 -> x6, local copies, waits for them, and re-layouts: 5.03 us -> 0.66 us
    pallas_call x2 -> x4, Pallas kernels: 10 us -> 12.5 us  [the longest x2 9.47 us: colours(): pl.pallas_call(functools.partial(colour_kernel, slices, span), out_shape=...]
    pallas_call x1, Pallas kernels: 2.52 us -> 4.52 us  [opacities(): pl.pallas_call(functools.partial(opacity_kernel, slices, width // LANES,...]
    ppermute x1, waiting for transfers between devices: 0.01 us -> 1.81 us  [shards(): after = lax.ppermute(initial, 'gz', down)]
    all_to_all x1, starting transfers between devices: 4.77 us -> 6.16 us  [exchange(): return lax.all_to_all(x, 'gz', split_axis=0, concat_axis=0, tiled=True)]
  transfers between devices with their start and end apart: 9 -> 15, of which waited for: 5 -> 6; matrix products, arithmetic and copies ran while one was open for 0% -> 0% of each run, Pallas kernels for 15% -> 17%
where the time goes in v7:
time: 90.8 us; the launch traced here: 90.5 us
  waiting for transfers between devices  45.9 us (51%)
  starting transfers between devices  24.8 us (27%)
  Pallas kernels  17.1 us (19%)
  other arithmetic  1.9 us (2%)
    ppermute x6, waiting for transfers between devices, across_planes(): lax.ppermute(part, 'gz', [(i, (i + s * turns) % devices) for i in range(d...  31.1 us
    ppermute x6, waiting for transfers between devices, in_plane(): lax.ppermute(part, 'gz', [(i, i ^ m) for i in range(devices)])  13 us
    pallas_call x2, Pallas kernels, colours(): pl.pallas_call(functools.partial(colour_kernel, slices, span), out_shape=...  9.47 us
    ppermute x6, starting transfers between devices, across_planes(): lax.ppermute(part, 'gz', [(i, (i + s * turns) % devices) for i in range(d...  7.38 us
    all_to_all x1, starting transfers between devices, exchange(): return lax.all_to_all(x, 'gz', split_axis=0, concat_axis=0, tiled=True)  6.16 us
    ppermute x6, starting transfers between devices, in_plane(): lax.ppermute(part, 'gz', [(i, i ^ m) for i in range(devices)])  5.71 us
    pallas_call x1, Pallas kernels, opacities(): pl.pallas_call(functools.partial(opacity_kernel, slices, width // LANES,...  4.52 us
    ppermute x1, starting transfers between devices, shards(): before = lax.ppermute(last, 'gz', up)  3.02 us
  transfers between devices with their start and end apart: 15, of which 6 were waited for; matrix products, arithmetic and copies ran while one was open for 0% of the time, Pallas kernels for 17%

profile of v7, /device:TPU:13, one launch (start us, length us, event | category | flops | bytes accessed | tf_op | source)
XLA Modules:
  0.0 90.5 jit_solution(1700780022612396579)
XLA Ops:
  0.0 1.9 %fusion.1 = (s16[256,1024]{1,0:T(8,128)(2,1)S(1)}, s16[256,1024]{1,0:T(8,128)(2,1)S(1)}) fusion(f32[4,256,1024]{2,1,0:T(8,128)} %volume_hbm.1), kind=kLoop, calls=%fused_computation.3 | loop fusion | flops 1572864 | bytes 3145728 | tf_op jit(solution)/shard_map/convert_element_type | solution.py:274
  1.9 2.6 %collective-permute-start.4 = (s16[256,1024]{1,0:T(8,128)(2,1)S(1)}, s16[256,1024]{1,0:T(8,128)(2,1)S(1)}, u32[]{:S(2)}, u32[]{:S(2)}) collective-permute-start(s16[256,1024]{1,0:T(8,128)(2,1)S(1)} %get-tuple-element.71), channel_id=1, source_target_pairs={{1,0},{2,1},{3,2},{4,3},{5,4},{6,5},{7,6},{8,7},{9,8},{10,9},{11,1... | collective-permute-start | bytes 1572872 | tf_op jit(solution)/shard_map/ppermute | solution.py:297
  4.5 0.0 copy-start
  4.5 3.0 %collective-permute-start.3 = (s16[256,1024]{1,0:T(8,128)(2,1)S(1)}, s16[256,1024]{1,0:T(8,128)(2,1)S(1)}, u32[]{:S(2)}, u32[]{:S(2)}) collective-permute-start(s16[256,1024]{1,0:T(8,128)(2,1)S(1)} %get-tuple-element.72), channel_id=1, source_target_pairs={{0,1},{1,2},{2,3},{3,4},{4,5},{5,6},{6,7},{7,8},{8,9},{9,10},{10,1... | collective-permute-start | bytes 1572872 | tf_op jit(solution)/shard_map/ppermute | solution.py:296
  7.5 0.0 copy-start.1
  7.5 0.6 copy-done.1
  8.2 4.5 %opacities.1 = (bf16[4,16,1024]{2,1,0:T(8,128)(2,1)S(1)}, bf16[4,16,1024]{2,1,0:T(8,128)(2,1)S(1)}, bf16[4,16,1024]{2,1,0:T(8,128)(2,1)S(1)}, bf16[4,16,1024]{2,...) custom-call(f32[4,256,1024]{2,1,0:T(8,128)} %volume_hbm.1, s32[4,256,1024]{2,1,0:T(8,128)} %index_hbm.1, ...), custom_call_target="tpu_custom_call" | custom-call | flops 15728640 | bytes 9437184 | tf_op jit(solution)/shard_map/opacities/pallas_call | solution.py:79
  12.7 1.3 %collective-permute-start = (bf16[4,16,1024]{2,1,0:T(8,128)(2,1)S(1)}, bf16[4,16,1024]{2,1,0:T(8,128)(2,1)S(1)}, u32[]{:S(2)}, u32[]{:S(2)}) collective-permute-start(bf16[4,16,1024]{2,1,0:T(8,128)(2,1)S(1)} %get-tuple-element.39), channel_id=1, source_target_pairs={{0,4},{1,5},{2,6},{3,7},{4,8},{5,9},{6,10},{7,11},{8,12},{9,13},{1... | collective-permute-start | bytes 393224 | tf_op jit(solution)/shard_map/ppermute | solution.py:279
  14.1 1.1 %collective-permute-start.1 = (bf16[4,16,1024]{2,1,0:T(8,128)(2,1)S(1)}, bf16[4,16,1024]{2,1,0:T(8,128)(2,1)S(1)}, u32[]{:S(2)}, u32[]{:S(2)}) collective-permute-start(bf16[4,16,1024]{2,1,0:T(8,128)(2,1)S(1)} %get-tuple-element.40), channel_id=1, source_target_pairs={{0,8},{1,9},{2,10},{3,11},{4,12},{5,13},{6,14},{7,15},{8,0},{9,1},... | collective-permute-start | bytes 393224 | tf_op jit(solution)/shard_map/ppermute | solution.py:279
  15.2 1.4 %collective-permute-start.2 = (bf16[4,16,1024]{2,1,0:T(8,128)(2,1)S(1)}, bf16[4,16,1024]{2,1,0:T(8,128)(2,1)S(1)}, u32[]{:S(2)}, u32[]{:S(2)}) collective-permute-start(bf16[4,16,1024]{2,1,0:T(8,128)(2,1)S(1)} %get-tuple-element.41), channel_id=1, source_target_pairs={{0,12},{1,13},{2,14},{3,15},{4,0},{5,1},{6,2},{7,3},{8,4},{9,5},{1... | collective-permute-start | bytes 393224 | tf_op jit(solution)/shard_map/ppermute | solution.py:279
  16.5 1.8 %collective-permute-done.4.after_ref = s16[256,1024]{1,0:T(8,128)(2,1)S(1)} collective-permute-done((s16[256,1024]{1,0:T(8,128)(2,1)S(1)}, s16[256,1024]{1,0:T(8,128)(2,1)S(1)}, u32[]{:S(2)}, u32[]{:S(2)}) %collective-permute-start.4) | collective-permute-done | bytes 524320 | tf_op jit(solution)/shard_map/ppermute | solution.py:297
  18.4 4.3 %colours.2 = (bf16[4,3,16,512]{3,2,1,0:T(8,128)(2,1)S(1)}, bf16[4,3,16,512]{3,2,1,0:T(8,128)(2,1)S(1)}, bf16[4,3,16,512]{3,2,1,0:T(8,128)(2,1)S(1)}, bf16[4,3,16,512]{3,2,1,0:T(8,128)(2,1)S(1)}) custom-call(f32[4,256,1024]{2,1,0:T(8,128)S(1)} %get-tuple-element.48.vol, s32[4,256,1024]{2,1,0:T(8,128)S(1)} %get-tuple-element.49.idx, ...), custom_call_target="tpu_custom_call" | custom-call | flops 26214400 | bytes 20971520 | tf_op jit(solution)/shard_map/colours/pallas_call | solution.py:162
  22.7 0.0 copy-start.2
  22.7 5.2 %colours.3 = bf16[16,3,16,512]{3,2,1,0:T(8,128)(2,1)} custom-call(f32[4,256,1024]{2,1,0:T(8,128)S(1)} %get-tuple-element.48.vol, s32[4,256,1024]{2,1,0:T(8,128)S(1)} %get-tuple-element.49.idx, s16[256,1024]{1,0:T(8,128)(2,1)S(1)} %collective-permute-done.3.before_ref, s16[256,1024]{1,0:T(8,128)(2,1)S(1)} %collective-permute-done.4.after_ref, ...), custom_call_target="tpu_custom_call" | custom-call | flops 26214400 | bytes 20971520 | tf_op jit(solution)/shard_map/colours/pallas_call | solution.py:162
  27.9 6.2 %all-to-all-start = ((bf16[16,3,16,512]{3,2,1,0:T(8,128)(2,1)}), bf16[16,3,16,512]{3,2,1,0:T(8,128)(2,1)S(1)}, u32[]{:S(2)}, u32[]{:S(2)}) async-start(bf16[16,3,16,512]{3,2,1,0:T(8,128)(2,1)} %colours.3), calls=%async_computation | async-start | bytes 1572864 | tf_op jit(solution)/shard_map/all_to_all | solution.py:270
  34.0 1.2 %collective-permute-start.8 = (bf16[4,3,16,512]{3,2,1,0:T(8,128)(2,1)S(1)}, bf16[4,3,16,512]{3,2,1,0:T(8,128)(2,1)S(1)}, u32[]{:S(2)}, u32[]{:S(2)}) collective-permute-start(bf16[4,3,16,512]{3,2,1,0:T(8,128)(2,1)S(1)} %get-tuple-element.64), channel_id=1, source_target_pairs={{0,4},{1,5},{2,6},{3,7},{4,8},{5,9},{6,10},{7,11},{8,12},{9,13},{1... | collective-permute-start | bytes 589832 | tf_op jit(solution)/shard_map/ppermute | solution.py:279
  35.2 1.0 %collective-permute-start.9 = (bf16[4,3,16,512]{3,2,1,0:T(8,128)(2,1)S(1)}, bf16[4,3,16,512]{3,2,1,0:T(8,128)(2,1)S(1)}, u32[]{:S(2)}, u32[]{:S(2)}) collective-permute-start(bf16[4,3,16,512]{3,2,1,0:T(8,128)(2,1)S(1)} %get-tuple-element.65), channel_id=1, source_target_pairs={{0,8},{1,9},{2,10},{3,11},{4,12},{5,13},{6,14},{7,15},{8,0},{9,1},... | collective-permute-start | bytes 589832 | tf_op jit(solution)/shard_map/ppermute | solution.py:279
  36.2 1.4 %collective-permute-start.10 = (bf16[4,3,16,512]{3,2,1,0:T(8,128)(2,1)S(1)}, bf16[4,3,16,512]{3,2,1,0:T(8,128)(2,1)S(1)}, u32[]{:S(2)}, u32[]{:S(2)}) collective-permute-start(bf16[4,3,16,512]{3,2,1,0:T(8,128)(2,1)S(1)} %get-tuple-element.66), channel_id=1, source_target_pairs={{0,12},{1,13},{2,14},{3,15},{4,0},{5,1},{6,2},{7,3},{8,4},{9,5},{1... | collective-permute-start | bytes 589832 | tf_op jit(solution)/shard_map/ppermute | solution.py:279
  37.6 1.3 %collective-permute-start.5 = (bf16[4,16,1024]{2,1,0:T(8,128)(2,1)S(1)}, bf16[4,16,1024]{2,1,0:T(8,128)(2,1)S(1)}, u32[]{:S(2)}, u32[]{:S(2)}) collective-permute-start(bf16[4,16,1024]{2,1,0:T(8,128)(2,1)S(1)} %get-tuple-element.59), channel_id=1, source_target_pairs={{0,1},{1,0},{2,3},{3,2},{4,5},{5,4},{6,7},{7,6},{8,9},{9,8},{10,11... | collective-permute-start | bytes 393224 | tf_op jit(solution)/shard_map/ppermute | solution.py:286
  38.9 24.9 %collective-permute-done.8.refs_1_ = bf16[4,3,16,512]{3,2,1,0:T(8,128)(2,1)S(1)} collective-permute-done((bf16[4,3,16,512]{3,2,1,0:T(8,128)(2,1)S(1)}, bf16[4,3,16,512]{3,2,1,0:T(8,128)(2,1)S(1)}, u32[]{:S(2)}, u32[]{:S(2)}) %collective-permute-start.8) | collective-permute-done | bytes 196640 | tf_op jit(solution)/shard_map/ppermute | solution.py:279
  63.8 4.2 %collective-permute-done.9.refs_2_ = bf16[4,3,16,512]{3,2,1,0:T(8,128)(2,1)S(1)} collective-permute-done((bf16[4,3,16,512]{3,2,1,0:T(8,128)(2,1)S(1)}, bf16[4,3,16,512]{3,2,1,0:T(8,128)(2,1)S(1)}, u32[]{:S(2)}, u32[]{:S(2)}) %collective-permute-start.9) | collective-permute-done | bytes 196640 | tf_op jit(solution)/shard_map/ppermute | solution.py:279
  68.0 1.9 %collective-permute-done.10.refs_3_ = bf16[4,3,16,512]{3,2,1,0:T(8,128)(2,1)S(1)} collective-permute-done((bf16[4,3,16,512]{3,2,1,0:T(8,128)(2,1)S(1)}, bf16[4,3,16,512]{3,2,1,0:T(8,128)(2,1)S(1)}, u32[]{:S(2)}, u32[]{:S(2)}) %collective-permute-start.10) | collective-permute-done | bytes 196640 | tf_op jit(solution)/shard_map/ppermute | solution.py:279
  70.0 0.1 regroup.3
  70.0 0.9 %collective-permute-start.11 = (bf16[4,3,16,512]{3,2,1,0:T(8,128)(2,1)S(1)}, bf16[4,3,16,512]{3,2,1,0:T(8,128)(2,1)S(1)}, u32[]{:S(2)}, u32[]{:S(2)}) collective-permute-start(bf16[4,3,16,512]{3,2,1,0:T(8,128)(2,1)S(1)} %get-tuple-element.68), channel_id=1, source_target_pairs={{0,1},{1,0},{2,3},{3,2},{4,5},{5,4},{6,7},{7,6},{8,9},{9,8},{10,11... | collective-permute-start | bytes 589832 | tf_op jit(solution)/shard_map/ppermute | solution.py:286
  71.0 1.2 %collective-permute-start.12 = (bf16[4,3,16,512]{3,2,1,0:T(8,128)(2,1)S(1)}, bf16[4,3,16,512]{3,2,1,0:T(8,128)(2,1)S(1)}, u32[]{:S(2)}, u32[]{:S(2)}) collective-permute-start(bf16[4,3,16,512]{3,2,1,0:T(8,128)(2,1)S(1)} %get-tuple-element.69), channel_id=1, source_target_pairs={{0,2},{1,3},{2,0},{3,1},{4,6},{5,7},{6,4},{7,5},{8,10},{9,11},{10,... | collective-permute-start | bytes 589832 | tf_op jit(solution)/shard_map/ppermute | solution.py:286
  72.2 0.5 collective-permute-start.13
  72.7 1.2 %collective-permute-start.6 = (bf16[4,16,1024]{2,1,0:T(8,128)(2,1)S(1)}, bf16[4,16,1024]{2,1,0:T(8,128)(2,1)S(1)}, u32[]{:S(2)}, u32[]{:S(2)}) collective-permute-start(bf16[4,16,1024]{2,1,0:T(8,128)(2,1)S(1)} %get-tuple-element.60), channel_id=1, source_target_pairs={{0,2},{1,3},{2,0},{3,1},{4,6},{5,7},{6,4},{7,5},{8,10},{9,11},{10,... | collective-permute-start | bytes 393224 | tf_op jit(solution)/shard_map/ppermute | solution.py:286
  73.9 0.6 collective-permute-start.7
  74.5 10.0 %collective-permute-done.6.rest_2_ = bf16[4,16,1024]{2,1,0:T(8,128)(2,1)S(1)} collective-permute-done((bf16[4,16,1024]{2,1,0:T(8,128)(2,1)S(1)}, bf16[4,16,1024]{2,1,0:T(8,128)(2,1)S(1)}, u32[]{:S(2)}, u32[]{:S(2)}) %collective-permute-start.6) | collective-permute-done | bytes 131104 | tf_op jit(solution)/shard_map/ppermute | solution.py:286
  84.5 3.0 %collective-permute-done.7.rest_3_ = bf16[4,16,1024]{2,1,0:T(8,128)(2,1)S(1)} collective-permute-done((bf16[4,16,1024]{2,1,0:T(8,128)(2,1)S(1)}, bf16[4,16,1024]{2,1,0:T(8,128)(2,1)S(1)}, u32[]{:S(2)}, u32[]{:S(2)}) %collective-permute-start.7) | collective-permute-done | bytes 131104 | tf_op jit(solution)/shard_map/ppermute | solution.py:286
  87.5 1.5 %blend.2.rest_5_ = f32[4,16,1024]{2,1,0:T(8,128)} custom-call(s32[16]{0:T(128)S(1)} %copy-done.2, bf16[4,16,1024]{2,1,0:T(8,128)(2,1)S(1)} %get-tuple-element.58.rest_0_, bf16[4,16,1024]{2,1,0:T(8,128)(2,1)S(1)} %collective-permute-done.5.rest_1_, bf16[4,16,1024]{2,1,0:T(8,128)(2,1)S(1)} %collective-permute-done.6.rest_2_, ...), custom_call_target="tpu_custom_call" | custom-call | tf_op jit(solution)/shard_map/blend/pallas_call | solution.py:227
  89.0 1.5 %blend.3 = f32[4,16,1024]{2,1,0:T(8,128)} custom-call(s32[16]{0:T(128)S(1)} %copy-done.2, bf16[4,16,1024]{2,1,0:T(8,128)(2,1)S(1)} %get-tuple-element.58.rest_0_, bf16[4,16,1024]{2,1,0:T(8,128)(2,1)S(1)} %collective-permute-done.5.rest_1_, bf16[4,16,1024]{2,1,0:T(8,128)(2,1)S(1)} %collective-permute-done.6.rest_2_, ...), custom_call_target="tpu_custom_call", output_to_operand_aliasing={{}: (6, {})} | custom-call | tf_op jit(solution)/shard_map/blend/pallas_call | solution.py:227
  (12 shorter events, 0.1 us)
Async XLA Ops:
  1.9 16.5 %collective-permute-start.4 = (s16[256,1024]{1,0:T(8,128)(2,1)S(1)}, s16[256,1024]{1,0:T(8,128)(2,1)S(1)}, u32[]{:S(2)}, u32[]{:S(2)}) collective-permute-start(s16[256,1024]{1,0:T(8,128)(2,1)S(1)} %get-tuple-element.71), channel_id=1, source_target_pairs={{1,0},{2,1},{3,2},{4,3},{5,4},{6,5},{7,6},{8,7},{9,8},{10,9},{11,1... | collective-permute-start | bytes 1572872 | tf_op jit(solution)/shard_map/ppermute | solution.py:297
  4.5 13.9 %copy-start = (f32[3,8]{1,0:T(4,128)S(1)}, f32[3,8]{1,0:T(4,128)}, u32[]{:S(2)}) copy-start(f32[3,8]{1,0:T(4,128)} %colour_ref.2) | copy-start | bytes 292
  4.5 13.8 %collective-permute-start.3 = (s16[256,1024]{1,0:T(8,128)(2,1)S(1)}, s16[256,1024]{1,0:T(8,128)(2,1)S(1)}, u32[]{:S(2)}, u32[]{:S(2)}) collective-permute-start(s16[256,1024]{1,0:T(8,128)(2,1)S(1)} %get-tuple-element.72), channel_id=1, source_target_pairs={{0,1},{1,2},{2,3},{3,4},{4,5},{5,6},{6,7},{7,8},{8,9},{9,10},{10,1... | collective-permute-start | bytes 1572872 | tf_op jit(solution)/shard_map/ppermute | solution.py:296
  7.5 0.7 copy-start.1
  12.7 15.1 %collective-permute-start = (bf16[4,16,1024]{2,1,0:T(8,128)(2,1)S(1)}, bf16[4,16,1024]{2,1,0:T(8,128)(2,1)S(1)}, u32[]{:S(2)}, u32[]{:S(2)}) collective-permute-start(bf16[4,16,1024]{2,1,0:T(8,128)(2,1)S(1)} %get-tuple-element.39), channel_id=1, source_target_pairs={{0,4},{1,5},{2,6},{3,7},{4,8},{5,9},{6,10},{7,11},{8,12},{9,13},{1... | collective-permute-start | bytes 393224 | tf_op jit(solution)/shard_map/ppermute | solution.py:279
  14.1 13.8 %collective-permute-start.1 = (bf16[4,16,1024]{2,1,0:T(8,128)(2,1)S(1)}, bf16[4,16,1024]{2,1,0:T(8,128)(2,1)S(1)}, u32[]{:S(2)}, u32[]{:S(2)}) collective-permute-start(bf16[4,16,1024]{2,1,0:T(8,128)(2,1)S(1)} %get-tuple-element.40), channel_id=1, source_target_pairs={{0,8},{1,9},{2,10},{3,11},{4,12},{5,13},{6,14},{7,15},{8,0},{9,1},... | collective-permute-start | bytes 393224 | tf_op jit(solution)/shard_map/ppermute | solution.py:279
  15.2 12.7 %collective-permute-start.2 = (bf16[4,16,1024]{2,1,0:T(8,128)(2,1)S(1)}, bf16[4,16,1024]{2,1,0:T(8,128)(2,1)S(1)}, u32[]{:S(2)}, u32[]{:S(2)}) collective-permute-start(bf16[4,16,1024]{2,1,0:T(8,128)(2,1)S(1)} %get-tuple-element.41), channel_id=1, source_target_pairs={{0,12},{1,13},{2,14},{3,15},{4,0},{5,1},{6,2},{7,3},{8,4},{9,5},{1... | collective-permute-start | bytes 393224 | tf_op jit(solution)/shard_map/ppermute | solution.py:279
  22.7 64.8 %copy-start.2 = (s32[16]{0:T(128)S(1)}, s32[16]{0:T(128)}, u32[]{:S(2)}) copy-start(s32[16]{0:T(128)} %order_ref.3) | copy-start | bytes 196
  27.9 61.1 %all-to-all-start = ((bf16[16,3,16,512]{3,2,1,0:T(8,128)(2,1)}), bf16[16,3,16,512]{3,2,1,0:T(8,128)(2,1)S(1)}, u32[]{:S(2)}, u32[]{:S(2)}) async-start(bf16[16,3,16,512]{3,2,1,0:T(8,128)(2,1)} %colours.3), calls=%async_computation | async-start | bytes 1572864 | tf_op jit(solution)/shard_map/all_to_all | solution.py:270
  34.0 29.8 %collective-permute-start.8 = (bf16[4,3,16,512]{3,2,1,0:T(8,128)(2,1)S(1)}, bf16[4,3,16,512]{3,2,1,0:T(8,128)(2,1)S(1)}, u32[]{:S(2)}, u32[]{:S(2)}) collective-permute-start(bf16[4,3,16,512]{3,2,1,0:T(8,128)(2,1)S(1)} %get-tuple-element.64), channel_id=1, source_target_pairs={{0,4},{1,5},{2,6},{3,7},{4,8},{5,9},{6,10},{7,11},{8,12},{9,13},{1... | collective-permute-start | bytes 589832 | tf_op jit(solution)/shard_map/ppermute | solution.py:279
  35.2 32.8 %collective-permute-start.9 = (bf16[4,3,16,512]{3,2,1,0:T(8,128)(2,1)S(1)}, bf16[4,3,16,512]{3,2,1,0:T(8,128)(2,1)S(1)}, u32[]{:S(2)}, u32[]{:S(2)}) collective-permute-start(bf16[4,3,16,512]{3,2,1,0:T(8,128)(2,1)S(1)} %get-tuple-element.65), channel_id=1, source_target_pairs={{0,8},{1,9},{2,10},{3,11},{4,12},{5,13},{6,14},{7,15},{8,0},{9,1},... | collective-permute-start | bytes 589832 | tf_op jit(solution)/shard_map/ppermute | solution.py:279
  36.2 33.8 %collective-permute-start.10 = (bf16[4,3,16,512]{3,2,1,0:T(8,128)(2,1)S(1)}, bf16[4,3,16,512]{3,2,1,0:T(8,128)(2,1)S(1)}, u32[]{:S(2)}, u32[]{:S(2)}) collective-permute-start(bf16[4,3,16,512]{3,2,1,0:T(8,128)(2,1)S(1)} %get-tuple-element.66), channel_id=1, source_target_pairs={{0,12},{1,13},{2,14},{3,15},{4,0},{5,1},{6,2},{7,3},{8,4},{9,5},{1... | collective-permute-start | bytes 589832 | tf_op jit(solution)/shard_map/ppermute | solution.py:279
  37.6 36.3 %collective-permute-start.5 = (bf16[4,16,1024]{2,1,0:T(8,128)(2,1)S(1)}, bf16[4,16,1024]{2,1,0:T(8,128)(2,1)S(1)}, u32[]{:S(2)}, u32[]{:S(2)}) collective-permute-start(bf16[4,16,1024]{2,1,0:T(8,128)(2,1)S(1)} %get-tuple-element.59), channel_id=1, source_target_pairs={{0,1},{1,0},{2,3},{3,2},{4,5},{5,4},{6,7},{7,6},{8,9},{9,8},{10,11... | collective-permute-start | bytes 393224 | tf_op jit(solution)/shard_map/ppermute | solution.py:286
  70.0 17.4 %collective-permute-start.11 = (bf16[4,3,16,512]{3,2,1,0:T(8,128)(2,1)S(1)}, bf16[4,3,16,512]{3,2,1,0:T(8,128)(2,1)S(1)}, u32[]{:S(2)}, u32[]{:S(2)}) collective-permute-start(bf16[4,3,16,512]{3,2,1,0:T(8,128)(2,1)S(1)} %get-tuple-element.68), channel_id=1, source_target_pairs={{0,1},{1,0},{2,3},{3,2},{4,5},{5,4},{6,7},{7,6},{8,9},{9,8},{10,11... | collective-permute-start | bytes 589832 | tf_op jit(solution)/shard_map/ppermute | solution.py:286
  71.0 16.5 %collective-permute-start.12 = (bf16[4,3,16,512]{3,2,1,0:T(8,128)(2,1)S(1)}, bf16[4,3,16,512]{3,2,1,0:T(8,128)(2,1)S(1)}, u32[]{:S(2)}, u32[]{:S(2)}) collective-permute-start(bf16[4,3,16,512]{3,2,1,0:T(8,128)(2,1)S(1)} %get-tuple-element.69), channel_id=1, source_target_pairs={{0,2},{1,3},{2,0},{3,1},{4,6},{5,7},{6,4},{7,5},{8,10},{9,11},{10,... | collective-permute-start | bytes 589832 | tf_op jit(solution)/shard_map/ppermute | solution.py:286
  72.2 15.3 %collective-permute-start.13 = (bf16[4,3,16,512]{3,2,1,0:T(8,128)(2,1)S(1)}, bf16[4,3,16,512]{3,2,1,0:T(8,128)(2,1)S(1)}, u32[]{:S(2)}, u32[]{:S(2)}) collective-permute-start(bf16[4,3,16,512]{3,2,1,0:T(8,128)(2,1)S(1)} %get-tuple-element.70), channel_id=1, source_target_pairs={{0,3},{1,2},{2,1},{3,0},{4,7},{5,6},{6,5},{7,4},{8,11},{9,10},{10,... | collective-permute-start | bytes 589832 | tf_op jit(solution)/shard_map/ppermute | solution.py:286
  72.7 11.8 %collective-permute-start.6 = (bf16[4,16,1024]{2,1,0:T(8,128)(2,1)S(1)}, bf16[4,16,1024]{2,1,0:T(8,128)(2,1)S(1)}, u32[]{:S(2)}, u32[]{:S(2)}) collective-permute-start(bf16[4,16,1024]{2,1,0:T(8,128)(2,1)S(1)} %get-tuple-element.60), channel_id=1, source_target_pairs={{0,2},{1,3},{2,0},{3,1},{4,6},{5,7},{6,4},{7,5},{8,10},{9,11},{10,... | collective-permute-start | bytes 393224 | tf_op jit(solution)/shard_map/ppermute | solution.py:286
  73.9 13.6 %collective-permute-start.7 = (bf16[4,16,1024]{2,1,0:T(8,128)(2,1)S(1)}, bf16[4,16,1024]{2,1,0:T(8,128)(2,1)S(1)}, u32[]{:S(2)}, u32[]{:S(2)}) collective-permute-start(bf16[4,16,1024]{2,1,0:T(8,128)(2,1)S(1)} %get-tuple-element.61), channel_id=1, source_target_pairs={{0,3},{1,2},{2,1},{3,0},{4,7},{5,6},{6,5},{7,4},{8,11},{9,10},{10,... | collective-permute-start | bytes 393224 | tf_op jit(solution)/shard_map/ppermute | solution.py:286

commit v8 on v7

--- a/solution.py
+++ b/solution.py
@@ -16,7 +16,7 @@
 LIMIT = 24 * 1024 * 1024
 FETCH_LIMIT = 43 * 1024 * 1024
 BLEND_LIMIT = 16 * 1024 * 1024
-UNROLL = 4
+FIRST = 4
 PLANES = 4
 
 
@@ -90,12 +90,13 @@
     )(volume, tf_index, tf_opacity)
 
 
-def colour_kernel(slices, span, vol, idx, before_ref, after_ref, colour_ref, opacity_ref, *out_refs):
+def colour_kernel(slices, span, turns, by_member, vol, idx, before_ref, after_ref, colour_ref, opacity_ref, *rest):
+    out_refs = rest[-turns:]
     height, width = before_ref.shape
     blocks, tiles = height // BLOCK, width // LANES
-    turns = len(out_refs)
     each = blocks // turns
-    plane = lax.axis_index("gz") // (lax.axis_size("gz") // turns)
+    device, members = lax.axis_index("gz"), lax.axis_size("gz") // turns
+    plane, member = device // members, lax.rem(device, members)
     lane = lax.broadcasted_iota(jnp.int32, (BLOCK, LANES), 1)
     first_lane, last_lane = lane == 0, lane == LANES - 1
     sublane = lax.broadcasted_iota(jnp.int32, (PAD, LANES), 0)
@@ -147,71 +148,134 @@
             for c in range(3):
                 out_ref[j, c, :, pl.ds((t - span[0]) * LANES, LANES)] = sums[c].astype(jnp.bfloat16)
 
-    for turn, out_ref in enumerate(out_refs):
-        base = lax.rem(plane + turn, turns) * each
-
-        @pl.loop(0, each)
+    if not by_member:
+        for turn, out_ref in enumerate(out_refs):
+            base = lax.rem(plane + turn, turns) * each
+
+            @pl.loop(0, each)
+            def _(j):
+                shade(base + j, out_ref, j)
+
+        return
+    for m, out_ref in enumerate(out_refs):
+        @pl.loop(0, turns)
         def _(j):
-            shade(base + j, out_ref, j)
-
-
-def colours(volume, tf_index, before, after, tf_color, tf_opacity, span, turns):
+            shade(lax.rem(plane + j, turns) * members + (member ^ m), out_ref, j)
+
+
+def colours(volume, tf_index, before, after, tf_color, tf_opacity, span, turns, earlier=()):
     slices, height, _ = volume.shape
     part = jax.ShapeDtypeStruct((height // BLOCK // turns, 3, BLOCK, (span[1] - span[0]) * LANES), jnp.bfloat16)
     cells = slices * height * (span[1] - span[0]) * LANES
     return pl.pallas_call(
-        functools.partial(colour_kernel, slices, span),
+        functools.partial(colour_kernel, slices, span, turns, bool(earlier)),
         out_shape=[part] * turns,
-        in_specs=[pl.BlockSpec(memory_space=pltpu.VMEM)] * 4 + [pl.BlockSpec(memory_space=pltpu.SMEM)] * 2,
+        in_specs=[pl.BlockSpec(memory_space=pltpu.VMEM)] * 4
+        + [pl.BlockSpec(memory_space=pltpu.SMEM)] * 2
+        + [pl.BlockSpec(memory_space=pl.ANY)] * len(earlier),
         out_specs=[pl.BlockSpec(memory_space=pltpu.VMEM)] * turns,
         compiler_params=pltpu.CompilerParams(vmem_limit_bytes=LIMIT),
         cost_estimate=pl.CostEstimate(flops=50 * cells, bytes_accessed=40 * cells, transcendentals=2 * cells),
         name="colours",
-    )(volume, tf_index, before, after, tf_color, tf_opacity)
-
-
-def regroup_kernel(turns, *refs):
+    )(volume, tf_index, before, after, tf_color, tf_opacity, *earlier)
+
+
+def on_chip(kernel, out_shapes, operands, earlier=()):
+    return pl.pallas_call(
+        kernel,
+        out_shape=out_shapes,
+        in_specs=[pl.BlockSpec(memory_space=pltpu.VMEM)] * len(operands)
+        + [pl.BlockSpec(memory_space=pl.ANY)] * len(earlier),
+        out_specs=[pl.BlockSpec(memory_space=pltpu.VMEM)] * len(out_shapes),
+        compiler_params=pltpu.CompilerParams(vmem_limit_bytes=BLEND_LIMIT),
+        name=kernel.func.__name__.removesuffix("_kernel"),
+    )(*operands, *earlier)
+
+
+def hold_kernel(count, *refs):
+    for ref, out_ref in zip(refs[:count], refs[-count:]):
+        out_ref[...] = ref[...]
+
+
+def hold(parts, earlier):
+    shapes = [jax.ShapeDtypeStruct(part.shape, part.dtype) for part in parts]
+    return list(on_chip(functools.partial(hold_kernel, len(parts)), shapes, parts, earlier))
+
+
+def to_core_kernel(turns, *refs):
     here = lax.rem(lax.axis_index("gz"), turns)
-    for s, ref in enumerate(refs[:turns]):
-        for m, out_ref in enumerate(refs[turns:]):
-            out_ref[s] = ref[here ^ m]
-
-
-def regroup(parts):
-    turns = len(parts)
-    return pl.pallas_call(
-        functools.partial(regroup_kernel, turns),
-        out_shape=[jax.ShapeDtypeStruct(parts[0].shape, parts[0].dtype)] * turns,
-        in_specs=[pl.BlockSpec(memory_space=pltpu.VMEM)] * turns,
-        out_specs=[pl.BlockSpec(memory_space=pltpu.VMEM)] * turns,
-        compiler_params=pltpu.CompilerParams(vmem_limit_bytes=BLEND_LIMIT),
-        name="regroup",
-    )(*parts)
-
-
-def blend_kernel(ranks, turns, colour_count, start, order_ref, *rest):
-    opacity_refs, rest = rest[:turns], rest[turns:]
-    colour_refs, (out_hbm, place, opacity_ref, out_ref, sem) = rest[:colour_count], rest[-5:]
+    colour_refs, opacity_refs, second_refs = refs[:turns], refs[turns : 2 * turns], refs[2 * turns :][:2]
+    own_ref, far_ref, passed_ref = refs[-3:]
+    width, total = colour_refs[0].shape[-1], opacity_refs[0].shape[-1]
+    for s, (colour_ref, opacity_ref) in enumerate(zip(colour_refs, opacity_refs)):
+        for m, (out_ref, at) in enumerate([(own_ref, s), (passed_ref, s), (far_ref, s), (passed_ref, turns + s)]):
+            for c in range(3):
+                out_ref[at, :, pl.ds(c * width, width)] = colour_ref[here ^ m, c]
+            out_ref[at, :, pl.ds(3 * width, total)] = opacity_ref[here ^ m]
+    width, start = second_refs[0].shape[-1], 3 * width + total
+    for x, ref in enumerate(second_refs):
+        for s in range(turns):
+            for c in range(3):
+                passed_ref[x * turns + s, :, pl.ds(start + c * width, width)] = ref[s, c]
+
+
+def to_core(first, opacity, second, earlier):
+    turns, (_, _, height, width) = len(first), first[0].shape
+    wide = 3 * width + opacity[0].shape[-1]
+    part = jax.ShapeDtypeStruct((turns, height, wide), jnp.bfloat16)
+    passed = jax.ShapeDtypeStruct((2 * turns, height, wide + 3 * second[0].shape[-1]), jnp.bfloat16)
+    operands = [*first, *opacity, *second]
+    return on_chip(functools.partial(to_core_kernel, turns), [part, part, passed], operands, earlier)
+
+
+def to_rest_kernel(turns, far_ref, passed_ref, own_ref, other_ref, out_ref, *plane_refs):
+    wide, width = far_ref.shape[2], own_ref.shape[-1]
+    out_ref[pl.ds(0, turns)] = far_ref[...]
+    out_ref[pl.ds(turns, turns)] = passed_ref[pl.ds(turns, turns), :, pl.ds(0, wide)]
+    for s, plane_ref in enumerate(plane_refs):
+        plane_ref[0] = own_ref[s]
+        plane_ref[2] = other_ref[s]
+        for c in range(3):
+            cols = pl.ds(wide + c * width, width)
+            plane_ref[1, c] = passed_ref[s, :, cols]
+            plane_ref[3, c] = passed_ref[turns + s, :, cols]
+
+
+def to_rest(far, passed, own, other):
+    turns = far.shape[0]
+    shapes = [jax.ShapeDtypeStruct((2 * turns,) + far.shape[1:], far.dtype)]
+    shapes += [jax.ShapeDtypeStruct(own.shape, own.dtype)] * turns
+    return on_chip(functools.partial(to_rest_kernel, turns), shapes, [far, passed, own, other])
+
+
+def swap(part, devices, stride):
+    return lax.ppermute(part, "gz", [(i, i ^ stride) for i in range(devices)])
+
+
+def blend_kernel(ranks, turns, side, order_ref, *rest):
+    (own_ref, passed_ref, far_ref), second_refs = rest[:3], rest[3:-6]
+    out_hbm, place, colour_ref, opacity_ref, out_ref, sem = rest[-6:]
     device = lax.axis_index("gz")
     plane, member = device // turns, lax.rem(device, turns)
-    width = out_ref.shape[2]
+    width, total = out_ref.shape[2], out_hbm.shape[2]
+    start = total - width if side else 0
+    before = own_ref.shape[2] - total
     for b in range(ranks):
         place[order_ref[b]] = b
-    for m, ref in enumerate(opacity_refs):
+    for m in range(turns):
         for s in range(turns):
             brick = lax.rem(plane + turns - s, turns) * turns + (member ^ m)
-            opacity_ref[brick, 3] = ref[s, :, pl.ds(start, width)]
-            if len(colour_refs) > 1:
-                for c in range(3):
-                    opacity_ref[brick, c] = colour_refs[m][s, c]
-    colour_ref = opacity_ref if len(colour_refs) > 1 else colour_refs[0]
+            ref, at = [(own_ref, s), (passed_ref, s), (far_ref, s), (far_ref, turns + s)][m]
+            for c in range(3):
+                colour_ref[brick, c] = second_refs[s][m, c] if side else ref[at, :, pl.ds(c * width, width)]
+            opacity_ref[brick] = ref[at, :, pl.ds(before + start, width)]
     for j in range(width // LANES):
         cols = pl.ds(j * LANES, LANES)
         canvas = (jnp.zeros((out_ref.shape[1], LANES), jnp.float32),) * 4
         for rank in range(ranks):
             b = place[rank]
             clear = 1.0 - canvas[3]
-            layers = [colour_ref[b, c, :, cols] for c in range(3)] + [opacity_ref[b, 3, :, cols]]
+            layers = [colour_ref[b, c, :, cols] for c in range(3)] + [opacity_ref[b, :, cols]]
             canvas = tuple(front + clear * back.astype(jnp.float32) for front, back in zip(canvas, layers))
         for c in range(4):
             out_ref[c, :, cols] = canvas[c]
@@ -220,12 +284,12 @@
     copy.wait()
 
 
-def blend(order, opacity_parts, colours_here, start, total, image=()):
-    turns, ranks = len(opacity_parts), order.shape[0]
-    height, width = colours_here[0].shape[-2:]
-    operands = [order, *opacity_parts, *colours_here]
+def blend(order, turns, total, first, second=(), image=()):
+    ranks, height = order.shape[0], first[0].shape[1]
+    width = second[0].shape[-1] if second else (first[0].shape[2] - total) // 3
+    operands = [order, *first, *second]
     return pl.pallas_call(
-        functools.partial(blend_kernel, ranks, turns, len(colours_here), start),
+        functools.partial(blend_kernel, ranks, turns, 1 if second else 0),
         out_shape=jax.ShapeDtypeStruct((4, height, total), jnp.float32),
         in_specs=[pl.BlockSpec(memory_space=pltpu.SMEM)]
         + [pl.BlockSpec(memory_space=pltpu.VMEM)] * (len(operands) - 1)
@@ -233,7 +297,8 @@
         out_specs=pl.BlockSpec(memory_space=pltpu.HBM),
         scratch_shapes=[
             pltpu.SMEM((ranks,), jnp.int32),
-            pltpu.VMEM((ranks, 4, height, width), jnp.bfloat16),
+            pltpu.VMEM((ranks, 3, height, width), jnp.bfloat16),
+            pltpu.VMEM((ranks, height, width), jnp.bfloat16),
             pltpu.VMEM((4, height, width), jnp.float32),
             pltpu.SemaphoreType.DMA,
         ],
@@ -278,12 +343,6 @@
     return [parts[0]] + [
         lax.ppermute(part, "gz", [(i, (i + s * turns) % devices) for i in range(devices)])
         for s, part in enumerate(parts[1:], 1)
-    ]
-
-
-def in_plane(parts, devices):
-    return [parts[0]] + [
-        lax.ppermute(part, "gz", [(i, i ^ m) for i in range(devices)]) for m, part in enumerate(parts[1:], 1)
     ]
 
 
@@ -302,17 +361,19 @@
     if turns == 1:
         colour = by_owner(colours(*held, (0, tiles), 1)[0], devices)
         return blend_plain(order, exchange(colour), exchange(by_owner(opacity[0], devices)))
+    split = tiles * FIRST // 8
     opacity = across_planes(opacity, turns, devices)
-    first = colours(*held, (0, tiles // 2), turns)
-    first, held = lax.optimization_barrier((first, held))
-    first = across_planes(first, turns, devices)
-    (second,) = colours(*held, (tiles // 2, tiles), 1)
-    opacity, second = lax.optimization_barrier((opacity, second))
-    second = exchange(second)
-    opacity = in_plane(regroup(opacity), devices)
-    first = in_plane(regroup(first), devices)
-    image = blend(order, opacity, first, 0, width)
-    return blend(order, opacity, [second], width // 2, width, (image,))
+    own, *others = colours(*held, (0, split), turns)
+    second = colours(*held, (split, tiles), turns, (own,))
+    first = across_planes([own] + hold(others, opacity[1:]), turns, devices)
+    near, core, *far = second
+    far = [swap(part, devices, 2) for part in far]
+    own, other, passed = to_core(first, opacity, [core, far[1]], far[:1])
+    passed = swap(passed, devices, 1)
+    other, *second = to_rest(other, passed, near, far[0])
+    second = across_planes(second, turns, devices)
+    first = [own, passed, swap(other, devices, 2)]
+    return blend(order, turns, width, first, second, (blend(order, turns, width, first),))
 
 
 def solution(mesh):

time: 90.8 us -> 72.7 us (0.80)
  waiting for transfers between devices: 45.9 us -> 35.8 us
  starting transfers between devices: 24.8 us -> 17.6 us
    ppermute x6 -> x9, waiting for transfers between devices: 31.1 us -> 19.3 us  [across_planes(): lax.ppermute(part, 'gz', [(i, (i + s * turns) % devices) for i in range(d...]
    all_to_all x1 -> x0, starting transfers between devices: 6.16 us -> none  [exchange(): return lax.all_to_all(x, 'gz', split_axis=0, concat_axis=0, tiled=True)]
    ppermute x6 -> x4, starting transfers between devices: 5.71 us -> 3.34 us  [swap(): return lax.ppermute(part, 'gz', [(i, i ^ stride) for i in range(devices)])]
    ppermute x6 -> x9, starting transfers between devices: 7.38 us -> 8.71 us  [across_planes(): lax.ppermute(part, 'gz', [(i, (i + s * turns) % devices) for i in range(d...]
    ppermute x6 -> x4, waiting for transfers between devices: 13 us -> 13.9 us  [swap(): return lax.ppermute(part, 'gz', [(i, i ^ stride) for i in range(devices)])]
    pallas_call x6 -> x7, Pallas kernels: 12.6 us -> 11.9 us  [the longest x2 8.59 us: colours(): pl.pallas_call(functools.partial(colour_kernel, slices, span, turns, bool...]
  transfers between devices with their start and end apart: 15 -> 15, of which waited for: 6 -> 9; matrix products, arithmetic and copies ran while one was open for 0% -> 0% of each run, Pallas kernels for 17% -> 20%
where the time goes in v8:
time: 72.7 us; the launch traced here: 72.5 us
  waiting for transfers between devices  35.8 us (49%)
  starting transfers between devices  17.6 us (24%)
  Pallas kernels  16.4 us (23%)
  other arithmetic  1.9 us (3%)
    ppermute x9, waiting for transfers between devices, across_planes(): lax.ppermute(part, 'gz', [(i, (i + s * turns) % devices) for i in range(d...  19.3 us
    ppermute x4, waiting for transfers between devices, swap(): return lax.ppermute(part, 'gz', [(i, i ^ stride) for i in range(devices)])  13.9 us
    ppermute x9, starting transfers between devices, across_planes(): lax.ppermute(part, 'gz', [(i, (i + s * turns) % devices) for i in range(d...  8.71 us
    pallas_call x2, Pallas kernels, colours(): pl.pallas_call(functools.partial(colour_kernel, slices, span, turns, bool...  8.59 us
    pallas_call x1, Pallas kernels, opacities(): pl.pallas_call(functools.partial(opacity_kernel, slices, width // LANES,...  4.52 us
    ppermute x1, starting transfers between devices, shards(): before = lax.ppermute(last, 'gz', up)  3.68 us
    ppermute x4, starting transfers between devices, swap(): return lax.ppermute(part, 'gz', [(i, i ^ stride) for i in range(devices)])  3.34 us
    pallas_call x2, Pallas kernels, blend(): pl.pallas_call(functools.partial(blend_kernel, ranks, turns, 1 if second...  3.03 us
  transfers between devices with their start and end apart: 15, of which 9 were waited for; matrix products, arithmetic and copies ran while one was open for 0% of the time, Pallas kernels for 20%

profile of v8, /device:TPU:13, one launch (start us, length us, event | category | flops | bytes accessed | tf_op | source)
XLA Modules:
  0.0 72.5 jit_solution(4191285037093673575)
XLA Ops:
  0.0 1.9 %fusion.1 = (s16[256,1024]{1,0:T(8,128)(2,1)S(1)}, s16[256,1024]{1,0:T(8,128)(2,1)S(1)}) fusion(f32[4,256,1024]{2,1,0:T(8,128)} %volume_hbm.1), kind=kLoop, calls=%fused_computation.3 | loop fusion | flops 1572864 | bytes 3145728 | tf_op jit(solution)/shard_map/convert_element_type | solution.py:339
  1.9 3.7 %collective-permute-start = (s16[256,1024]{1,0:T(8,128)(2,1)S(1)}, s16[256,1024]{1,0:T(8,128)(2,1)S(1)}, u32[]{:S(2)}, u32[]{:S(2)}) collective-permute-start(s16[256,1024]{1,0:T(8,128)(2,1)S(1)} %get-tuple-element.56), channel_id=1, source_target_pairs={{0,1},{1,2},{2,3},{3,4},{4,5},{5,6},{6,7},{7,8},{8,9},{9,10},{10,1... | collective-permute-start | bytes 1572872 | tf_op jit(solution)/shard_map/ppermute | solution.py:355
  5.6 1.9 %collective-permute-start.1 = (s16[256,1024]{1,0:T(8,128)(2,1)S(1)}, s16[256,1024]{1,0:T(8,128)(2,1)S(1)}, u32[]{:S(2)}, u32[]{:S(2)}) collective-permute-start(s16[256,1024]{1,0:T(8,128)(2,1)S(1)} %get-tuple-element.55), channel_id=1, source_target_pairs={{1,0},{2,1},{3,2},{4,3},{5,4},{6,5},{7,6},{8,7},{9,8},{10,9},{11,1... | collective-permute-start | bytes 1572872 | tf_op jit(solution)/shard_map/ppermute | solution.py:356
  7.5 0.6 copy-done.1
  8.2 4.5 %opacities.1 = (bf16[4,16,1024]{2,1,0:T(8,128)(2,1)S(1)}, bf16[4,16,1024]{2,1,0:T(8,128)(2,1)S(1)}, bf16[4,16,1024]{2,1,0:T(8,128)(2,1)S(1)}, bf16[4,16,1024]{2,...) custom-call(f32[4,256,1024]{2,1,0:T(8,128)} %volume_hbm.1, s32[4,256,1024]{2,1,0:T(8,128)} %index_hbm.1, ...), custom_call_target="tpu_custom_call" | custom-call | flops 15728640 | bytes 9437184 | tf_op jit(solution)/shard_map/opacities/pallas_call | solution.py:79
  12.7 1.3 %collective-permute-start.2 = (bf16[4,16,1024]{2,1,0:T(8,128)(2,1)S(1)}, bf16[4,16,1024]{2,1,0:T(8,128)(2,1)S(1)}, u32[]{:S(2)}, u32[]{:S(2)}) collective-permute-start(bf16[4,16,1024]{2,1,0:T(8,128)(2,1)S(1)} %get-tuple-element.36), channel_id=1, source_target_pairs={{0,4},{1,5},{2,6},{3,7},{4,8},{5,9},{6,10},{7,11},{8,12},{9,13},{1... | collective-permute-start | bytes 393224 | tf_op jit(solution)/shard_map/ppermute | solution.py:344
  14.1 1.1 %collective-permute-start.3 = (bf16[4,16,1024]{2,1,0:T(8,128)(2,1)S(1)}, bf16[4,16,1024]{2,1,0:T(8,128)(2,1)S(1)}, u32[]{:S(2)}, u32[]{:S(2)}) collective-permute-start(bf16[4,16,1024]{2,1,0:T(8,128)(2,1)S(1)} %get-tuple-element.37), channel_id=1, source_target_pairs={{0,8},{1,9},{2,10},{3,11},{4,12},{5,13},{6,14},{7,15},{8,0},{9,1},... | collective-permute-start | bytes 393224 | tf_op jit(solution)/shard_map/ppermute | solution.py:344
  15.2 1.4 %collective-permute-start.4 = (bf16[4,16,1024]{2,1,0:T(8,128)(2,1)S(1)}, bf16[4,16,1024]{2,1,0:T(8,128)(2,1)S(1)}, u32[]{:S(2)}, u32[]{:S(2)}) collective-permute-start(bf16[4,16,1024]{2,1,0:T(8,128)(2,1)S(1)} %get-tuple-element.38), channel_id=1, source_target_pairs={{0,12},{1,13},{2,14},{3,15},{4,0},{5,1},{6,2},{7,3},{8,4},{9,5},{1... | collective-permute-start | bytes 393224 | tf_op jit(solution)/shard_map/ppermute | solution.py:344
  16.5 0.1 collective-permute-done.before_ref
  16.7 2.5 %collective-permute-done.1.after_ref = s16[256,1024]{1,0:T(8,128)(2,1)S(1)} collective-permute-done((s16[256,1024]{1,0:T(8,128)(2,1)S(1)}, s16[256,1024]{1,0:T(8,128)(2,1)S(1)}, u32[]{:S(2)}, u32[]{:S(2)}) %collective-permute-start.1) | collective-permute-done | bytes 524320 | tf_op jit(solution)/shard_map/ppermute | solution.py:356
  19.2 4.3 %colours.2 = (bf16[4,3,16,512]{3,2,1,0:T(8,128)(2,1)S(1)}, bf16[4,3,16,512]{3,2,1,0:T(8,128)(2,1)S(1)}, bf16[4,3,16,512]{3,2,1,0:T(8,128)(2,1)S(1)}, bf16[4,3,16,512]{3,2,1,0:T(8,128)(2,1)S(1)}) custom-call(f32[4,256,1024]{2,1,0:T(8,128)S(1)} %get-tuple-element.30.vol, s32[4,256,1024]{2,1,0:T(8,128)S(1)} %get-tuple-element.31.idx, ...), custom_call_target="tpu_custom_call" | custom-call | flops 26214400 | bytes 20971520 | tf_op jit(solution)/shard_map/colours/pallas_call | solution.py:170
  23.5 4.3 %collective-permute-done.4.refs_5_.refs_7_ = bf16[4,16,1024]{2,1,0:T(8,128)(2,1)S(1)} collective-permute-done((bf16[4,16,1024]{2,1,0:T(8,128)(2,1)S(1)}, bf16[4,16,1024]{2,1,0:T(8,128)(2,1)S(1)}, u32[]{:S(2)}, u32[]{:S(2)}) %collective-permute-start.4) | collective-permute-done | bytes 131104 | tf_op jit(solution)/shard_map/ppermute | solution.py:344
  27.9 0.1 collective-permute-start.5
  27.9 0.1 collective-permute-start.6
  28.0 1.4 %collective-permute-start.7 = (bf16[4,3,16,512]{3,2,1,0:T(8,128)(2,1)S(1)}, bf16[4,3,16,512]{3,2,1,0:T(8,128)(2,1)S(1)}, u32[]{:S(2)}, u32[]{:S(2)}) collective-permute-start(bf16[4,3,16,512]{3,2,1,0:T(8,128)(2,1)S(1)} %get-tuple-element.41), channel_id=1, source_target_pairs={{0,12},{1,13},{2,14},{3,15},{4,0},{5,1},{6,2},{7,3},{8,4},{9,5},{1... | collective-permute-start | bytes 589832 | tf_op jit(solution)/shard_map/ppermute | solution.py:344
  29.4 4.3 %colours.3 = (bf16[4,3,16,512]{3,2,1,0:T(8,128)(2,1)S(1)}, bf16[4,3,16,512]{3,2,1,0:T(8,128)(2,1)S(1)}, bf16[4,3,16,512]{3,2,1,0:T(8,128)(2,1)S(1)}, bf16[4,3,16,512]{3,2,1,0:T(8,128)(2,1)S(1)}) custom-call(f32[4,256,1024]{2,1,0:T(8,128)S(1)} %get-tuple-element.30.vol, s32[4,256,1024]{2,1,0:T(8,128)S(1)} %get-tuple-element.31.idx, ...), custom_call_target="tpu_custom_call" | custom-call | flops 26214400 | bytes 20971520 | tf_op jit(solution)/shard_map/colours/pallas_call | solution.py:170
  33.7 1.4 %collective-permute-start.8 = (bf16[4,3,16,512]{3,2,1,0:T(8,128)(2,1)S(1)}, bf16[4,3,16,512]{3,2,1,0:T(8,128)(2,1)S(1)}, u32[]{:S(2)}, u32[]{:S(2)}) collective-permute-start(bf16[4,3,16,512]{3,2,1,0:T(8,128)(2,1)S(1)} %get-tuple-element.44), channel_id=1, source_target_pairs={{0,2},{1,3},{2,0},{3,1},{4,6},{5,7},{6,4},{7,5},{8,10},{9,11},{10,... | collective-permute-start | bytes 589832 | tf_op jit(solution)/shard_map/ppermute | solution.py:252
  35.0 0.2 collective-permute-start.9
  35.2 1.2 %collective-permute-done.6.refs_2_ = bf16[4,3,16,512]{3,2,1,0:T(8,128)(2,1)S(1)} collective-permute-done((bf16[4,3,16,512]{3,2,1,0:T(8,128)(2,1)S(1)}, bf16[4,3,16,512]{3,2,1,0:T(8,128)(2,1)S(1)}, u32[]{:S(2)}, u32[]{:S(2)}) %collective-permute-start.6) | collective-permute-done | bytes 196640 | tf_op jit(solution)/shard_map/ppermute | solution.py:344
  36.5 9.6 %collective-permute-done.7.refs_3_ = bf16[4,3,16,512]{3,2,1,0:T(8,128)(2,1)S(1)} collective-permute-done((bf16[4,3,16,512]{3,2,1,0:T(8,128)(2,1)S(1)}, bf16[4,3,16,512]{3,2,1,0:T(8,128)(2,1)S(1)}, u32[]{:S(2)}, u32[]{:S(2)}) %collective-permute-start.7) | collective-permute-done | bytes 196640 | tf_op jit(solution)/shard_map/ppermute | solution.py:344
  46.1 0.1 to_core.1
  46.2 0.8 %collective-permute-start.10 = (bf16[8,16,4096]{2,1,0:T(8,128)(2,1)S(1)}, bf16[8,16,4096]{2,1,0:T(8,128)(2,1)S(1)}, u32[]{:S(2)}, u32[]{:S(2)}) collective-permute-start(bf16[8,16,4096]{2,1,0:T(8,128)(2,1)S(1)} %get-tuple-element.47), channel_id=1, source_target_pairs={{0,1},{1,0},{2,3},{3,2},{4,5},{5,4},{6,7},{7,6},{8,9},{9,8},{10,11... | collective-permute-start | bytes 3145736 | tf_op jit(solution)/shard_map/ppermute | solution.py:252
  46.9 2.3 %collective-permute-done.10.passed_ref.rest_1_ = bf16[8,16,4096]{2,1,0:T(8,128)(2,1)S(1)} collective-permute-done((bf16[8,16,4096]{2,1,0:T(8,128)(2,1)S(1)}, bf16[8,16,4096]{2,1,0:T(8,128)(2,1)S(1)}, u32[]{:S(2)}, u32[]{:S(2)}) %collective-permute-start.10) | collective-permute-done | bytes 1048608 | tf_op jit(solution)/shard_map/ppermute | solution.py:252
  49.2 0.1 to_rest.1
  49.3 1.0 %collective-permute-start.11 = (bf16[8,16,2560]{2,1,0:T(8,128)(2,1)S(1)}, bf16[8,16,2560]{2,1,0:T(8,128)(2,1)S(1)}, u32[]{:S(2)}, u32[]{:S(2)}) collective-permute-start(bf16[8,16,2560]{2,1,0:T(8,128)(2,1)S(1)} %get-tuple-element.50), channel_id=1, source_target_pairs={{0,2},{1,3},{2,0},{3,1},{4,6},{5,7},{6,4},{7,5},{8,10},{9,11},{10,... | collective-permute-start | bytes 1966088 | tf_op jit(solution)/shard_map/ppermute | solution.py:252
  50.4 2.6 %collective-permute-start.13 = (bf16[4,3,16,512]{3,2,1,0:T(8,128)(2,1)S(1)}, bf16[4,3,16,512]{3,2,1,0:T(8,128)(2,1)S(1)}, u32[]{:S(2)}, u32[]{:S(2)}) collective-permute-start(bf16[4,3,16,512]{3,2,1,0:T(8,128)(2,1)S(1)} %get-tuple-element.53), channel_id=1, source_target_pairs={{0,8},{1,9},{2,10},{3,11},{4,12},{5,13},{6,14},{7,15},{8,0},{9,1},... | collective-permute-start | bytes 589832 | tf_op jit(solution)/shard_map/ppermute | solution.py:344
  53.0 0.8 %collective-permute-start.14 = (bf16[4,3,16,512]{3,2,1,0:T(8,128)(2,1)S(1)}, bf16[4,3,16,512]{3,2,1,0:T(8,128)(2,1)S(1)}, u32[]{:S(2)}, u32[]{:S(2)}) collective-permute-start(bf16[4,3,16,512]{3,2,1,0:T(8,128)(2,1)S(1)} %get-tuple-element.54), channel_id=1, source_target_pairs={{0,12},{1,13},{2,14},{3,15},{4,0},{5,1},{6,2},{7,3},{8,4},{9,5},{1... | collective-permute-start | bytes 589832 | tf_op jit(solution)/shard_map/ppermute | solution.py:344
  53.7 11.6 %collective-permute-done.11.rest_2_ = bf16[8,16,2560]{2,1,0:T(8,128)(2,1)S(1)} collective-permute-done((bf16[8,16,2560]{2,1,0:T(8,128)(2,1)S(1)}, bf16[8,16,2560]{2,1,0:T(8,128)(2,1)S(1)}, u32[]{:S(2)}, u32[]{:S(2)}) %collective-permute-start.11) | collective-permute-done | bytes 655392 | tf_op jit(solution)/shard_map/ppermute | solution.py:252
  65.3 1.5 %blend.2.rest_7_ = f32[4,16,1024]{2,1,0:T(8,128)} custom-call(s32[16]{0:T(128)S(1)} %copy-done.2, bf16[4,16,2560]{2,1,0:T(8,128)(2,1)S(1)} %get-tuple-element.46.rest_0_, bf16[8,16,4096]{2,1,0:T(8,128)(2,1)S(1)} %collective-permute-done.10.passed_ref.rest_1_, bf16[8,16,2560]{2,1,0:T(8,128)(2,1)S(1)} %collective-permute-done.11.rest_2_), custom_call_target="tpu_custom_call" | custom-call | tf_op jit(solution)/shard_map/blend/pallas_call | solution.py:291
  66.9 0.1 collective-permute-done.13.rest_5_
  66.9 4.1 %collective-permute-done.14.rest_6_ = bf16[4,3,16,512]{3,2,1,0:T(8,128)(2,1)S(1)} collective-permute-done((bf16[4,3,16,512]{3,2,1,0:T(8,128)(2,1)S(1)}, bf16[4,3,16,512]{3,2,1,0:T(8,128)(2,1)S(1)}, u32[]{:S(2)}, u32[]{:S(2)}) %collective-permute-start.14) | collective-permute-done | bytes 196640 | tf_op jit(solution)/shard_map/ppermute | solution.py:344
  71.0 1.5 %blend.3 = f32[4,16,1024]{2,1,0:T(8,128)} custom-call(s32[16]{0:T(128)S(1)} %copy-done.2, bf16[4,16,2560]{2,1,0:T(8,128)(2,1)S(1)} %get-tuple-element.46.rest_0_, bf16[8,16,4096]{2,1,0:T(8,128)(2,1)S(1)} %collective-permute-done.10.passed_ref.rest_1_, bf16[8,16,2560]{2,1,0:T(8,128)(2,1)S(1)} %collective-permute-done.11.rest_2_, ...), custom_call_target="tpu_custom_call", output_to_operand_aliasing={{}: (8, {})} | custom-call | tf_op jit(solution)/shard_map/blend/pallas_call | solution.py:291
  (13 shorter events, 0.1 us)
Async XLA Ops:
  1.9 14.8 %collective-permute-start = (s16[256,1024]{1,0:T(8,128)(2,1)S(1)}, s16[256,1024]{1,0:T(8,128)(2,1)S(1)}, u32[]{:S(2)}, u32[]{:S(2)}) collective-permute-start(s16[256,1024]{1,0:T(8,128)(2,1)S(1)} %get-tuple-element.56), channel_id=1, source_target_pairs={{0,1},{1,2},{2,3},{3,4},{4,5},{5,6},{6,7},{7,8},{8,9},{9,10},{10,1... | collective-permute-start | bytes 1572872 | tf_op jit(solution)/shard_map/ppermute | solution.py:355
  5.6 13.6 %copy-start = (f32[3,8]{1,0:T(4,128)S(1)}, f32[3,8]{1,0:T(4,128)}, u32[]{:S(2)}) copy-start(f32[3,8]{1,0:T(4,128)} %colour_ref.3) | copy-start | bytes 292
  5.6 13.6 %collective-permute-start.1 = (s16[256,1024]{1,0:T(8,128)(2,1)S(1)}, s16[256,1024]{1,0:T(8,128)(2,1)S(1)}, u32[]{:S(2)}, u32[]{:S(2)}) collective-permute-start(s16[256,1024]{1,0:T(8,128)(2,1)S(1)} %get-tuple-element.55), channel_id=1, source_target_pairs={{1,0},{2,1},{3,2},{4,3},{5,4},{6,5},{7,6},{8,7},{9,8},{10,9},{11,1... | collective-permute-start | bytes 1572872 | tf_op jit(solution)/shard_map/ppermute | solution.py:356
  7.5 0.7 copy-start.1
  12.7 10.8 %collective-permute-start.2 = (bf16[4,16,1024]{2,1,0:T(8,128)(2,1)S(1)}, bf16[4,16,1024]{2,1,0:T(8,128)(2,1)S(1)}, u32[]{:S(2)}, u32[]{:S(2)}) collective-permute-start(bf16[4,16,1024]{2,1,0:T(8,128)(2,1)S(1)} %get-tuple-element.36), channel_id=1, source_target_pairs={{0,4},{1,5},{2,6},{3,7},{4,8},{5,9},{6,10},{7,11},{8,12},{9,13},{1... | collective-permute-start | bytes 393224 | tf_op jit(solution)/shard_map/ppermute | solution.py:344
  14.1 9.5 %collective-permute-start.3 = (bf16[4,16,1024]{2,1,0:T(8,128)(2,1)S(1)}, bf16[4,16,1024]{2,1,0:T(8,128)(2,1)S(1)}, u32[]{:S(2)}, u32[]{:S(2)}) collective-permute-start(bf16[4,16,1024]{2,1,0:T(8,128)(2,1)S(1)} %get-tuple-element.37), channel_id=1, source_target_pairs={{0,8},{1,9},{2,10},{3,11},{4,12},{5,13},{6,14},{7,15},{8,0},{9,1},... | collective-permute-start | bytes 393224 | tf_op jit(solution)/shard_map/ppermute | solution.py:344
  15.2 12.7 %collective-permute-start.4 = (bf16[4,16,1024]{2,1,0:T(8,128)(2,1)S(1)}, bf16[4,16,1024]{2,1,0:T(8,128)(2,1)S(1)}, u32[]{:S(2)}, u32[]{:S(2)}) collective-permute-start(bf16[4,16,1024]{2,1,0:T(8,128)(2,1)S(1)} %get-tuple-element.38), channel_id=1, source_target_pairs={{0,12},{1,13},{2,14},{3,15},{4,0},{5,1},{6,2},{7,3},{8,4},{9,5},{1... | collective-permute-start | bytes 393224 | tf_op jit(solution)/shard_map/ppermute | solution.py:344
  27.9 7.3 %collective-permute-start.5 = (bf16[4,3,16,512]{3,2,1,0:T(8,128)(2,1)S(1)}, bf16[4,3,16,512]{3,2,1,0:T(8,128)(2,1)S(1)}, u32[]{:S(2)}, u32[]{:S(2)}) collective-permute-start(bf16[4,3,16,512]{3,2,1,0:T(8,128)(2,1)S(1)} %get-tuple-element.39), channel_id=1, source_target_pairs={{0,4},{1,5},{2,6},{3,7},{4,8},{5,9},{6,10},{7,11},{8,12},{9,13},{1... | collective-permute-start | bytes 589832 | tf_op jit(solution)/shard_map/ppermute | solution.py:344
  27.9 8.5 %collective-permute-start.6 = (bf16[4,3,16,512]{3,2,1,0:T(8,128)(2,1)S(1)}, bf16[4,3,16,512]{3,2,1,0:T(8,128)(2,1)S(1)}, u32[]{:S(2)}, u32[]{:S(2)}) collective-permute-start(bf16[4,3,16,512]{3,2,1,0:T(8,128)(2,1)S(1)} %get-tuple-element.40), channel_id=1, source_target_pairs={{0,8},{1,9},{2,10},{3,11},{4,12},{5,13},{6,14},{7,15},{8,0},{9,1},... | collective-permute-start | bytes 589832 | tf_op jit(solution)/shard_map/ppermute | solution.py:344
  28.0 18.0 %collective-permute-start.7 = (bf16[4,3,16,512]{3,2,1,0:T(8,128)(2,1)S(1)}, bf16[4,3,16,512]{3,2,1,0:T(8,128)(2,1)S(1)}, u32[]{:S(2)}, u32[]{:S(2)}) collective-permute-start(bf16[4,3,16,512]{3,2,1,0:T(8,128)(2,1)S(1)} %get-tuple-element.41), channel_id=1, source_target_pairs={{0,12},{1,13},{2,14},{3,15},{4,0},{5,1},{6,2},{7,3},{8,4},{9,5},{1... | collective-permute-start | bytes 589832 | tf_op jit(solution)/shard_map/ppermute | solution.py:344
  29.4 35.9 %copy-start.2 = (s32[16]{0:T(128)S(1)}, s32[16]{0:T(128)}, u32[]{:S(2)}) copy-start(s32[16]{0:T(128)} %order_ref.3) | copy-start | bytes 196
  33.7 12.4 %collective-permute-start.8 = (bf16[4,3,16,512]{3,2,1,0:T(8,128)(2,1)S(1)}, bf16[4,3,16,512]{3,2,1,0:T(8,128)(2,1)S(1)}, u32[]{:S(2)}, u32[]{:S(2)}) collective-permute-start(bf16[4,3,16,512]{3,2,1,0:T(8,128)(2,1)S(1)} %get-tuple-element.44), channel_id=1, source_target_pairs={{0,2},{1,3},{2,0},{3,1},{4,6},{5,7},{6,4},{7,5},{8,10},{9,11},{10,... | collective-permute-start | bytes 589832 | tf_op jit(solution)/shard_map/ppermute | solution.py:252
  35.0 11.0 %collective-permute-start.9 = (bf16[4,3,16,512]{3,2,1,0:T(8,128)(2,1)S(1)}, bf16[4,3,16,512]{3,2,1,0:T(8,128)(2,1)S(1)}, u32[]{:S(2)}, u32[]{:S(2)}) collective-permute-start(bf16[4,3,16,512]{3,2,1,0:T(8,128)(2,1)S(1)} %get-tuple-element.45), channel_id=1, source_target_pairs={{0,2},{1,3},{2,0},{3,1},{4,6},{5,7},{6,4},{7,5},{8,10},{9,11},{10,... | collective-permute-start | bytes 589832 | tf_op jit(solution)/shard_map/ppermute | solution.py:252
  46.2 3.0 %collective-permute-start.10 = (bf16[8,16,4096]{2,1,0:T(8,128)(2,1)S(1)}, bf16[8,16,4096]{2,1,0:T(8,128)(2,1)S(1)}, u32[]{:S(2)}, u32[]{:S(2)}) collective-permute-start(bf16[8,16,4096]{2,1,0:T(8,128)(2,1)S(1)} %get-tuple-element.47), channel_id=1, source_target_pairs={{0,1},{1,0},{2,3},{3,2},{4,5},{5,4},{6,7},{7,6},{8,9},{9,8},{10,11... | collective-permute-start | bytes 3145736 | tf_op jit(solution)/shard_map/ppermute | solution.py:252
  49.3 16.0 %collective-permute-start.11 = (bf16[8,16,2560]{2,1,0:T(8,128)(2,1)S(1)}, bf16[8,16,2560]{2,1,0:T(8,128)(2,1)S(1)}, u32[]{:S(2)}, u32[]{:S(2)}) collective-permute-start(bf16[8,16,2560]{2,1,0:T(8,128)(2,1)S(1)} %get-tuple-element.50), channel_id=1, source_target_pairs={{0,2},{1,3},{2,0},{3,1},{4,6},{5,7},{6,4},{7,5},{8,10},{9,11},{10,... | collective-permute-start | bytes 1966088 | tf_op jit(solution)/shard_map/ppermute | solution.py:252
  50.4 16.5 %collective-permute-start.12 = (bf16[4,3,16,512]{3,2,1,0:T(8,128)(2,1)S(1)}, bf16[4,3,16,512]{3,2,1,0:T(8,128)(2,1)S(1)}, u32[]{:S(2)}, u32[]{:S(2)}) collective-permute-start(bf16[4,3,16,512]{3,2,1,0:T(8,128)(2,1)S(1)} %get-tuple-element.52), channel_id=1, source_target_pairs={{0,4},{1,5},{2,6},{3,7},{4,8},{5,9},{6,10},{7,11},{8,12},{9,13},{1... | collective-permute-start | bytes 589832 | tf_op jit(solution)/shard_map/ppermute | solution.py:344
  50.4 16.6 %collective-permute-start.13 = (bf16[4,3,16,512]{3,2,1,0:T(8,128)(2,1)S(1)}, bf16[4,3,16,512]{3,2,1,0:T(8,128)(2,1)S(1)}, u32[]{:S(2)}, u32[]{:S(2)}) collective-permute-start(bf16[4,3,16,512]{3,2,1,0:T(8,128)(2,1)S(1)} %get-tuple-element.53), channel_id=1, source_target_pairs={{0,8},{1,9},{2,10},{3,11},{4,12},{5,13},{6,14},{7,15},{8,0},{9,1},... | collective-permute-start | bytes 589832 | tf_op jit(solution)/shard_map/ppermute | solution.py:344
  53.0 18.0 %collective-permute-start.14 = (bf16[4,3,16,512]{3,2,1,0:T(8,128)(2,1)S(1)}, bf16[4,3,16,512]{3,2,1,0:T(8,128)(2,1)S(1)}, u32[]{:S(2)}, u32[]{:S(2)}) collective-permute-start(bf16[4,3,16,512]{3,2,1,0:T(8,128)(2,1)S(1)} %get-tuple-element.54), channel_id=1, source_target_pairs={{0,12},{1,13},{2,14},{3,15},{4,0},{5,1},{6,2},{7,3},{8,4},{9,5},{1... | collective-permute-start | bytes 589832 | tf_op jit(solution)/shard_map/ppermute | solution.py:344

commit v9 on v8

--- a/solution.py
+++ b/solution.py
@@ -202,73 +202,51 @@
     return list(on_chip(functools.partial(hold_kernel, len(parts)), shapes, parts, earlier))
 
 
-def to_core_kernel(turns, *refs):
+def turn_over_kernel(turns, *refs):
     here = lax.rem(lax.axis_index("gz"), turns)
-    colour_refs, opacity_refs, second_refs = refs[:turns], refs[turns : 2 * turns], refs[2 * turns :][:2]
-    own_ref, far_ref, passed_ref = refs[-3:]
+    colour_refs, opacity_refs, second_refs, member_refs, plane_refs = (
+        refs[turns * n : turns * (n + 1)] for n in range(5)
+    )
     width, total = colour_refs[0].shape[-1], opacity_refs[0].shape[-1]
-    for s, (colour_ref, opacity_ref) in enumerate(zip(colour_refs, opacity_refs)):
-        for m, (out_ref, at) in enumerate([(own_ref, s), (passed_ref, s), (far_ref, s), (passed_ref, turns + s)]):
+    for s, (colour_ref, opacity_ref, plane_ref) in enumerate(zip(colour_refs, opacity_refs, plane_refs)):
+        for m, (second_ref, member_ref) in enumerate(zip(second_refs, member_refs)):
+            plane_ref[m] = second_ref[s]
             for c in range(3):
-                out_ref[at, :, pl.ds(c * width, width)] = colour_ref[here ^ m, c]
-            out_ref[at, :, pl.ds(3 * width, total)] = opacity_ref[here ^ m]
-    width, start = second_refs[0].shape[-1], 3 * width + total
-    for x, ref in enumerate(second_refs):
-        for s in range(turns):
-            for c in range(3):
-                passed_ref[x * turns + s, :, pl.ds(start + c * width, width)] = ref[s, c]
-
-
-def to_core(first, opacity, second, earlier):
+                member_ref[s, :, pl.ds(c * width, width)] = colour_ref[here ^ m, c]
+            member_ref[s, :, pl.ds(3 * width, total)] = opacity_ref[here ^ m]
+
+
+def turn_over(first, opacity, second):
     turns, (_, _, height, width) = len(first), first[0].shape
-    wide = 3 * width + opacity[0].shape[-1]
-    part = jax.ShapeDtypeStruct((turns, height, wide), jnp.bfloat16)
-    passed = jax.ShapeDtypeStruct((2 * turns, height, wide + 3 * second[0].shape[-1]), jnp.bfloat16)
+    member = jax.ShapeDtypeStruct((turns, height, 3 * width + opacity[0].shape[-1]), jnp.bfloat16)
+    plane = jax.ShapeDtypeStruct(second[0].shape, jnp.bfloat16)
     operands = [*first, *opacity, *second]
-    return on_chip(functools.partial(to_core_kernel, turns), [part, part, passed], operands, earlier)
-
-
-def to_rest_kernel(turns, far_ref, passed_ref, own_ref, other_ref, out_ref, *plane_refs):
-    wide, width = far_ref.shape[2], own_ref.shape[-1]
-    out_ref[pl.ds(0, turns)] = far_ref[...]
-    out_ref[pl.ds(turns, turns)] = passed_ref[pl.ds(turns, turns), :, pl.ds(0, wide)]
-    for s, plane_ref in enumerate(plane_refs):
-        plane_ref[0] = own_ref[s]
-        plane_ref[2] = other_ref[s]
-        for c in range(3):
-            cols = pl.ds(wide + c * width, width)
-            plane_ref[1, c] = passed_ref[s, :, cols]
-            plane_ref[3, c] = passed_ref[turns + s, :, cols]
-
-
-def to_rest(far, passed, own, other):
-    turns = far.shape[0]
-    shapes = [jax.ShapeDtypeStruct((2 * turns,) + far.shape[1:], far.dtype)]
-    shapes += [jax.ShapeDtypeStruct(own.shape, own.dtype)] * turns
-    return on_chip(functools.partial(to_rest_kernel, turns), shapes, [far, passed, own, other])
-
-
-def swap(part, devices, stride):
-    return lax.ppermute(part, "gz", [(i, i ^ stride) for i in range(devices)])
+    done = on_chip(functools.partial(turn_over_kernel, turns), [member] * turns + [plane] * turns, operands)
+    return done[:turns], done[turns:]
+
+
+def in_plane(parts, devices):
+    return [parts[0]] + [
+        lax.ppermute(part, "gz", [(i, i ^ m) for i in range(devices)]) for m, part in enumerate(parts[1:], 1)
+    ]
 
 
 def blend_kernel(ranks, turns, side, order_ref, *rest):
-    (own_ref, passed_ref, far_ref), second_refs = rest[:3], rest[3:-6]
+    first_refs, second_refs = rest[:turns], rest[turns:-6]
     out_hbm, place, colour_ref, opacity_ref, out_ref, sem = rest[-6:]
     device = lax.axis_index("gz")
     plane, member = device // turns, lax.rem(device, turns)
     width, total = out_ref.shape[2], out_hbm.shape[2]
     start = total - width if side else 0
-    before = own_ref.shape[2] - total
+    before = first_refs[0].shape[2] - total
     for b in range(ranks):
         place[order_ref[b]] = b
     for m in range(turns):
         for s in range(turns):
             brick = lax.rem(plane + turns - s, turns) * turns + (member ^ m)
-            ref, at = [(own_ref, s), (passed_ref, s), (far_ref, s), (far_ref, turns + s)][m]
             for c in range(3):
-                colour_ref[brick, c] = second_refs[s][m, c] if side else ref[at, :, pl.ds(c * width, width)]
-            opacity_ref[brick] = ref[at, :, pl.ds(before + start, width)]
+                colour_ref[brick, c] = second_refs[s][m, c] if side else first_refs[m][s, :, pl.ds(c * width, width)]
+            opacity_ref[brick] = first_refs[m][s, :, pl.ds(before + start, width)]
     for j in range(width // LANES):
         cols = pl.ds(j * LANES, LANES)
         canvas = (jnp.zeros((out_ref.shape[1], LANES), jnp.float32),) * 4
@@ -364,15 +342,10 @@
     split = tiles * FIRST // 8
     opacity = across_planes(opacity, turns, devices)
     own, *others = colours(*held, (0, split), turns)
-    second = colours(*held, (split, tiles), turns, (own,))
+    second = in_plane(colours(*held, (split, tiles), turns, (own,)), devices)
     first = across_planes([own] + hold(others, opacity[1:]), turns, devices)
-    near, core, *far = second
-    far = [swap(part, devices, 2) for part in far]
-    own, other, passed = to_core(first, opacity, [core, far[1]], far[:1])
-    passed = swap(passed, devices, 1)
-    other, *second = to_rest(other, passed, near, far[0])
-    second = across_planes(second, turns, devices)
-    first = [own, passed, swap(other, devices, 2)]
+    first, second = turn_over(first, opacity, second)
+    first, second = in_plane(first, devices), across_planes(second, turns, devices)
     return blend(order, turns, width, first, second, (blend(order, turns, width, first),))
 
 

time: 72.7 us -> 73.8 us (1.015)
  starting transfers between devices: 17.6 us -> 24.5 us
  waiting for transfers between devices: 35.8 us -> 30 us
    ppermute x4 -> x6, starting transfers between devices: 3.34 us -> 9.56 us  [in_plane(): lax.ppermute(part, 'gz', [(i, i ^ m) for i in range(devices)])]
    ppermute x9, waiting for transfers between devices: 19.3 us -> 15.5 us  [across_planes(): lax.ppermute(part, 'gz', [(i, (i + s * turns) % devices) for i in range(d...]
    ppermute x4 -> x6, waiting for transfers between devices: 13.9 us -> 11.8 us  [in_plane(): lax.ppermute(part, 'gz', [(i, i ^ m) for i in range(devices)])]
  transfers between devices with their start and end apart: 15 -> 17, of which waited for: 9 -> 9; matrix products, arithmetic and copies ran while one was open for 0% -> 0% of each run, Pallas kernels for 20% -> 20%
where the time goes in v9:
time: 73.8 us; the launch traced here: 73.5 us
  waiting for transfers between devices  30 us (41%)
  starting transfers between devices  24.5 us (33%)
  Pallas kernels  16.3 us (22%)
  other arithmetic  1.9 us (3%)
    ppermute x9, waiting for transfers between devices, across_planes(): lax.ppermute(part, 'gz', [(i, (i + s * turns) % devices) for i in range(d...  15.5 us
    ppermute x6, waiting for transfers between devices, in_plane(): lax.ppermute(part, 'gz', [(i, i ^ m) for i in range(devices)])  11.8 us
    ppermute x6, starting transfers between devices, in_plane(): lax.ppermute(part, 'gz', [(i, i ^ m) for i in range(devices)])  9.56 us
    ppermute x9, starting transfers between devices, across_planes(): lax.ppermute(part, 'gz', [(i, (i + s * turns) % devices) for i in range(d...  9.32 us
    pallas_call x2, Pallas kernels, colours(): pl.pallas_call(functools.partial(colour_kernel, slices, span, turns, bool...  8.59 us
    pallas_call x1, Pallas kernels, opacities(): pl.pallas_call(functools.partial(opacity_kernel, slices, width // LANES,...  4.52 us
    ppermute x1, starting transfers between devices, shards(): before = lax.ppermute(last, 'gz', up)  3.68 us
    pallas_call x2, Pallas kernels, blend(): pl.pallas_call(functools.partial(blend_kernel, ranks, turns, 1 if second...  3.03 us
  transfers between devices with their start and end apart: 17, of which 9 were waited for; matrix products, arithmetic and copies ran while one was open for 0% of the time, Pallas kernels for 20%

profile of v9, /device:TPU:13, one launch (start us, length us, event | category | flops | bytes accessed | tf_op | source)
XLA Modules:
  0.0 73.5 jit_solution(16078459788929466343)
XLA Ops:
  0.0 1.9 %fusion.1 = (s16[256,1024]{1,0:T(8,128)(2,1)S(1)}, s16[256,1024]{1,0:T(8,128)(2,1)S(1)}) fusion(f32[4,256,1024]{2,1,0:T(8,128)} %volume_hbm.1), kind=kLoop, calls=%fused_computation.3 | loop fusion | flops 1572864 | bytes 3145728 | tf_op jit(solution)/shard_map/convert_element_type | solution.py:317
  1.9 3.7 %collective-permute-start = (s16[256,1024]{1,0:T(8,128)(2,1)S(1)}, s16[256,1024]{1,0:T(8,128)(2,1)S(1)}, u32[]{:S(2)}, u32[]{:S(2)}) collective-permute-start(s16[256,1024]{1,0:T(8,128)(2,1)S(1)} %get-tuple-element.56), channel_id=1, source_target_pairs={{0,1},{1,2},{2,3},{3,4},{4,5},{5,6},{6,7},{7,8},{8,9},{9,10},{10,1... | collective-permute-start | bytes 1572872 | tf_op jit(solution)/shard_map/ppermute | solution.py:333
  5.6 1.9 %collective-permute-start.1 = (s16[256,1024]{1,0:T(8,128)(2,1)S(1)}, s16[256,1024]{1,0:T(8,128)(2,1)S(1)}, u32[]{:S(2)}, u32[]{:S(2)}) collective-permute-start(s16[256,1024]{1,0:T(8,128)(2,1)S(1)} %get-tuple-element.55), channel_id=1, source_target_pairs={{1,0},{2,1},{3,2},{4,3},{5,4},{6,5},{7,6},{8,7},{9,8},{10,9},{11,1... | collective-permute-start | bytes 1572872 | tf_op jit(solution)/shard_map/ppermute | solution.py:334
  7.5 0.0 copy-start.1
  7.5 0.6 copy-done.1
  8.2 4.5 %opacities.1 = (bf16[4,16,1024]{2,1,0:T(8,128)(2,1)S(1)}, bf16[4,16,1024]{2,1,0:T(8,128)(2,1)S(1)}, bf16[4,16,1024]{2,1,0:T(8,128)(2,1)S(1)}, bf16[4,16,1024]{2,...) custom-call(f32[4,256,1024]{2,1,0:T(8,128)} %volume_hbm.1, s32[4,256,1024]{2,1,0:T(8,128)} %index_hbm.1, ...), custom_call_target="tpu_custom_call" | custom-call | flops 15728640 | bytes 9437184 | tf_op jit(solution)/shard_map/opacities/pallas_call | solution.py:79
  12.7 1.3 %collective-permute-start.2 = (bf16[4,16,1024]{2,1,0:T(8,128)(2,1)S(1)}, bf16[4,16,1024]{2,1,0:T(8,128)(2,1)S(1)}, u32[]{:S(2)}, u32[]{:S(2)}) collective-permute-start(bf16[4,16,1024]{2,1,0:T(8,128)(2,1)S(1)} %get-tuple-element.36), channel_id=1, source_target_pairs={{0,4},{1,5},{2,6},{3,7},{4,8},{5,9},{6,10},{7,11},{8,12},{9,13},{1... | collective-permute-start | bytes 393224 | tf_op jit(solution)/shard_map/ppermute | solution.py:322
  14.1 1.1 %collective-permute-start.3 = (bf16[4,16,1024]{2,1,0:T(8,128)(2,1)S(1)}, bf16[4,16,1024]{2,1,0:T(8,128)(2,1)S(1)}, u32[]{:S(2)}, u32[]{:S(2)}) collective-permute-start(bf16[4,16,1024]{2,1,0:T(8,128)(2,1)S(1)} %get-tuple-element.37), channel_id=1, source_target_pairs={{0,8},{1,9},{2,10},{3,11},{4,12},{5,13},{6,14},{7,15},{8,0},{9,1},... | collective-permute-start | bytes 393224 | tf_op jit(solution)/shard_map/ppermute | solution.py:322
  15.2 1.4 %collective-permute-start.4 = (bf16[4,16,1024]{2,1,0:T(8,128)(2,1)S(1)}, bf16[4,16,1024]{2,1,0:T(8,128)(2,1)S(1)}, u32[]{:S(2)}, u32[]{:S(2)}) collective-permute-start(bf16[4,16,1024]{2,1,0:T(8,128)(2,1)S(1)} %get-tuple-element.38), channel_id=1, source_target_pairs={{0,12},{1,13},{2,14},{3,15},{4,0},{5,1},{6,2},{7,3},{8,4},{9,5},{1... | collective-permute-start | bytes 393224 | tf_op jit(solution)/shard_map/ppermute | solution.py:322
  16.5 0.1 collective-permute-done.before_ref
  16.7 2.5 %collective-permute-done.1.after_ref = s16[256,1024]{1,0:T(8,128)(2,1)S(1)} collective-permute-done((s16[256,1024]{1,0:T(8,128)(2,1)S(1)}, s16[256,1024]{1,0:T(8,128)(2,1)S(1)}, u32[]{:S(2)}, u32[]{:S(2)}) %collective-permute-start.1) | collective-permute-done | bytes 524320 | tf_op jit(solution)/shard_map/ppermute | solution.py:334
  19.2 4.3 %colours.2 = (bf16[4,3,16,512]{3,2,1,0:T(8,128)(2,1)S(1)}, bf16[4,3,16,512]{3,2,1,0:T(8,128)(2,1)S(1)}, bf16[4,3,16,512]{3,2,1,0:T(8,128)(2,1)S(1)}, bf16[4,3,16,512]{3,2,1,0:T(8,128)(2,1)S(1)}) custom-call(f32[4,256,1024]{2,1,0:T(8,128)S(1)} %get-tuple-element.30.vol, s32[4,256,1024]{2,1,0:T(8,128)S(1)} %get-tuple-element.31.idx, ...), custom_call_target="tpu_custom_call" | custom-call | flops 26214400 | bytes 20971520 | tf_op jit(solution)/shard_map/colours/pallas_call | solution.py:170
  23.5 4.3 %collective-permute-done.4.refs_5_.refs_7_ = bf16[4,16,1024]{2,1,0:T(8,128)(2,1)S(1)} collective-permute-done((bf16[4,16,1024]{2,1,0:T(8,128)(2,1)S(1)}, bf16[4,16,1024]{2,1,0:T(8,128)(2,1)S(1)}, u32[]{:S(2)}, u32[]{:S(2)}) %collective-permute-start.4) | collective-permute-done | bytes 131104 | tf_op jit(solution)/shard_map/ppermute | solution.py:322
  27.9 0.1 collective-permute-start.5
  27.9 0.1 collective-permute-start.6
  28.0 1.4 %collective-permute-start.7 = (bf16[4,3,16,512]{3,2,1,0:T(8,128)(2,1)S(1)}, bf16[4,3,16,512]{3,2,1,0:T(8,128)(2,1)S(1)}, u32[]{:S(2)}, u32[]{:S(2)}) collective-permute-start(bf16[4,3,16,512]{3,2,1,0:T(8,128)(2,1)S(1)} %get-tuple-element.41), channel_id=1, source_target_pairs={{0,12},{1,13},{2,14},{3,15},{4,0},{5,1},{6,2},{7,3},{8,4},{9,5},{1... | collective-permute-start | bytes 589832 | tf_op jit(solution)/shard_map/ppermute | solution.py:322
  29.4 4.3 %colours.3 = (bf16[4,3,16,512]{3,2,1,0:T(8,128)(2,1)S(1)}, bf16[4,3,16,512]{3,2,1,0:T(8,128)(2,1)S(1)}, bf16[4,3,16,512]{3,2,1,0:T(8,128)(2,1)S(1)}, bf16[4,3,16,512]{3,2,1,0:T(8,128)(2,1)S(1)}) custom-call(f32[4,256,1024]{2,1,0:T(8,128)S(1)} %get-tuple-element.30.vol, s32[4,256,1024]{2,1,0:T(8,128)S(1)} %get-tuple-element.31.idx, ...), custom_call_target="tpu_custom_call" | custom-call | flops 26214400 | bytes 20971520 | tf_op jit(solution)/shard_map/colours/pallas_call | solution.py:170
  33.7 4.0 %collective-permute-start.8 = (bf16[4,3,16,512]{3,2,1,0:T(8,128)(2,1)S(1)}, bf16[4,3,16,512]{3,2,1,0:T(8,128)(2,1)S(1)}, u32[]{:S(2)}, u32[]{:S(2)}) collective-permute-start(bf16[4,3,16,512]{3,2,1,0:T(8,128)(2,1)S(1)} %get-tuple-element.44), channel_id=1, source_target_pairs={{0,1},{1,0},{2,3},{3,2},{4,5},{5,4},{6,7},{7,6},{8,9},{9,8},{10,11... | collective-permute-start | bytes 589832 | tf_op jit(solution)/shard_map/ppermute | solution.py:230
  37.6 1.7 %collective-permute-start.10 = (bf16[4,3,16,512]{3,2,1,0:T(8,128)(2,1)S(1)}, bf16[4,3,16,512]{3,2,1,0:T(8,128)(2,1)S(1)}, u32[]{:S(2)}, u32[]{:S(2)}) collective-permute-start(bf16[4,3,16,512]{3,2,1,0:T(8,128)(2,1)S(1)} %get-tuple-element.46), channel_id=1, source_target_pairs={{0,3},{1,2},{2,1},{3,0},{4,7},{5,6},{6,5},{7,4},{8,11},{9,10},{10,... | collective-permute-start | bytes 589832 | tf_op jit(solution)/shard_map/ppermute | solution.py:230
  39.4 6.7 %collective-permute-done.7.refs_3_ = bf16[4,3,16,512]{3,2,1,0:T(8,128)(2,1)S(1)} collective-permute-done((bf16[4,3,16,512]{3,2,1,0:T(8,128)(2,1)S(1)}, bf16[4,3,16,512]{3,2,1,0:T(8,128)(2,1)S(1)}, u32[]{:S(2)}, u32[]{:S(2)}) %collective-permute-start.7) | collective-permute-done | bytes 196640 | tf_op jit(solution)/shard_map/ppermute | solution.py:322
  46.1 1.0 %collective-permute-done.10.refs_11_ = bf16[4,3,16,512]{3,2,1,0:T(8,128)(2,1)S(1)} collective-permute-done((bf16[4,3,16,512]{3,2,1,0:T(8,128)(2,1)S(1)}, bf16[4,3,16,512]{3,2,1,0:T(8,128)(2,1)S(1)}, u32[]{:S(2)}, u32[]{:S(2)}) %collective-permute-start.10) | collective-permute-done | bytes 196640 | tf_op jit(solution)/shard_map/ppermute | solution.py:230
  47.1 0.1 turn_over.1
  47.2 2.2 %collective-permute-start.11 = (bf16[4,16,2560]{2,1,0:T(8,128)(2,1)S(1)}, bf16[4,16,2560]{2,1,0:T(8,128)(2,1)S(1)}, u32[]{:S(2)}, u32[]{:S(2)}) collective-permute-start(bf16[4,16,2560]{2,1,0:T(8,128)(2,1)S(1)} %get-tuple-element.48), channel_id=1, source_target_pairs={{0,1},{1,0},{2,3},{3,2},{4,5},{5,4},{6,7},{7,6},{8,9},{9,8},{10,11... | collective-permute-start | bytes 983048 | tf_op jit(solution)/shard_map/ppermute | solution.py:230
  49.4 1.7 %collective-permute-start.13 = (bf16[4,16,2560]{2,1,0:T(8,128)(2,1)S(1)}, bf16[4,16,2560]{2,1,0:T(8,128)(2,1)S(1)}, u32[]{:S(2)}, u32[]{:S(2)}) collective-permute-start(bf16[4,16,2560]{2,1,0:T(8,128)(2,1)S(1)} %get-tuple-element.50), channel_id=1, source_target_pairs={{0,3},{1,2},{2,1},{3,0},{4,7},{5,6},{6,5},{7,4},{8,11},{9,10},{10,... | collective-permute-start | bytes 983048 | tf_op jit(solution)/shard_map/ppermute | solution.py:230
  51.1 1.7 %collective-permute-start.14 = (bf16[4,3,16,512]{3,2,1,0:T(8,128)(2,1)S(1)}, bf16[4,3,16,512]{3,2,1,0:T(8,128)(2,1)S(1)}, u32[]{:S(2)}, u32[]{:S(2)}) collective-permute-start(bf16[4,3,16,512]{3,2,1,0:T(8,128)(2,1)S(1)} %get-tuple-element.52), channel_id=1, source_target_pairs={{0,4},{1,5},{2,6},{3,7},{4,8},{5,9},{6,10},{7,11},{8,12},{9,13},{1... | collective-permute-start | bytes 589832 | tf_op jit(solution)/shard_map/ppermute | solution.py:322
  52.8 2.2 %collective-permute-start.15 = (bf16[4,3,16,512]{3,2,1,0:T(8,128)(2,1)S(1)}, bf16[4,3,16,512]{3,2,1,0:T(8,128)(2,1)S(1)}, u32[]{:S(2)}, u32[]{:S(2)}) collective-permute-start(bf16[4,3,16,512]{3,2,1,0:T(8,128)(2,1)S(1)} %get-tuple-element.53), channel_id=1, source_target_pairs={{0,8},{1,9},{2,10},{3,11},{4,12},{5,13},{6,14},{7,15},{8,0},{9,1},... | collective-permute-start | bytes 589832 | tf_op jit(solution)/shard_map/ppermute | solution.py:322
  55.1 3.6 %collective-permute-done.12.rest_2_ = bf16[4,16,2560]{2,1,0:T(8,128)(2,1)S(1)} collective-permute-done((bf16[4,16,2560]{2,1,0:T(8,128)(2,1)S(1)}, bf16[4,16,2560]{2,1,0:T(8,128)(2,1)S(1)}, u32[]{:S(2)}, u32[]{:S(2)}) %collective-permute-start.12) | collective-permute-done | bytes 327712 | tf_op jit(solution)/shard_map/ppermute | solution.py:230
  58.7 7.2 %collective-permute-done.13.rest_3_ = bf16[4,16,2560]{2,1,0:T(8,128)(2,1)S(1)} collective-permute-done((bf16[4,16,2560]{2,1,0:T(8,128)(2,1)S(1)}, bf16[4,16,2560]{2,1,0:T(8,128)(2,1)S(1)}, u32[]{:S(2)}, u32[]{:S(2)}) %collective-permute-start.13) | collective-permute-done | bytes 327712 | tf_op jit(solution)/shard_map/ppermute | solution.py:230
  65.9 1.5 %blend.2.rest_8_ = f32[4,16,1024]{2,1,0:T(8,128)} custom-call(s32[16]{0:T(128)S(1)} %copy-done.2, bf16[4,16,2560]{2,1,0:T(8,128)(2,1)S(1)} %get-tuple-element.47.rest_0_, bf16[4,16,2560]{2,1,0:T(8,128)(2,1)S(1)} %collective-permute-done.11.rest_1_, bf16[4,16,2560]{2,1,0:T(8,128)(2,1)S(1)} %collective-permute-done.12.rest_2_, ...), custom_call_target="tpu_custom_call" | custom-call | tf_op jit(solution)/shard_map/blend/pallas_call | solution.py:269
  67.4 2.2 %collective-permute-done.15.rest_6_ = bf16[4,3,16,512]{3,2,1,0:T(8,128)(2,1)S(1)} collective-permute-done((bf16[4,3,16,512]{3,2,1,0:T(8,128)(2,1)S(1)}, bf16[4,3,16,512]{3,2,1,0:T(8,128)(2,1)S(1)}, u32[]{:S(2)}, u32[]{:S(2)}) %collective-permute-start.15) | collective-permute-done | bytes 196640 | tf_op jit(solution)/shard_map/ppermute | solution.py:322
  69.6 2.3 %collective-permute-done.16.rest_7_ = bf16[4,3,16,512]{3,2,1,0:T(8,128)(2,1)S(1)} collective-permute-done((bf16[4,3,16,512]{3,2,1,0:T(8,128)(2,1)S(1)}, bf16[4,3,16,512]{3,2,1,0:T(8,128)(2,1)S(1)}, u32[]{:S(2)}, u32[]{:S(2)}) %collective-permute-start.16) | collective-permute-done | bytes 196640 | tf_op jit(solution)/shard_map/ppermute | solution.py:322
  71.9 1.5 %blend.3 = f32[4,16,1024]{2,1,0:T(8,128)} custom-call(s32[16]{0:T(128)S(1)} %copy-done.2, bf16[4,16,2560]{2,1,0:T(8,128)(2,1)S(1)} %get-tuple-element.47.rest_0_, bf16[4,16,2560]{2,1,0:T(8,128)(2,1)S(1)} %collective-permute-done.11.rest_1_, bf16[4,16,2560]{2,1,0:T(8,128)(2,1)S(1)} %collective-permute-done.12.rest_2_, ...), custom_call_target="tpu_custom_call", output_to_operand_aliasing={{}: (9, {})} | custom-call | tf_op jit(solution)/shard_map/blend/pallas_call | solution.py:269
  (16 shorter events, 0.1 us)
Async XLA Ops:
  1.9 14.8 %collective-permute-start = (s16[256,1024]{1,0:T(8,128)(2,1)S(1)}, s16[256,1024]{1,0:T(8,128)(2,1)S(1)}, u32[]{:S(2)}, u32[]{:S(2)}) collective-permute-start(s16[256,1024]{1,0:T(8,128)(2,1)S(1)} %get-tuple-element.56), channel_id=1, source_target_pairs={{0,1},{1,2},{2,3},{3,4},{4,5},{5,6},{6,7},{7,8},{8,9},{9,10},{10,1... | collective-permute-start | bytes 1572872 | tf_op jit(solution)/shard_map/ppermute | solution.py:333
  5.6 13.6 %copy-start = (f32[3,8]{1,0:T(4,128)S(1)}, f32[3,8]{1,0:T(4,128)}, u32[]{:S(2)}) copy-start(f32[3,8]{1,0:T(4,128)} %colour_ref.3) | copy-start | bytes 292
  5.6 13.6 %collective-permute-start.1 = (s16[256,1024]{1,0:T(8,128)(2,1)S(1)}, s16[256,1024]{1,0:T(8,128)(2,1)S(1)}, u32[]{:S(2)}, u32[]{:S(2)}) collective-permute-start(s16[256,1024]{1,0:T(8,128)(2,1)S(1)} %get-tuple-element.55), channel_id=1, source_target_pairs={{1,0},{2,1},{3,2},{4,3},{5,4},{6,5},{7,6},{8,7},{9,8},{10,9},{11,1... | collective-permute-start | bytes 1572872 | tf_op jit(solution)/shard_map/ppermute | solution.py:334
  7.5 0.7 copy-start.1
  12.7 10.8 %collective-permute-start.2 = (bf16[4,16,1024]{2,1,0:T(8,128)(2,1)S(1)}, bf16[4,16,1024]{2,1,0:T(8,128)(2,1)S(1)}, u32[]{:S(2)}, u32[]{:S(2)}) collective-permute-start(bf16[4,16,1024]{2,1,0:T(8,128)(2,1)S(1)} %get-tuple-element.36), channel_id=1, source_target_pairs={{0,4},{1,5},{2,6},{3,7},{4,8},{5,9},{6,10},{7,11},{8,12},{9,13},{1... | collective-permute-start | bytes 393224 | tf_op jit(solution)/shard_map/ppermute | solution.py:322
  14.1 9.5 %collective-permute-start.3 = (bf16[4,16,1024]{2,1,0:T(8,128)(2,1)S(1)}, bf16[4,16,1024]{2,1,0:T(8,128)(2,1)S(1)}, u32[]{:S(2)}, u32[]{:S(2)}) collective-permute-start(bf16[4,16,1024]{2,1,0:T(8,128)(2,1)S(1)} %get-tuple-element.37), channel_id=1, source_target_pairs={{0,8},{1,9},{2,10},{3,11},{4,12},{5,13},{6,14},{7,15},{8,0},{9,1},... | collective-permute-start | bytes 393224 | tf_op jit(solution)/shard_map/ppermute | solution.py:322
  15.2 12.7 %collective-permute-start.4 = (bf16[4,16,1024]{2,1,0:T(8,128)(2,1)S(1)}, bf16[4,16,1024]{2,1,0:T(8,128)(2,1)S(1)}, u32[]{:S(2)}, u32[]{:S(2)}) collective-permute-start(bf16[4,16,1024]{2,1,0:T(8,128)(2,1)S(1)} %get-tuple-element.38), channel_id=1, source_target_pairs={{0,12},{1,13},{2,14},{3,15},{4,0},{5,1},{6,2},{7,3},{8,4},{9,5},{1... | collective-permute-start | bytes 393224 | tf_op jit(solution)/shard_map/ppermute | solution.py:322
  27.9 9.8 %collective-permute-start.5 = (bf16[4,3,16,512]{3,2,1,0:T(8,128)(2,1)S(1)}, bf16[4,3,16,512]{3,2,1,0:T(8,128)(2,1)S(1)}, u32[]{:S(2)}, u32[]{:S(2)}) collective-permute-start(bf16[4,3,16,512]{3,2,1,0:T(8,128)(2,1)S(1)} %get-tuple-element.39), channel_id=1, source_target_pairs={{0,4},{1,5},{2,6},{3,7},{4,8},{5,9},{6,10},{7,11},{8,12},{9,13},{1... | collective-permute-start | bytes 589832 | tf_op jit(solution)/shard_map/ppermute | solution.py:322
  27.9 11.4 %collective-permute-start.6 = (bf16[4,3,16,512]{3,2,1,0:T(8,128)(2,1)S(1)}, bf16[4,3,16,512]{3,2,1,0:T(8,128)(2,1)S(1)}, u32[]{:S(2)}, u32[]{:S(2)}) collective-permute-start(bf16[4,3,16,512]{3,2,1,0:T(8,128)(2,1)S(1)} %get-tuple-element.40), channel_id=1, source_target_pairs={{0,8},{1,9},{2,10},{3,11},{4,12},{5,13},{6,14},{7,15},{8,0},{9,1},... | collective-permute-start | bytes 589832 | tf_op jit(solution)/shard_map/ppermute | solution.py:322
  28.0 18.0 %collective-permute-start.7 = (bf16[4,3,16,512]{3,2,1,0:T(8,128)(2,1)S(1)}, bf16[4,3,16,512]{3,2,1,0:T(8,128)(2,1)S(1)}, u32[]{:S(2)}, u32[]{:S(2)}) collective-permute-start(bf16[4,3,16,512]{3,2,1,0:T(8,128)(2,1)S(1)} %get-tuple-element.41), channel_id=1, source_target_pairs={{0,12},{1,13},{2,14},{3,15},{4,0},{5,1},{6,2},{7,3},{8,4},{9,5},{1... | collective-permute-start | bytes 589832 | tf_op jit(solution)/shard_map/ppermute | solution.py:322
  29.4 36.5 %copy-start.2 = (s32[16]{0:T(128)S(1)}, s32[16]{0:T(128)}, u32[]{:S(2)}) copy-start(s32[16]{0:T(128)} %order_ref.3) | copy-start | bytes 196
  33.7 12.4 %collective-permute-start.8 = (bf16[4,3,16,512]{3,2,1,0:T(8,128)(2,1)S(1)}, bf16[4,3,16,512]{3,2,1,0:T(8,128)(2,1)S(1)}, u32[]{:S(2)}, u32[]{:S(2)}) collective-permute-start(bf16[4,3,16,512]{3,2,1,0:T(8,128)(2,1)S(1)} %get-tuple-element.44), channel_id=1, source_target_pairs={{0,1},{1,0},{2,3},{3,2},{4,5},{5,4},{6,7},{7,6},{8,9},{9,8},{10,11... | collective-permute-start | bytes 589832 | tf_op jit(solution)/shard_map/ppermute | solution.py:230
  37.6 8.4 %collective-permute-start.9 = (bf16[4,3,16,512]{3,2,1,0:T(8,128)(2,1)S(1)}, bf16[4,3,16,512]{3,2,1,0:T(8,128)(2,1)S(1)}, u32[]{:S(2)}, u32[]{:S(2)}) collective-permute-start(bf16[4,3,16,512]{3,2,1,0:T(8,128)(2,1)S(1)} %get-tuple-element.45), channel_id=1, source_target_pairs={{0,2},{1,3},{2,0},{3,1},{4,6},{5,7},{6,4},{7,5},{8,10},{9,11},{10,... | collective-permute-start | bytes 589832 | tf_op jit(solution)/shard_map/ppermute | solution.py:230
  37.6 9.4 %collective-permute-start.10 = (bf16[4,3,16,512]{3,2,1,0:T(8,128)(2,1)S(1)}, bf16[4,3,16,512]{3,2,1,0:T(8,128)(2,1)S(1)}, u32[]{:S(2)}, u32[]{:S(2)}) collective-permute-start(bf16[4,3,16,512]{3,2,1,0:T(8,128)(2,1)S(1)} %get-tuple-element.46), channel_id=1, source_target_pairs={{0,3},{1,2},{2,1},{3,0},{4,7},{5,6},{6,5},{7,4},{8,11},{9,10},{10,... | collective-permute-start | bytes 589832 | tf_op jit(solution)/shard_map/ppermute | solution.py:230
  47.2 7.9 %collective-permute-start.11 = (bf16[4,16,2560]{2,1,0:T(8,128)(2,1)S(1)}, bf16[4,16,2560]{2,1,0:T(8,128)(2,1)S(1)}, u32[]{:S(2)}, u32[]{:S(2)}) collective-permute-start(bf16[4,16,2560]{2,1,0:T(8,128)(2,1)S(1)} %get-tuple-element.48), channel_id=1, source_target_pairs={{0,1},{1,0},{2,3},{3,2},{4,5},{5,4},{6,7},{7,6},{8,9},{9,8},{10,11... | collective-permute-start | bytes 983048 | tf_op jit(solution)/shard_map/ppermute | solution.py:230
  49.4 9.3 %collective-permute-start.12 = (bf16[4,16,2560]{2,1,0:T(8,128)(2,1)S(1)}, bf16[4,16,2560]{2,1,0:T(8,128)(2,1)S(1)}, u32[]{:S(2)}, u32[]{:S(2)}) collective-permute-start(bf16[4,16,2560]{2,1,0:T(8,128)(2,1)S(1)} %get-tuple-element.49), channel_id=1, source_target_pairs={{0,2},{1,3},{2,0},{3,1},{4,6},{5,7},{6,4},{7,5},{8,10},{9,11},{10,... | collective-permute-start | bytes 983048 | tf_op jit(solution)/shard_map/ppermute | solution.py:230
  49.4 16.5 %collective-permute-start.13 = (bf16[4,16,2560]{2,1,0:T(8,128)(2,1)S(1)}, bf16[4,16,2560]{2,1,0:T(8,128)(2,1)S(1)}, u32[]{:S(2)}, u32[]{:S(2)}) collective-permute-start(bf16[4,16,2560]{2,1,0:T(8,128)(2,1)S(1)} %get-tuple-element.50), channel_id=1, source_target_pairs={{0,3},{1,2},{2,1},{3,0},{4,7},{5,6},{6,5},{7,4},{8,11},{9,10},{10,... | collective-permute-start | bytes 983048 | tf_op jit(solution)/shard_map/ppermute | solution.py:230
  51.1 16.3 %collective-permute-start.14 = (bf16[4,3,16,512]{3,2,1,0:T(8,128)(2,1)S(1)}, bf16[4,3,16,512]{3,2,1,0:T(8,128)(2,1)S(1)}, u32[]{:S(2)}, u32[]{:S(2)}) collective-permute-start(bf16[4,3,16,512]{3,2,1,0:T(8,128)(2,1)S(1)} %get-tuple-element.52), channel_id=1, source_target_pairs={{0,4},{1,5},{2,6},{3,7},{4,8},{5,9},{6,10},{7,11},{8,12},{9,13},{1... | collective-permute-start | bytes 589832 | tf_op jit(solution)/shard_map/ppermute | solution.py:322
  52.8 16.8 %collective-permute-start.15 = (bf16[4,3,16,512]{3,2,1,0:T(8,128)(2,1)S(1)}, bf16[4,3,16,512]{3,2,1,0:T(8,128)(2,1)S(1)}, u32[]{:S(2)}, u32[]{:S(2)}) collective-permute-start(bf16[4,3,16,512]{3,2,1,0:T(8,128)(2,1)S(1)} %get-tuple-element.53), channel_id=1, source_target_pairs={{0,8},{1,9},{2,10},{3,11},{4,12},{5,13},{6,14},{7,15},{8,0},{9,1},... | collective-permute-start | bytes 589832 | tf_op jit(solution)/shard_map/ppermute | solution.py:322
  55.1 16.8 %collective-permute-start.16 = (bf16[4,3,16,512]{3,2,1,0:T(8,128)(2,1)S(1)}, bf16[4,3,16,512]{3,2,1,0:T(8,128)(2,1)S(1)}, u32[]{:S(2)}, u32[]{:S(2)}) collective-permute-start(bf16[4,3,16,512]{3,2,1,0:T(8,128)(2,1)S(1)} %get-tuple-element.54), channel_id=1, source_target_pairs={{0,12},{1,13},{2,14},{3,15},{4,0},{5,1},{6,2},{7,3},{8,4},{9,5},{1... | collective-permute-start | bytes 589832 | tf_op jit(solution)/shard_map/ppermute | solution.py:322

commit v10 on v9

--- a/solution.py
+++ b/solution.py
@@ -15,8 +15,9 @@
 NT = 8
 LIMIT = 24 * 1024 * 1024
 FETCH_LIMIT = 43 * 1024 * 1024
+REFETCH_LIMIT = 50 * 1024 * 1024
 BLEND_LIMIT = 16 * 1024 * 1024
-FIRST = 4
+FIRST = 5
 PLANES = 4
 
 
@@ -41,10 +42,10 @@
 
 
 def opacity_kernel(slices, tiles, turns, volume_hbm, index_hbm, opacity_ref, *rest):
-    out_refs, (vol, idx, sems) = rest[:turns], rest[turns:]
+    out_refs, (vol, idx, sems) = rest[:-3], rest[-3:]
     height = vol.shape[1] // turns
     plane = lax.axis_index("gz") // (lax.axis_size("gz") // turns)
-    bases = [pl.multiple_of(lax.rem(plane + turn, turns) * height, height) for turn in range(turns)]
+    bases = [pl.multiple_of((plane ^ turn) * height, height) for turn in range(turns)]
     copies = []
     for turn, base in enumerate(bases):
         some = pl.ds(base, height)
@@ -56,11 +57,14 @@
             copy.start()
         copies.append(pair)
     table = spread(opacity_ref)
-    for base, pair, out_ref in zip(bases, copies, out_refs):
+    shared = turns // len(out_refs)
+    blocks = height // BLOCK
+    for turn, (base, pair) in enumerate(zip(bases, copies)):
+        out_ref, at = out_refs[turn // shared], turn % shared * blocks
         for copy in pair:
             copy.wait()
 
-        @pl.loop(0, height // BLOCK)
+        @pl.loop(0, blocks)
         def _(i):
             rows = pl.ds(pl.multiple_of(base + i * BLOCK, BLOCK), BLOCK)
             for t in range(tiles):
@@ -69,18 +73,19 @@
                 for k in range(slices):
                     clear = 1.0 - alpha_of(vol[k, rows, cols], idx[k, rows, cols], table)
                     transmit = clear if transmit is None else transmit * clear
-                out_ref[i, :, cols] = (1.0 - transmit).astype(jnp.bfloat16)
+                out_ref[at + i, :, cols] = (1.0 - transmit).astype(jnp.bfloat16)
 
 
 def opacities(volume, tf_index, tf_opacity, turns):
     slices, height, width = volume.shape
-    part = jax.ShapeDtypeStruct((height // BLOCK // turns, BLOCK, width), jnp.bfloat16)
+    parts = min(turns, 2)
+    part = jax.ShapeDtypeStruct((height // BLOCK // parts, BLOCK, width), jnp.bfloat16)
     held = [jax.ShapeDtypeStruct(x.shape, x.dtype) for x in (volume, tf_index)]
     return pl.pallas_call(
         functools.partial(opacity_kernel, slices, width // LANES, turns),
-        out_shape=[part] * turns + held,
+        out_shape=[part] * parts + held,
         in_specs=[pl.BlockSpec(memory_space=pltpu.HBM)] * 2 + [pl.BlockSpec(memory_space=pltpu.SMEM)],
-        out_specs=[pl.BlockSpec(memory_space=pltpu.VMEM)] * (turns + 2),
+        out_specs=[pl.BlockSpec(memory_space=pltpu.VMEM)] * (parts + 2),
         scratch_shapes=[pltpu.SemaphoreType.DMA((2, turns))],
         compiler_params=pltpu.CompilerParams(vmem_limit_bytes=FETCH_LIMIT),
         cost_estimate=pl.CostEstimate(
@@ -91,7 +96,20 @@
 
 
 def colour_kernel(slices, span, turns, by_member, vol, idx, before_ref, after_ref, colour_ref, opacity_ref, *rest):
-    out_refs = rest[-turns:]
+    out_refs, skipped = rest[-turns:], 0
+    if by_member:
+        out_refs, (volume_here, index_here, sems) = rest[-turns - 3 : -3], rest[-3:]
+        skipped = span[0] - 1
+        some = pl.ds(skipped * LANES, volume_here.shape[2])
+        copies = [
+            pltpu.make_async_copy(source.at[:, :, some], target, sems.at[n])
+            for n, (source, target) in enumerate([(vol, volume_here), (idx, index_here)])
+        ]
+        for copy in copies:
+            copy.start()
+        for copy in copies:
+            copy.wait()
+        vol, idx = volume_here, index_here
     height, width = before_ref.shape
     blocks, tiles = height // BLOCK, width // LANES
     each = blocks // turns
@@ -110,8 +128,9 @@
         above = pl.ds(pl.multiple_of(jnp.maximum(start - PAD, 0), PAD), PAD)
         below = pl.ds(pl.multiple_of(jnp.minimum(start + BLOCK, height - PAD), PAD), PAD)
         for t in range(*span):
-            cols = pl.ds(t * LANES, LANES)
-            halo = [ref[rows, cols].astype(jnp.float32) * (REACH / STEPS) for ref in (before_ref, after_ref)]
+            u = t - skipped
+            cols = pl.ds(u * LANES, LANES)
+            halo = [ref[rows, pl.ds(t * LANES, LANES)].astype(jnp.float32) * (REACH / STEPS) for ref in (before_ref, after_ref)]
             centres = [halo[0]] + [vol[k, rows, cols] for k in range(slices)] + [halo[1]]
             transmit, sums = None, None
             for k in range(slices):
@@ -128,8 +147,8 @@
                     ],
                     0,
                 )
-                beside_left = vol[k, rows, pl.ds((t - 1) * LANES, LANES)] if t > 0 else 0.0
-                beside_right = vol[k, rows, pl.ds((t + 1) * LANES, LANES)] if t + 1 < tiles else 0.0
+                beside_left = vol[k, rows, pl.ds((u - 1) * LANES, LANES)] if t > 0 else 0.0
+                beside_right = vol[k, rows, pl.ds((u + 1) * LANES, LANES)] if t + 1 < tiles else 0.0
                 left = pltpu.roll(jnp.where(last_lane, beside_left, centre), 1, 1)
                 right = pltpu.roll(jnp.where(first_lane, beside_right, centre), LANES - 1, 1)
                 along = right - left
@@ -166,15 +185,21 @@
 def colours(volume, tf_index, before, after, tf_color, tf_opacity, span, turns, earlier=()):
     slices, height, _ = volume.shape
     part = jax.ShapeDtypeStruct((height // BLOCK // turns, 3, BLOCK, (span[1] - span[0]) * LANES), jnp.bfloat16)
+    held = []
+    if earlier:
+        near = (slices, height, volume.shape[2] - (span[0] - 1) * LANES)
+        held = [pltpu.VMEM(near, volume.dtype), pltpu.VMEM(near, tf_index.dtype), pltpu.SemaphoreType.DMA((2,))]
     cells = slices * height * (span[1] - span[0]) * LANES
     return pl.pallas_call(
         functools.partial(colour_kernel, slices, span, turns, bool(earlier)),
         out_shape=[part] * turns,
-        in_specs=[pl.BlockSpec(memory_space=pltpu.VMEM)] * 4
+        in_specs=[pl.BlockSpec(memory_space=pltpu.HBM if earlier else pltpu.VMEM)] * 2
+        + [pl.BlockSpec(memory_space=pltpu.VMEM)] * 2
         + [pl.BlockSpec(memory_space=pltpu.SMEM)] * 2
         + [pl.BlockSpec(memory_space=pl.ANY)] * len(earlier),
         out_specs=[pl.BlockSpec(memory_space=pltpu.VMEM)] * turns,
-        compiler_params=pltpu.CompilerParams(vmem_limit_bytes=LIMIT),
+        scratch_shapes=held,
+        compiler_params=pltpu.CompilerParams(vmem_limit_bytes=REFETCH_LIMIT if earlier else LIMIT),
         cost_estimate=pl.CostEstimate(flops=50 * cells, bytes_accessed=40 * cells, transcendentals=2 * cells),
         name="colours",
     )(volume, tf_index, before, after, tf_color, tf_opacity, *earlier)
@@ -192,61 +217,83 @@
     )(*operands, *earlier)
 
 
-def hold_kernel(count, *refs):
-    for ref, out_ref in zip(refs[:count], refs[-count:]):
-        out_ref[...] = ref[...]
-
-
-def hold(parts, earlier):
-    shapes = [jax.ShapeDtypeStruct(part.shape, part.dtype) for part in parts]
-    return list(on_chip(functools.partial(hold_kernel, len(parts)), shapes, parts, earlier))
-
-
-def turn_over_kernel(turns, *refs):
-    here = lax.rem(lax.axis_index("gz"), turns)
-    colour_refs, opacity_refs, second_refs, member_refs, plane_refs = (
-        refs[turns * n : turns * (n + 1)] for n in range(5)
-    )
-    width, total = colour_refs[0].shape[-1], opacity_refs[0].shape[-1]
-    for s, (colour_ref, opacity_ref, plane_ref) in enumerate(zip(colour_refs, opacity_refs, plane_refs)):
-        for m, (second_ref, member_ref) in enumerate(zip(second_refs, member_refs)):
-            plane_ref[m] = second_ref[s]
-            for c in range(3):
-                member_ref[s, :, pl.ds(c * width, width)] = colour_ref[here ^ m, c]
-            member_ref[s, :, pl.ds(3 * width, total)] = opacity_ref[here ^ m]
-
-
-def turn_over(first, opacity, second):
-    turns, (_, _, height, width) = len(first), first[0].shape
-    member = jax.ShapeDtypeStruct((turns, height, 3 * width + opacity[0].shape[-1]), jnp.bfloat16)
-    plane = jax.ShapeDtypeStruct(second[0].shape, jnp.bfloat16)
-    operands = [*first, *opacity, *second]
-    done = on_chip(functools.partial(turn_over_kernel, turns), [member] * turns + [plane] * turns, operands)
-    return done[:turns], done[turns:]
-
-
-def in_plane(parts, devices):
+def to_planes_kernel(turns, *refs):
+    for m, ref in enumerate(refs[:turns]):
+        for s, out_ref in enumerate(refs[turns:]):
+            out_ref[m] = ref[s]
+
+
+def to_planes(parts):
+    turns = len(parts)
+    shapes = [jax.ShapeDtypeStruct(parts[0].shape, parts[0].dtype)] * turns
+    return on_chip(functools.partial(to_planes_kernel, turns), shapes, parts)
+
+
+def to_others(parts, devices):
     return [parts[0]] + [
         lax.ppermute(part, "gz", [(i, i ^ m) for i in range(devices)]) for m, part in enumerate(parts[1:], 1)
     ]
 
 
-def blend_kernel(ranks, turns, side, order_ref, *rest):
-    first_refs, second_refs = rest[:turns], rest[turns:-6]
+def to_members_kernel(turns, *refs):
+    here = lax.rem(lax.axis_index("gz"), turns)
+    for t in range(turns):
+        for m in range(turns):
+            refs[m // 2 - 2][m % 2 * turns + t] = swapped_in(refs[:3], turns, t, here ^ m)
+
+
+def to_members(arrived, turns, earlier=()):
+    part = jax.ShapeDtypeStruct(arrived[0].shape, jnp.bfloat16)
+    return on_chip(functools.partial(to_members_kernel, turns), [part] * 2, arrived, earlier)
+
+
+def hold_kernel(ref, *rest):
+    rest[-1][...] = ref[...]
+
+
+def hold(part, earlier):
+    shape = jax.ShapeDtypeStruct(part.shape, part.dtype)
+    return on_chip(functools.partial(hold_kernel), [shape], [part], earlier)[0]
+
+
+def to_near_kernel(turns, near_ref, far_ref, *rest):
+    rest[-1][pl.ds(0, turns)] = near_ref[pl.ds(turns, turns)]
+    rest[-1][pl.ds(turns, turns)] = far_ref[pl.ds(turns, turns)]
+
+
+def swap(part, devices, stride):
+    return lax.ppermute(part, "gz", [(i, i ^ stride) for i in range(devices)])
+
+
+def swap_near(near, far, devices, stride, earlier=()):
+    shape = jax.ShapeDtypeStruct(near.shape, near.dtype)
+    kernel = functools.partial(to_near_kernel, near.shape[0] // 2)
+    (passed,) = on_chip(kernel, [shape], [near, far], earlier)
+    return [near, far, swap(passed, devices, stride)]
+
+
+def swapped_in(refs, turns, m, entry):
+    near_ref, far_ref, passed_ref = refs
+    return [near_ref, passed_ref, far_ref, passed_ref][m][entry if m < 3 else turns + entry]
+
+
+def blend_kernel(ranks, turns, start, order_ref, *rest):
+    opacity_refs, colour_refs = rest[:3], rest[3:-6]
     out_hbm, place, colour_ref, opacity_ref, out_ref, sem = rest[-6:]
     device = lax.axis_index("gz")
     plane, member = device // turns, lax.rem(device, turns)
-    width, total = out_ref.shape[2], out_hbm.shape[2]
-    start = total - width if side else 0
-    before = first_refs[0].shape[2] - total
+    width = out_ref.shape[2]
     for b in range(ranks):
         place[order_ref[b]] = b
     for m in range(turns):
         for s in range(turns):
             brick = lax.rem(plane + turns - s, turns) * turns + (member ^ m)
-            for c in range(3):
-                colour_ref[brick, c] = second_refs[s][m, c] if side else first_refs[m][s, :, pl.ds(c * width, width)]
-            opacity_ref[brick] = first_refs[m][s, :, pl.ds(before + start, width)]
+            at = (plane ^ s) * turns + (member ^ m)
+            opacity_ref[at] = swapped_in(opacity_refs, turns, m, s)[:, start : start + width]
+            if start > 0:
+                colour_ref[brick] = colour_refs[s][m]
+    if start == 0:
+        colour_ref = colour_refs[0]
     for j in range(width // LANES):
         cols = pl.ds(j * LANES, LANES)
         canvas = (jnp.zeros((out_ref.shape[1], LANES), jnp.float32),) * 4
@@ -262,12 +309,12 @@
     copy.wait()
 
 
-def blend(order, turns, total, first, second=(), image=()):
-    ranks, height = order.shape[0], first[0].shape[1]
-    width = second[0].shape[-1] if second else (first[0].shape[2] - total) // 3
-    operands = [order, *first, *second]
+def blend(order, turns, total, start, opacity, colour, image=()):
+    ranks = order.shape[0]
+    height, width = colour[0].shape[-2:]
+    operands = [order, *opacity, *colour]
     return pl.pallas_call(
-        functools.partial(blend_kernel, ranks, turns, 1 if second else 0),
+        functools.partial(blend_kernel, ranks, turns, start),
         out_shape=jax.ShapeDtypeStruct((4, height, total), jnp.float32),
         in_specs=[pl.BlockSpec(memory_space=pltpu.SMEM)]
         + [pl.BlockSpec(memory_space=pltpu.VMEM)] * (len(operands) - 1)
@@ -333,20 +380,25 @@
     before = lax.ppermute(last, "gz", up)
     after = lax.ppermute(initial, "gz", down)
     turns = PLANES if devices == PLANES * PLANES and height // devices == BLOCK else 1
+    whole, tiles = (volume, tf_index), width // LANES
     *opacity, volume, tf_index = opacities(volume, tf_index, tf_opacity, turns)
-    tiles = width // LANES
-    held = (volume, tf_index, before, after, tf_color, tf_opacity)
+    others = (before, after, tf_color, tf_opacity)
+    held = (volume, tf_index, *others)
     if turns == 1:
         colour = by_owner(colours(*held, (0, tiles), 1)[0], devices)
         return blend_plain(order, exchange(colour), exchange(by_owner(opacity[0], devices)))
     split = tiles * FIRST // 8
-    opacity = across_planes(opacity, turns, devices)
-    own, *others = colours(*held, (0, split), turns)
-    second = in_plane(colours(*held, (split, tiles), turns, (own,)), devices)
-    first = across_planes([own] + hold(others, opacity[1:]), turns, devices)
-    first, second = turn_over(first, opacity, second)
-    first, second = in_plane(first, devices), across_planes(second, turns, devices)
-    return blend(order, turns, width, first, second, (blend(order, turns, width, first),))
+    near, far = opacity
+    far = swap(far, devices, 2 * turns)
+    (first,) = colours(*held, (0, split), 1)
+    second = colours(*whole, *others, (split, tiles), turns, (first,))
+    opacity = swap_near(near, far, devices, turns, (first,))
+    first = exchange(hold(first, (far,)))
+    near, far = to_members(opacity, turns, second[:1])
+    opacity = swap_near(near, swap(far, devices, 2), devices, 1)
+    second = across_planes(to_planes(to_others(second, devices)), turns, devices)
+    image = blend(order, turns, width, 0, opacity, [first])
+    return blend(order, turns, width, split * LANES, opacity, second, (image,))
 
 
 def solution(mesh):

time: 73.8 us -> 89.5 us (1.21)
  waiting for transfers between devices: 30 us -> 43.2 us
  Pallas kernels: 16.3 us -> 19.3 us
    ppermute x6 -> x7, waiting for transfers between devices: 11.8 us -> 28.4 us  [the longest x4 23.9 us: swap(): return lax.ppermute(part, 'gz', [(i, i ^ stride) for i in range(devices)])]
    all_to_all x0 -> x1, starting transfers between devices: none -> 6.18 us  [exchange(): return lax.all_to_all(x, 'gz', split_axis=0, concat_axis=0, tiled=True)]
    ppermute x9 -> x3, starting transfers between devices: 9.32 us -> 3.26 us  [across_planes(): lax.ppermute(part, 'gz', [(i, (i + s * turns) % devices) for i in range(d...]
    ppermute x9 -> x3, waiting for transfers between devices: 15.5 us -> 11.5 us  [across_planes(): lax.ppermute(part, 'gz', [(i, (i + s * turns) % devices) for i in range(d...]
    pallas_call x2, Pallas kernels: 8.59 us -> 10.7 us  [colours(): pl.pallas_call(functools.partial(colour_kernel, slices, span, turns, bool...]
    pallas_call x2 -> x5, Pallas kernels: 0.18 us -> 1.16 us  [on_chip(): pl.pallas_call(kernel, out_shape=out_shapes, in_specs=[pl.BlockSpec(memor...]
    ppermute x6 -> x7, starting transfers between devices: 9.56 us -> 8.95 us  [the longest x4 6.16 us: swap(): return lax.ppermute(part, 'gz', [(i, i ^ stride) for i in range(devices)])]
  transfers between devices with their start and end apart: 17 -> 13, of which waited for: 9 -> 9; matrix products, arithmetic and copies ran while one was open for 0% -> 0% of each run, Pallas kernels for 20% -> 19%
where the time goes in v10:
time: 89.5 us; the launch traced here: 89.2 us
  waiting for transfers between devices  43.2 us (48%)
  starting transfers between devices  24 us (27%)
  Pallas kernels  19.3 us (22%)
  other arithmetic  1.9 us (2%)
    ppermute x4, waiting for transfers between devices, swap(): return lax.ppermute(part, 'gz', [(i, i ^ stride) for i in range(devices)])  23.9 us
    ppermute x3, waiting for transfers between devices, across_planes(): lax.ppermute(part, 'gz', [(i, (i + s * turns) % devices) for i in range(d...  11.5 us
    pallas_call x2, Pallas kernels, colours(): pl.pallas_call(functools.partial(colour_kernel, slices, span, turns, bool...  10.7 us
    all_to_all x1, starting transfers between devices, exchange(): return lax.all_to_all(x, 'gz', split_axis=0, concat_axis=0, tiled=True)  6.18 us
    ppermute x4, starting transfers between devices, swap(): return lax.ppermute(part, 'gz', [(i, i ^ stride) for i in range(devices)])  6.16 us
    pallas_call x1, Pallas kernels, opacities(): pl.pallas_call(functools.partial(opacity_kernel, slices, width // LANES,...  4.52 us
    ppermute x3, waiting for transfers between devices, to_others(): lax.ppermute(part, 'gz', [(i, i ^ m) for i in range(devices)])  4.49 us
    ppermute x1, waiting for transfers between devices, shards(): after = lax.ppermute(initial, 'gz', down)  3.27 us
  transfers between devices with their start and end apart: 13, of which 9 were waited for; matrix products, arithmetic and copies ran while one was open for 0% of the time, Pallas kernels for 19%

profile of v10, /device:TPU:13, one launch (start us, length us, event | category | flops | bytes accessed | tf_op | source)
XLA Modules:
  0.0 89.2 jit_solution(16689218507591398210)
XLA Ops:
  0.0 1.9 %fusion.1 = (s16[256,1024]{1,0:T(8,128)(2,1)S(1)}, s16[256,1024]{1,0:T(8,128)(2,1)S(1)}) fusion(f32[4,256,1024]{2,1,0:T(8,128)} %vol.1), kind=kLoop, calls=%fused_computation.3 | loop fusion | flops 1572864 | bytes 3145728 | tf_op jit(solution)/shard_map/convert_element_type | solution.py:364
  1.9 2.6 %collective-permute-start.2 = (s16[256,1024]{1,0:T(8,128)(2,1)S(1)}, s16[256,1024]{1,0:T(8,128)(2,1)S(1)}, u32[]{:S(2)}, u32[]{:S(2)}) collective-permute-start(s16[256,1024]{1,0:T(8,128)(2,1)S(1)} %get-tuple-element.33), channel_id=1, source_target_pairs={{1,0},{2,1},{3,2},{4,3},{5,4},{6,5},{7,6},{8,7},{9,8},{10,9},{11,1... | collective-permute-start | bytes 1572872 | tf_op jit(solution)/shard_map/ppermute | solution.py:381
  4.5 0.0 copy-start
  4.5 3.0 %collective-permute-start.1 = (s16[256,1024]{1,0:T(8,128)(2,1)S(1)}, s16[256,1024]{1,0:T(8,128)(2,1)S(1)}, u32[]{:S(2)}, u32[]{:S(2)}) collective-permute-start(s16[256,1024]{1,0:T(8,128)(2,1)S(1)} %get-tuple-element.34), channel_id=1, source_target_pairs={{0,1},{1,2},{2,3},{3,4},{4,5},{5,6},{6,7},{7,8},{8,9},{9,10},{10,1... | collective-permute-start | bytes 1572872 | tf_op jit(solution)/shard_map/ppermute | solution.py:380
  7.5 0.6 copy-done.1
  8.2 4.5 %opacities.1 = (bf16[8,16,1024]{2,1,0:T(8,128)(2,1)S(1)}, bf16[8,16,1024]{2,1,0:T(8,128)(2,1)S(1)}, f32[4,256,1024]{2,1,0:T(8,128)S(1)}, s32[4,256,1024]{2,1,0:T(8,128)S(1)}) custom-call(f32[4,256,1024]{2,1,0:T(8,128)} %vol.1, s32[4,256,1024]{2,1,0:T(8,128)} %idx.1, f32[8]{0:T(128)S(1)} %copy-done.1), custom_call_target="tpu_custom_call" | custom-call | flops 15728640 | bytes 9437184 | tf_op jit(solution)/shard_map/opacities/pallas_call | solution.py:84
  12.7 2.4 %collective-permute-start = (bf16[8,16,1024]{2,1,0:T(8,128)(2,1)S(1)}, bf16[8,16,1024]{2,1,0:T(8,128)(2,1)S(1)}, u32[]{:S(2)}, u32[]{:S(2)}) collective-permute-start(bf16[8,16,1024]{2,1,0:T(8,128)(2,1)S(1)} %get-tuple-element.20), channel_id=1, source_target_pairs={{0,8},{1,9},{2,10},{3,11},{4,12},{5,13},{6,14},{7,15},{8,0},{9,1},... | collective-permute-start | bytes 786440 | tf_op jit(solution)/shard_map/ppermute | solution.py:265
  15.1 3.3 %collective-permute-done.2.after_ref = s16[256,1024]{1,0:T(8,128)(2,1)S(1)} collective-permute-done((s16[256,1024]{1,0:T(8,128)(2,1)S(1)}, s16[256,1024]{1,0:T(8,128)(2,1)S(1)}, u32[]{:S(2)}, u32[]{:S(2)}) %collective-permute-start.2) | collective-permute-done | bytes 524320 | tf_op jit(solution)/shard_map/ppermute | solution.py:381
  18.4 5.1 %colours.2.rest_0_.ref = bf16[16,3,16,640]{3,2,1,0:T(8,128)(2,1)S(1)} custom-call(f32[4,256,1024]{2,1,0:T(8,128)S(1)} %get-tuple-element.21.vol, s32[4,256,1024]{2,1,0:T(8,128)S(1)} %get-tuple-element.22.idx, s16[256,1024]{1,0:T(8,128)(2,1)S(1)} %collective-permute-done.1.before_ref, s16[256,1024]{1,0:T(8,128)(2,1)S(1)} %collective-permute-done.2.after_ref, ...), custom_call_target="tpu_custom_call" | custom-call | flops 32768000 | bytes 26214400 | tf_op jit(solution)/shard_map/colours/pallas_call | solution.py:193
  23.4 3.3 %collective-permute-done.far_ref.refs_1_.rest_0_ = bf16[8,16,1024]{2,1,0:T(8,128)(2,1)S(1)} collective-permute-done((bf16[8,16,1024]{2,1,0:T(8,128)(2,1)S(1)}, bf16[8,16,1024]{2,1,0:T(8,128)(2,1)S(1)}, u32[]{:S(2)}, u32[]{:S(2)}) %collective-permute-start) | collective-permute-done | bytes 262176 | tf_op jit(solution)/shard_map/ppermute | solution.py:265
  26.7 1.0 %hold.1 = bf16[16,3,16,640]{3,2,1,0:T(8,128)(2,1)} custom-call(bf16[16,3,16,640]{3,2,1,0:T(8,128)(2,1)S(1)} %colours.2.rest_0_.ref, bf16[8,16,1024]{2,1,0:T(8,128)(2,1)S(1)} %collective-permute-done.far_ref.refs_1_.rest_0_), custom_call_target="tpu_custom_call" | custom-call | tf_op jit(solution)/shard_map/hold/pallas_call | solution.py:209
  27.7 6.2 %all-to-all-start = ((bf16[16,3,16,640]{3,2,1,0:T(8,128)(2,1)}), bf16[16,3,16,640]{3,2,1,0:T(8,128)(2,1)S(1)}, u32[]{:S(2)}, u32[]{:S(2)}) async-start(bf16[16,3,16,640]{3,2,1,0:T(8,128)(2,1)} %hold.1), calls=%async_computation | async-start | bytes 1966080 | tf_op jit(solution)/shard_map/all_to_all | solution.py:360
  34.0 0.2 collective-permute-start.3
  34.1 5.6 %colours.3 = (bf16[4,3,16,384]{3,2,1,0:T(8,128)(2,1)S(1)}, bf16[4,3,16,384]{3,2,1,0:T(8,128)(2,1)S(1)}, bf16[4,3,16,384]{3,2,1,0:T(8,128)(2,1)S(1)}, bf16[4,3,16,384]{3,2,1,0:T(8,128)(2,1)S(1)}) custom-call(f32[4,256,1024]{2,1,0:T(8,128)} %vol.1, s32[4,256,1024]{2,1,0:T(8,128)} %idx.1, s16[256,1024]{1,0:T(8,128)(2,1)S(1)} %collective-permute-done.1.before_ref, ...), custom_call_target="tpu_custom_call" | custom-call | flops 19660800 | bytes 15728640 | tf_op jit(solution)/shard_map/colours/pallas_call | solution.py:193
  39.8 17.1 %collective-permute-done.3.refs_2_ = bf16[8,16,1024]{2,1,0:T(8,128)(2,1)S(1)} collective-permute-done((bf16[8,16,1024]{2,1,0:T(8,128)(2,1)S(1)}, bf16[8,16,1024]{2,1,0:T(8,128)(2,1)S(1)}, u32[]{:S(2)}, u32[]{:S(2)}) %collective-permute-start.3) | collective-permute-done | bytes 262176 | tf_op jit(solution)/shard_map/ppermute | solution.py:265
  56.9 1.1 %collective-permute-start.4 = (bf16[8,16,1024]{2,1,0:T(8,128)(2,1)S(1)}, bf16[8,16,1024]{2,1,0:T(8,128)(2,1)S(1)}, u32[]{:S(2)}, u32[]{:S(2)}) collective-permute-start(bf16[8,16,1024]{2,1,0:T(8,128)(2,1)S(1)} %get-tuple-element.25), channel_id=1, source_target_pairs={{0,2},{1,3},{2,0},{3,1},{4,6},{5,7},{6,4},{7,5},{8,10},{9,11},{10,... | collective-permute-start | bytes 786440 | tf_op jit(solution)/shard_map/ppermute | solution.py:265
  58.0 1.2 %collective-permute-start.6 = (bf16[4,3,16,384]{3,2,1,0:T(8,128)(2,1)S(1)}, bf16[4,3,16,384]{3,2,1,0:T(8,128)(2,1)S(1)}, u32[]{:S(2)}, u32[]{:S(2)}) collective-permute-start(bf16[4,3,16,384]{3,2,1,0:T(8,128)(2,1)S(1)} %get-tuple-element.26), channel_id=1, source_target_pairs={{0,1},{1,0},{2,3},{3,2},{4,5},{5,4},{6,7},{7,6},{8,9},{9,8},{10,11... | collective-permute-start | bytes 442376 | tf_op jit(solution)/shard_map/ppermute | solution.py:234
  59.1 0.2 collective-permute-start.7
  59.3 1.4 %collective-permute-start.8 = (bf16[4,3,16,384]{3,2,1,0:T(8,128)(2,1)S(1)}, bf16[4,3,16,384]{3,2,1,0:T(8,128)(2,1)S(1)}, u32[]{:S(2)}, u32[]{:S(2)}) collective-permute-start(bf16[4,3,16,384]{3,2,1,0:T(8,128)(2,1)S(1)} %get-tuple-element.28), channel_id=1, source_target_pairs={{0,3},{1,2},{2,1},{3,0},{4,7},{5,6},{6,5},{7,4},{8,11},{9,10},{10,... | collective-permute-start | bytes 442376 | tf_op jit(solution)/shard_map/ppermute | solution.py:234
  60.8 3.5 %collective-permute-done.4.far_ref.rest_1_ = bf16[8,16,1024]{2,1,0:T(8,128)(2,1)S(1)} collective-permute-done((bf16[8,16,1024]{2,1,0:T(8,128)(2,1)S(1)}, bf16[8,16,1024]{2,1,0:T(8,128)(2,1)S(1)}, u32[]{:S(2)}, u32[]{:S(2)}) %collective-permute-start.4) | collective-permute-done | bytes 262176 | tf_op jit(solution)/shard_map/ppermute | solution.py:265
  64.3 2.6 %collective-permute-start.5 = (bf16[8,16,1024]{2,1,0:T(8,128)(2,1)S(1)}, bf16[8,16,1024]{2,1,0:T(8,128)(2,1)S(1)}, u32[]{:S(2)}, u32[]{:S(2)}) collective-permute-start(bf16[8,16,1024]{2,1,0:T(8,128)(2,1)S(1)} %to_near.3), channel_id=1, source_target_pairs={{0,1},{1,0},{2,3},{3,2},{4,5},{5,4},{6,7},{7,6},{8,9},{9,8},{10,11... | collective-permute-start | bytes 786440 | tf_op jit(solution)/shard_map/ppermute | solution.py:265
  66.8 0.6 collective-permute-done.7.refs_2_
  67.4 3.9 %collective-permute-done.8.refs_3_ = bf16[4,3,16,384]{3,2,1,0:T(8,128)(2,1)S(1)} collective-permute-done((bf16[4,3,16,384]{3,2,1,0:T(8,128)(2,1)S(1)}, bf16[4,3,16,384]{3,2,1,0:T(8,128)(2,1)S(1)}, u32[]{:S(2)}, u32[]{:S(2)}) %collective-permute-start.8) | collective-permute-done | bytes 147488 | tf_op jit(solution)/shard_map/ppermute | solution.py:234
  71.3 0.1 to_planes.1
  71.4 2.0 %collective-permute-start.9 = (bf16[4,3,16,384]{3,2,1,0:T(8,128)(2,1)S(1)}, bf16[4,3,16,384]{3,2,1,0:T(8,128)(2,1)S(1)}, u32[]{:S(2)}, u32[]{:S(2)}) collective-permute-start(bf16[4,3,16,384]{3,2,1,0:T(8,128)(2,1)S(1)} %get-tuple-element.30), channel_id=1, source_target_pairs={{0,4},{1,5},{2,6},{3,7},{4,8},{5,9},{6,10},{7,11},{8,12},{9,13},{1... | collective-permute-start | bytes 442376 | tf_op jit(solution)/shard_map/ppermute | solution.py:369
  73.4 1.0 %collective-permute-start.10 = (bf16[4,3,16,384]{3,2,1,0:T(8,128)(2,1)S(1)}, bf16[4,3,16,384]{3,2,1,0:T(8,128)(2,1)S(1)}, u32[]{:S(2)}, u32[]{:S(2)}) collective-permute-start(bf16[4,3,16,384]{3,2,1,0:T(8,128)(2,1)S(1)} %get-tuple-element.31), channel_id=1, source_target_pairs={{0,8},{1,9},{2,10},{3,11},{4,12},{5,13},{6,14},{7,15},{8,0},{9,1},... | collective-permute-start | bytes 442376 | tf_op jit(solution)/shard_map/ppermute | solution.py:369
  74.4 0.2 collective-permute-start.11
  74.7 1.5 %blend.2.rest_7_ = f32[4,16,1024]{2,1,0:T(8,128)} custom-call(s32[16]{0:T(128)S(1)} %copy-done.3, bf16[8,16,1024]{2,1,0:T(8,128)(2,1)S(1)} %get-tuple-element.24.near_ref.rest_0_, bf16[8,16,1024]{2,1,0:T(8,128)(2,1)S(1)} %collective-permute-done.4.far_ref.rest_1_, bf16[8,16,1024]{2,1,0:T(8,128)(2,1)S(1)} %collective-permute-done.5.rest_2_, ...), custom_call_target="tpu_custom_call" | custom-call | tf_op jit(solution)/shard_map/blend/pallas_call | solution.py:316
  76.2 6.9 %collective-permute-done.9.rest_4_ = bf16[4,3,16,384]{3,2,1,0:T(8,128)(2,1)S(1)} collective-permute-done((bf16[4,3,16,384]{3,2,1,0:T(8,128)(2,1)S(1)}, bf16[4,3,16,384]{3,2,1,0:T(8,128)(2,1)S(1)}, u32[]{:S(2)}, u32[]{:S(2)}) %collective-permute-start.9) | collective-permute-done | bytes 147488 | tf_op jit(solution)/shard_map/ppermute | solution.py:369
  83.1 3.3 %collective-permute-done.10.rest_5_ = bf16[4,3,16,384]{3,2,1,0:T(8,128)(2,1)S(1)} collective-permute-done((bf16[4,3,16,384]{3,2,1,0:T(8,128)(2,1)S(1)}, bf16[4,3,16,384]{3,2,1,0:T(8,128)(2,1)S(1)}, u32[]{:S(2)}, u32[]{:S(2)}) %collective-permute-start.10) | collective-permute-done | bytes 147488 | tf_op jit(solution)/shard_map/ppermute | solution.py:369
  86.4 1.3 %collective-permute-done.11.rest_6_ = bf16[4,3,16,384]{3,2,1,0:T(8,128)(2,1)S(1)} collective-permute-done((bf16[4,3,16,384]{3,2,1,0:T(8,128)(2,1)S(1)}, bf16[4,3,16,384]{3,2,1,0:T(8,128)(2,1)S(1)}, u32[]{:S(2)}, u32[]{:S(2)}) %collective-permute-start.11) | collective-permute-done | bytes 147488 | tf_op jit(solution)/shard_map/ppermute | solution.py:369
  87.7 1.5 %blend.3 = f32[4,16,1024]{2,1,0:T(8,128)} custom-call(s32[16]{0:T(128)S(1)} %copy-done.3, bf16[8,16,1024]{2,1,0:T(8,128)(2,1)S(1)} %get-tuple-element.24.near_ref.rest_0_, bf16[8,16,1024]{2,1,0:T(8,128)(2,1)S(1)} %collective-permute-done.4.far_ref.rest_1_, bf16[8,16,1024]{2,1,0:T(8,128)(2,1)S(1)} %collective-permute-done.5.rest_2_, ...), custom_call_target="tpu_custom_call", output_to_operand_aliasing={{}: (8, {})} | custom-call | tf_op jit(solution)/shard_map/blend/pallas_call | solution.py:316
  (13 shorter events, 0.1 us)
Async XLA Ops:
  1.9 16.5 %collective-permute-start.2 = (s16[256,1024]{1,0:T(8,128)(2,1)S(1)}, s16[256,1024]{1,0:T(8,128)(2,1)S(1)}, u32[]{:S(2)}, u32[]{:S(2)}) collective-permute-start(s16[256,1024]{1,0:T(8,128)(2,1)S(1)} %get-tuple-element.33), channel_id=1, source_target_pairs={{1,0},{2,1},{3,2},{4,3},{5,4},{6,5},{7,6},{8,7},{9,8},{10,9},{11,1... | collective-permute-start | bytes 1572872 | tf_op jit(solution)/shard_map/ppermute | solution.py:381
  4.5 13.9 %copy-start = (f32[3,8]{1,0:T(4,128)S(1)}, f32[3,8]{1,0:T(4,128)}, u32[]{:S(2)}) copy-start(f32[3,8]{1,0:T(4,128)} %colour_ref.3) | copy-start | bytes 292
  4.5 13.8 %collective-permute-start.1 = (s16[256,1024]{1,0:T(8,128)(2,1)S(1)}, s16[256,1024]{1,0:T(8,128)(2,1)S(1)}, u32[]{:S(2)}, u32[]{:S(2)}) collective-permute-start(s16[256,1024]{1,0:T(8,128)(2,1)S(1)} %get-tuple-element.34), channel_id=1, source_target_pairs={{0,1},{1,2},{2,3},{3,4},{4,5},{5,6},{6,7},{7,8},{8,9},{9,10},{10,1... | collective-permute-start | bytes 1572872 | tf_op jit(solution)/shard_map/ppermute | solution.py:380
  7.5 0.7 copy-start.1
  12.7 14.0 %collective-permute-start = (bf16[8,16,1024]{2,1,0:T(8,128)(2,1)S(1)}, bf16[8,16,1024]{2,1,0:T(8,128)(2,1)S(1)}, u32[]{:S(2)}, u32[]{:S(2)}) collective-permute-start(bf16[8,16,1024]{2,1,0:T(8,128)(2,1)S(1)} %get-tuple-element.20), channel_id=1, source_target_pairs={{0,8},{1,9},{2,10},{3,11},{4,12},{5,13},{6,14},{7,15},{8,0},{9,1},... | collective-permute-start | bytes 786440 | tf_op jit(solution)/shard_map/ppermute | solution.py:265
  23.4 10.7 %copy-start.2 = (f32[8]{0:T(128)S(1)}, f32[8]{0:T(128)}, u32[]{:S(2)}) copy-start(f32[8]{0:T(128)} %opacity_ref.5) | copy-start | bytes 100
  27.7 46.9 %all-to-all-start = ((bf16[16,3,16,640]{3,2,1,0:T(8,128)(2,1)}), bf16[16,3,16,640]{3,2,1,0:T(8,128)(2,1)S(1)}, u32[]{:S(2)}, u32[]{:S(2)}) async-start(bf16[16,3,16,640]{3,2,1,0:T(8,128)(2,1)} %hold.1), calls=%async_computation | async-start | bytes 1966080 | tf_op jit(solution)/shard_map/all_to_all | solution.py:360
  33.9 40.7 %copy-start.3 = (s32[16]{0:T(128)S(1)}, s32[16]{0:T(128)}, u32[]{:S(2)}) copy-start(s32[16]{0:T(128)} %order_ref.3) | copy-start | bytes 196
  34.0 22.9 %collective-permute-start.3 = (bf16[8,16,1024]{2,1,0:T(8,128)(2,1)S(1)}, bf16[8,16,1024]{2,1,0:T(8,128)(2,1)S(1)}, u32[]{:S(2)}, u32[]{:S(2)}) collective-permute-start(bf16[8,16,1024]{2,1,0:T(8,128)(2,1)S(1)} %to_near.2), channel_id=1, source_target_pairs={{0,4},{1,5},{2,6},{3,7},{4,0},{5,1},{6,2},{7,3},{8,12},{9,13},{10,... | collective-permute-start | bytes 786440 | tf_op jit(solution)/shard_map/ppermute | solution.py:265
  56.9 7.3 %collective-permute-start.4 = (bf16[8,16,1024]{2,1,0:T(8,128)(2,1)S(1)}, bf16[8,16,1024]{2,1,0:T(8,128)(2,1)S(1)}, u32[]{:S(2)}, u32[]{:S(2)}) collective-permute-start(bf16[8,16,1024]{2,1,0:T(8,128)(2,1)S(1)} %get-tuple-element.25), channel_id=1, source_target_pairs={{0,2},{1,3},{2,0},{3,1},{4,6},{5,7},{6,4},{7,5},{8,10},{9,11},{10,... | collective-permute-start | bytes 786440 | tf_op jit(solution)/shard_map/ppermute | solution.py:265
  58.0 8.9 %collective-permute-start.6 = (bf16[4,3,16,384]{3,2,1,0:T(8,128)(2,1)S(1)}, bf16[4,3,16,384]{3,2,1,0:T(8,128)(2,1)S(1)}, u32[]{:S(2)}, u32[]{:S(2)}) collective-permute-start(bf16[4,3,16,384]{3,2,1,0:T(8,128)(2,1)S(1)} %get-tuple-element.26), channel_id=1, source_target_pairs={{0,1},{1,0},{2,3},{3,2},{4,5},{5,4},{6,7},{7,6},{8,9},{9,8},{10,11... | collective-permute-start | bytes 442376 | tf_op jit(solution)/shard_map/ppermute | solution.py:234
  59.1 8.3 %collective-permute-start.7 = (bf16[4,3,16,384]{3,2,1,0:T(8,128)(2,1)S(1)}, bf16[4,3,16,384]{3,2,1,0:T(8,128)(2,1)S(1)}, u32[]{:S(2)}, u32[]{:S(2)}) collective-permute-start(bf16[4,3,16,384]{3,2,1,0:T(8,128)(2,1)S(1)} %get-tuple-element.27), channel_id=1, source_target_pairs={{0,2},{1,3},{2,0},{3,1},{4,6},{5,7},{6,4},{7,5},{8,10},{9,11},{10,... | collective-permute-start | bytes 442376 | tf_op jit(solution)/shard_map/ppermute | solution.py:234
  59.3 12.0 %collective-permute-start.8 = (bf16[4,3,16,384]{3,2,1,0:T(8,128)(2,1)S(1)}, bf16[4,3,16,384]{3,2,1,0:T(8,128)(2,1)S(1)}, u32[]{:S(2)}, u32[]{:S(2)}) collective-permute-start(bf16[4,3,16,384]{3,2,1,0:T(8,128)(2,1)S(1)} %get-tuple-element.28), channel_id=1, source_target_pairs={{0,3},{1,2},{2,1},{3,0},{4,7},{5,6},{6,5},{7,4},{8,11},{9,10},{10,... | collective-permute-start | bytes 442376 | tf_op jit(solution)/shard_map/ppermute | solution.py:234
  64.3 10.4 %collective-permute-start.5 = (bf16[8,16,1024]{2,1,0:T(8,128)(2,1)S(1)}, bf16[8,16,1024]{2,1,0:T(8,128)(2,1)S(1)}, u32[]{:S(2)}, u32[]{:S(2)}) collective-permute-start(bf16[8,16,1024]{2,1,0:T(8,128)(2,1)S(1)} %to_near.3), channel_id=1, source_target_pairs={{0,1},{1,0},{2,3},{3,2},{4,5},{5,4},{6,7},{7,6},{8,9},{9,8},{10,11... | collective-permute-start | bytes 786440 | tf_op jit(solution)/shard_map/ppermute | solution.py:265
  71.4 11.7 %collective-permute-start.9 = (bf16[4,3,16,384]{3,2,1,0:T(8,128)(2,1)S(1)}, bf16[4,3,16,384]{3,2,1,0:T(8,128)(2,1)S(1)}, u32[]{:S(2)}, u32[]{:S(2)}) collective-permute-start(bf16[4,3,16,384]{3,2,1,0:T(8,128)(2,1)S(1)} %get-tuple-element.30), channel_id=1, source_target_pairs={{0,4},{1,5},{2,6},{3,7},{4,8},{5,9},{6,10},{7,11},{8,12},{9,13},{1... | collective-permute-start | bytes 442376 | tf_op jit(solution)/shard_map/ppermute | solution.py:369
  73.4 13.0 %collective-permute-start.10 = (bf16[4,3,16,384]{3,2,1,0:T(8,128)(2,1)S(1)}, bf16[4,3,16,384]{3,2,1,0:T(8,128)(2,1)S(1)}, u32[]{:S(2)}, u32[]{:S(2)}) collective-permute-start(bf16[4,3,16,384]{3,2,1,0:T(8,128)(2,1)S(1)} %get-tuple-element.31), channel_id=1, source_target_pairs={{0,8},{1,9},{2,10},{3,11},{4,12},{5,13},{6,14},{7,15},{8,0},{9,1},... | collective-permute-start | bytes 442376 | tf_op jit(solution)/shard_map/ppermute | solution.py:369
  74.4 13.3 %collective-permute-start.11 = (bf16[4,3,16,384]{3,2,1,0:T(8,128)(2,1)S(1)}, bf16[4,3,16,384]{3,2,1,0:T(8,128)(2,1)S(1)}, u32[]{:S(2)}, u32[]{:S(2)}) collective-permute-start(bf16[4,3,16,384]{3,2,1,0:T(8,128)(2,1)S(1)} %get-tuple-element.32), channel_id=1, source_target_pairs={{0,12},{1,13},{2,14},{3,15},{4,0},{5,1},{6,2},{7,3},{8,4},{9,5},{1... | collective-permute-start | bytes 442376 | tf_op jit(solution)/shard_map/ppermute | solution.py:369

commit v11 on v6

--- a/solution.py
+++ b/solution.py
@@ -14,8 +14,8 @@
 PAD = 8
 NT = 8
 LIMIT = 24 * 1024 * 1024
+FETCH_LIMIT = 43 * 1024 * 1024
 BLEND_LIMIT = 16 * 1024 * 1024
-UNROLL = 4
 PLANES = 4
 
 
@@ -39,12 +39,25 @@
     return lookup(table, index) * (1.0 - jnp.exp(-centre * centre))
 
 
-def opacity_kernel(slices, tiles, turns, vol, idx, opacity_ref, *out_refs):
-    table = spread(opacity_ref)
+def opacity_kernel(slices, tiles, turns, volume_hbm, index_hbm, opacity_ref, *rest):
+    out_refs, (vol, idx, sems) = rest[:turns], rest[turns:]
     height = vol.shape[1] // turns
     plane = lax.axis_index("gz") // (lax.axis_size("gz") // turns)
-    for turn, out_ref in enumerate(out_refs):
-        base = lax.rem(plane + turn, turns) * height
+    bases = [pl.multiple_of(lax.rem(plane + turn, turns) * height, height) for turn in range(turns)]
+    copies = []
+    for turn, base in enumerate(bases):
+        some = pl.ds(base, height)
+        pair = [
+            pltpu.make_async_copy(source.at[:, some, :], target.at[:, some, :], sems.at[kind, turn])
+            for kind, (source, target) in enumerate([(volume_hbm, vol), (index_hbm, idx)])
+        ]
+        for copy in pair:
+            copy.start()
+        copies.append(pair)
+    table = spread(opacity_ref)
+    for base, pair, out_ref in zip(bases, copies, out_refs):
+        for copy in pair:
+            copy.wait()
 
         @pl.loop(0, height // BLOCK)
         def _(i):
@@ -60,12 +73,15 @@
 
 def opacities(volume, tf_index, tf_opacity, turns):
     slices, height, width = volume.shape
+    part = jax.ShapeDtypeStruct((height // BLOCK // turns, BLOCK, width), jnp.bfloat16)
+    held = [jax.ShapeDtypeStruct(x.shape, x.dtype) for x in (volume, tf_index)]
     return pl.pallas_call(
         functools.partial(opacity_kernel, slices, width // LANES, turns),
-        out_shape=[jax.ShapeDtypeStruct((height // BLOCK // turns, BLOCK, width), jnp.bfloat16)] * turns,
-        in_specs=[pl.BlockSpec(memory_space=pltpu.VMEM)] * 2 + [pl.BlockSpec(memory_space=pltpu.SMEM)],
-        out_specs=[pl.BlockSpec(memory_space=pltpu.VMEM)] * turns,
-        compiler_params=pltpu.CompilerParams(vmem_limit_bytes=LIMIT),
+        out_shape=[part] * turns + held,
+        in_specs=[pl.BlockSpec(memory_space=pltpu.HBM)] * 2 + [pl.BlockSpec(memory_space=pltpu.SMEM)],
+        out_specs=[pl.BlockSpec(memory_space=pltpu.VMEM)] * (turns + 2),
+        scratch_shapes=[pltpu.SemaphoreType.DMA((2, turns))],
+        compiler_params=pltpu.CompilerParams(vmem_limit_bytes=FETCH_LIMIT),
         cost_estimate=pl.CostEstimate(
             flops=15 * volume.size, bytes_accessed=9 * volume.size, transcendentals=volume.size
         ),
@@ -74,7 +90,7 @@
 
 
 def colour_kernel(
-    slices, tiles, vol, idx, before_ref, after_ref, colour_ref, opacity_ref, out_hbm, out_ref, out_sems
+    slices, tiles, vol, idx, before_ref, after_ref, colour_ref, opacity_ref, out_ref
 ):
     height = before_ref.shape[0]
     blocks = height // BLOCK
@@ -84,7 +100,6 @@
     first_row, last_row = sublane == 0, sublane == PAD - 1
     opacity_table = spread(opacity_ref)
     colour_tables = [spread(colour_ref, c) for c in range(3)]
-    steps = blocks // UNROLL
 
     def shade(i):
         start = pl.multiple_of(i * BLOCK, BLOCK)
@@ -130,18 +145,9 @@
             for c in range(3):
                 out_ref[i, c, :, cols] = sums[c].astype(jnp.bfloat16)
 
-    def sent(step):
-        some = pl.ds(step * UNROLL, UNROLL)
-        return pltpu.make_async_copy(out_ref.at[some], out_hbm.at[some], out_sems.at[step])
-
-    for step in range(steps):
-        @pl.loop(step * UNROLL, (step + 1) * UNROLL)
-        def _(i):
-            shade(i)
-
-        sent(step).start()
-    for step in range(steps):
-        sent(step).wait()
+    @pl.loop(0, blocks)
+    def _(i):
+        shade(i)
 
 
 def colours(volume, tf_index, before, after, tf_color, tf_opacity):
@@ -152,8 +158,7 @@
         functools.partial(colour_kernel, slices, width // LANES),
         out_shape=jax.ShapeDtypeStruct(shape, jnp.bfloat16),
         in_specs=[pl.BlockSpec(memory_space=pltpu.VMEM)] * 4 + [pl.BlockSpec(memory_space=pltpu.SMEM)] * 2,
-        out_specs=pl.BlockSpec(memory_space=pltpu.HBM),
-        scratch_shapes=[pltpu.VMEM(shape, jnp.bfloat16), pltpu.SemaphoreType.DMA((blocks // UNROLL,))],
+        out_specs=pl.BlockSpec(memory_space=pltpu.VMEM),
         compiler_params=pltpu.CompilerParams(vmem_limit_bytes=LIMIT),
         cost_estimate=pl.CostEstimate(
             flops=50 * volume.size, bytes_accessed=40 * volume.size, transcendentals=2 * volume.size
@@ -257,7 +262,7 @@
     before = lax.ppermute(last, "gz", up)
     after = lax.ppermute(initial, "gz", down)
     turns = PLANES if devices == PLANES * PLANES and height // devices == BLOCK else 1
-    own, *others = opacities(volume, tf_index, tf_opacity, turns)
+    own, *others, volume, tf_index = opacities(volume, tf_index, tf_opacity, turns)
     colour = by_owner(colours(volume, tf_index, before, after, tf_color, tf_opacity), devices)
     if turns == 1:
         return blend_plain(order, exchange(colour), exchange(by_owner(own, devices)))

time: 72.9 us -> 71.4 us (0.979)
  local copies, waits for them, and re-layouts: 5.03 us -> 0.66 us
  Pallas kernels: 12.6 us -> 14.9 us
  starting transfers between devices: 16.4 us -> 17.4 us
    unnamed x10 -> x6, local copies, waits for them, and re-layouts: 5.03 us -> 0.66 us
    ppermute x3, waiting for transfers between devices: 2.61 us -> 0.46 us  [shards(): lax.ppermute(part, 'gz', [(i, (i + s * turns) % devices) for i in range(d...]
    pallas_call x1, Pallas kernels: 2.52 us -> 4.52 us  [opacities(): pl.pallas_call(functools.partial(opacity_kernel, slices, width // LANES,...]
    ppermute x1, waiting for transfers between devices: 0.01 us -> 1.81 us  [shards(): after = lax.ppermute(initial, 'gz', down)]
    all_to_all x1, starting transfers between devices: 4.77 us -> 5.71 us  [exchange(): return lax.all_to_all(x, 'gz', split_axis=0, concat_axis=0, tiled=True)]
  transfers between devices with their start and end apart: 9 -> 9, of which waited for: 5 -> 5; matrix products, arithmetic and copies ran while one was open for 0% -> 0% of each run, Pallas kernels for 15% -> 19%
where the time goes in v11:
time: 71.4 us; the launch traced here: 70.4 us
  waiting for transfers between devices  35.5 us (50%)
  starting transfers between devices  17.4 us (24%)
  Pallas kernels  14.9 us (21%)
  other arithmetic  1.9 us (3%)
    all_to_all x1, waiting for transfers between devices, exchange(): return lax.all_to_all(x, 'gz', split_axis=0, concat_axis=0, tiled=True)  17.8 us
    ppermute x3, waiting for transfers between devices, shards(): lax.ppermute(part, 'gz', [(i, i ^ m) for i in range(devices)])  15.5 us
    pallas_call x1, Pallas kernels, colours(): pl.pallas_call(functools.partial(colour_kernel, slices, width // LANES),...  8.6 us
    all_to_all x1, starting transfers between devices, exchange(): return lax.all_to_all(x, 'gz', split_axis=0, concat_axis=0, tiled=True)  5.71 us
    pallas_call x1, Pallas kernels, opacities(): pl.pallas_call(functools.partial(opacity_kernel, slices, width // LANES,...  4.52 us
    ppermute x3, starting transfers between devices, shards(): lax.ppermute(part, 'gz', [(i, (i + s * turns) % devices) for i in range(d...  3.83 us
    ppermute x1, starting transfers between devices, shards(): before = lax.ppermute(last, 'gz', up)  3.02 us
    ppermute x1, starting transfers between devices, shards(): after = lax.ppermute(initial, 'gz', down)  2.58 us
  transfers between devices with their start and end apart: 9, of which 5 were waited for; matrix products, arithmetic and copies ran while one was open for 0% of the time, Pallas kernels for 19%

profile of v11, /device:TPU:13, one launch (start us, length us, event | category | flops | bytes accessed | tf_op | source)
XLA Modules:
  0.0 70.4 jit_solution(3354566976779709162)
XLA Ops:
  0.0 1.9 %fusion.1 = (s16[256,1024]{1,0:T(8,128)(2,1)S(1)}, s16[256,1024]{1,0:T(8,128)(2,1)S(1)}) fusion(f32[4,256,1024]{2,1,0:T(8,128)} %volume_hbm.1), kind=kLoop, calls=%fused_computation.3 | loop fusion | flops 1572864 | bytes 3145728 | tf_op jit(solution)/shard_map/convert_element_type | solution.py:253
  1.9 2.6 %collective-permute-start.4 = (s16[256,1024]{1,0:T(8,128)(2,1)S(1)}, s16[256,1024]{1,0:T(8,128)(2,1)S(1)}, u32[]{:S(2)}, u32[]{:S(2)}) collective-permute-start(s16[256,1024]{1,0:T(8,128)(2,1)S(1)} %get-tuple-element.33), channel_id=1, source_target_pairs={{1,0},{2,1},{3,2},{4,3},{5,4},{6,5},{7,6},{8,7},{9,8},{10,9},{11,1... | collective-permute-start | bytes 1572872 | tf_op jit(solution)/shard_map/ppermute | solution.py:263
  4.5 0.0 copy-start
  4.5 3.0 %collective-permute-start.3 = (s16[256,1024]{1,0:T(8,128)(2,1)S(1)}, s16[256,1024]{1,0:T(8,128)(2,1)S(1)}, u32[]{:S(2)}, u32[]{:S(2)}) collective-permute-start(s16[256,1024]{1,0:T(8,128)(2,1)S(1)} %get-tuple-element.34), channel_id=1, source_target_pairs={{0,1},{1,2},{2,3},{3,4},{4,5},{5,6},{6,7},{7,8},{8,9},{9,10},{10,1... | collective-permute-start | bytes 1572872 | tf_op jit(solution)/shard_map/ppermute | solution.py:262
  7.5 0.0 copy-start.1
  7.5 0.6 copy-done.1
  8.2 4.5 %opacities.1 = (bf16[4,16,1024]{2,1,0:T(8,128)(2,1)S(1)}, bf16[4,16,1024]{2,1,0:T(8,128)(2,1)S(1)}, bf16[4,16,1024]{2,1,0:T(8,128)(2,1)S(1)}, bf16[4,16,1024]{2,...) custom-call(f32[4,256,1024]{2,1,0:T(8,128)} %volume_hbm.1, s32[4,256,1024]{2,1,0:T(8,128)} %index_hbm.1, ...), custom_call_target="tpu_custom_call" | custom-call | flops 15728640 | bytes 9437184 | tf_op jit(solution)/shard_map/opacities/pallas_call | solution.py:78
  12.7 1.3 %collective-permute-start = (bf16[4,16,1024]{2,1,0:T(8,128)(2,1)S(1)}, bf16[4,16,1024]{2,1,0:T(8,128)(2,1)S(1)}, u32[]{:S(2)}, u32[]{:S(2)}) collective-permute-start(bf16[4,16,1024]{2,1,0:T(8,128)(2,1)S(1)} %get-tuple-element.19), channel_id=1, source_target_pairs={{0,4},{1,5},{2,6},{3,7},{4,8},{5,9},{6,10},{7,11},{8,12},{9,13},{1... | collective-permute-start | bytes 393224 | tf_op jit(solution)/shard_map/ppermute | solution.py:270
  14.1 1.1 %collective-permute-start.1 = (bf16[4,16,1024]{2,1,0:T(8,128)(2,1)S(1)}, bf16[4,16,1024]{2,1,0:T(8,128)(2,1)S(1)}, u32[]{:S(2)}, u32[]{:S(2)}) collective-permute-start(bf16[4,16,1024]{2,1,0:T(8,128)(2,1)S(1)} %get-tuple-element.20), channel_id=1, source_target_pairs={{0,8},{1,9},{2,10},{3,11},{4,12},{5,13},{6,14},{7,15},{8,0},{9,1},... | collective-permute-start | bytes 393224 | tf_op jit(solution)/shard_map/ppermute | solution.py:270
  15.2 1.4 %collective-permute-start.2 = (bf16[4,16,1024]{2,1,0:T(8,128)(2,1)S(1)}, bf16[4,16,1024]{2,1,0:T(8,128)(2,1)S(1)}, u32[]{:S(2)}, u32[]{:S(2)}) collective-permute-start(bf16[4,16,1024]{2,1,0:T(8,128)(2,1)S(1)} %get-tuple-element.21), channel_id=1, source_target_pairs={{0,12},{1,13},{2,14},{3,15},{4,0},{5,1},{6,2},{7,3},{8,4},{9,5},{1... | collective-permute-start | bytes 393224 | tf_op jit(solution)/shard_map/ppermute | solution.py:270
  16.5 1.8 %collective-permute-done.4.after_ref = s16[256,1024]{1,0:T(8,128)(2,1)S(1)} collective-permute-done((s16[256,1024]{1,0:T(8,128)(2,1)S(1)}, s16[256,1024]{1,0:T(8,128)(2,1)S(1)}, u32[]{:S(2)}, u32[]{:S(2)}) %collective-permute-start.4) | collective-permute-done | bytes 524320 | tf_op jit(solution)/shard_map/ppermute | solution.py:263
  18.4 0.0 collective-permute-done.3.before_ref
  18.4 0.0 copy-done
  18.4 0.0 copy-start.2
  18.4 8.6 %colours.1 = bf16[16,3,16,1024]{3,2,1,0:T(8,128)(2,1)} custom-call(f32[4,256,1024]{2,1,0:T(8,128)S(1)} %get-tuple-element.22.vol, s32[4,256,1024]{2,1,0:T(8,128)S(1)} %get-tuple-element.23.idx, s16[256,1024]{1,0:T(8,128)(2,1)S(1)} %collective-permute-done.3.before_ref, s16[256,1024]{1,0:T(8,128)(2,1)S(1)} %collective-permute-done.4.after_ref, ...), custom_call_target="tpu_custom_call" | custom-call | flops 52428800 | bytes 41943040 | tf_op jit(solution)/shard_map/colours/pallas_call | solution.py:157
  27.0 0.0 collective-permute-done.refs_1_
  27.0 0.0 collective-permute-done.1.refs_2_
  27.0 0.5 collective-permute-done.2.refs_3_
  27.4 5.7 %all-to-all-start = ((bf16[16,3,16,1024]{3,2,1,0:T(8,128)(2,1)}), bf16[16,3,16,1024]{3,2,1,0:T(8,128)(2,1)S(1)}, u32[]{:S(2)}, u32[]{:S(2)}) async-start(bf16[16,3,16,1024]{3,2,1,0:T(8,128)(2,1)} %colours.1), calls=%async_computation | async-start | bytes 3145728 | tf_op jit(solution)/shard_map/all_to_all | solution.py:249
  33.2 0.4 collective-permute-start.5
  33.6 1.2 %collective-permute-start.6 = (bf16[4,16,1024]{2,1,0:T(8,128)(2,1)S(1)}, bf16[4,16,1024]{2,1,0:T(8,128)(2,1)S(1)}, u32[]{:S(2)}, u32[]{:S(2)}) collective-permute-start(bf16[4,16,1024]{2,1,0:T(8,128)(2,1)S(1)} %get-tuple-element.31), channel_id=1, source_target_pairs={{0,2},{1,3},{2,0},{3,1},{4,6},{5,7},{6,4},{7,5},{8,10},{9,11},{10,... | collective-permute-start | bytes 393224 | tf_op jit(solution)/shard_map/ppermute | solution.py:275
  34.8 0.6 collective-permute-start.7
  35.4 0.0 collective-permute-done.5.rest_1_
  35.4 9.0 %collective-permute-done.6.rest_2_ = bf16[4,16,1024]{2,1,0:T(8,128)(2,1)S(1)} collective-permute-done((bf16[4,16,1024]{2,1,0:T(8,128)(2,1)S(1)}, bf16[4,16,1024]{2,1,0:T(8,128)(2,1)S(1)}, u32[]{:S(2)}, u32[]{:S(2)}) %collective-permute-start.6) | collective-permute-done | bytes 131104 | tf_op jit(solution)/shard_map/ppermute | solution.py:275
  44.4 6.5 %collective-permute-done.7.rest_3_ = bf16[4,16,1024]{2,1,0:T(8,128)(2,1)S(1)} collective-permute-done((bf16[4,16,1024]{2,1,0:T(8,128)(2,1)S(1)}, bf16[4,16,1024]{2,1,0:T(8,128)(2,1)S(1)}, u32[]{:S(2)}, u32[]{:S(2)}) %collective-permute-start.7) | collective-permute-done | bytes 131104 | tf_op jit(solution)/shard_map/ppermute | solution.py:275
  50.9 17.8 %all-to-all-done.colour_ref = bf16[16,3,16,1024]{3,2,1,0:T(8,128)(2,1)S(1)} async-done(((bf16[16,3,16,1024]{3,2,1,0:T(8,128)(2,1)}), bf16[16,3,16,1024]{3,2,1,0:T(8,128)(2,1)S(1)}, u32[]{:S(2)}, u32[]{:S(2)}) %all-to-all-start) | async-done | bytes 1572896 | tf_op jit(solution)/shard_map/all_to_all | solution.py:249
  68.6 0.0 copy-done.2
  68.6 1.8 %blend.1 = f32[4,16,1024]{2,1,0:T(8,128)} custom-call(s32[16]{0:T(128)S(1)} %copy-done.2, bf16[16,3,16,1024]{3,2,1,0:T(8,128)(2,1)S(1)} %all-to-all-done.colour_ref, bf16[4,16,1024]{2,1,0:T(8,128)(2,1)S(1)} %get-tuple-element.29.rest_0_, bf16[4,16,1024]{2,1,0:T(8,128)(2,1)S(1)} %collective-permute-done.5.rest_1_, ...), custom_call_target="tpu_custom_call" | custom-call | tf_op jit(solution)/shard_map/blend/pallas_call | solution.py:214
  (1 shorter events, 0.0 us)
Async XLA Ops:
  1.9 16.5 %collective-permute-start.4 = (s16[256,1024]{1,0:T(8,128)(2,1)S(1)}, s16[256,1024]{1,0:T(8,128)(2,1)S(1)}, u32[]{:S(2)}, u32[]{:S(2)}) collective-permute-start(s16[256,1024]{1,0:T(8,128)(2,1)S(1)} %get-tuple-element.33), channel_id=1, source_target_pairs={{1,0},{2,1},{3,2},{4,3},{5,4},{6,5},{7,6},{8,7},{9,8},{10,9},{11,1... | collective-permute-start | bytes 1572872 | tf_op jit(solution)/shard_map/ppermute | solution.py:263
  4.5 13.9 %copy-start = (f32[3,8]{1,0:T(4,128)S(1)}, f32[3,8]{1,0:T(4,128)}, u32[]{:S(2)}) copy-start(f32[3,8]{1,0:T(4,128)} %colour_ref.1) | copy-start | bytes 292
  4.5 13.8 %collective-permute-start.3 = (s16[256,1024]{1,0:T(8,128)(2,1)S(1)}, s16[256,1024]{1,0:T(8,128)(2,1)S(1)}, u32[]{:S(2)}, u32[]{:S(2)}) collective-permute-start(s16[256,1024]{1,0:T(8,128)(2,1)S(1)} %get-tuple-element.34), channel_id=1, source_target_pairs={{0,1},{1,2},{2,3},{3,4},{4,5},{5,6},{6,7},{7,8},{8,9},{9,10},{10,1... | collective-permute-start | bytes 1572872 | tf_op jit(solution)/shard_map/ppermute | solution.py:262
  7.5 0.7 copy-start.1
  12.7 14.2 %collective-permute-start = (bf16[4,16,1024]{2,1,0:T(8,128)(2,1)S(1)}, bf16[4,16,1024]{2,1,0:T(8,128)(2,1)S(1)}, u32[]{:S(2)}, u32[]{:S(2)}) collective-permute-start(bf16[4,16,1024]{2,1,0:T(8,128)(2,1)S(1)} %get-tuple-element.19), channel_id=1, source_target_pairs={{0,4},{1,5},{2,6},{3,7},{4,8},{5,9},{6,10},{7,11},{8,12},{9,13},{1... | collective-permute-start | bytes 393224 | tf_op jit(solution)/shard_map/ppermute | solution.py:270
  14.1 12.9 %collective-permute-start.1 = (bf16[4,16,1024]{2,1,0:T(8,128)(2,1)S(1)}, bf16[4,16,1024]{2,1,0:T(8,128)(2,1)S(1)}, u32[]{:S(2)}, u32[]{:S(2)}) collective-permute-start(bf16[4,16,1024]{2,1,0:T(8,128)(2,1)S(1)} %get-tuple-element.20), channel_id=1, source_target_pairs={{0,8},{1,9},{2,10},{3,11},{4,12},{5,13},{6,14},{7,15},{8,0},{9,1},... | collective-permute-start | bytes 393224 | tf_op jit(solution)/shard_map/ppermute | solution.py:270
  15.2 12.3 %collective-permute-start.2 = (bf16[4,16,1024]{2,1,0:T(8,128)(2,1)S(1)}, bf16[4,16,1024]{2,1,0:T(8,128)(2,1)S(1)}, u32[]{:S(2)}, u32[]{:S(2)}) collective-permute-start(bf16[4,16,1024]{2,1,0:T(8,128)(2,1)S(1)} %get-tuple-element.21), channel_id=1, source_target_pairs={{0,12},{1,13},{2,14},{3,15},{4,0},{5,1},{6,2},{7,3},{8,4},{9,5},{1... | collective-permute-start | bytes 393224 | tf_op jit(solution)/shard_map/ppermute | solution.py:270
  18.4 50.3 %copy-start.2 = (s32[16]{0:T(128)S(1)}, s32[16]{0:T(128)}, u32[]{:S(2)}) copy-start(s32[16]{0:T(128)} %order_ref.1) | copy-start | bytes 196
  27.4 41.2 %all-to-all-start = ((bf16[16,3,16,1024]{3,2,1,0:T(8,128)(2,1)}), bf16[16,3,16,1024]{3,2,1,0:T(8,128)(2,1)S(1)}, u32[]{:S(2)}, u32[]{:S(2)}) async-start(bf16[16,3,16,1024]{3,2,1,0:T(8,128)(2,1)} %colours.1), calls=%async_computation | async-start | bytes 3145728 | tf_op jit(solution)/shard_map/all_to_all | solution.py:249
  33.2 2.2 %collective-permute-start.5 = (bf16[4,16,1024]{2,1,0:T(8,128)(2,1)S(1)}, bf16[4,16,1024]{2,1,0:T(8,128)(2,1)S(1)}, u32[]{:S(2)}, u32[]{:S(2)}) collective-permute-start(bf16[4,16,1024]{2,1,0:T(8,128)(2,1)S(1)} %get-tuple-element.30), channel_id=1, source_target_pairs={{0,1},{1,0},{2,3},{3,2},{4,5},{5,4},{6,7},{7,6},{8,9},{9,8},{10,11... | collective-permute-start | bytes 393224 | tf_op jit(solution)/shard_map/ppermute | solution.py:275
  33.6 10.8 %collective-permute-start.6 = (bf16[4,16,1024]{2,1,0:T(8,128)(2,1)S(1)}, bf16[4,16,1024]{2,1,0:T(8,128)(2,1)S(1)}, u32[]{:S(2)}, u32[]{:S(2)}) collective-permute-start(bf16[4,16,1024]{2,1,0:T(8,128)(2,1)S(1)} %get-tuple-element.31), channel_id=1, source_target_pairs={{0,2},{1,3},{2,0},{3,1},{4,6},{5,7},{6,4},{7,5},{8,10},{9,11},{10,... | collective-permute-start | bytes 393224 | tf_op jit(solution)/shard_map/ppermute | solution.py:275
  34.8 16.1 %collective-permute-start.7 = (bf16[4,16,1024]{2,1,0:T(8,128)(2,1)S(1)}, bf16[4,16,1024]{2,1,0:T(8,128)(2,1)S(1)}, u32[]{:S(2)}, u32[]{:S(2)}) collective-permute-start(bf16[4,16,1024]{2,1,0:T(8,128)(2,1)S(1)} %get-tuple-element.32), channel_id=1, source_target_pairs={{0,3},{1,2},{2,1},{3,0},{4,7},{5,6},{6,5},{7,4},{8,11},{9,10},{10,... | collective-permute-start | bytes 393224 | tf_op jit(solution)/shard_map/ppermute | solution.py:275

commit v12 on v11

--- a/solution.py
+++ b/solution.py
@@ -15,6 +15,7 @@
 NT = 8
 LIMIT = 24 * 1024 * 1024
 FETCH_LIMIT = 43 * 1024 * 1024
+CODED_LIMIT = 51 * 1024 * 1024
 BLEND_LIMIT = 16 * 1024 * 1024
 PLANES = 4
 
@@ -249,8 +250,40 @@
     return lax.all_to_all(x, "gz", split_axis=0, concat_axis=0, tiled=True)
 
 
-def coded(a_slice):
-    return jnp.round(a_slice * (STEPS / REACH)).astype(jnp.int16)
+def coded_kernel(pieces, volume_hbm, *rest):
+    out_refs, (here, sems) = rest[:2], rest[2:]
+    height = here.shape[1] // pieces
+    copies = [
+        pltpu.make_async_copy(
+            volume_hbm.at[k, pl.ds(p * height, height), :], here.at[n, pl.ds(p * height, height), :], sems.at[n, p]
+        )
+        for n, k in enumerate([0, volume_hbm.shape[0] - 1])
+        for p in range(pieces)
+    ]
+    for copy in copies:
+        copy.start()
+    for n, out_ref in enumerate(out_refs):
+        for p in range(pieces):
+            copies[n * pieces + p].wait()
+
+            @pl.loop(0, height // BLOCK)
+            def _(i):
+                rows = pl.ds(pl.multiple_of(p * height + i * BLOCK, BLOCK), BLOCK)
+                out_ref[rows, :] = jnp.round(here[n, rows, :] * (STEPS / REACH)).astype(jnp.int32).astype(jnp.int16)
+
+
+def coded(volume):
+    _, height, width = volume.shape
+    part = jax.ShapeDtypeStruct((height, width), jnp.int16)
+    return pl.pallas_call(
+        functools.partial(coded_kernel, PLANES),
+        out_shape=[part] * 2,
+        in_specs=[pl.BlockSpec(memory_space=pltpu.HBM)],
+        out_specs=[pl.BlockSpec(memory_space=pltpu.VMEM)] * 2,
+        scratch_shapes=[pltpu.VMEM((2, height, width), volume.dtype), pltpu.SemaphoreType.DMA((2, PLANES))],
+        compiler_params=pltpu.CompilerParams(vmem_limit_bytes=CODED_LIMIT),
+        name="coded",
+    )(volume)
 
 
 def shards(volume, tf_index, tf_color, tf_opacity, order):
@@ -258,7 +291,7 @@
     slices, height, width = volume.shape
     up = [(i, i + 1) for i in range(devices - 1)]
     down = [(j, i) for i, j in up]
-    last, initial = coded(volume[slices - 1]), coded(volume[0])
+    initial, last = coded(volume)
     before = lax.ppermute(last, "gz", up)
     after = lax.ppermute(initial, "gz", down)
     turns = PLANES if devices == PLANES * PLANES and height // devices == BLOCK else 1

time: 71.4 us -> 72.8 us (1.020)
  other arithmetic: 1.9 us -> 0 us
  Pallas kernels: 14.9 us -> 16.5 us
  starting transfers between devices: 17.4 us -> 18.7 us
  waiting for transfers between devices: 35.5 us -> 36.5 us
    convert_element_type x1 -> x0, other arithmetic: 1.9 us -> none  [coded(): return jnp.round(a_slice * (STEPS / REACH)).astype(jnp.int16)]
    pallas_call x0 -> x1, Pallas kernels: none -> 1.62 us  [coded(): pl.pallas_call(functools.partial(coded_kernel, PLANES), out_shape=[part]...]
    all_to_all x1, starting transfers between devices: 5.71 us -> 7.07 us  [exchange(): return lax.all_to_all(x, 'gz', split_axis=0, concat_axis=0, tiled=True)]
    ppermute x1, waiting for transfers between devices: 1.81 us -> 3.17 us  [shards(): after = lax.ppermute(initial, 'gz', down)]
  transfers between devices with their start and end apart: 9 -> 9, of which waited for: 5 -> 5; matrix products, arithmetic and copies ran while one was open for 0% -> 0% of each run, Pallas kernels for 19% -> 18%
where the time goes in v12:
time: 72.8 us; the launch traced here: 71.9 us
  waiting for transfers between devices  36.5 us (50%)
  starting transfers between devices  18.7 us (26%)
  Pallas kernels  16.5 us (23%)
    all_to_all x1, waiting for transfers between devices, exchange(): return lax.all_to_all(x, 'gz', split_axis=0, concat_axis=0, tiled=True)  17.8 us
    ppermute x3, waiting for transfers between devices, shards(): lax.ppermute(part, 'gz', [(i, i ^ m) for i in range(devices)])  15.5 us
    pallas_call x1, Pallas kernels, colours(): pl.pallas_call(functools.partial(colour_kernel, slices, width // LANES),...  8.59 us
    all_to_all x1, starting transfers between devices, exchange(): return lax.all_to_all(x, 'gz', split_axis=0, concat_axis=0, tiled=True)  7.07 us
    pallas_call x1, Pallas kernels, opacities(): pl.pallas_call(functools.partial(opacity_kernel, slices, width // LANES,...  4.52 us
    ppermute x3, starting transfers between devices, shards(): lax.ppermute(part, 'gz', [(i, (i + s * turns) % devices) for i in range(d...  3.83 us
    ppermute x1, starting transfers between devices, shards(): before = lax.ppermute(last, 'gz', up)  3.68 us
    ppermute x1, waiting for transfers between devices, shards(): after = lax.ppermute(initial, 'gz', down)  3.17 us
  transfers between devices with their start and end apart: 9, of which 5 were waited for; matrix products, arithmetic and copies ran while one was open for 0% of the time, Pallas kernels for 18%

profile of v12, /device:TPU:13, one launch (start us, length us, event | category | flops | bytes accessed | tf_op | source)
XLA Modules:
  0.0 71.9 jit_solution(1429757244724992516)
XLA Ops:
  0.0 0.0 copy-start.1
  0.0 1.6 %coded.1 = (s16[256,1024]{1,0:T(8,128)(2,1)S(1)}, s16[256,1024]{1,0:T(8,128)(2,1)S(1)}) custom-call(f32[4,256,1024]{2,1,0:T(8,128)} %volume_hbm.3), custom_call_target="tpu_custom_call" | custom-call | tf_op jit(solution)/shard_map/coded/pallas_call | solution.py:278
  1.6 3.7 %collective-permute-start.3 = (s16[256,1024]{1,0:T(8,128)(2,1)S(1)}, s16[256,1024]{1,0:T(8,128)(2,1)S(1)}, u32[]{:S(2)}, u32[]{:S(2)}) collective-permute-start(s16[256,1024]{1,0:T(8,128)(2,1)S(1)} %get-tuple-element.26), channel_id=1, source_target_pairs={{0,1},{1,2},{2,3},{3,4},{4,5},{5,6},{6,7},{7,8},{8,9},{9,10},{10,1... | collective-permute-start | bytes 1572872 | tf_op jit(solution)/shard_map/ppermute | solution.py:295
  5.3 0.0 copy-start
  5.3 1.9 %collective-permute-start.4 = (s16[256,1024]{1,0:T(8,128)(2,1)S(1)}, s16[256,1024]{1,0:T(8,128)(2,1)S(1)}, u32[]{:S(2)}, u32[]{:S(2)}) collective-permute-start(s16[256,1024]{1,0:T(8,128)(2,1)S(1)} %get-tuple-element.27), channel_id=1, source_target_pairs={{1,0},{2,1},{3,2},{4,3},{5,4},{6,5},{7,6},{8,7},{9,8},{10,9},{11,1... | collective-permute-start | bytes 1572872 | tf_op jit(solution)/shard_map/ppermute | solution.py:296
  7.3 0.0 copy-done.1
  7.3 4.5 %opacities.1 = (bf16[4,16,1024]{2,1,0:T(8,128)(2,1)S(1)}, bf16[4,16,1024]{2,1,0:T(8,128)(2,1)S(1)}, bf16[4,16,1024]{2,1,0:T(8,128)(2,1)S(1)}, bf16[4,16,1024]{2,...) custom-call(f32[4,256,1024]{2,1,0:T(8,128)} %volume_hbm.3, s32[4,256,1024]{2,1,0:T(8,128)} %index_hbm.1, ...), custom_call_target="tpu_custom_call" | custom-call | flops 15728640 | bytes 9437184 | tf_op jit(solution)/shard_map/opacities/pallas_call | solution.py:79
  11.8 1.3 %collective-permute-start = (bf16[4,16,1024]{2,1,0:T(8,128)(2,1)S(1)}, bf16[4,16,1024]{2,1,0:T(8,128)(2,1)S(1)}, u32[]{:S(2)}, u32[]{:S(2)}) collective-permute-start(bf16[4,16,1024]{2,1,0:T(8,128)(2,1)S(1)} %get-tuple-element.21), channel_id=1, source_target_pairs={{0,4},{1,5},{2,6},{3,7},{4,8},{5,9},{6,10},{7,11},{8,12},{9,13},{1... | collective-permute-start | bytes 393224 | tf_op jit(solution)/shard_map/ppermute | solution.py:303
  13.1 1.1 %collective-permute-start.1 = (bf16[4,16,1024]{2,1,0:T(8,128)(2,1)S(1)}, bf16[4,16,1024]{2,1,0:T(8,128)(2,1)S(1)}, u32[]{:S(2)}, u32[]{:S(2)}) collective-permute-start(bf16[4,16,1024]{2,1,0:T(8,128)(2,1)S(1)} %get-tuple-element.22), channel_id=1, source_target_pairs={{0,8},{1,9},{2,10},{3,11},{4,12},{5,13},{6,14},{7,15},{8,0},{9,1},... | collective-permute-start | bytes 393224 | tf_op jit(solution)/shard_map/ppermute | solution.py:303
  14.2 1.4 %collective-permute-start.2 = (bf16[4,16,1024]{2,1,0:T(8,128)(2,1)S(1)}, bf16[4,16,1024]{2,1,0:T(8,128)(2,1)S(1)}, u32[]{:S(2)}, u32[]{:S(2)}) collective-permute-start(bf16[4,16,1024]{2,1,0:T(8,128)(2,1)S(1)} %get-tuple-element.23), channel_id=1, source_target_pairs={{0,12},{1,13},{2,14},{3,15},{4,0},{5,1},{6,2},{7,3},{8,4},{9,5},{1... | collective-permute-start | bytes 393224 | tf_op jit(solution)/shard_map/ppermute | solution.py:303
  15.6 0.1 collective-permute-done.3.before_ref
  15.8 3.2 %collective-permute-done.4.after_ref = s16[256,1024]{1,0:T(8,128)(2,1)S(1)} collective-permute-done((s16[256,1024]{1,0:T(8,128)(2,1)S(1)}, s16[256,1024]{1,0:T(8,128)(2,1)S(1)}, u32[]{:S(2)}, u32[]{:S(2)}) %collective-permute-start.4) | collective-permute-done | bytes 524320 | tf_op jit(solution)/shard_map/ppermute | solution.py:296
  18.9 0.0 copy-done
  18.9 0.0 copy-start.2
  18.9 8.6 %colours.1 = bf16[16,3,16,1024]{3,2,1,0:T(8,128)(2,1)} custom-call(f32[4,256,1024]{2,1,0:T(8,128)S(1)} %get-tuple-element.24.vol, s32[4,256,1024]{2,1,0:T(8,128)S(1)} %get-tuple-element.25.idx, s16[256,1024]{1,0:T(8,128)(2,1)S(1)} %collective-permute-done.3.before_ref, s16[256,1024]{1,0:T(8,128)(2,1)S(1)} %collective-permute-done.4.after_ref, ...), custom_call_target="tpu_custom_call" | custom-call | flops 52428800 | bytes 41943040 | tf_op jit(solution)/shard_map/colours/pallas_call | solution.py:158
  27.5 0.0 collective-permute-done.refs_1_
  27.5 0.0 collective-permute-done.1.refs_2_
  27.5 0.0 collective-permute-done.2.refs_3_
  27.5 7.1 %all-to-all-start = ((bf16[16,3,16,1024]{3,2,1,0:T(8,128)(2,1)}), bf16[16,3,16,1024]{3,2,1,0:T(8,128)(2,1)S(1)}, u32[]{:S(2)}, u32[]{:S(2)}) async-start(bf16[16,3,16,1024]{3,2,1,0:T(8,128)(2,1)} %colours.1), calls=%async_computation | async-start | bytes 3145728 | tf_op jit(solution)/shard_map/all_to_all | solution.py:250
  34.7 0.4 collective-permute-start.5
  35.1 1.2 %collective-permute-start.6 = (bf16[4,16,1024]{2,1,0:T(8,128)(2,1)S(1)}, bf16[4,16,1024]{2,1,0:T(8,128)(2,1)S(1)}, u32[]{:S(2)}, u32[]{:S(2)}) collective-permute-start(bf16[4,16,1024]{2,1,0:T(8,128)(2,1)S(1)} %get-tuple-element.35), channel_id=1, source_target_pairs={{0,2},{1,3},{2,0},{3,1},{4,6},{5,7},{6,4},{7,5},{8,10},{9,11},{10,... | collective-permute-start | bytes 393224 | tf_op jit(solution)/shard_map/ppermute | solution.py:308
  36.3 0.6 collective-permute-start.7
  36.9 0.0 collective-permute-done.5.rest_1_
  36.9 9.0 %collective-permute-done.6.rest_2_ = bf16[4,16,1024]{2,1,0:T(8,128)(2,1)S(1)} collective-permute-done((bf16[4,16,1024]{2,1,0:T(8,128)(2,1)S(1)}, bf16[4,16,1024]{2,1,0:T(8,128)(2,1)S(1)}, u32[]{:S(2)}, u32[]{:S(2)}) %collective-permute-start.6) | collective-permute-done | bytes 131104 | tf_op jit(solution)/shard_map/ppermute | solution.py:308
  45.9 6.5 %collective-permute-done.7.rest_3_ = bf16[4,16,1024]{2,1,0:T(8,128)(2,1)S(1)} collective-permute-done((bf16[4,16,1024]{2,1,0:T(8,128)(2,1)S(1)}, bf16[4,16,1024]{2,1,0:T(8,128)(2,1)S(1)}, u32[]{:S(2)}, u32[]{:S(2)}) %collective-permute-start.7) | collective-permute-done | bytes 131104 | tf_op jit(solution)/shard_map/ppermute | solution.py:308
  52.3 17.8 %all-to-all-done.colour_ref = bf16[16,3,16,1024]{3,2,1,0:T(8,128)(2,1)S(1)} async-done(((bf16[16,3,16,1024]{3,2,1,0:T(8,128)(2,1)}), bf16[16,3,16,1024]{3,2,1,0:T(8,128)(2,1)S(1)}, u32[]{:S(2)}, u32[]{:S(2)}) %all-to-all-start) | async-done | bytes 1572896 | tf_op jit(solution)/shard_map/all_to_all | solution.py:250
  70.1 0.0 copy-done.2
  70.1 1.8 %blend.1 = f32[4,16,1024]{2,1,0:T(8,128)} custom-call(s32[16]{0:T(128)S(1)} %copy-done.2, bf16[16,3,16,1024]{3,2,1,0:T(8,128)(2,1)S(1)} %all-to-all-done.colour_ref, bf16[4,16,1024]{2,1,0:T(8,128)(2,1)S(1)} %get-tuple-element.33.rest_0_, bf16[4,16,1024]{2,1,0:T(8,128)(2,1)S(1)} %collective-permute-done.5.rest_1_, ...), custom_call_target="tpu_custom_call" | custom-call | tf_op jit(solution)/shard_map/blend/pallas_call | solution.py:215
  (1 shorter events, 0.0 us)
Async XLA Ops:
  0.0 7.3 %copy-start.1 = (f32[8]{0:T(128)S(1)}, f32[8]{0:T(128)}, u32[]{:S(2)}) copy-start(f32[8]{0:T(128)} %opacity_ref.3) | copy-start | bytes 100
  1.6 14.1 %collective-permute-start.3 = (s16[256,1024]{1,0:T(8,128)(2,1)S(1)}, s16[256,1024]{1,0:T(8,128)(2,1)S(1)}, u32[]{:S(2)}, u32[]{:S(2)}) collective-permute-start(s16[256,1024]{1,0:T(8,128)(2,1)S(1)} %get-tuple-element.26), channel_id=1, source_target_pairs={{0,1},{1,2},{2,3},{3,4},{4,5},{5,6},{6,7},{7,8},{8,9},{9,10},{10,1... | collective-permute-start | bytes 1572872 | tf_op jit(solution)/shard_map/ppermute | solution.py:295
  5.3 13.6 %copy-start = (f32[3,8]{1,0:T(4,128)S(1)}, f32[3,8]{1,0:T(4,128)}, u32[]{:S(2)}) copy-start(f32[3,8]{1,0:T(4,128)} %colour_ref.1) | copy-start | bytes 292
  5.3 13.6 %collective-permute-start.4 = (s16[256,1024]{1,0:T(8,128)(2,1)S(1)}, s16[256,1024]{1,0:T(8,128)(2,1)S(1)}, u32[]{:S(2)}, u32[]{:S(2)}) collective-permute-start(s16[256,1024]{1,0:T(8,128)(2,1)S(1)} %get-tuple-element.27), channel_id=1, source_target_pairs={{1,0},{2,1},{3,2},{4,3},{5,4},{6,5},{7,6},{8,7},{9,8},{10,9},{11,1... | collective-permute-start | bytes 1572872 | tf_op jit(solution)/shard_map/ppermute | solution.py:296
  11.8 15.7 %collective-permute-start = (bf16[4,16,1024]{2,1,0:T(8,128)(2,1)S(1)}, bf16[4,16,1024]{2,1,0:T(8,128)(2,1)S(1)}, u32[]{:S(2)}, u32[]{:S(2)}) collective-permute-start(bf16[4,16,1024]{2,1,0:T(8,128)(2,1)S(1)} %get-tuple-element.21), channel_id=1, source_target_pairs={{0,4},{1,5},{2,6},{3,7},{4,8},{5,9},{6,10},{7,11},{8,12},{9,13},{1... | collective-permute-start | bytes 393224 | tf_op jit(solution)/shard_map/ppermute | solution.py:303
  13.1 14.4 %collective-permute-start.1 = (bf16[4,16,1024]{2,1,0:T(8,128)(2,1)S(1)}, bf16[4,16,1024]{2,1,0:T(8,128)(2,1)S(1)}, u32[]{:S(2)}, u32[]{:S(2)}) collective-permute-start(bf16[4,16,1024]{2,1,0:T(8,128)(2,1)S(1)} %get-tuple-element.22), channel_id=1, source_target_pairs={{0,8},{1,9},{2,10},{3,11},{4,12},{5,13},{6,14},{7,15},{8,0},{9,1},... | collective-permute-start | bytes 393224 | tf_op jit(solution)/shard_map/ppermute | solution.py:303
  14.2 13.3 %collective-permute-start.2 = (bf16[4,16,1024]{2,1,0:T(8,128)(2,1)S(1)}, bf16[4,16,1024]{2,1,0:T(8,128)(2,1)S(1)}, u32[]{:S(2)}, u32[]{:S(2)}) collective-permute-start(bf16[4,16,1024]{2,1,0:T(8,128)(2,1)S(1)} %get-tuple-element.23), channel_id=1, source_target_pairs={{0,12},{1,13},{2,14},{3,15},{4,0},{5,1},{6,2},{7,3},{8,4},{9,5},{1... | collective-permute-start | bytes 393224 | tf_op jit(solution)/shard_map/ppermute | solution.py:303
  18.9 51.2 %copy-start.2 = (s32[16]{0:T(128)S(1)}, s32[16]{0:T(128)}, u32[]{:S(2)}) copy-start(s32[16]{0:T(128)} %order_ref.1) | copy-start | bytes 196
  27.5 42.6 %all-to-all-start = ((bf16[16,3,16,1024]{3,2,1,0:T(8,128)(2,1)}), bf16[16,3,16,1024]{3,2,1,0:T(8,128)(2,1)S(1)}, u32[]{:S(2)}, u32[]{:S(2)}) async-start(bf16[16,3,16,1024]{3,2,1,0:T(8,128)(2,1)} %colours.1), calls=%async_computation | async-start | bytes 3145728 | tf_op jit(solution)/shard_map/all_to_all | solution.py:250
  34.7 2.2 %collective-permute-start.5 = (bf16[4,16,1024]{2,1,0:T(8,128)(2,1)S(1)}, bf16[4,16,1024]{2,1,0:T(8,128)(2,1)S(1)}, u32[]{:S(2)}, u32[]{:S(2)}) collective-permute-start(bf16[4,16,1024]{2,1,0:T(8,128)(2,1)S(1)} %get-tuple-element.34), channel_id=1, source_target_pairs={{0,1},{1,0},{2,3},{3,2},{4,5},{5,4},{6,7},{7,6},{8,9},{9,8},{10,11... | collective-permute-start | bytes 393224 | tf_op jit(solution)/shard_map/ppermute | solution.py:308
  35.1 10.8 %collective-permute-start.6 = (bf16[4,16,1024]{2,1,0:T(8,128)(2,1)S(1)}, bf16[4,16,1024]{2,1,0:T(8,128)(2,1)S(1)}, u32[]{:S(2)}, u32[]{:S(2)}) collective-permute-start(bf16[4,16,1024]{2,1,0:T(8,128)(2,1)S(1)} %get-tuple-element.35), channel_id=1, source_target_pairs={{0,2},{1,3},{2,0},{3,1},{4,6},{5,7},{6,4},{7,5},{8,10},{9,11},{10,... | collective-permute-start | bytes 393224 | tf_op jit(solution)/shard_map/ppermute | solution.py:308
  36.3 16.1 %collective-permute-start.7 = (bf16[4,16,1024]{2,1,0:T(8,128)(2,1)S(1)}, bf16[4,16,1024]{2,1,0:T(8,128)(2,1)S(1)}, u32[]{:S(2)}, u32[]{:S(2)}) collective-permute-start(bf16[4,16,1024]{2,1,0:T(8,128)(2,1)S(1)} %get-tuple-element.36), channel_id=1, source_target_pairs={{0,3},{1,2},{2,1},{3,0},{4,7},{5,6},{6,5},{7,4},{8,11},{9,10},{10,... | collective-permute-start | bytes 393224 | tf_op jit(solution)/shard_map/ppermute | solution.py:308

commit v13 on v12

--- a/solution.py
+++ b/solution.py
@@ -91,7 +91,7 @@
 
 
 def colour_kernel(
-    slices, tiles, vol, idx, before_ref, after_ref, colour_ref, opacity_ref, out_ref
+    slices, tiles, vol, idx, after_ref, before_ref, colour_ref, opacity_ref, out_ref
 ):
     height = before_ref.shape[0]
     blocks = height // BLOCK
@@ -165,7 +165,7 @@
             flops=50 * volume.size, bytes_accessed=40 * volume.size, transcendentals=2 * volume.size
         ),
         name="colours",
-    )(volume, tf_index, before, after, tf_color, tf_opacity)
+    )(volume, tf_index, after, before, tf_color, tf_opacity)
 
 
 def regroup_kernel(turns, *refs):
@@ -292,8 +292,8 @@
     up = [(i, i + 1) for i in range(devices - 1)]
     down = [(j, i) for i, j in up]
     initial, last = coded(volume)
+    after = lax.ppermute(initial, "gz", down)
     before = lax.ppermute(last, "gz", up)
-    after = lax.ppermute(initial, "gz", down)
     turns = PLANES if devices == PLANES * PLANES and height // devices == BLOCK else 1
     own, *others, volume, tf_index = opacities(volume, tf_index, tf_opacity, turns)
     colour = by_owner(colours(volume, tf_index, before, after, tf_color, tf_opacity), devices)

time: 72.8 us -> 71.1 us (0.977)
  starting transfers between devices: 18.7 us -> 17.8 us
  waiting for transfers between devices: 36.5 us -> 35.7 us
    all_to_all x1, starting transfers between devices: 7.07 us -> 6.15 us  [exchange(): return lax.all_to_all(x, 'gz', split_axis=0, concat_axis=0, tiled=True)]
  transfers between devices with their start and end apart: 9 -> 9, of which waited for: 5 -> 4; matrix products, arithmetic and copies ran while one was open for 0% -> 0% of each run, Pallas kernels for 18% -> 19%
where the time goes in v13:
time: 71.1 us; the launch traced here: 70.1 us
  waiting for transfers between devices  35.7 us (50%)
  starting transfers between devices  17.8 us (25%)
  Pallas kernels  16.5 us (23%)
    all_to_all x1, waiting for transfers between devices, exchange(): return lax.all_to_all(x, 'gz', split_axis=0, concat_axis=0, tiled=True)  17.8 us
    ppermute x3, waiting for transfers between devices, shards(): lax.ppermute(part, 'gz', [(i, i ^ m) for i in range(devices)])  15.5 us
    pallas_call x1, Pallas kernels, colours(): pl.pallas_call(functools.partial(colour_kernel, slices, width // LANES),...  8.6 us
    all_to_all x1, starting transfers between devices, exchange(): return lax.all_to_all(x, 'gz', split_axis=0, concat_axis=0, tiled=True)  6.15 us
    pallas_call x1, Pallas kernels, opacities(): pl.pallas_call(functools.partial(opacity_kernel, slices, width // LANES,...  4.52 us
    ppermute x3, starting transfers between devices, shards(): lax.ppermute(part, 'gz', [(i, (i + s * turns) % devices) for i in range(d...  3.83 us
    ppermute x1, starting transfers between devices, shards(): before = lax.ppermute(last, 'gz', up)  3.02 us
    ppermute x1, starting transfers between devices, shards(): after = lax.ppermute(initial, 'gz', down)  2.58 us
  transfers between devices with their start and end apart: 9, of which 4 were waited for; matrix products, arithmetic and copies ran while one was open for 0% of the time, Pallas kernels for 19%

profile of v13, /device:TPU:13, one launch (start us, length us, event | category | flops | bytes accessed | tf_op | source)
XLA Modules:
  0.0 70.1 jit_solution(15487281012413780700)
XLA Ops:
  0.0 0.0 copy-start.1
  0.0 1.6 %coded.1 = (s16[256,1024]{1,0:T(8,128)(2,1)S(1)}, s16[256,1024]{1,0:T(8,128)(2,1)S(1)}) custom-call(f32[4,256,1024]{2,1,0:T(8,128)} %volume_hbm.3), custom_call_target="tpu_custom_call" | custom-call | tf_op jit(solution)/shard_map/coded/pallas_call | solution.py:278
  1.6 2.6 %collective-permute-start.3 = (s16[256,1024]{1,0:T(8,128)(2,1)S(1)}, s16[256,1024]{1,0:T(8,128)(2,1)S(1)}, u32[]{:S(2)}, u32[]{:S(2)}) collective-permute-start(s16[256,1024]{1,0:T(8,128)(2,1)S(1)} %get-tuple-element.26), channel_id=1, source_target_pairs={{1,0},{2,1},{3,2},{4,3},{5,4},{6,5},{7,6},{8,7},{9,8},{10,9},{11,1... | collective-permute-start | bytes 1572872 | tf_op jit(solution)/shard_map/ppermute | solution.py:295
  4.2 0.0 copy-start
  4.2 3.0 %collective-permute-start.4 = (s16[256,1024]{1,0:T(8,128)(2,1)S(1)}, s16[256,1024]{1,0:T(8,128)(2,1)S(1)}, u32[]{:S(2)}, u32[]{:S(2)}) collective-permute-start(s16[256,1024]{1,0:T(8,128)(2,1)S(1)} %get-tuple-element.27), channel_id=1, source_target_pairs={{0,1},{1,2},{2,3},{3,4},{4,5},{5,6},{6,7},{7,8},{8,9},{9,10},{10,1... | collective-permute-start | bytes 1572872 | tf_op jit(solution)/shard_map/ppermute | solution.py:296
  7.3 0.0 copy-done.1
  7.3 4.5 %opacities.1 = (bf16[4,16,1024]{2,1,0:T(8,128)(2,1)S(1)}, bf16[4,16,1024]{2,1,0:T(8,128)(2,1)S(1)}, bf16[4,16,1024]{2,1,0:T(8,128)(2,1)S(1)}, bf16[4,16,1024]{2,...) custom-call(f32[4,256,1024]{2,1,0:T(8,128)} %volume_hbm.3, s32[4,256,1024]{2,1,0:T(8,128)} %index_hbm.1, ...), custom_call_target="tpu_custom_call" | custom-call | flops 15728640 | bytes 9437184 | tf_op jit(solution)/shard_map/opacities/pallas_call | solution.py:79
  11.8 1.3 %collective-permute-start = (bf16[4,16,1024]{2,1,0:T(8,128)(2,1)S(1)}, bf16[4,16,1024]{2,1,0:T(8,128)(2,1)S(1)}, u32[]{:S(2)}, u32[]{:S(2)}) collective-permute-start(bf16[4,16,1024]{2,1,0:T(8,128)(2,1)S(1)} %get-tuple-element.21), channel_id=1, source_target_pairs={{0,4},{1,5},{2,6},{3,7},{4,8},{5,9},{6,10},{7,11},{8,12},{9,13},{1... | collective-permute-start | bytes 393224 | tf_op jit(solution)/shard_map/ppermute | solution.py:303
  13.1 1.1 %collective-permute-start.1 = (bf16[4,16,1024]{2,1,0:T(8,128)(2,1)S(1)}, bf16[4,16,1024]{2,1,0:T(8,128)(2,1)S(1)}, u32[]{:S(2)}, u32[]{:S(2)}) collective-permute-start(bf16[4,16,1024]{2,1,0:T(8,128)(2,1)S(1)} %get-tuple-element.22), channel_id=1, source_target_pairs={{0,8},{1,9},{2,10},{3,11},{4,12},{5,13},{6,14},{7,15},{8,0},{9,1},... | collective-permute-start | bytes 393224 | tf_op jit(solution)/shard_map/ppermute | solution.py:303
  14.2 1.4 %collective-permute-start.2 = (bf16[4,16,1024]{2,1,0:T(8,128)(2,1)S(1)}, bf16[4,16,1024]{2,1,0:T(8,128)(2,1)S(1)}, u32[]{:S(2)}, u32[]{:S(2)}) collective-permute-start(bf16[4,16,1024]{2,1,0:T(8,128)(2,1)S(1)} %get-tuple-element.23), channel_id=1, source_target_pairs={{0,12},{1,13},{2,14},{3,15},{4,0},{5,1},{6,2},{7,3},{8,4},{9,5},{1... | collective-permute-start | bytes 393224 | tf_op jit(solution)/shard_map/ppermute | solution.py:303
  15.6 2.5 %collective-permute-done.3.after_ref = s16[256,1024]{1,0:T(8,128)(2,1)S(1)} collective-permute-done((s16[256,1024]{1,0:T(8,128)(2,1)S(1)}, s16[256,1024]{1,0:T(8,128)(2,1)S(1)}, u32[]{:S(2)}, u32[]{:S(2)}) %collective-permute-start.3) | collective-permute-done | bytes 524320 | tf_op jit(solution)/shard_map/ppermute | solution.py:295
  18.1 0.0 collective-permute-done.4.before_ref
  18.1 0.0 copy-done
  18.1 0.0 copy-start.2
  18.1 8.6 %colours.1 = bf16[16,3,16,1024]{3,2,1,0:T(8,128)(2,1)} custom-call(f32[4,256,1024]{2,1,0:T(8,128)S(1)} %get-tuple-element.24.vol, s32[4,256,1024]{2,1,0:T(8,128)S(1)} %get-tuple-element.25.idx, s16[256,1024]{1,0:T(8,128)(2,1)S(1)} %collective-permute-done.3.after_ref, s16[256,1024]{1,0:T(8,128)(2,1)S(1)} %collective-permute-done.4.before_ref, ...), custom_call_target="tpu_custom_call" | custom-call | flops 52428800 | bytes 41943040 | tf_op jit(solution)/shard_map/colours/pallas_call | solution.py:158
  26.7 0.0 collective-permute-done.refs_1_
  26.7 0.0 collective-permute-done.1.refs_2_
  26.7 0.0 collective-permute-done.2.refs_3_
  26.7 6.2 %all-to-all-start = ((bf16[16,3,16,1024]{3,2,1,0:T(8,128)(2,1)}), bf16[16,3,16,1024]{3,2,1,0:T(8,128)(2,1)S(1)}, u32[]{:S(2)}, u32[]{:S(2)}) async-start(bf16[16,3,16,1024]{3,2,1,0:T(8,128)(2,1)} %colours.1), calls=%async_computation | async-start | bytes 3145728 | tf_op jit(solution)/shard_map/all_to_all | solution.py:250
  32.9 0.4 collective-permute-start.5
  33.3 1.2 %collective-permute-start.6 = (bf16[4,16,1024]{2,1,0:T(8,128)(2,1)S(1)}, bf16[4,16,1024]{2,1,0:T(8,128)(2,1)S(1)}, u32[]{:S(2)}, u32[]{:S(2)}) collective-permute-start(bf16[4,16,1024]{2,1,0:T(8,128)(2,1)S(1)} %get-tuple-element.35), channel_id=1, source_target_pairs={{0,2},{1,3},{2,0},{3,1},{4,6},{5,7},{6,4},{7,5},{8,10},{9,11},{10,... | collective-permute-start | bytes 393224 | tf_op jit(solution)/shard_map/ppermute | solution.py:308
  34.5 0.6 collective-permute-start.7
  35.1 0.0 collective-permute-done.5.rest_1_
  35.1 9.0 %collective-permute-done.6.rest_2_ = bf16[4,16,1024]{2,1,0:T(8,128)(2,1)S(1)} collective-permute-done((bf16[4,16,1024]{2,1,0:T(8,128)(2,1)S(1)}, bf16[4,16,1024]{2,1,0:T(8,128)(2,1)S(1)}, u32[]{:S(2)}, u32[]{:S(2)}) %collective-permute-start.6) | collective-permute-done | bytes 131104 | tf_op jit(solution)/shard_map/ppermute | solution.py:308
  44.1 6.5 %collective-permute-done.7.rest_3_ = bf16[4,16,1024]{2,1,0:T(8,128)(2,1)S(1)} collective-permute-done((bf16[4,16,1024]{2,1,0:T(8,128)(2,1)S(1)}, bf16[4,16,1024]{2,1,0:T(8,128)(2,1)S(1)}, u32[]{:S(2)}, u32[]{:S(2)}) %collective-permute-start.7) | collective-permute-done | bytes 131104 | tf_op jit(solution)/shard_map/ppermute | solution.py:308
  50.6 17.8 %all-to-all-done.colour_ref = bf16[16,3,16,1024]{3,2,1,0:T(8,128)(2,1)S(1)} async-done(((bf16[16,3,16,1024]{3,2,1,0:T(8,128)(2,1)}), bf16[16,3,16,1024]{3,2,1,0:T(8,128)(2,1)S(1)}, u32[]{:S(2)}, u32[]{:S(2)}) %all-to-all-start) | async-done | bytes 1572896 | tf_op jit(solution)/shard_map/all_to_all | solution.py:250
  68.3 0.0 copy-done.2
  68.3 1.8 %blend.1 = f32[4,16,1024]{2,1,0:T(8,128)} custom-call(s32[16]{0:T(128)S(1)} %copy-done.2, bf16[16,3,16,1024]{3,2,1,0:T(8,128)(2,1)S(1)} %all-to-all-done.colour_ref, bf16[4,16,1024]{2,1,0:T(8,128)(2,1)S(1)} %get-tuple-element.33.rest_0_, bf16[4,16,1024]{2,1,0:T(8,128)(2,1)S(1)} %collective-permute-done.5.rest_1_, ...), custom_call_target="tpu_custom_call" | custom-call | tf_op jit(solution)/shard_map/blend/pallas_call | solution.py:215
  (1 shorter events, 0.0 us)
Async XLA Ops:
  0.0 7.3 %copy-start.1 = (f32[8]{0:T(128)S(1)}, f32[8]{0:T(128)}, u32[]{:S(2)}) copy-start(f32[8]{0:T(128)} %opacity_ref.3) | copy-start | bytes 100
  1.6 16.5 %collective-permute-start.3 = (s16[256,1024]{1,0:T(8,128)(2,1)S(1)}, s16[256,1024]{1,0:T(8,128)(2,1)S(1)}, u32[]{:S(2)}, u32[]{:S(2)}) collective-permute-start(s16[256,1024]{1,0:T(8,128)(2,1)S(1)} %get-tuple-element.26), channel_id=1, source_target_pairs={{1,0},{2,1},{3,2},{4,3},{5,4},{6,5},{7,6},{8,7},{9,8},{10,9},{11,1... | collective-permute-start | bytes 1572872 | tf_op jit(solution)/shard_map/ppermute | solution.py:295
  4.2 13.9 %copy-start = (f32[3,8]{1,0:T(4,128)S(1)}, f32[3,8]{1,0:T(4,128)}, u32[]{:S(2)}) copy-start(f32[3,8]{1,0:T(4,128)} %colour_ref.1) | copy-start | bytes 292
  4.2 13.8 %collective-permute-start.4 = (s16[256,1024]{1,0:T(8,128)(2,1)S(1)}, s16[256,1024]{1,0:T(8,128)(2,1)S(1)}, u32[]{:S(2)}, u32[]{:S(2)}) collective-permute-start(s16[256,1024]{1,0:T(8,128)(2,1)S(1)} %get-tuple-element.27), channel_id=1, source_target_pairs={{0,1},{1,2},{2,3},{3,4},{4,5},{5,6},{6,7},{7,8},{8,9},{9,10},{10,1... | collective-permute-start | bytes 1572872 | tf_op jit(solution)/shard_map/ppermute | solution.py:296
  11.8 14.9 %collective-permute-start = (bf16[4,16,1024]{2,1,0:T(8,128)(2,1)S(1)}, bf16[4,16,1024]{2,1,0:T(8,128)(2,1)S(1)}, u32[]{:S(2)}, u32[]{:S(2)}) collective-permute-start(bf16[4,16,1024]{2,1,0:T(8,128)(2,1)S(1)} %get-tuple-element.21), channel_id=1, source_target_pairs={{0,4},{1,5},{2,6},{3,7},{4,8},{5,9},{6,10},{7,11},{8,12},{9,13},{1... | collective-permute-start | bytes 393224 | tf_op jit(solution)/shard_map/ppermute | solution.py:303
  13.1 13.5 %collective-permute-start.1 = (bf16[4,16,1024]{2,1,0:T(8,128)(2,1)S(1)}, bf16[4,16,1024]{2,1,0:T(8,128)(2,1)S(1)}, u32[]{:S(2)}, u32[]{:S(2)}) collective-permute-start(bf16[4,16,1024]{2,1,0:T(8,128)(2,1)S(1)} %get-tuple-element.22), channel_id=1, source_target_pairs={{0,8},{1,9},{2,10},{3,11},{4,12},{5,13},{6,14},{7,15},{8,0},{9,1},... | collective-permute-start | bytes 393224 | tf_op jit(solution)/shard_map/ppermute | solution.py:303
  14.2 12.5 %collective-permute-start.2 = (bf16[4,16,1024]{2,1,0:T(8,128)(2,1)S(1)}, bf16[4,16,1024]{2,1,0:T(8,128)(2,1)S(1)}, u32[]{:S(2)}, u32[]{:S(2)}) collective-permute-start(bf16[4,16,1024]{2,1,0:T(8,128)(2,1)S(1)} %get-tuple-element.23), channel_id=1, source_target_pairs={{0,12},{1,13},{2,14},{3,15},{4,0},{5,1},{6,2},{7,3},{8,4},{9,5},{1... | collective-permute-start | bytes 393224 | tf_op jit(solution)/shard_map/ppermute | solution.py:303
  18.1 50.3 %copy-start.2 = (s32[16]{0:T(128)S(1)}, s32[16]{0:T(128)}, u32[]{:S(2)}) copy-start(s32[16]{0:T(128)} %order_ref.1) | copy-start | bytes 196
  26.7 41.6 %all-to-all-start = ((bf16[16,3,16,1024]{3,2,1,0:T(8,128)(2,1)}), bf16[16,3,16,1024]{3,2,1,0:T(8,128)(2,1)S(1)}, u32[]{:S(2)}, u32[]{:S(2)}) async-start(bf16[16,3,16,1024]{3,2,1,0:T(8,128)(2,1)} %colours.1), calls=%async_computation | async-start | bytes 3145728 | tf_op jit(solution)/shard_map/all_to_all | solution.py:250
  32.9 2.2 %collective-permute-start.5 = (bf16[4,16,1024]{2,1,0:T(8,128)(2,1)S(1)}, bf16[4,16,1024]{2,1,0:T(8,128)(2,1)S(1)}, u32[]{:S(2)}, u32[]{:S(2)}) collective-permute-start(bf16[4,16,1024]{2,1,0:T(8,128)(2,1)S(1)} %get-tuple-element.34), channel_id=1, source_target_pairs={{0,1},{1,0},{2,3},{3,2},{4,5},{5,4},{6,7},{7,6},{8,9},{9,8},{10,11... | collective-permute-start | bytes 393224 | tf_op jit(solution)/shard_map/ppermute | solution.py:308
  33.3 10.8 %collective-permute-start.6 = (bf16[4,16,1024]{2,1,0:T(8,128)(2,1)S(1)}, bf16[4,16,1024]{2,1,0:T(8,128)(2,1)S(1)}, u32[]{:S(2)}, u32[]{:S(2)}) collective-permute-start(bf16[4,16,1024]{2,1,0:T(8,128)(2,1)S(1)} %get-tuple-element.35), channel_id=1, source_target_pairs={{0,2},{1,3},{2,0},{3,1},{4,6},{5,7},{6,4},{7,5},{8,10},{9,11},{10,... | collective-permute-start | bytes 393224 | tf_op jit(solution)/shard_map/ppermute | solution.py:308
  34.5 16.1 %collective-permute-start.7 = (bf16[4,16,1024]{2,1,0:T(8,128)(2,1)S(1)}, bf16[4,16,1024]{2,1,0:T(8,128)(2,1)S(1)}, u32[]{:S(2)}, u32[]{:S(2)}) collective-permute-start(bf16[4,16,1024]{2,1,0:T(8,128)(2,1)S(1)} %get-tuple-element.36), channel_id=1, source_target_pairs={{0,3},{1,2},{2,1},{3,0},{4,7},{5,6},{6,5},{7,4},{8,11},{9,10},{10,... | collective-permute-start | bytes 393224 | tf_op jit(solution)/shard_map/ppermute | solution.py:308

commit v14 on v13

--- a/solution.py
+++ b/solution.py
@@ -11,6 +11,7 @@
 STEPS = 32767.0
 BLOCK = 16
 LANES = 128
+WIDE = 256
 PAD = 8
 NT = 8
 LIMIT = 24 * 1024 * 1024
@@ -197,9 +198,9 @@
         for s in range(turns):
             brick = lax.rem(plane + turns - s, turns) * turns + (member ^ m)
             opacity_ref[brick] = ref[s]
-    for j in range(colour_ref.shape[3] // LANES):
-        cols = pl.ds(j * LANES, LANES)
-        canvas = (jnp.zeros((colour_ref.shape[2], LANES), jnp.float32),) * 4
+    for j in range(colour_ref.shape[3] // WIDE):
+        cols = pl.ds(j * WIDE, WIDE)
+        canvas = (jnp.zeros((colour_ref.shape[2], WIDE), jnp.float32),) * 4
         for rank in range(ranks):
             b = place[rank]
             clear = 1.0 - canvas[3]

time: 71.1 us -> 71 us (level)
  no operation moved by 1% of the time
where the time goes in v14:
time: 71 us; the launch traced here: 70.1 us
  waiting for transfers between devices  35.7 us (50%)
  starting transfers between devices  17.8 us (25%)
  Pallas kernels  16.5 us (23%)
    all_to_all x1, waiting for transfers between devices, exchange(): return lax.all_to_all(x, 'gz', split_axis=0, concat_axis=0, tiled=True)  17.8 us
    ppermute x3, waiting for transfers between devices, shards(): lax.ppermute(part, 'gz', [(i, i ^ m) for i in range(devices)])  15.5 us
    pallas_call x1, Pallas kernels, colours(): pl.pallas_call(functools.partial(colour_kernel, slices, width // LANES),...  8.6 us
    all_to_all x1, starting transfers between devices, exchange(): return lax.all_to_all(x, 'gz', split_axis=0, concat_axis=0, tiled=True)  6.15 us
    pallas_call x1, Pallas kernels, opacities(): pl.pallas_call(functools.partial(opacity_kernel, slices, width // LANES,...  4.52 us
    ppermute x3, starting transfers between devices, shards(): lax.ppermute(part, 'gz', [(i, (i + s * turns) % devices) for i in range(d...  3.83 us
    ppermute x1, starting transfers between devices, shards(): before = lax.ppermute(last, 'gz', up)  3.02 us
    ppermute x1, starting transfers between devices, shards(): after = lax.ppermute(initial, 'gz', down)  2.58 us
  transfers between devices with their start and end apart: 9, of which 4 were waited for; matrix products, arithmetic and copies ran while one was open for 0% of the time, Pallas kernels for 19%

profile of v14, /device:TPU:13, one launch (start us, length us, event | category | flops | bytes accessed | tf_op | source)
XLA Modules:
  0.0 70.1 jit_solution(18164578668956329149)
XLA Ops:
  0.0 0.0 copy-start.1
  0.0 1.6 %coded.1 = (s16[256,1024]{1,0:T(8,128)(2,1)S(1)}, s16[256,1024]{1,0:T(8,128)(2,1)S(1)}) custom-call(f32[4,256,1024]{2,1,0:T(8,128)} %volume_hbm.3), custom_call_target="tpu_custom_call" | custom-call | tf_op jit(solution)/shard_map/coded/pallas_call | solution.py:279
  1.6 2.6 %collective-permute-start.3 = (s16[256,1024]{1,0:T(8,128)(2,1)S(1)}, s16[256,1024]{1,0:T(8,128)(2,1)S(1)}, u32[]{:S(2)}, u32[]{:S(2)}) collective-permute-start(s16[256,1024]{1,0:T(8,128)(2,1)S(1)} %get-tuple-element.26), channel_id=1, source_target_pairs={{1,0},{2,1},{3,2},{4,3},{5,4},{6,5},{7,6},{8,7},{9,8},{10,9},{11,1... | collective-permute-start | bytes 1572872 | tf_op jit(solution)/shard_map/ppermute | solution.py:296
  4.2 0.0 copy-start
  4.2 3.0 %collective-permute-start.4 = (s16[256,1024]{1,0:T(8,128)(2,1)S(1)}, s16[256,1024]{1,0:T(8,128)(2,1)S(1)}, u32[]{:S(2)}, u32[]{:S(2)}) collective-permute-start(s16[256,1024]{1,0:T(8,128)(2,1)S(1)} %get-tuple-element.27), channel_id=1, source_target_pairs={{0,1},{1,2},{2,3},{3,4},{4,5},{5,6},{6,7},{7,8},{8,9},{9,10},{10,1... | collective-permute-start | bytes 1572872 | tf_op jit(solution)/shard_map/ppermute | solution.py:297
  7.3 0.0 copy-done.1
  7.3 4.5 %opacities.1 = (bf16[4,16,1024]{2,1,0:T(8,128)(2,1)S(1)}, bf16[4,16,1024]{2,1,0:T(8,128)(2,1)S(1)}, bf16[4,16,1024]{2,1,0:T(8,128)(2,1)S(1)}, bf16[4,16,1024]{2,...) custom-call(f32[4,256,1024]{2,1,0:T(8,128)} %volume_hbm.3, s32[4,256,1024]{2,1,0:T(8,128)} %index_hbm.1, ...), custom_call_target="tpu_custom_call" | custom-call | flops 15728640 | bytes 9437184 | tf_op jit(solution)/shard_map/opacities/pallas_call | solution.py:80
  11.8 1.3 %collective-permute-start = (bf16[4,16,1024]{2,1,0:T(8,128)(2,1)S(1)}, bf16[4,16,1024]{2,1,0:T(8,128)(2,1)S(1)}, u32[]{:S(2)}, u32[]{:S(2)}) collective-permute-start(bf16[4,16,1024]{2,1,0:T(8,128)(2,1)S(1)} %get-tuple-element.21), channel_id=1, source_target_pairs={{0,4},{1,5},{2,6},{3,7},{4,8},{5,9},{6,10},{7,11},{8,12},{9,13},{1... | collective-permute-start | bytes 393224 | tf_op jit(solution)/shard_map/ppermute | solution.py:304
  13.1 1.1 %collective-permute-start.1 = (bf16[4,16,1024]{2,1,0:T(8,128)(2,1)S(1)}, bf16[4,16,1024]{2,1,0:T(8,128)(2,1)S(1)}, u32[]{:S(2)}, u32[]{:S(2)}) collective-permute-start(bf16[4,16,1024]{2,1,0:T(8,128)(2,1)S(1)} %get-tuple-element.22), channel_id=1, source_target_pairs={{0,8},{1,9},{2,10},{3,11},{4,12},{5,13},{6,14},{7,15},{8,0},{9,1},... | collective-permute-start | bytes 393224 | tf_op jit(solution)/shard_map/ppermute | solution.py:304
  14.2 1.4 %collective-permute-start.2 = (bf16[4,16,1024]{2,1,0:T(8,128)(2,1)S(1)}, bf16[4,16,1024]{2,1,0:T(8,128)(2,1)S(1)}, u32[]{:S(2)}, u32[]{:S(2)}) collective-permute-start(bf16[4,16,1024]{2,1,0:T(8,128)(2,1)S(1)} %get-tuple-element.23), channel_id=1, source_target_pairs={{0,12},{1,13},{2,14},{3,15},{4,0},{5,1},{6,2},{7,3},{8,4},{9,5},{1... | collective-permute-start | bytes 393224 | tf_op jit(solution)/shard_map/ppermute | solution.py:304
  15.6 2.5 %collective-permute-done.3.after_ref = s16[256,1024]{1,0:T(8,128)(2,1)S(1)} collective-permute-done((s16[256,1024]{1,0:T(8,128)(2,1)S(1)}, s16[256,1024]{1,0:T(8,128)(2,1)S(1)}, u32[]{:S(2)}, u32[]{:S(2)}) %collective-permute-start.3) | collective-permute-done | bytes 524320 | tf_op jit(solution)/shard_map/ppermute | solution.py:296
  18.1 0.0 collective-permute-done.4.before_ref
  18.1 0.0 copy-done
  18.1 0.0 copy-start.2
  18.1 8.6 %colours.1 = bf16[16,3,16,1024]{3,2,1,0:T(8,128)(2,1)} custom-call(f32[4,256,1024]{2,1,0:T(8,128)S(1)} %get-tuple-element.24.vol, s32[4,256,1024]{2,1,0:T(8,128)S(1)} %get-tuple-element.25.idx, s16[256,1024]{1,0:T(8,128)(2,1)S(1)} %collective-permute-done.3.after_ref, s16[256,1024]{1,0:T(8,128)(2,1)S(1)} %collective-permute-done.4.before_ref, ...), custom_call_target="tpu_custom_call" | custom-call | flops 52428800 | bytes 41943040 | tf_op jit(solution)/shard_map/colours/pallas_call | solution.py:159
  26.7 0.0 collective-permute-done.refs_1_
  26.7 0.0 collective-permute-done.1.refs_2_
  26.7 0.0 collective-permute-done.2.refs_3_
  26.7 6.2 %all-to-all-start = ((bf16[16,3,16,1024]{3,2,1,0:T(8,128)(2,1)}), bf16[16,3,16,1024]{3,2,1,0:T(8,128)(2,1)S(1)}, u32[]{:S(2)}, u32[]{:S(2)}) async-start(bf16[16,3,16,1024]{3,2,1,0:T(8,128)(2,1)} %colours.1), calls=%async_computation | async-start | bytes 3145728 | tf_op jit(solution)/shard_map/all_to_all | solution.py:251
  32.9 0.4 collective-permute-start.5
  33.3 1.2 %collective-permute-start.6 = (bf16[4,16,1024]{2,1,0:T(8,128)(2,1)S(1)}, bf16[4,16,1024]{2,1,0:T(8,128)(2,1)S(1)}, u32[]{:S(2)}, u32[]{:S(2)}) collective-permute-start(bf16[4,16,1024]{2,1,0:T(8,128)(2,1)S(1)} %get-tuple-element.35), channel_id=1, source_target_pairs={{0,2},{1,3},{2,0},{3,1},{4,6},{5,7},{6,4},{7,5},{8,10},{9,11},{10,... | collective-permute-start | bytes 393224 | tf_op jit(solution)/shard_map/ppermute | solution.py:309
  34.5 0.6 collective-permute-start.7
  35.1 0.0 collective-permute-done.5.rest_1_
  35.1 9.0 %collective-permute-done.6.rest_2_ = bf16[4,16,1024]{2,1,0:T(8,128)(2,1)S(1)} collective-permute-done((bf16[4,16,1024]{2,1,0:T(8,128)(2,1)S(1)}, bf16[4,16,1024]{2,1,0:T(8,128)(2,1)S(1)}, u32[]{:S(2)}, u32[]{:S(2)}) %collective-permute-start.6) | collective-permute-done | bytes 131104 | tf_op jit(solution)/shard_map/ppermute | solution.py:309
  44.1 6.5 %collective-permute-done.7.rest_3_ = bf16[4,16,1024]{2,1,0:T(8,128)(2,1)S(1)} collective-permute-done((bf16[4,16,1024]{2,1,0:T(8,128)(2,1)S(1)}, bf16[4,16,1024]{2,1,0:T(8,128)(2,1)S(1)}, u32[]{:S(2)}, u32[]{:S(2)}) %collective-permute-start.7) | collective-permute-done | bytes 131104 | tf_op jit(solution)/shard_map/ppermute | solution.py:309
  50.6 17.8 %all-to-all-done.colour_ref = bf16[16,3,16,1024]{3,2,1,0:T(8,128)(2,1)S(1)} async-done(((bf16[16,3,16,1024]{3,2,1,0:T(8,128)(2,1)}), bf16[16,3,16,1024]{3,2,1,0:T(8,128)(2,1)S(1)}, u32[]{:S(2)}, u32[]{:S(2)}) %all-to-all-start) | async-done | bytes 1572896 | tf_op jit(solution)/shard_map/all_to_all | solution.py:251
  68.3 0.0 copy-done.2
  68.3 1.7 %blend.1 = f32[4,16,1024]{2,1,0:T(8,128)} custom-call(s32[16]{0:T(128)S(1)} %copy-done.2, bf16[16,3,16,1024]{3,2,1,0:T(8,128)(2,1)S(1)} %all-to-all-done.colour_ref, bf16[4,16,1024]{2,1,0:T(8,128)(2,1)S(1)} %get-tuple-element.33.rest_0_, bf16[4,16,1024]{2,1,0:T(8,128)(2,1)S(1)} %collective-permute-done.5.rest_1_, ...), custom_call_target="tpu_custom_call" | custom-call | tf_op jit(solution)/shard_map/blend/pallas_call | solution.py:216
  (1 shorter events, 0.0 us)
Async XLA Ops:
  0.0 7.3 %copy-start.1 = (f32[8]{0:T(128)S(1)}, f32[8]{0:T(128)}, u32[]{:S(2)}) copy-start(f32[8]{0:T(128)} %opacity_ref.3) | copy-start | bytes 100
  1.6 16.5 %collective-permute-start.3 = (s16[256,1024]{1,0:T(8,128)(2,1)S(1)}, s16[256,1024]{1,0:T(8,128)(2,1)S(1)}, u32[]{:S(2)}, u32[]{:S(2)}) collective-permute-start(s16[256,1024]{1,0:T(8,128)(2,1)S(1)} %get-tuple-element.26), channel_id=1, source_target_pairs={{1,0},{2,1},{3,2},{4,3},{5,4},{6,5},{7,6},{8,7},{9,8},{10,9},{11,1... | collective-permute-start | bytes 1572872 | tf_op jit(solution)/shard_map/ppermute | solution.py:296
  4.2 13.9 %copy-start = (f32[3,8]{1,0:T(4,128)S(1)}, f32[3,8]{1,0:T(4,128)}, u32[]{:S(2)}) copy-start(f32[3,8]{1,0:T(4,128)} %colour_ref.1) | copy-start | bytes 292
  4.2 13.8 %collective-permute-start.4 = (s16[256,1024]{1,0:T(8,128)(2,1)S(1)}, s16[256,1024]{1,0:T(8,128)(2,1)S(1)}, u32[]{:S(2)}, u32[]{:S(2)}) collective-permute-start(s16[256,1024]{1,0:T(8,128)(2,1)S(1)} %get-tuple-element.27), channel_id=1, source_target_pairs={{0,1},{1,2},{2,3},{3,4},{4,5},{5,6},{6,7},{7,8},{8,9},{9,10},{10,1... | collective-permute-start | bytes 1572872 | tf_op jit(solution)/shard_map/ppermute | solution.py:297
  11.8 14.9 %collective-permute-start = (bf16[4,16,1024]{2,1,0:T(8,128)(2,1)S(1)}, bf16[4,16,1024]{2,1,0:T(8,128)(2,1)S(1)}, u32[]{:S(2)}, u32[]{:S(2)}) collective-permute-start(bf16[4,16,1024]{2,1,0:T(8,128)(2,1)S(1)} %get-tuple-element.21), channel_id=1, source_target_pairs={{0,4},{1,5},{2,6},{3,7},{4,8},{5,9},{6,10},{7,11},{8,12},{9,13},{1... | collective-permute-start | bytes 393224 | tf_op jit(solution)/shard_map/ppermute | solution.py:304
  13.1 13.5 %collective-permute-start.1 = (bf16[4,16,1024]{2,1,0:T(8,128)(2,1)S(1)}, bf16[4,16,1024]{2,1,0:T(8,128)(2,1)S(1)}, u32[]{:S(2)}, u32[]{:S(2)}) collective-permute-start(bf16[4,16,1024]{2,1,0:T(8,128)(2,1)S(1)} %get-tuple-element.22), channel_id=1, source_target_pairs={{0,8},{1,9},{2,10},{3,11},{4,12},{5,13},{6,14},{7,15},{8,0},{9,1},... | collective-permute-start | bytes 393224 | tf_op jit(solution)/shard_map/ppermute | solution.py:304
  14.2 12.5 %collective-permute-start.2 = (bf16[4,16,1024]{2,1,0:T(8,128)(2,1)S(1)}, bf16[4,16,1024]{2,1,0:T(8,128)(2,1)S(1)}, u32[]{:S(2)}, u32[]{:S(2)}) collective-permute-start(bf16[4,16,1024]{2,1,0:T(8,128)(2,1)S(1)} %get-tuple-element.23), channel_id=1, source_target_pairs={{0,12},{1,13},{2,14},{3,15},{4,0},{5,1},{6,2},{7,3},{8,4},{9,5},{1... | collective-permute-start | bytes 393224 | tf_op jit(solution)/shard_map/ppermute | solution.py:304
  18.1 50.3 %copy-start.2 = (s32[16]{0:T(128)S(1)}, s32[16]{0:T(128)}, u32[]{:S(2)}) copy-start(s32[16]{0:T(128)} %order_ref.1) | copy-start | bytes 196
  26.7 41.6 %all-to-all-start = ((bf16[16,3,16,1024]{3,2,1,0:T(8,128)(2,1)}), bf16[16,3,16,1024]{3,2,1,0:T(8,128)(2,1)S(1)}, u32[]{:S(2)}, u32[]{:S(2)}) async-start(bf16[16,3,16,1024]{3,2,1,0:T(8,128)(2,1)} %colours.1), calls=%async_computation | async-start | bytes 3145728 | tf_op jit(solution)/shard_map/all_to_all | solution.py:251
  32.9 2.2 %collective-permute-start.5 = (bf16[4,16,1024]{2,1,0:T(8,128)(2,1)S(1)}, bf16[4,16,1024]{2,1,0:T(8,128)(2,1)S(1)}, u32[]{:S(2)}, u32[]{:S(2)}) collective-permute-start(bf16[4,16,1024]{2,1,0:T(8,128)(2,1)S(1)} %get-tuple-element.34), channel_id=1, source_target_pairs={{0,1},{1,0},{2,3},{3,2},{4,5},{5,4},{6,7},{7,6},{8,9},{9,8},{10,11... | collective-permute-start | bytes 393224 | tf_op jit(solution)/shard_map/ppermute | solution.py:309
  33.3 10.8 %collective-permute-start.6 = (bf16[4,16,1024]{2,1,0:T(8,128)(2,1)S(1)}, bf16[4,16,1024]{2,1,0:T(8,128)(2,1)S(1)}, u32[]{:S(2)}, u32[]{:S(2)}) collective-permute-start(bf16[4,16,1024]{2,1,0:T(8,128)(2,1)S(1)} %get-tuple-element.35), channel_id=1, source_target_pairs={{0,2},{1,3},{2,0},{3,1},{4,6},{5,7},{6,4},{7,5},{8,10},{9,11},{10,... | collective-permute-start | bytes 393224 | tf_op jit(solution)/shard_map/ppermute | solution.py:309
  34.5 16.1 %collective-permute-start.7 = (bf16[4,16,1024]{2,1,0:T(8,128)(2,1)S(1)}, bf16[4,16,1024]{2,1,0:T(8,128)(2,1)S(1)}, u32[]{:S(2)}, u32[]{:S(2)}) collective-permute-start(bf16[4,16,1024]{2,1,0:T(8,128)(2,1)S(1)} %get-tuple-element.36), channel_id=1, source_target_pairs={{0,3},{1,2},{2,1},{3,0},{4,7},{5,6},{6,5},{7,4},{8,11},{9,10},{10,... | collective-permute-start | bytes 393224 | tf_op jit(solution)/shard_map/ppermute | solution.py:309
